TPU v7x, 32 devices: a whole 2x2x4 slice. The times are simulated.
32 devices in a mesh: dp: 8 (over z, x), mlp: 4 (over y, core).
Axes of the slice: x: 2, y: 2, z: 4, core: 2. Of those that a mesh axis runs over, the one named last changes fastest.
Arguments:
- clean_patches: float32 [8192, 16], P(('dp', 'mlp')), may hold values from -6 to 6
- noise_patches: float32 [8192, 16], P(('dp', 'mlp')), may hold values from -6 to 6
- patch_grid: int32 [32, 2], P(('dp', 'mlp')), may hold values from 1 to 16, as said below
- labels: int32 [32], P(('dp', 'mlp')), may hold values from 0 to 1000
- timesteps: int32 [32], P(('dp', 'mlp')), may hold values from 20 to 999
- matrices: float32 [1152, 15008], P('dp'), may hold values from -0.94280904 to 0.94280904
- embeddings: float32 [1273, 1152], P(None, 'dp'), may hold values from -4 to 4
- swiglu_weights: float32 [3, 1152, 3072], P(None, 'dp', 'mlp'), may hold values from -0.1875 to 0.1875
- biases: float32 [17312], replicated, may hold values from -1 to 3
- matrices_first: float32 [1152, 15008], P('dp'), may hold values from -0.00012207031 to 0.00012207031
- embeddings_first: float32 [1273, 1152], P(None, 'dp'), may hold values from -0.00012207031 to 0.00012207031
- swiglu_first: float32 [3, 1152, 3072], P(None, 'dp', 'mlp'), may hold values from -0.00012207031 to 0.00012207031
- biases_first: float32 [17312], replicated, may hold values from -0.00030517578 to 0.00030517578
- matrices_second: float32 [1152, 15008], P('dp'), may hold values from 3.4025345e-11 to 1.3610138e-10
- embeddings_second: float32 [1273, 1152], P(None, 'dp'), may hold values from 3.4025345e-11 to 1.3610138e-10
- swiglu_second: float32 [3, 1152, 3072], P(None, 'dp', 'mlp'), may hold values from 3.4025345e-11 to 1.3610138e-10
- biases_second: float32 [17312], replicated, may hold values from 2.7220276e-10 to 1.088811e-09
- matrices_average: float32 [1152, 15008], P('dp'), may hold values from -0.1875 to 0.1875
- embeddings_average: float32 [1273, 1152], P(None, 'dp'), may hold values from -3 to 3
- swiglu_average: float32 [3, 1152, 3072], P(None, 'dp', 'mlp'), may hold values from -0.1875 to 0.1875
- biases_average: float32 [17312], replicated, may hold values from -1.75 to 1.75
Outputs:
- loss_sum: float32 [], replicated
- grad_norm: float32 [], replicated
- matrices_new: float32 [1152, 15008], P('dp')
- embeddings_new: float32 [1273, 1152], P(None, 'dp')
- swiglu_new: float32 [3, 1152, 3072], P(None, 'dp', 'mlp')
- biases_new: float32 [17312], replicated
- matrices_first_new: float32 [1152, 15008], P('dp')
- embeddings_first_new: float32 [1273, 1152], P(None, 'dp')
- swiglu_first_new: float32 [3, 1152, 3072], P(None, 'dp', 'mlp')
- biases_first_new: float32 [17312], replicated
- matrices_second_new: float32 [1152, 15008], P('dp')
- embeddings_second_new: float32 [1273, 1152], P(None, 'dp')
- swiglu_second_new: float32 [3, 1152, 3072], P(None, 'dp', 'mlp')
- biases_second_new: float32 [17312], replicated
- matrices_average_new: float32 [1152, 15008], P('dp')
- embeddings_average_new: float32 [1273, 1152], P(None, 'dp')
- swiglu_average_new: float32 [3, 1152, 3072], P(None, 'dp', 'mlp')
- biases_average_new: float32 [17312], replicated
- biases_grad: float32 [17312], replicated
Inputs may be any that keep to these rules, and one draw needn't show every extreme that they name: `patch_grid`: patch rows and columns of each image; the last image of the batch is 16 x 16. `labels`: label 1000 is the null class.
All inputs are finite; a program needn't handle non-finite values.
Results may differ from a plain program's by a relative error of at most 0.012.
Values may be sent and summed in bfloat16 or wider, within the bound.
A program may use at most 320 MiB of HBM per device.

v0:
```python
import math

import jax
import jax.numpy as jnp
from jax import lax
from jax.sharding import PartitionSpec as P

HEADS = 16
HDIM = 72
D = 1152
CH = 16
CLASSES = 1000
FREQ = 256
STEP = 10


CLIP_LIMIT = 1.0
LEARN_RATE = 0.03
TABLE_RATE = 0.4
FIRST_DECAY = 0.9
SECOND_DECAY = 0.999
ADAM_EPSILON = 1e-08
WEIGHT_DECAY = 0.01
AVERAGE_DECAY = 0.9999


def cut_along(value, dim, count):
    dims = value.shape
    blocks = value.reshape(*dims[:dim], count, dims[dim] // count, *dims[dim + 1 :])
    return jnp.moveaxis(blocks, dim, 0)


def sum_at_owner(value, axis, dim):
    blocks = cut_along(value, dim, lax.axis_size(axis))
    arrived = lax.all_to_all(blocks, axis, split_axis=0, concat_axis=0, tiled=True)
    return arrived.astype(jnp.float32).sum(axis=0)


def plan(steps_in):
    step_index = jnp.arange(1000, dtype=jnp.int32)
    beta_table = 0.0001 + (0.02 - 0.0001) * step_index.astype(jnp.float32) / 999.0
    logbar = jnp.cumsum(jnp.log1p(-beta_table))

    def lookup(values, wanted):
        return jnp.sum(
            jnp.where(wanted[:, None] == step_index[None, :], values[None, :], 0.0), axis=1
        )

    return (
        lookup(beta_table, steps_in),
        jnp.exp(lookup(logbar, steps_in)),
        jnp.exp(lookup(logbar, steps_in - 1)),
    )


def sinusoid(steps_in):
    halfway = FREQ // 2
    frequency = jnp.exp(-math.log(10000.0) * jnp.arange(halfway, dtype=jnp.float32) / halfway)
    angles = steps_in.astype(jnp.float32)[:, None] * frequency[None, :]
    return jnp.concatenate([jnp.cos(angles), jnp.sin(angles)], axis=1)


def places(patch_grid, length):
    slot_index = jnp.arange(length, dtype=jnp.int32)[None, :]
    grid_rows = patch_grid[:, 0:1]
    grid_cols = patch_grid[:, 1:2]
    valid_slot = slot_index < grid_rows * grid_cols
    row_place = (slot_index // grid_cols).astype(jnp.float32)
    col_place = (slot_index % grid_cols).astype(jnp.float32)
    quarter = HDIM // 4
    frequency = jnp.exp(-math.log(10000.0) * jnp.arange(quarter, dtype=jnp.float32) / quarter)
    row_angle = row_place[..., None] * frequency
    col_angle = col_place[..., None] * frequency
    return (
        (jnp.cos(row_angle), jnp.sin(row_angle), jnp.cos(col_angle), jnp.sin(col_angle)),
        valid_slot,
    )


def rotate(values, tables):
    cos_row, sin_row, cos_col, sin_col = tables
    quarter = HDIM // 4

    def turn(halfpart, cosine, sine_part):
        first = halfpart[..., :quarter]
        second = halfpart[..., quarter:]
        cosine = cosine[:, :, None, :]
        sine_part = sine_part[:, :, None, :]
        return jnp.concatenate(
            [first * cosine - second * sine_part, first * sine_part + second * cosine], axis=-1
        )

    return jnp.concatenate(
        [
            turn(values[..., : 2 * quarter], cos_row, sin_row),
            turn(values[..., 2 * quarter :], cos_col, sin_col),
        ],
        axis=-1,
    )


def modulate(hidden, shift_by, scale_by):
    row_mean = jnp.mean(hidden, axis=-1, keepdims=True)
    centered = hidden - row_mean
    variance = jnp.mean(centered * centered, axis=-1, keepdims=True)
    return (
        centered * lax.rsqrt(variance + 1e-06) * (1.0 + scale_by[:, None, :]) + shift_by[:, None, :]
    )


def noisy_input(clean_patches, noise_patches, steps_in):
    beta_now, bar_now, bar_prev = plan(steps_in)
    bar_now = bar_now[:, None, None]
    return jnp.sqrt(bar_now) * clean_patches + jnp.sqrt(1.0 - bar_now) * noise_patches


def loss_terms(output, clean_patches, noise_patches, steps_in, valid_slot):
    beta_now, bar_now, bar_prev = plan(steps_in)
    beta_now = beta_now[:, None, None]
    bar_now = bar_now[:, None, None]
    bar_prev = bar_prev[:, None, None]
    noisy = jnp.sqrt(bar_now) * clean_patches + jnp.sqrt(1.0 - bar_now) * noise_patches
    eps_pred = output[..., :CH]
    var_raw = output[..., CH:]
    squared = jnp.sum((eps_pred - noise_patches) ** 2, axis=-1)
    post_log = jnp.log(beta_now * (1.0 - bar_prev) / (1.0 - bar_now))
    fraction = (var_raw + 1.0) * 0.5
    model_log = fraction * jnp.log(beta_now) + (1.0 - fraction) * post_log
    coefficient = beta_now * jnp.sqrt(bar_prev) / (1.0 - bar_now)
    start_est = (noisy - jnp.sqrt(1.0 - bar_now) * eps_pred) / jnp.sqrt(bar_now)
    mean_gap = coefficient * (clean_patches - start_est)
    divergence = (
        0.5
        * (
            -1.0
            + model_log
            - post_log
            + jnp.exp(post_log - model_log)
            + mean_gap * mean_gap * jnp.exp(-model_log)
        )
        / math.log(2.0)
    )
    return jnp.sum(jnp.where(valid_slot, squared + jnp.sum(divergence, axis=-1), 0.0))


def adam_step(weight, first, second, gradient, average, factor, rate):
    average_decay = min(AVERAGE_DECAY, (1.0 + STEP) / (10.0 + STEP))
    clipped = gradient * factor
    first = FIRST_DECAY * first + (1.0 - FIRST_DECAY) * clipped
    second = SECOND_DECAY * second + (1.0 - SECOND_DECAY) * clipped * clipped
    ratio = (
        first
        / (1.0 - FIRST_DECAY**STEP)
        / (jnp.sqrt(second / (1.0 - SECOND_DECAY**STEP)) + ADAM_EPSILON)
    )
    weight = weight - rate * (ratio + WEIGHT_DECAY * weight)
    return (weight, first, second, average_decay * average + (1.0 - average_decay) * weight)


def backward_product(gradient, weight):
    return lax.dot_general(
        gradient,
        weight,
        (((gradient.ndim - 1,), (1,)), ((), ())),
        preferred_element_type=jnp.float32,
    )


def weight_grad(inputs, gradient):
    flat_in = inputs.reshape(-1, inputs.shape[-1])
    flat_grad = gradient.reshape(-1, gradient.shape[-1])
    return lax.dot_general(
        flat_in, flat_grad, (((0,), (0,)), ((), ())), preferred_element_type=jnp.float32
    )


def column_sum(gradient):
    return jnp.sum(gradient.astype(jnp.float32).reshape(-1, gradient.shape[-1]), axis=0)


def attention_scores(queries, keys_in, valid_slot):
    scores = jnp.einsum(
        "bqhd,bkhd->bhqk", queries, keys_in, preferred_element_type=jnp.float32
    ) / math.sqrt(HDIM)
    return jnp.where(valid_slot[:, None, None, :], scores, -1e30)


def cut_columns(values, start, amount):
    return lax.dynamic_slice_in_dim(values, start, amount, 1)


def on_device(
    clean_patches,
    noise_patches,
    patch_grid,
    labels,
    timesteps,
    matrices,
    embeddings,
    swiglu_weights,
    biases,
    matrices_first,
    embeddings_first,
    swiglu_first,
    biases_first,
    matrices_second,
    embeddings_second,
    swiglu_second,
    biases_second,
    matrices_average,
    embeddings_average,
    swiglu_average,
    biases_average,
):
    bfloat = jnp.bfloat16
    single = jnp.float32
    images = labels.shape[0]
    length = clean_patches.shape[0] // images
    row_total = images * length
    n_model = lax.axis_size("mlp")
    n_data = lax.axis_size("dp")
    total_images = images * n_data * n_model
    rows_owned = D // n_data
    owned_start = lax.axis_index("dp") * rows_owned
    model_index = lax.axis_index("mlp")
    mats_all, embed_all, swiglu_use = (
        lax.all_gather(matrices.astype(bfloat), "dp", axis=0, tiled=True),
        lax.all_gather(embeddings.astype(bfloat), "dp", axis=1, tiled=True),
        lax.all_gather(swiglu_weights.astype(bfloat), "dp", axis=1, tiled=True),
    )
    time_second = mats_all[:, :D]
    mod_weight = mats_all[:, D : 9 * D]
    qkv_weight = mats_all[:, 9 * D : 12 * D]
    out_weight = mats_all[:, 12 * D : 13 * D]
    final_weight = mats_all[:, 13 * D :]
    patch_weight = embed_all[:CH]
    time_first = embed_all[CH : CH + FREQ]
    class_table = embed_all[CH + FREQ :]
    patch_bias = biases[:D]
    first_bias = biases[D : 2 * D]
    second_bias = biases[2 * D : 3 * D]
    mod_bias = biases[3 * D : 11 * D]
    qkv_bias = biases[11 * D : 14 * D]
    out_bias = biases[14 * D : 15 * D]
    final_bias = biases[15 * D :]
    sinus_emb = sinusoid(timesteps).astype(bfloat)
    time_pre = jnp.dot(sinus_emb, time_first, preferred_element_type=single) + first_bias
    time_act = jax.nn.silu(time_pre).astype(bfloat)
    time_emb = jnp.dot(time_act, time_second, preferred_element_type=single) + second_bias
    onehot = (labels[:, None] == jnp.arange(CLASSES + 1, dtype=jnp.int32)[None, :]).astype(single)
    condition = time_emb + jnp.dot(
        onehot.astype(bfloat), class_table, preferred_element_type=single
    )
    cond_act = jax.nn.silu(condition).astype(bfloat)
    modulation = jnp.dot(cond_act, mod_weight, preferred_element_type=single) + mod_bias
    shift_one, scale_one, gate_one, shift_two, scale_two, gate_two, shift_end, scale_end = (
        jnp.split(modulation, 8, axis=1)
    )
    tables, valid_slot = places(patch_grid, length)
    clean_three = clean_patches.reshape(images, length, CH)
    noise_three = noise_patches.reshape(images, length, CH)
    noisy_low = noisy_input(clean_three, noise_three, timesteps).astype(bfloat)
    hidden = jnp.dot(noisy_low, patch_weight, preferred_element_type=single) + patch_bias
    normed_one = modulate(hidden, shift_one, scale_one).astype(bfloat)
    qkv = (jnp.dot(normed_one, qkv_weight, preferred_element_type=single) + qkv_bias).reshape(
        images, length, 3, HEADS, HDIM
    )
    queries = rotate(qkv[:, :, 0], tables).astype(bfloat)
    keys_in = rotate(qkv[:, :, 1], tables).astype(bfloat)
    values = qkv[:, :, 2].astype(bfloat)
    masked = attention_scores(queries, keys_in, valid_slot)
    row_max = jnp.max(masked, axis=-1, keepdims=True)
    exponent = jnp.exp(masked - row_max)
    row_total_exp = jnp.sum(exponent, axis=-1, keepdims=True)
    attn_probs = exponent / row_total_exp
    log_total = row_max + jnp.log(row_total_exp)
    attended = (
        jnp.einsum(
            "bhqk,bkhd->bqhd", attn_probs.astype(bfloat), values, preferred_element_type=single
        )
        .astype(bfloat)
        .reshape(images, length, D)
    )
    branch = jnp.dot(attended, out_weight, preferred_element_type=single) + out_bias
    hidden_mid = hidden + gate_one[:, None, :] * branch
    normed_two = modulate(hidden_mid, shift_two, scale_two).astype(bfloat)
    rows_ready = lax.all_gather(normed_two.reshape(row_total, D), "mlp", axis=0, tiled=True)
    gate_val = jnp.dot(rows_ready, swiglu_use[0], preferred_element_type=single)
    up_val = jnp.dot(rows_ready, swiglu_use[1], preferred_element_type=single)
    inner_act = (jax.nn.silu(gate_val) * up_val).astype(bfloat)
    mixed = (
        lax.psum_scatter(
            backward_product(inner_act, swiglu_use[2]).astype(jnp.bfloat16),
            "mlp",
            scatter_dimension=0,
            tiled=True,
        )
        .astype(jnp.float32)
        .reshape(images, length, D)
    )
    hidden_end = hidden_mid + gate_two[:, None, :] * mixed
    normed_end = modulate(hidden_end, shift_end, scale_end).astype(bfloat)
    output = jnp.dot(normed_end, final_weight, preferred_element_type=single) + final_bias
    local_loss, loss_pull = jax.vjp(
        lambda values_out: loss_terms(values_out, clean_three, noise_three, timesteps, valid_slot),
        output,
    )
    d_output = loss_pull(jnp.asarray(1.0 / total_images, single))[0].astype(bfloat)
    d_normed_end = backward_product(d_output, final_weight)
    unused, pull_end = jax.vjp(modulate, hidden_end, shift_end, scale_end)
    d_hidden_end, d_shift_end, d_scale_end = pull_end(d_normed_end)
    d_mixed = (gate_two[:, None, :] * d_hidden_end).astype(bfloat)
    d_gate_two = jnp.sum(mixed * d_hidden_end, axis=1)
    dmixed_ready = lax.all_gather(d_mixed.reshape(row_total, D), "mlp", axis=0, tiled=True)
    grad_down = weight_grad(dmixed_ready, inner_act)
    d_inner = jnp.dot(dmixed_ready, swiglu_use[2], preferred_element_type=single)
    unused, pull_glu = jax.vjp(
        lambda gate_in, up_in: jax.nn.silu(gate_in) * up_in, gate_val, up_val
    )
    d_gate, d_up = pull_glu(d_inner)
    d_gate = d_gate.astype(bfloat)
    d_up = d_up.astype(bfloat)
    grad_swiglu = jnp.stack(
        [weight_grad(rows_ready, d_gate), weight_grad(rows_ready, d_up), grad_down]
    )
    d_normed_two = lax.psum_scatter(
        (backward_product(d_gate, swiglu_use[0]) + backward_product(d_up, swiglu_use[1])).astype(
            jnp.bfloat16
        ),
        "mlp",
        scatter_dimension=0,
        tiled=True,
    ).astype(jnp.float32)
    unused, pull_two = jax.vjp(modulate, hidden_mid, shift_two, scale_two)
    d_mid_part, d_shift_two, d_scale_two = pull_two(d_normed_two.reshape(images, length, D))
    d_hidden_mid = d_hidden_end + d_mid_part
    d_branch = (gate_one[:, None, :] * d_hidden_mid).astype(bfloat)
    d_gate_one = jnp.sum(branch * d_hidden_mid, axis=1)
    d_attended = (
        backward_product(d_branch, out_weight).astype(bfloat).reshape(images, length, HEADS, HDIM)
    )
    again_probs = jnp.exp(attention_scores(queries, keys_in, valid_slot) - log_total)
    d_probs = jnp.einsum("bqhd,bkhd->bhqk", d_attended, values, preferred_element_type=single)
    d_scores = (
        again_probs * (d_probs - jnp.sum(again_probs * d_probs, axis=-1, keepdims=True))
    ).astype(bfloat)
    d_queries = jnp.einsum(
        "bhqk,bkhd->bqhd", d_scores, keys_in, preferred_element_type=single
    ) / math.sqrt(HDIM)
    d_keys = jnp.einsum(
        "bhqk,bqhd->bkhd", d_scores, queries, preferred_element_type=single
    ) / math.sqrt(HDIM)
    d_values = jnp.einsum(
        "bhqk,bqhd->bkhd", again_probs.astype(bfloat), d_attended, preferred_element_type=single
    )
    unused, pull_turn = jax.vjp(
        lambda query_raw, key_raw: (rotate(query_raw, tables), rotate(key_raw, tables)),
        qkv[:, :, 0],
        qkv[:, :, 1],
    )
    d_query_raw, d_key_raw = pull_turn((d_queries, d_keys))
    d_qkv = (
        jnp.stack([d_query_raw, d_key_raw, d_values], axis=2)
        .reshape(images, length, 3 * D)
        .astype(bfloat)
    )
    d_normed_one = backward_product(d_qkv, qkv_weight)
    unused, pull_one = jax.vjp(modulate, hidden, shift_one, scale_one)
    d_hidden_part, d_shift_one, d_scale_one = pull_one(d_normed_one)
    d_hidden = (d_hidden_mid + d_hidden_part).astype(bfloat)
    d_modulation = jnp.concatenate(
        [
            d_shift_one,
            d_scale_one,
            d_gate_one,
            d_shift_two,
            d_scale_two,
            d_gate_two,
            d_shift_end,
            d_scale_end,
        ],
        axis=1,
    ).astype(bfloat)
    d_cond_act = backward_product(d_modulation, mod_weight)
    unused, pull_cond = jax.vjp(jax.nn.silu, condition)
    d_condition = pull_cond(d_cond_act)[0]
    d_time_emb = d_condition.astype(bfloat)
    d_time_act = backward_product(d_time_emb, time_second)
    unused, pull_time = jax.vjp(jax.nn.silu, time_pre)
    d_time_pre = pull_time(d_time_act)[0]
    every_image = (
        lax.all_gather(
            time_act.astype(single).astype(jnp.bfloat16), ("dp", "mlp"), axis=0, tiled=True
        ).astype(jnp.float32),
        lax.all_gather(
            d_time_emb.astype(single).astype(jnp.bfloat16), ("dp", "mlp"), axis=0, tiled=True
        ).astype(jnp.float32),
        lax.all_gather(
            cond_act.astype(single).astype(jnp.bfloat16), ("dp", "mlp"), axis=0, tiled=True
        ).astype(jnp.float32),
        lax.all_gather(
            d_modulation.astype(single).astype(jnp.bfloat16), ("dp", "mlp"), axis=0, tiled=True
        ).astype(jnp.float32),
        lax.all_gather(d_condition.astype(jnp.bfloat16), ("dp", "mlp"), axis=0, tiled=True).astype(
            d_condition.dtype
        ),
        lax.all_gather(d_time_pre.astype(jnp.bfloat16), ("dp", "mlp"), axis=0, tiled=True).astype(
            d_time_pre.dtype
        ),
        lax.all_gather(
            sinus_emb.astype(single).astype(jnp.bfloat16), ("dp", "mlp"), axis=0, tiled=True
        ).astype(jnp.float32),
        lax.all_gather(onehot.astype(jnp.bfloat16), ("dp", "mlp"), axis=0, tiled=True).astype(
            onehot.dtype
        ),
    )
    act_time_all, dtime_all, act_cond_all, dmod_all, dcond_all, dpre_all, sinus_all, onehot_all = (
        every_image
    )
    grad_time_second = weight_grad(
        cut_columns(act_time_all, owned_start, rows_owned).astype(bfloat), dtime_all.astype(bfloat)
    )
    grad_mod = weight_grad(
        cut_columns(act_cond_all, owned_start, rows_owned).astype(bfloat), dmod_all.astype(bfloat)
    )
    grad_time_first = jnp.dot(
        sinus_all.T,
        cut_columns(dpre_all, owned_start, rows_owned),
        precision=lax.Precision.HIGHEST,
        preferred_element_type=single,
    )
    grad_table = jnp.dot(
        onehot_all.T,
        cut_columns(dcond_all, owned_start, rows_owned),
        precision=lax.Precision.HIGHEST,
        preferred_element_type=single,
    )
    qkv_cols = 3 * D // n_model
    out_cols = D // n_model
    final_cols = 2 * CH // n_model
    flat_one = normed_one.reshape(row_total, D)
    flat_attended = attended.reshape(row_total, D)
    flat_end = normed_end.reshape(row_total, D)
    flat_dqkv = d_qkv.reshape(row_total, 3 * D)
    flat_dbranch = d_branch.reshape(row_total, D)
    flat_doutput = d_output.reshape(row_total, 2 * CH)
    one_all, attended_all, end_all, dqkv_all, dbranch_all, doutput_all = (
        lax.all_gather(flat_one, "mlp", axis=0, tiled=True),
        lax.all_gather(flat_attended, "mlp", axis=0, tiled=True),
        lax.all_gather(flat_end, "mlp", axis=0, tiled=True),
        lax.all_gather(flat_dqkv, "mlp", axis=0, tiled=True),
        lax.all_gather(flat_dbranch, "mlp", axis=0, tiled=True),
        lax.all_gather(flat_doutput, "mlp", axis=0, tiled=True),
    )
    dqkv_part = cut_columns(dqkv_all, model_index * qkv_cols, qkv_cols)
    dbranch_part = cut_columns(dbranch_all, model_index * out_cols, out_cols)
    doutput_part = cut_columns(doutput_all, model_index * final_cols, final_cols)
    first_row = jnp.int32(0)
    owned_block = sum_at_owner(
        jnp.concatenate(
            [
                weight_grad(
                    cut_columns(one_all, first_row, rows_owned * lax.axis_size("dp")), dqkv_part
                ),
                weight_grad(
                    cut_columns(attended_all, first_row, rows_owned * lax.axis_size("dp")),
                    dbranch_part,
                ),
                weight_grad(
                    cut_columns(end_all, first_row, rows_owned * lax.axis_size("dp")), doutput_part
                ),
            ],
            axis=1,
        ).astype(jnp.bfloat16),
        "dp",
        0,
    )
    arranged = (
        lax.all_gather(owned_block.astype(jnp.bfloat16), "mlp", axis=1, tiled=True)
        .astype(owned_block.dtype)
        .reshape(rows_owned, n_model, qkv_cols + out_cols + final_cols)
    )
    grad_qkv = arranged[:, :, :qkv_cols].reshape(rows_owned, 3 * D)
    grad_out = arranged[:, :, qkv_cols : qkv_cols + out_cols].reshape(rows_owned, D)
    grad_final = arranged[:, :, qkv_cols + out_cols :].reshape(rows_owned, 2 * CH)
    grad_mats = jnp.concatenate(
        [grad_time_second, grad_mod, grad_qkv, grad_out, grad_final], axis=1
    )
    grad_swiglu = lax.psum_scatter(grad_swiglu, "dp", scatter_dimension=1, tiled=True)
    grad_bias = jnp.concatenate(
        [
            column_sum(d_hidden),
            jnp.sum(d_time_pre, axis=0),
            column_sum(d_time_emb),
            column_sum(d_modulation),
            column_sum(d_qkv),
            column_sum(d_branch),
            column_sum(d_output),
        ]
    )
    grad_patch = weight_grad(noisy_low, d_hidden)
    grad_bias, grad_patch, loss_sum = lax.psum((grad_bias, grad_patch, local_loss), ("dp", "mlp"))
    grad_embed = jnp.concatenate(
        [cut_columns(grad_patch, owned_start, rows_owned), grad_time_first, grad_table], axis=0
    )
    local_squares = (
        (jnp.sum(grad_mats * grad_mats) + jnp.sum(grad_embed * grad_embed)) / n_model
        + jnp.sum(grad_swiglu * grad_swiglu)
        + jnp.sum(grad_bias * grad_bias) / (n_model * n_data)
    )
    grad_norm = jnp.sqrt(lax.psum(local_squares, ("dp", "mlp")))
    factor = jnp.minimum(1.0, CLIP_LIMIT / grad_norm)
    mats_out = adam_step(
        matrices, matrices_first, matrices_second, grad_mats, matrices_average, factor, LEARN_RATE
    )
    embed_out = adam_step(
        embeddings,
        embeddings_first,
        embeddings_second,
        grad_embed,
        embeddings_average,
        factor,
        TABLE_RATE,
    )
    swiglu_out = adam_step(
        swiglu_weights, swiglu_first, swiglu_second, grad_swiglu, swiglu_average, factor, LEARN_RATE
    )
    bias_out = adam_step(
        biases, biases_first, biases_second, grad_bias, biases_average, factor, TABLE_RATE
    )
    return (
        loss_sum,
        grad_norm,
        mats_out[0],
        embed_out[0],
        swiglu_out[0],
        bias_out[0],
        mats_out[1],
        embed_out[1],
        swiglu_out[1],
        bias_out[1],
        mats_out[2],
        embed_out[2],
        swiglu_out[2],
        bias_out[2],
        mats_out[3],
        embed_out[3],
        swiglu_out[3],
        bias_out[3],
        grad_bias * factor,
    )


def solution(mesh):
    placed = (
        P(("dp", "mlp"), None),
        P(("dp", "mlp"), None),
        P(("dp", "mlp"), None),
        P(("dp", "mlp")),
        P(("dp", "mlp")),
        P("dp", None),
        P(None, "dp"),
        P(None, "dp", "mlp"),
        P(),
        P("dp", None),
        P(None, "dp"),
        P(None, "dp", "mlp"),
        P(),
        P("dp", None),
        P(None, "dp"),
        P(None, "dp", "mlp"),
        P(),
        P("dp", None),
        P(None, "dp"),
        P(None, "dp", "mlp"),
        P(),
    )
    return jax.shard_map(
        on_device,
        mesh=mesh,
        in_specs=placed,
        out_specs=(
            P(),
            P(),
            P("dp", None),
            P(None, "dp"),
            P(None, "dp", "mlp"),
            P(),
            P("dp", None),
            P(None, "dp"),
            P(None, "dp", "mlp"),
            P(),
            P("dp", None),
            P(None, "dp"),
            P(None, "dp", "mlp"),
            P(),
            P("dp", None),
            P(None, "dp"),
            P(None, "dp", "mlp"),
            P(),
            P(),
        ),
        check_vma=False,
    )
```

profile of v0, /device:TPU:15, one launch (start us, length us, event | category | flops | bytes accessed | tf_op | source)
XLA Modules:
  0.0 1627.7 jit_solution(13423619522455625838)
XLA Ops:
  26.0 42.2 %all-gather.25.cloned.1.call-done = bf16[1273,1152]{0,1:T(8,128)(2,1)} async-done(((bf16[1273,144]{0,1:T(8,128)(2,1)}), bf16[1273,1152]{0,1:T(8,128)(2,1)}) %all-gather.25.cloned.1.call-update) | async-done | bytes 2933008 | tf_op jit(solution)/shard_map/all_gather | solution.py:228
  72.4 658.9 %all-gather.27.cloned.1.call-done = bf16[1152,15008]{1,0:T(8,128)(2,1)} async-done(((bf16[144,15008]{1,0:T(8,128)(2,1)}), bf16[1152,15008]{1,0:T(8,128)(2,1)}) %all-gather.27.cloned.1.call-update) | async-done | bytes 34578448 | tf_op jit(solution)/shard_map/all_gather | solution.py:227
  733.6 8.3 fusion.2
  744.7 7.8 fusion.9
  771.5 47.4 %all-gather.31.cloned.1.call-done = bf16[3,1152,768]{2,1,0:T(8,128)(2,1)} async-done(((bf16[3,144,768]{2,1,0:T(8,128)(2,1)}), bf16[3,1152,768]{2,1,0:T(8,128)(2,1)}) %all-gather.31.cloned.1.call-update) | async-done | bytes 5308432 | tf_op jit(solution)/shard_map/all_gather | solution.py:229
  818.9 26.8 %all-gather.29.cloned.1.call-done = bf16[1024,1152]{1,0:T(8,128)(2,1)} async-done(((bf16[256,1152]{1,0:T(8,128)(2,1)}), bf16[1024,1152]{1,0:T(8,128)(2,1)}) %all-gather.29.cloned.1.call-update) | async-done | bytes 2359312 | tf_op jit(solution)/shard_map/all_gather | solution.py:287
  864.0 28.1 %reduce-scatter.4.cloned.1.call-done = bf16[256,1152]{1,0:T(8,128)(2,1)} async-done(((bf16[1024,1152]{1,0:T(8,128)(2,1)}), bf16[256,1152]{1,0:T(8,128)(2,1)}) %reduce-scatter.4.cloned.1.call-update) | async-done | bytes 589840 | tf_op jit(solution)/shard_map/reduce_scatter | solution.py:292
  906.0 24.4 %all-gather.33.cloned.1.call-done = bf16[1024,1152]{1,0:T(8,128)(2,1)} async-done(((bf16[256,1152]{1,0:T(8,128)(2,1)}), bf16[1024,1152]{1,0:T(8,128)(2,1)}) %all-gather.33.cloned.1.call-update) | async-done | bytes 2359312 | tf_op jit(solution)/shard_map/all_gather | solution.py:314
  948.9 31.3 %reduce-scatter.6.cloned.1.call-done = bf16[256,1152]{1,0:T(8,128)(2,1)} async-done(((bf16[1024,1152]{1,0:T(8,128)(2,1)}), bf16[256,1152]{1,0:T(8,128)(2,1)}) %reduce-scatter.6.cloned.1.call-update) | async-done | bytes 589840 | tf_op jit(solution)/shard_map/reduce_scatter | solution.py:326
  1015.9 7.5 multiply_reduce_fusion.3
  1030.2 10.0 fusion.58
  1058.1 7.8 pad_maximum_fusion
  1078.1 7.6 all-gather.35.cloned.1.call-done
  1085.7 53.8 %all-gather.37.cloned.1.call-done = bf16[1024,3456]{0,1:T(8,128)(2,1)} async-done(((bf16[256,3456]{0,1:T(8,128)(2,1)}), bf16[1024,3456]{0,1:T(8,128)(2,1)}) %all-gather.37.cloned.1.call-update) | async-done | bytes 7077904 | tf_op jit(solution)/shard_map/all_gather | solution.py:451
  1157.2 90.9 %all-gather.10 = bf16[32,1,256]{2,1,0:T(2,128)(2,1)S(1)} all-gather(bf16[1,1,256]{2,1,0:T(2,128)(2,1)S(1)} %maximum_bitcast_fusion), channel_id=1, replica_groups=mesh['dp'=8,'mlp'=4] {'dp','mlp'}, dimensions={0}, use_global_device_ids=true | all-gather | bytes 16896 | tf_op jit(solution)/shard_map/all_gather | solution.py:410
  1248.1 31.9 %all-gather.12 = bf16[32,1,1001]{2,1,0:T(2,128)(2,1)S(1)} all-gather(bf16[1,1,1001]{2,1,0:T(2,128)(2,1)S(1)} %fusion.118), channel_id=1, replica_groups=mesh['dp'=8,'mlp'=4] {'dp','mlp'}, dimensions={0}, use_global_device_ids=true | all-gather | bytes 66066 | tf_op jit(solution)/shard_map/all_gather | solution.py:413
  1280.0 33.6 %all-gather.5 = bf16[32,1,1152]{2,1,0:T(2,128)(2,1)S(1)} all-gather(bf16[1,1,1152]{2,1,0:T(2,128)(2,1)S(1)} %reshape.1244), channel_id=2, replica_groups=mesh['dp'=8,'mlp'=4] {'dp','mlp'}, dimensions={0}, use_global_device_ids=true | all-gather | bytes 76032 | tf_op jit(solution)/shard_map/all_gather | solution.py:392
  1313.8 38.1 %all-gather.7 = bf16[32,1,1152]{2,1,0:T(2,128)(2,1)S(1)} all-gather(bf16[1,1,1152]{2,1,0:T(2,128)(2,1)S(1)} %reshape.1248), channel_id=4, replica_groups=mesh['dp'=8,'mlp'=4] {'dp','mlp'}, dimensions={0}, use_global_device_ids=true | all-gather | bytes 76032 | tf_op jit(solution)/shard_map/all_gather | solution.py:398
  1352.6 40.4 %all-gather.6 = bf16[32,1,1152]{2,1,0:T(2,128)(2,1)S(1)} all-gather(bf16[1,1,1152]{2,1,0:T(2,128)(2,1)S(1)} %reshape.1246), channel_id=3, replica_groups=mesh['dp'=8,'mlp'=4] {'dp','mlp'}, dimensions={0}, use_global_device_ids=true | all-gather | bytes 76032 | tf_op jit(solution)/shard_map/all_gather | solution.py:395
  1393.1 39.1 %all-gather.11 = bf16[32,1,1152]{2,1,0:T(2,128)(2,1)S(1)} all-gather(bf16[1,1,1152]{2,1,0:T(2,128)(2,1)S(1)} %reshape.1256), channel_id=6, replica_groups=mesh['dp'=8,'mlp'=4] {'dp','mlp'}, dimensions={0}, use_global_device_ids=true | all-gather | bytes 76032 | tf_op jit(solution)/shard_map/all_gather | solution.py:407
  1435.6 45.1 %all-gather.8 = bf16[32,1,9216]{2,1,0:T(2,128)(2,1)S(1)} all-gather(bf16[1,1,9216]{2,1,0:T(2,128)(2,1)S(1)} %bitcast.214), channel_id=1, replica_groups=mesh['dp'=8,'mlp'=4] {'dp','mlp'}, dimensions={0}, use_global_device_ids=true | all-gather | bytes 608256 | tf_op jit(solution)/shard_map/all_gather | solution.py:401
  1497.0 19.1 %all-gather.45.cloned.1.call-done = bf16[4,1160,144]{1,2,0:T(8,128)(2,1)} async-done(((bf16[1,1160,144]{1,2,0:T(8,128)(2,1)}), bf16[4,1160,144]{1,2,0:T(8,128)(2,1)}) %all-gather.45.cloned.1.call-update) | async-done | bytes 1336336 | tf_op jit(solution)/shard_map/all_gather | solution.py:479
  1543.6 39.6 %all-reduce.15 = (f32[]{:T(128)}, f32[]{:T(128)}) all-reduce(f32[]{:T(128)} %select_reduce_fusion.3, f32[]{:T(128)S(6)} %add.486), channel_id=1, replica_groups=mesh['dp'=8,'mlp'=4] {'dp','mlp'}, use_global_device_ids=true, to_apply=%region_17.18 | all-reduce | flops 2 | bytes 16 | tf_op jit(solution)/shard_map/psum | solution.py:502
  1584.1 28.2 %multiply_add_fusion = (f32[144,15008]{1,0:T(8,128)}, f32[144,15008]{1,0:T(8,128)}, f32[144,15008]{1,0:T(8,128)}, f32[144,15008]{1,0:T(8,128)}) fusion(f32[144,15008]{1,0:T(8,128)} %param.38, f32[144,15008]{1,0:T(8,128)} %param.26, f32[144,15008]{1,0:T(8,128)} %constant_dynamic-update-slice_fusion.8, f32[]{:T(128)S(6)} %min.3, f32[144,15008]{1,0:T(8,128)} %param.30, ...), kind=kLoop, calls=%fused_computation.8 | loop fusion | flops 41061888 | bytes 77801472 | tf_op jit(solution)/shard_map/add | solution.py:157
  (490 shorter events, 230.7 us)
Async XLA Ops:
  7.2 61.0 %all-gather.25.cloned.1.call-start = ((), (), s32[]{:S(2)}) async-start(), calls=%async_computation.4 | async-start | bytes 3317760 | tf_op jit(solution)/shard_map/all_gather | solution.py:228
  9.2 722.1 %all-gather.27.cloned.1.call-start = ((), (), s32[]{:S(2)}) async-start(), calls=%async_computation.5 | async-start | bytes 39149568 | tf_op jit(solution)/shard_map/all_gather | solution.py:227
  15.3 803.7 %all-gather.31.cloned.1.call-start = ((), (), s32[]{:S(2)}) async-start(), calls=%async_computation.7 | async-start | bytes 5971968 | tf_op jit(solution)/shard_map/all_gather | solution.py:229
  17.4 828.3 %all-gather.29.cloned.1.call-start = ((), (), s32[]{:S(2)}) async-start(), calls=%async_computation.6 | async-start | bytes 2949120 | tf_op jit(solution)/shard_map/all_gather | solution.py:287
  25.6 717.0 %copy-start.63 = (bf16[256,16]{0,1:T(8,128)(2,1)}, bf16[256,16]{0,1:T(8,128)(2,1)S(1)}, u32[]{:S(2)}) copy-start(bf16[256,16]{0,1:T(8,128)(2,1)S(1)} %fusion.108) | copy-start | bytes 24580
  25.9 733.9 %copy-start.44 = (f32[256,18]{0,1:T(8,128)}, f32[256,18]{0,1:T(8,128)S(1)}, u32[]{:S(2)}) copy-start(f32[256,18]{0,1:T(8,128)S(1)} %get-tuple-element.116) | copy-start | bytes 55300
  25.9 733.9 %copy-start.46 = (f32[256,18]{0,1:T(8,128)}, f32[256,18]{0,1:T(8,128)S(1)}, u32[]{:S(2)}) copy-start(f32[256,18]{0,1:T(8,128)S(1)} %get-tuple-element.117) | copy-start | bytes 55300
  25.9 733.9 %copy-start.48 = (f32[256,18]{0,1:T(8,128)}, f32[256,18]{0,1:T(8,128)S(1)}, u32[]{:S(2)}) copy-start(f32[256,18]{0,1:T(8,128)S(1)} %get-tuple-element.120) | copy-start | bytes 55300
  26.0 733.9 %copy-start.50 = (f32[256,18]{0,1:T(8,128)}, f32[256,18]{0,1:T(8,128)S(1)}, u32[]{:S(2)}) copy-start(f32[256,18]{0,1:T(8,128)S(1)} %get-tuple-element.121) | copy-start | bytes 55300
  69.7 663.8 %copy-start.69 = (f32[1152]{0:T(1024)}, f32[1152]{0:T(1024)S(1)}, u32[]{:S(2)}) copy-start(f32[1152]{0:T(1024)S(1)} %convolution_reduce_fusion) | copy-start | bytes 13828
  69.8 663.7 %copy-start.93 = (bf16[1152]{0:T(1024)(128)(2,1)}, bf16[1152]{0:T(1024)(128)(2,1)S(1)}, u32[]{:S(2)}) copy-start(bf16[1152]{0:T(1024)(128)(2,1)S(1)} %multiply_convert_fusion.6) | copy-start | bytes 6916
  72.4 669.5 %copy-start.65 = (f32[1152]{0:T(1024)}, f32[1152]{0:T(1024)S(1)}, u32[]{:S(2)}) copy-start(f32[1152]{0:T(1024)S(1)} %fusion.55) | copy-start | bytes 13828
  771.3 120.8 %reduce-scatter.4.cloned.1.call-start = ((), (), s32[]{:S(2)}) async-start(), calls=%async_computation.8 | async-start | bytes 2949120 | tf_op jit(solution)/shard_map/reduce_scatter | solution.py:292
  859.3 71.1 %all-gather.33.cloned.1.call-start = ((), (), s32[]{:S(2)}) async-start(), calls=%async_computation.9 | async-start | bytes 2949120 | tf_op jit(solution)/shard_map/all_gather | solution.py:314
  905.7 74.5 %reduce-scatter.6.cloned.1.call-start = ((), (), s32[]{:S(2)}) async-start(), calls=%async_computation.10 | async-start | bytes 2949120 | tf_op jit(solution)/shard_map/reduce_scatter | solution.py:326
  947.4 124.8 %all-gather.43.cloned.1.call-start = ((), (), s32[]{:S(2)}) async-start(), calls=%async_computation.15 | async-start | bytes 2949120 | tf_op jit(solution)/shard_map/all_gather | solution.py:450
  948.1 126.4 %all-gather.39.cloned.1.call-start = ((), (), s32[]{:S(2)}) async-start(), calls=%async_computation.13 | async-start | bytes 2949120 | tf_op jit(solution)/shard_map/all_gather | solution.py:449
  948.9 125.7 %all-gather.41.cloned.1.call-start = ((), (), s32[]{:S(2)}) async-start(), calls=%async_computation.14 | async-start | bytes 2949120 | tf_op jit(solution)/shard_map/all_gather | solution.py:452
  985.2 100.5 %all-gather.35.cloned.1.call-start = ((), (), s32[]{:S(2)}) async-start(), calls=%async_computation.11 | async-start | bytes 2949120 | tf_op jit(solution)/shard_map/all_gather | solution.py:448
  986.0 153.5 %all-gather.37.cloned.1.call-start = ((), (), s32[]{:S(2)}) async-start(), calls=%async_computation.12 | async-start | bytes 8847360 | tf_op jit(solution)/shard_map/all_gather | solution.py:451
  1001.5 482.4 %all-reduce.19.cloned.1.call-start = ((), (), s32[]{:S(2)}) async-start(), calls=%async_computation.18 | async-start | bytes 286720 | tf_op jit(solution)/shard_map/psum | solution.py:502
  1058.0 436.8 %reduce-scatter.8.cloned.1.call-start = ((), (), s32[]{:S(2)}) async-start(), calls=%async_computation.16 | async-start | bytes 11943936 | tf_op jit(solution)/shard_map/reduce_scatter | solution.py:489
  1151.6 280.9 %all-to-all-start = ((bf16[8,144,1160]{2,1,0:T(8,128)(2,1)}), bf16[8,144,1160]{2,1,0:T(8,128)(2,1)S(1)}, u32[]{:S(2)}, u32[]{:S(2)}) async-start(bf16[8,144,1160]{2,1,0:T(8,128)(2,1)} %concatenate.136), calls=%async_computation.2 | async-start | bytes 5898240 | tf_op jit(solution)/shard_map/all_to_all | solution.py:35
  1157.1 359.0 %all-gather.45.cloned.1.call-start = ((), (), s32[]{:S(2)}) async-start(), calls=%async_computation.17 | async-start | bytes 1843200 | tf_op jit(solution)/shard_map/all_gather | solution.py:479
  (128 other events, 4210.2 us)
Sparse Core Ops, SparseCore 0:
  10.8 57.3 all-gather.24
  70.3 660.9 all-gather.26
  734.0 84.8 all-gather.30
  820.9 24.7 all-gather.28
  859.4 32.6 reduce-scatter.3
  905.8 24.4 all-gather.32
  947.5 32.6 reduce-scatter.5
  982.3 24.4 all-gather.42
  1009.0 24.3 all-gather.38
  1035.4 24.0 all-gather.40
  1061.6 24.0 all-gather.34
  1087.7 51.7 all-gather.36
  1146.4 156.5 all-reduce.18
  1306.4 188.3 reduce-scatter.7
  1496.8 19.2 all-gather.44
where the time goes:
time: 1640 us; the launch traced here: 1630 us
  waiting for transfers between devices  948 us (58%)
  blocking collectives  364 us (22%)
  matrix products  126 us (8%)
  other arithmetic  95.9 us (6%)
  local copies, waits for them, and re-layouts  57.4 us (4%)
  between operations  29 us (2%)
    all_gather x1, waiting for transfers between devices, on_device(): lax.all_gather(matrices.astype(bfloat), 'dp', axis=0, tiled=True)  659 us
    all_gather x1, blocking collectives, on_device(): lax.all_gather(sinus_emb.astype(single).astype(jnp.bfloat16), ('dp', 'mlp...  90.9 us
    all_gather x1, waiting for transfers between devices, on_device(): lax.all_gather(flat_dqkv, 'mlp', axis=0, tiled=True)  53.8 us
    all_gather x1, waiting for transfers between devices, on_device(): lax.all_gather(swiglu_weights.astype(bfloat), 'dp', axis=1, tiled=True)  47.4 us
    all_gather x1, blocking collectives, on_device(): lax.all_gather(d_modulation.astype(single).astype(jnp.bfloat16), ('dp', '...  45.1 us
    all_gather x1, waiting for transfers between devices, on_device(): lax.all_gather(embeddings.astype(bfloat), 'dp', axis=1, tiled=True)  42.2 us
    all_gather x1, blocking collectives, on_device(): lax.all_gather(d_time_emb.astype(single).astype(jnp.bfloat16), ('dp', 'ml...  40.4 us
    psum x1, blocking collectives, on_device(): lax.psum((grad_bias, grad_patch, local_loss), ('dp', 'mlp'))  39.6 us
  transfers between devices with their start and end apart: 16, of which 11 were waited for; matrix products, arithmetic and copies ran while one was open for 10% of the time, Pallas kernels for 0%

commit v1 on v0

v1 whole, which is shorter than its diff:
```python
import functools
import math

import jax
import jax.numpy as jnp
from jax import lax
from jax.experimental import pallas as pl
from jax.experimental.pallas import tpu as pltpu
from jax.sharding import PartitionSpec as P

HEADS = 16
HDIM = 72
D = 1152
CH = 16
CLASSES = 1000
FREQ = 256
STEP = 10


CLIP_LIMIT = 1.0
LEARN_RATE = 0.03
TABLE_RATE = 0.4
FIRST_DECAY = 0.9
SECOND_DECAY = 0.999
ADAM_EPSILON = 1e-08
WEIGHT_DECAY = 0.01
AVERAGE_DECAY = 0.9999


def plan(steps_in):
    step_index = jnp.arange(1000, dtype=jnp.int32)
    beta_table = 0.0001 + (0.02 - 0.0001) * step_index.astype(jnp.float32) / 999.0
    logbar = jnp.cumsum(jnp.log1p(-beta_table))

    def lookup(values, wanted):
        return jnp.sum(
            jnp.where(wanted[:, None] == step_index[None, :], values[None, :], 0.0), axis=1
        )

    return (
        lookup(beta_table, steps_in),
        jnp.exp(lookup(logbar, steps_in)),
        jnp.exp(lookup(logbar, steps_in - 1)),
    )


def sinusoid(steps_in):
    halfway = FREQ // 2
    frequency = jnp.exp(-math.log(10000.0) * jnp.arange(halfway, dtype=jnp.float32) / halfway)
    angles = steps_in.astype(jnp.float32)[:, None] * frequency[None, :]
    return jnp.concatenate([jnp.cos(angles), jnp.sin(angles)], axis=1)


def modulate(hidden, shift_by, scale_by):
    row_mean = jnp.mean(hidden, axis=-1, keepdims=True)
    centered = hidden - row_mean
    variance = jnp.mean(centered * centered, axis=-1, keepdims=True)
    return (
        centered * lax.rsqrt(variance + 1e-06) * (1.0 + scale_by[:, None, :]) + shift_by[:, None, :]
    )


def noisy_input(clean_patches, noise_patches, steps_in):
    beta_now, bar_now, bar_prev = plan(steps_in)
    bar_now = bar_now[:, None, None]
    return jnp.sqrt(bar_now) * clean_patches + jnp.sqrt(1.0 - bar_now) * noise_patches


def loss_terms(output, clean_patches, noise_patches, steps_in, valid_slot):
    beta_now, bar_now, bar_prev = plan(steps_in)
    beta_now = beta_now[:, None, None]
    bar_now = bar_now[:, None, None]
    bar_prev = bar_prev[:, None, None]
    noisy = jnp.sqrt(bar_now) * clean_patches + jnp.sqrt(1.0 - bar_now) * noise_patches
    eps_pred = output[..., :CH]
    var_raw = output[..., CH:]
    squared = jnp.sum((eps_pred - noise_patches) ** 2, axis=-1)
    post_log = jnp.log(beta_now * (1.0 - bar_prev) / (1.0 - bar_now))
    fraction = (var_raw + 1.0) * 0.5
    model_log = fraction * jnp.log(beta_now) + (1.0 - fraction) * post_log
    coefficient = beta_now * jnp.sqrt(bar_prev) / (1.0 - bar_now)
    start_est = (noisy - jnp.sqrt(1.0 - bar_now) * eps_pred) / jnp.sqrt(bar_now)
    mean_gap = coefficient * (clean_patches - start_est)
    divergence = (
        0.5
        * (
            -1.0
            + model_log
            - post_log
            + jnp.exp(post_log - model_log)
            + mean_gap * mean_gap * jnp.exp(-model_log)
        )
        / math.log(2.0)
    )
    return jnp.sum(jnp.where(valid_slot, squared + jnp.sum(divergence, axis=-1), 0.0))


def adam_step(weight, first, second, gradient, average, factor, rate):
    average_decay = min(AVERAGE_DECAY, (1.0 + STEP) / (10.0 + STEP))
    clipped = gradient * factor
    first = FIRST_DECAY * first + (1.0 - FIRST_DECAY) * clipped
    second = SECOND_DECAY * second + (1.0 - SECOND_DECAY) * clipped * clipped
    ratio = (
        first
        / (1.0 - FIRST_DECAY**STEP)
        / (jnp.sqrt(second / (1.0 - SECOND_DECAY**STEP)) + ADAM_EPSILON)
    )
    weight = weight - rate * (ratio + WEIGHT_DECAY * weight)
    return (weight, first, second, average_decay * average + (1.0 - average_decay) * weight)


def backward_product(gradient, weight):
    return lax.dot_general(
        gradient,
        weight,
        (((gradient.ndim - 1,), (1,)), ((), ())),
        preferred_element_type=jnp.float32,
    )


def weight_grad(inputs, gradient):
    flat_in = inputs.reshape(-1, inputs.shape[-1])
    flat_grad = gradient.reshape(-1, gradient.shape[-1])
    return lax.dot_general(
        flat_in, flat_grad, (((0,), (0,)), ((), ())), preferred_element_type=jnp.float32
    )


def column_sum(gradient):
    return jnp.sum(gradient.astype(jnp.float32).reshape(-1, gradient.shape[-1]), axis=0)


def cut_columns(values, start, amount):
    return lax.dynamic_slice_in_dim(values, start, amount, 1)


MESH_IDS = pl.DeviceIdType.MESH
KERNEL_VMEM = 48 * 2**20


def exchange_kernel(axes, sizes, modes, *refs):
    count = len(modes)
    ins, outs = refs[:count], refs[count : 2 * count]
    send_sem, recv_sem = refs[2 * count :]
    if axes == "dp":
        total = sizes[0]
        me = lax.axis_index("dp")
    else:
        total = sizes[0] * sizes[1]
        me = lax.axis_index("dp") * sizes[1] + lax.axis_index("mlp")

    def device(spot):
        if axes == "dp":
            return (spot, lax.axis_index("mlp"))
        return (lax.div(spot, sizes[1]), lax.rem(spot, sizes[1]))

    barrier = pltpu.get_barrier_semaphore()

    def greet(step, carry):
        pl.semaphore_signal(
            barrier, inc=1, device_id=device(lax.rem(me + step, total)), device_id_type=MESH_IDS
        )
        return carry

    lax.fori_loop(1, total, greet, 0)
    pl.semaphore_wait(barrier, total - 1)

    def make(item, step):
        peer = lax.rem(me + step, total)
        source = ins[item].at[peer] if modes[item] == "each" else ins[item]
        return pltpu.make_async_remote_copy(
            src_ref=source,
            dst_ref=outs[item].at[me],
            send_sem=send_sem.at[item, step - 1],
            recv_sem=recv_sem.at[item, step - 1],
            device_id=device(peer),
            device_id_type=MESH_IDS,
        )

    def begin(step, carry):
        for item in range(count):
            make(item, step).start()
        return carry

    lax.fori_loop(1, total, begin, 0)
    for item in range(count):
        if modes[item] == "each":
            outs[item][me] = ins[item][me]
        else:
            outs[item][me] = ins[item][...]

    def finish(step, carry):
        for item in range(count):
            make(item, step).wait()
        return carry

    lax.fori_loop(1, total, finish, 0)


def exchange(items, axes, sizes, collective):
    total = sizes[0] if axes == "dp" else sizes[0] * sizes[1]
    modes = tuple(mode for _, mode in items)
    arrays = [array for array, _ in items]
    shapes = [
        jax.ShapeDtypeStruct(
            array.shape if mode == "each" else (total, *array.shape), array.dtype
        )
        for array, mode in items
    ]
    space = pl.BlockSpec(memory_space=pltpu.VMEM)
    return pl.pallas_call(
        functools.partial(exchange_kernel, axes, sizes, modes),
        out_shape=shapes,
        in_specs=[space] * len(items),
        out_specs=[space] * len(items),
        scratch_shapes=[
            pltpu.SemaphoreType.DMA((len(items), total - 1)),
            pltpu.SemaphoreType.DMA((len(items), total - 1)),
        ],
        compiler_params=pltpu.CompilerParams(
            collective_id=collective, has_side_effects=True, vmem_limit_bytes=KERNEL_VMEM
        ),
    )(*arrays)


def place_kernel(targets, *refs):
    pieces, out, sem = refs[:-2], refs[-2], refs[-1]
    copies = []
    for spot, (piece, target) in enumerate(zip(pieces, targets)):
        copy = pltpu.make_async_copy(piece, target(out), sem.at[spot])
        copy.start()
        copies.append(copy)
    for copy in copies:
        copy.wait()


def place(pieces, targets, shape, dtype):
    return pl.pallas_call(
        functools.partial(place_kernel, targets),
        out_shape=jax.ShapeDtypeStruct(shape, dtype),
        in_specs=[pl.BlockSpec(memory_space=pl.ANY)] * len(pieces),
        out_specs=pl.BlockSpec(memory_space=pl.ANY),
        scratch_shapes=[pltpu.SemaphoreType.DMA((len(pieces),))],
        compiler_params=pltpu.CompilerParams(vmem_limit_bytes=KERNEL_VMEM),
    )(*pieces)


NX = 2


def ring_pairs(depth, shift):
    return [
        (z * NX + x, ((z + shift) % depth) * NX + x) for z in range(depth) for x in range(NX)
    ]


def swap_pairs(count):
    return [(spot, spot ^ 1) for spot in range(count)]


def ring_pieces(half, depth, shift):
    arrived = [half]
    for _ in range(depth - 1):
        arrived.append(lax.ppermute(arrived[-1], "dp", ring_pairs(depth, shift)))
    return arrived


def gather_dp(first, second, selects, shape, depth):
    swaps = swap_pairs(depth * NX)
    pieces, targets = [], []

    def source(step, shift, other):
        def spot():
            d = lax.axis_index("dp")
            z, x = lax.div(d, NX), lax.rem(d, NX)
            z = lax.rem(z - step * shift + depth * NX, depth)
            x = 1 - x if other else x
            return z * NX + x

        return spot

    for half, shift, select in ((first, 1, selects[0]), (second, -1, selects[1])):
        for step, piece in enumerate(ring_pieces(half, depth, shift)):
            other = lax.ppermute(piece, "dp", swaps)
            for swapped, value in ((False, piece), (True, other)):
                pieces.append(value)
                spot = source(step, shift, swapped)
                targets.append(functools.partial(lambda sel, at, out: sel(out, at()), select, spot))
    return place(pieces, targets, shape, first.dtype)


def reduce_ring(blocks, depth, shift):
    z = lax.div(lax.axis_index("dp"), NX)

    def block(offset):
        return lax.dynamic_index_in_dim(
            blocks, lax.rem(z + offset + 2 * depth, depth), 0, keepdims=False
        )

    running = block(-shift)
    for step in range(1, depth):
        arrived = lax.ppermute(running.astype(jnp.bfloat16), "dp", ring_pairs(depth, shift))
        running = arrived.astype(jnp.float32) + block(-shift * (step + 1))
    return running


def reduce_dp(value, count, cut):
    if count != 8:
        return lax.psum_scatter(
            value.astype(jnp.bfloat16), "dp", scatter_dimension=0, tiled=True
        )[0].astype(jnp.float32)
    depth = count // NX
    x = lax.rem(lax.axis_index("dp"), NX)
    paired = value.reshape(depth, NX, *value.shape[1:])
    give = lax.dynamic_index_in_dim(paired, 1 - x, 1, keepdims=False).astype(jnp.bfloat16)
    got = lax.ppermute(give, "dp", swap_pairs(count)).astype(jnp.float32)
    blocks = lax.dynamic_index_in_dim(paired, x, 1, keepdims=False) + got
    return jnp.concatenate(
        [
            reduce_ring(blocks[:, :, :cut], depth, 1),
            reduce_ring(blocks[:, :, cut:], depth, -1),
        ],
        axis=1,
    )


def flip(value, bit, count):
    return lax.ppermute(value, "mlp", [(spot, spot ^ bit) for spot in range(count)])


def gather_rows(own, count):
    far = flip(own, 2, count)
    near = flip(own, 1, count)
    return own, near, far, flip(far, 1, count)


def scatter_rows(far_parts, near_parts, count):
    single = jnp.float32
    got = flip(far_parts[1], 1, count)
    far = flip((far_parts[0].astype(single) + got.astype(single)).astype(jnp.bfloat16), 2, count)
    near = flip(near_parts[1], 1, count)
    return near_parts[0].astype(single) + near.astype(single) + far.astype(single)


def out_pairs(depth, ranks, step, shift):
    pairs = []
    for rank in range(ranks):
        for x in range(NX):
            start = (rank + (step - 1) * shift) % depth
            stop = (rank + step * shift) % depth
            pairs.append(((start * NX + x) * ranks + rank, (stop * NX + x) * ranks + rank))
    return pairs


def gather_out(shard, sizes):
    n_data, n_model = sizes
    if n_data != 8 or n_model != 4:
        whole = lax.all_gather(shard, "dp", axis=0, tiled=True)
        height = D // n_model
        return lax.dynamic_slice_in_dim(whole, lax.axis_index("mlp") * height, height, 0)
    depth = n_data // NX
    d = lax.axis_index("dp")
    z, x = lax.div(d, NX), lax.rem(d, NX)
    mine = z == lax.axis_index("mlp")
    halves = []
    for part, shift in ((shard[:80], 1), (shard[80:], -1)):
        total = jnp.where(mine, part, jnp.zeros_like(part))
        moving = part
        for step in range(1, depth):
            moving = lax.ppermute(moving, ("dp", "mlp"), out_pairs(depth, n_model, step, shift))
            total = total + moving
        halves.append(total)
    own = jnp.concatenate(halves, axis=0)
    other = lax.ppermute(own, "dp", swap_pairs(n_data))
    low = jnp.where(x == 0, own, other)
    high = jnp.where(x == 0, other, own)
    return jnp.concatenate([low, high], axis=0)


def reduce_out(value, sizes):
    n_data, n_model = sizes
    single, bfloat = jnp.float32, jnp.bfloat16
    if n_data != 8 or n_model != 4:
        whole = jnp.zeros((D, D), single)
        whole = lax.dynamic_update_slice_in_dim(
            whole, value, lax.axis_index("mlp") * value.shape[0], 0
        )
        part = lax.psum_scatter(whole.astype(bfloat), "dp", scatter_dimension=0, tiled=True)
        return lax.psum(part.astype(single), "mlp")
    depth = n_data // NX
    d = lax.axis_index("dp")
    z, x = lax.div(d, NX), lax.rem(d, NX)
    mine = z == lax.axis_index("mlp")
    paired = value.reshape(NX, D // n_data, D)
    give = lax.dynamic_index_in_dim(paired, 1 - x, 0, keepdims=False).astype(bfloat)
    got = lax.ppermute(give, "dp", swap_pairs(n_data)).astype(single)
    blocks = lax.dynamic_index_in_dim(paired, x, 0, keepdims=False) + got
    halves = []
    for part, shift in ((blocks[:80], 1), (blocks[80:], -1)):
        running = part
        for step in range(1, depth):
            pairs = [
                (source, target)
                for source, target in out_pairs(depth, n_model, step + 1, shift)
            ]
            arrived = lax.ppermute(running.astype(bfloat), ("dp", "mlp"), pairs)
            running = arrived.astype(single) + part
        halves.append(running)
    summed = jnp.concatenate(halves, axis=0)
    shared = jnp.where(mine, summed, 0.0).astype(bfloat)
    shared = shared + flip(shared, 1, n_model)
    shared = shared + flip(shared, 2, n_model)
    return shared.astype(single)


def swapped(values):
    quarter = HDIM // 4
    return jnp.concatenate(
        [
            values[:, quarter : 2 * quarter],
            values[:, :quarter],
            values[:, 3 * quarter :],
            values[:, 2 * quarter : 3 * quarter],
        ],
        axis=1,
    )


def attention_kernel(heads, qkv_ref, cos_ref, sin_ref, mask_ref, low_ref, out_ref, total_ref):
    width = heads * HDIM
    cosine, sine, mask = cos_ref[0], sin_ref[0], mask_ref[0]
    totals = []
    for head in range(heads):
        start = head * HDIM

        def part(which):
            return qkv_ref[0, :, which * width + start : which * width + start + HDIM]

        raw_q, raw_k = part(0), part(1)
        query = (raw_q * cosine + swapped(raw_q) * sine).astype(jnp.bfloat16)
        key = (raw_k * cosine + swapped(raw_k) * sine).astype(jnp.bfloat16)
        value = part(2).astype(jnp.bfloat16)
        for which, kept in enumerate((query, key, value)):
            low_ref[0, :, which * width + start : which * width + start + HDIM] = kept
        scores = lax.dot_general(
            query, key, (((1,), (1,)), ((), ())), preferred_element_type=jnp.float32
        ) * (1.0 / math.sqrt(HDIM))
        scores = jnp.where(mask > 0.0, scores, -1e30)
        row_max = jnp.max(scores, axis=-1, keepdims=True)
        exponent = jnp.exp(scores - row_max)
        row_sum = jnp.sum(exponent, axis=-1, keepdims=True)
        probs = exponent / row_sum
        out_ref[0, :, start : start + HDIM] = jnp.dot(
            probs.astype(jnp.bfloat16), value, preferred_element_type=jnp.float32
        ).astype(jnp.bfloat16)
        totals.append(row_max + jnp.log(row_sum))
    total_ref[0] = jnp.concatenate(totals, axis=1)


def attention(qkv, cosine, sine, mask, heads):
    images, length, width = qkv.shape
    per_image = lambda *dims: pl.BlockSpec((1, *dims), lambda i: (i, 0, 0))
    return pl.pallas_call(
        functools.partial(attention_kernel, heads),
        grid=(images,),
        out_shape=[
            jax.ShapeDtypeStruct((images, length, width), jnp.bfloat16),
            jax.ShapeDtypeStruct((images, length, heads * HDIM), jnp.bfloat16),
            jax.ShapeDtypeStruct((images, length, heads), jnp.float32),
        ],
        in_specs=[
            per_image(length, width),
            per_image(length, HDIM),
            per_image(length, HDIM),
            per_image(1, length),
        ],
        out_specs=[
            per_image(length, width),
            per_image(length, heads * HDIM),
            per_image(length, heads),
        ],
        compiler_params=pltpu.CompilerParams(vmem_limit_bytes=KERNEL_VMEM),
    )(qkv, cosine, sine, mask)


def attention_back_kernel(
    heads, low_ref, total_ref, grad_ref, cos_ref, sin_ref, mask_ref, out_ref
):
    width = heads * HDIM
    scale_by = 1.0 / math.sqrt(HDIM)
    cosine, sine, mask = cos_ref[0], sin_ref[0], mask_ref[0]

    def contract(left, right, dims):
        return lax.dot_general(left, right, (dims, ((), ())), preferred_element_type=jnp.float32)

    for head in range(heads):
        start = head * HDIM

        def spot(which):
            return slice(which * width + start, which * width + start + HDIM)

        query, key, value = (low_ref[0, :, spot(which)] for which in range(3))
        grad = grad_ref[0, :, start : start + HDIM]
        scores = contract(query, key, ((1,), (1,))) * scale_by
        scores = jnp.where(mask > 0.0, scores, -1e30)
        probs = jnp.exp(scores - total_ref[0, :, head : head + 1])
        d_probs = contract(grad, value, ((1,), (1,)))
        row = jnp.sum(probs * d_probs, axis=-1, keepdims=True)
        d_scores = (probs * (d_probs - row)).astype(jnp.bfloat16)
        d_query = contract(d_scores, key, ((1,), (0,))) * scale_by
        d_key = contract(d_scores, query, ((0,), (0,))) * scale_by
        d_value = contract(probs.astype(jnp.bfloat16), grad, ((0,), (0,)))
        for which, turned in ((0, d_query), (1, d_key)):
            back = turned * cosine + swapped(turned * sine)
            out_ref[0, :, spot(which)] = back.astype(jnp.bfloat16)
        out_ref[0, :, spot(2)] = d_value.astype(jnp.bfloat16)


def attention_back(low, totals, grad, cosine, sine, mask, heads):
    images, length, width = low.shape
    per_image = lambda *dims: pl.BlockSpec((1, *dims), lambda i: (i, 0, 0))
    return pl.pallas_call(
        functools.partial(attention_back_kernel, heads),
        grid=(images,),
        out_shape=jax.ShapeDtypeStruct((images, length, width), jnp.bfloat16),
        in_specs=[
            per_image(length, width),
            per_image(length, heads),
            per_image(length, heads * HDIM),
            per_image(length, HDIM),
            per_image(length, HDIM),
            per_image(1, length),
        ],
        out_specs=per_image(length, width),
        compiler_params=pltpu.CompilerParams(vmem_limit_bytes=KERNEL_VMEM),
    )(low, totals, grad, cosine, sine, mask)


def turn_tables(patch_grid, length):
    slot_index = jnp.arange(length, dtype=jnp.int32)[None, :]
    grid_cols = patch_grid[:, 1:2]
    valid_slot = slot_index < patch_grid[:, 0:1] * grid_cols
    row_place = (slot_index // grid_cols).astype(jnp.float32)
    col_place = (slot_index % grid_cols).astype(jnp.float32)
    quarter = HDIM // 4
    frequency = jnp.exp(-math.log(10000.0) * jnp.arange(quarter, dtype=jnp.float32) / quarter)
    row_angle = row_place[..., None] * frequency
    col_angle = col_place[..., None] * frequency
    cos_row, sin_row = jnp.cos(row_angle), jnp.sin(row_angle)
    cos_col, sin_col = jnp.cos(col_angle), jnp.sin(col_angle)
    return (
        jnp.concatenate([cos_row, cos_row, cos_col, cos_col], axis=-1),
        jnp.concatenate([-sin_row, sin_row, -sin_col, sin_col], axis=-1),
        valid_slot.astype(jnp.float32)[:, None, :],
    )


def valid_slots(patch_grid, length):
    return jnp.arange(length, dtype=jnp.int32)[None, :] < patch_grid[:, 0:1] * patch_grid[:, 1:2]


def on_device(
    clean_patches,
    noise_patches,
    patch_grid,
    labels,
    timesteps,
    matrices,
    embeddings,
    swiglu_weights,
    biases,
    matrices_first,
    embeddings_first,
    swiglu_first,
    biases_first,
    matrices_second,
    embeddings_second,
    swiglu_second,
    biases_second,
    matrices_average,
    embeddings_average,
    swiglu_average,
    biases_average,
):
    bfloat = jnp.bfloat16
    single = jnp.float32
    images = labels.shape[0]
    length = clean_patches.shape[0] // images
    n_model = lax.axis_size("mlp")
    n_data = lax.axis_size("dp")
    sizes = (n_data, n_model)
    total_images = images * n_data * n_model
    rows = D // n_data
    owned_start = lax.axis_index("dp") * rows
    data_index = lax.axis_index("dp")
    model_index = lax.axis_index("mlp")
    heads = HEADS // n_model
    head_cols = heads * HDIM
    hidden_units = swiglu_weights.shape[2]

    qkv_shard = jnp.concatenate(
        [
            cut_columns(matrices, 9 * D + part * D + model_index * head_cols, head_cols)
            for part in range(3)
        ],
        axis=1,
    ).astype(bfloat)
    out_shard = matrices[:, 12 * D : 13 * D].astype(bfloat)
    swiglu_shard = swiglu_weights.astype(bfloat)
    if n_data == 8:
        depth = n_data // NX
        qkv_weight = gather_dp(
            qkv_shard[:80],
            qkv_shard[80:],
            (lambda out, at: out.at[at, 0:80], lambda out, at: out.at[at, 80:144]),
            (n_data, rows, 3 * head_cols),
            depth,
        ).reshape(D, 3 * head_cols)
        half = hidden_units // 2
        swiglu_use = gather_dp(
            swiglu_shard[:, :, :half],
            swiglu_shard[:, :, half:],
            (
                lambda out, at: out.at[:, at, :, 0:half],
                lambda out, at: out.at[:, at, :, half : 2 * half],
            ),
            (3, n_data, rows, hidden_units),
            depth,
        ).reshape(3, D, hidden_units)
    else:
        qkv_weight = lax.all_gather(qkv_shard, "dp", axis=0, tiled=True)
        swiglu_use = lax.all_gather(swiglu_shard, "dp", axis=1, tiled=True)
    out_weight = gather_out(out_shard, sizes)

    time_second = matrices[:, :D].astype(bfloat)
    mod_weight = matrices[:, D : 9 * D].astype(bfloat)
    time_first = embeddings[CH : CH + FREQ].astype(bfloat)
    class_table = embeddings[CH + FREQ :].astype(bfloat)
    patch_bias = biases[:D]
    first_bias = biases[D : 2 * D]
    second_bias = biases[2 * D : 3 * D]
    mod_bias = biases[3 * D : 11 * D]
    qkv_bias = biases[11 * D : 14 * D]
    out_bias = biases[14 * D : 15 * D]
    final_bias = biases[15 * D :]

    facts = jnp.concatenate([timesteps[:, None], labels[:, None], patch_grid], axis=1)
    facts = jnp.pad(facts, ((0, 8 - images), (0, 124)))
    (facts_all,) = exchange([(facts, "all")], "both", sizes, 0)
    facts_all = facts_all[:, 0, :4]
    steps_all, labels_all, grid_all = facts_all[:, 0], facts_all[:, 1], facts_all[:, 2:4]
    sinus_all = sinusoid(steps_all).astype(bfloat)
    first_bias_own = lax.dynamic_slice_in_dim(first_bias, owned_start, rows)
    second_bias_own = lax.dynamic_slice_in_dim(second_bias, owned_start, rows)
    time_pre = jnp.dot(sinus_all, time_first, preferred_element_type=single) + first_bias_own
    time_act = jax.nn.silu(time_pre).astype(bfloat)
    time_part = jnp.dot(time_act, time_second, preferred_element_type=single)
    small_shard = jnp.concatenate(
        [embeddings[:CH], matrices[:, 13 * D :].T], axis=0
    ).astype(bfloat)
    time_parts, small_all = exchange(
        [
            (time_part.reshape(total_images, n_data, rows).transpose(1, 0, 2), "each"),
            (small_shard, "all"),
        ],
        "dp",
        sizes,
        1,
    )
    small_all = small_all.transpose(1, 0, 2).reshape(3 * CH, D)
    patch_weight = small_all[:CH]
    final_weight = small_all[CH:].T
    time_emb = jnp.sum(time_parts, axis=0) + second_bias_own
    onehot = (labels_all[:, None] == jnp.arange(CLASSES + 1, dtype=jnp.int32)[None, :]).astype(
        bfloat
    )
    condition = time_emb + jnp.dot(onehot, class_table, preferred_element_type=single)
    cond_act = jax.nn.silu(condition).astype(bfloat)
    cond_rank = lax.dynamic_index_in_dim(
        cond_act.reshape(n_data, n_model, rows), model_index, 1, keepdims=False
    )
    mod_part = jnp.dot(cond_rank, mod_weight, preferred_element_type=single)
    (mod_parts,) = exchange(
        [(mod_part.reshape(n_data, 8, D), "each")],
        "dp",
        sizes,
        2,
    )
    modulation = jnp.sum(mod_parts, axis=0).reshape(1, 8 * D) + mod_bias
    shift_one, scale_one, gate_one, shift_two, scale_two, gate_two, shift_end, scale_end = (
        jnp.split(modulation, 8, axis=1)
    )

    group_grid = lax.dynamic_slice_in_dim(grid_all, data_index * n_model, n_model, 0)
    group_grid = jnp.stack(
        [
            lax.dynamic_index_in_dim(group_grid, model_index ^ rank, 0, keepdims=False)
            for rank in range(n_model)
        ]
    )
    cosine, sine, mask = turn_tables(group_grid, length)
    valid_slot = valid_slots(patch_grid, length)
    clean_three = clean_patches.reshape(images, length, CH)
    noise_three = noise_patches.reshape(images, length, CH)
    noisy_low = noisy_input(clean_three, noise_three, timesteps).astype(bfloat)
    hidden = jnp.dot(noisy_low, patch_weight, preferred_element_type=single) + patch_bias
    normed_one = modulate(hidden, shift_one, scale_one).astype(bfloat)
    one_rows = jnp.concatenate(gather_rows(normed_one.reshape(length, D), n_model), axis=0)
    qkv_bias_own = jnp.concatenate(
        [
            lax.dynamic_slice_in_dim(qkv_bias, part * D + model_index * head_cols, head_cols)
            for part in range(3)
        ]
    )
    qkv = jnp.dot(one_rows, qkv_weight, preferred_element_type=single) + qkv_bias_own
    low, attended, log_total = attention(
        qkv.reshape(n_model, length, 3 * head_cols), cosine, sine, mask, heads
    )
    attended_rows = attended.reshape(n_model * length, head_cols)
    branch_part = jnp.dot(attended_rows, out_weight, preferred_element_type=single).astype(bfloat)
    branch_part = branch_part.reshape(n_model, length, D)
    branch = (
        scatter_rows(
            (branch_part[2], branch_part[3]), (branch_part[0], branch_part[1]), n_model
        )[None]
        + out_bias
    )
    hidden_mid = hidden + gate_one[:, None, :] * branch
    normed_two = modulate(hidden_mid, shift_two, scale_two).astype(bfloat)

    two_rows = gather_rows(normed_two.reshape(length, D), n_model)
    two_halves = (
        jnp.concatenate(two_rows[:2], axis=0),
        jnp.concatenate(two_rows[2:], axis=0),
    )
    gates, ups, acts, parts = [], [], [], []
    for part in two_halves:
        gate_val = jnp.dot(part, swiglu_use[0], preferred_element_type=single)
        up_val = jnp.dot(part, swiglu_use[1], preferred_element_type=single)
        act = (jax.nn.silu(gate_val) * up_val).astype(bfloat)
        gates.append(gate_val)
        ups.append(up_val)
        acts.append(act)
        parts.append(backward_product(act, swiglu_use[2]).astype(bfloat).reshape(2, length, D))
    mixed = scatter_rows(parts[1], parts[0], n_model)[None]
    hidden_end = hidden_mid + gate_two[:, None, :] * mixed
    normed_end = modulate(hidden_end, shift_end, scale_end).astype(bfloat)
    output = jnp.dot(normed_end, final_weight, preferred_element_type=single) + final_bias
    local_loss, loss_pull = jax.vjp(
        lambda values_out: loss_terms(values_out, clean_three, noise_three, timesteps, valid_slot),
        output,
    )
    d_output = loss_pull(jnp.asarray(1.0 / total_images, single))[0].astype(bfloat)
    d_normed_end = backward_product(d_output, final_weight)
    unused, pull_end = jax.vjp(modulate, hidden_end, shift_end, scale_end)
    d_hidden_end, d_shift_end, d_scale_end = pull_end(d_normed_end)
    d_mixed = (gate_two[:, None, :] * d_hidden_end).astype(bfloat)
    d_gate_two = jnp.sum(mixed * d_hidden_end, axis=1)
    dmixed_rows = gather_rows(d_mixed.reshape(length, D), n_model)
    dmixed_halves = (
        jnp.concatenate(dmixed_rows[:2], axis=0),
        jnp.concatenate(dmixed_rows[2:], axis=0),
    )
    d_gates, d_ups, d_parts = [], [], []
    for part, gate_val, up_val in zip(dmixed_halves, gates, ups):
        d_inner = jnp.dot(part, swiglu_use[2], preferred_element_type=single)
        unused, pull_glu = jax.vjp(
            lambda gate_in, up_in: jax.nn.silu(gate_in) * up_in, gate_val, up_val
        )
        d_gate, d_up = pull_glu(d_inner)
        d_gate, d_up = d_gate.astype(bfloat), d_up.astype(bfloat)
        d_gates.append(d_gate)
        d_ups.append(d_up)
        d_parts.append(
            (backward_product(d_gate, swiglu_use[0]) + backward_product(d_up, swiglu_use[1]))
            .astype(bfloat)
            .reshape(2, length, D)
        )
    d_normed_two = scatter_rows(d_parts[1], d_parts[0], n_model)[None]
    rows_ready = jnp.concatenate(two_halves, axis=0)
    dmixed_ready = jnp.concatenate(dmixed_halves, axis=0)
    half = hidden_units // 2

    def owned(gradient, cut):
        return reduce_dp(gradient.reshape(n_data, rows, -1), n_data, cut)

    grad_swiglu = jnp.stack(
        [
            owned(weight_grad(rows_ready, jnp.concatenate(d_gates, axis=0)), half),
            owned(weight_grad(rows_ready, jnp.concatenate(d_ups, axis=0)), half),
            owned(weight_grad(dmixed_ready, jnp.concatenate(acts, axis=0)), half),
        ]
    )
    unused, pull_two = jax.vjp(modulate, hidden_mid, shift_two, scale_two)
    d_mid_part, d_shift_two, d_scale_two = pull_two(d_normed_two)
    d_hidden_mid = d_hidden_end + d_mid_part
    d_branch = (gate_one[:, None, :] * d_hidden_mid).astype(bfloat)
    d_gate_one = jnp.sum(branch * d_hidden_mid, axis=1)

    dbranch_rows = jnp.concatenate(gather_rows(d_branch.reshape(length, D), n_model), axis=0)
    d_attended = backward_product(dbranch_rows, out_weight).astype(bfloat)
    d_qkv = attention_back(
        low,
        log_total,
        d_attended.reshape(n_model, length, head_cols),
        cosine,
        sine,
        mask,
        heads,
    ).reshape(n_model * length, 3 * head_cols)
    grad_out = reduce_out(weight_grad(attended_rows, dbranch_rows), sizes)
    grad_qkv_own = owned(weight_grad(one_rows, d_qkv), 384)
    d_one_part = backward_product(d_qkv, qkv_weight).astype(bfloat).reshape(n_model, length, D)
    d_normed_one = scatter_rows(
        (d_one_part[2], d_one_part[3]), (d_one_part[0], d_one_part[1]), n_model
    )[None]
    unused, pull_one = jax.vjp(modulate, hidden, shift_one, scale_one)
    d_hidden_part, d_shift_one, d_scale_one = pull_one(d_normed_one)
    d_hidden = (d_hidden_mid + d_hidden_part).astype(bfloat)

    qkv_blocks = gather_rows(grad_qkv_own.astype(bfloat), n_model)
    qkv_stack = jnp.stack(qkv_blocks)
    qkv_stack = jnp.stack(
        [
            lax.dynamic_index_in_dim(qkv_stack, model_index ^ rank, 0, keepdims=False)
            for rank in range(n_model)
        ]
    ).astype(single)
    grad_qkv = (
        qkv_stack.reshape(n_model, rows, 3, head_cols).transpose(1, 2, 0, 3).reshape(rows, 3 * D)
    )

    d_modulation = jnp.concatenate(
        [
            d_shift_one,
            d_scale_one,
            d_gate_one,
            d_shift_two,
            d_scale_two,
            d_gate_two,
            d_shift_end,
            d_scale_end,
        ],
        axis=1,
    ).astype(bfloat)
    (dmod_all,) = exchange(
        [(d_modulation.reshape(16, D // 2), "all")], "both", sizes, 3
    )
    dmod_all = dmod_all.reshape(total_images, 8 * D)
    d_cond_act = backward_product(dmod_all, mod_weight)
    unused, pull_cond = jax.vjp(jax.nn.silu, condition)
    d_condition = pull_cond(d_cond_act)[0]
    d_time_emb = d_condition.astype(bfloat)
    (dtime_parts,) = exchange([(d_time_emb, "all")], "dp", sizes, 4)
    dtime_all = dtime_parts.transpose(1, 0, 2).reshape(total_images, D)
    d_time_act = backward_product(dtime_all, time_second)
    unused, pull_time = jax.vjp(jax.nn.silu, time_pre)
    d_time_pre = pull_time(d_time_act)[0]
    grad_time_second = weight_grad(time_act, dtime_all)
    grad_mod = weight_grad(cond_act, dmod_all)
    grad_time_first = jnp.dot(
        sinus_all.astype(single).T,
        d_time_pre,
        precision=lax.Precision.HIGHEST,
        preferred_element_type=single,
    )
    grad_table = jnp.dot(
        onehot.astype(single).T,
        d_condition,
        precision=lax.Precision.HIGHEST,
        preferred_element_type=single,
    )
    grad_final_patch = weight_grad(noisy_low, d_hidden)
    grad_final = weight_grad(normed_end, d_output)

    qkv_sums = column_sum(d_qkv).reshape(3, head_cols)
    qkv_bias_part = lax.dynamic_update_slice(
        jnp.zeros((3, D), single), qkv_sums, (0, model_index * head_cols)
    )
    local_sums = jnp.concatenate(
        [
            column_sum(d_hidden),
            qkv_bias_part.reshape(-1),
            column_sum(d_branch),
            column_sum(d_output),
            local_loss.reshape(1),
            jnp.zeros((95,), single),
            grad_final_patch.reshape(-1),
            grad_final.T.reshape(-1),
        ]
    )
    everyone = n_data * n_model
    chunk_rows = -(-local_sums.shape[0] // (everyone * 1024)) * 8
    local_sums = jnp.pad(local_sums, (0, everyone * chunk_rows * 128 - local_sums.shape[0]))
    (sum_parts,) = exchange(
        [(local_sums.reshape(everyone, chunk_rows, 128), "each")], "both", sizes, 5
    )
    chunk = jnp.sum(sum_parts, axis=0)
    local_squares = (
        jnp.sum(grad_time_second * grad_time_second)
        + jnp.sum(grad_mod * grad_mod)
        + jnp.sum(grad_out * grad_out)
        + jnp.sum(grad_time_first * grad_time_first)
        + jnp.sum(grad_table * grad_table)
    ) / n_model + jnp.sum(grad_swiglu * grad_swiglu) + jnp.sum(grad_qkv_own * grad_qkv_own)
    extra = jnp.concatenate([jnp.sum(d_time_pre, axis=0), local_squares.reshape(1)])
    extra = jnp.pad(extra, (0, 1024 - extra.shape[0])).reshape(8, 128)
    (late,) = exchange([(jnp.concatenate([chunk, extra], axis=0), "all")], "both", sizes, 6)
    sums = late[:, :chunk_rows].reshape(-1)
    extras = late[:, chunk_rows:].reshape(everyone, 1024)
    first_bias_grad = extras.reshape(n_data, n_model, 1024)[:, 0, :rows].reshape(D)
    squares = jnp.sum(extras[:, rows])
    ends = [D, 4 * D, 5 * D, 5 * D + 2 * CH, 5 * D + 2 * CH + 1]
    base = 5 * D + 128
    loss_sum = sums[5 * D + 2 * CH]
    grad_patch = sums[base : base + CH * D].reshape(CH, D)
    grad_final = sums[base + CH * D : base + 3 * CH * D].reshape(2 * CH, D)
    grad_patch = cut_columns(grad_patch, owned_start, rows)
    grad_final_own = cut_columns(grad_final, owned_start, rows).T
    grad_bias = jnp.concatenate(
        [
            sums[:D],
            first_bias_grad,
            column_sum(dtime_all),
            column_sum(dmod_all),
            sums[D : 4 * D],
            sums[4 * D : 5 * D],
            sums[5 * D : 5 * D + 2 * CH],
        ]
    )
    shared = sums[base : base + 3 * CH * D]
    squares = squares + jnp.sum(grad_bias * grad_bias) + jnp.sum(shared * shared)
    grad_norm = jnp.sqrt(squares)
    factor = jnp.minimum(1.0, CLIP_LIMIT / grad_norm)
    grad_mats = jnp.concatenate(
        [grad_time_second, grad_mod, grad_qkv, grad_out, grad_final_own], axis=1
    )
    grad_embed = jnp.concatenate([grad_patch, grad_time_first, grad_table], axis=0)
    mats_out = adam_step(
        matrices, matrices_first, matrices_second, grad_mats, matrices_average, factor, LEARN_RATE
    )
    embed_out = adam_step(
        embeddings,
        embeddings_first,
        embeddings_second,
        grad_embed,
        embeddings_average,
        factor,
        TABLE_RATE,
    )
    swiglu_out = adam_step(
        swiglu_weights, swiglu_first, swiglu_second, grad_swiglu, swiglu_average, factor, LEARN_RATE
    )
    bias_out = adam_step(
        biases, biases_first, biases_second, grad_bias, biases_average, factor, TABLE_RATE
    )
    return (
        loss_sum,
        grad_norm,
        mats_out[0],
        embed_out[0],
        swiglu_out[0],
        bias_out[0],
        mats_out[1],
        embed_out[1],
        swiglu_out[1],
        bias_out[1],
        mats_out[2],
        embed_out[2],
        swiglu_out[2],
        bias_out[2],
        mats_out[3],
        embed_out[3],
        swiglu_out[3],
        bias_out[3],
        grad_bias * factor,
    )


def solution(mesh):
    placed = (
        P(("dp", "mlp"), None),
        P(("dp", "mlp"), None),
        P(("dp", "mlp"), None),
        P(("dp", "mlp")),
        P(("dp", "mlp")),
        P("dp", None),
        P(None, "dp"),
        P(None, "dp", "mlp"),
        P(),
        P("dp", None),
        P(None, "dp"),
        P(None, "dp", "mlp"),
        P(),
        P("dp", None),
        P(None, "dp"),
        P(None, "dp", "mlp"),
        P(),
        P("dp", None),
        P(None, "dp"),
        P(None, "dp", "mlp"),
        P(),
    )
    return jax.shard_map(
        on_device,
        mesh=mesh,
        in_specs=placed,
        out_specs=(
            P(),
            P(),
            P("dp", None),
            P(None, "dp"),
            P(None, "dp", "mlp"),
            P(),
            P("dp", None),
            P(None, "dp"),
            P(None, "dp", "mlp"),
            P(),
            P("dp", None),
            P(None, "dp"),
            P(None, "dp", "mlp"),
            P(),
            P("dp", None),
            P(None, "dp"),
            P(None, "dp", "mlp"),
            P(),
            P(),
        ),
        check_vma=False,
    )
```

time: 1640 us -> 701 us (0.43)
  waiting for transfers between devices: 948 us -> 165 us
  blocking collectives: 364 us -> 0 us
  Pallas kernels: 0 us -> 130 us
  starting transfers between devices: 7.18 us -> 121 us
  matrix products: 126 us -> 68.6 us
  local copies, waits for them, and re-layouts: 57.4 us -> 94.4 us
    all_gather x11 -> x0, waiting for transfers between devices: 880 us -> none  [the longest x1 659 us: on_device(): lax.all_gather(matrices.astype(bfloat), 'dp', axis=0, tiled=True)]
    all_gather x8 -> x0, blocking collectives: 325 us -> none  [the longest x1 90.9 us: on_device(): lax.all_gather(sinus_emb.astype(single).astype(jnp.bfloat16), ('dp', 'mlp...]
    ppermute x0 -> x99, waiting for transfers between devices: none -> 165 us  [the longest x4 49.5 us: reduce_dp(): got = lax.ppermute(give, 'dp', swap_pairs(count)).astype(jnp.float32)]
    pallas_call x0 -> x11, Pallas kernels: none -> 130 us  [the longest x7 92.2 us: exchange(): pl.pallas_call(functools.partial(exchange_kernel, axes, sizes, modes), ou...]
    ppermute x0 -> x99, starting transfers between devices: none -> 121 us  [the longest x29 52.7 us: flip(): lax.ppermute(value, 'mlp', [(spot, spot ^ bit) for spot in range(count)])]
    reduce_scatter x3 -> x0, waiting for transfers between devices: 66 us -> none  [the longest x1 31.3 us: on_device(): lax.psum_scatter((backward_product(d_gate, swiglu_use[0]) + backward_prod...]
    psum x1 -> x0, blocking collectives: 39.6 us -> none  [on_device(): lax.psum((grad_bias, grad_patch, local_loss), ('dp', 'mlp'))]
    dot_general x8 -> x11, matrix products: 39.5 us -> 18.9 us  [backward_product(): lax.dot_general(gradient, weight, (((gradient.ndim - 1,), (1,)), ((), ())...]
  transfers between devices with their start and end apart: 16 -> 99, of which waited for: 11 -> 39; matrix products, arithmetic and copies ran while one was open for 10% -> 22% of each run, Pallas kernels for 0% -> 12%
where the time goes in v1:
time: 701 us; the launch traced here: 692 us
  waiting for transfers between devices  165 us (24%)
  Pallas kernels  130 us (19%)
  starting transfers between devices  121 us (17%)
  local copies, waits for them, and re-layouts  94.4 us (13%)
  other arithmetic  94.3 us (13%)
  matrix products  68.6 us (10%)
  between operations  18.4 us (3%)
    pallas_call x7, Pallas kernels, exchange(): pl.pallas_call(functools.partial(exchange_kernel, axes, sizes, modes), ou...  92.2 us
    ppermute x29, starting transfers between devices, flip(): lax.ppermute(value, 'mlp', [(spot, spot ^ bit) for spot in range(count)])  52.7 us
    ppermute x4, waiting for transfers between devices, reduce_dp(): got = lax.ppermute(give, 'dp', swap_pairs(count)).astype(jnp.float32)  49.5 us
    unnamed x334, local copies, waits for them, and re-layouts  41.2 us
    ppermute x12, waiting for transfers between devices, ring_pieces(): arrived.append(lax.ppermute(arrived[-1], 'dp', ring_pairs(depth, shift)))  41 us
    add x4, other arithmetic, adam_step(): average_decay * average + (1.0 - average_decay) * weight  36.3 us
    ppermute x24, waiting for transfers between devices, reduce_ring(): lax.ppermute(running.astype(jnp.bfloat16), 'dp', ring_pairs(depth, shift))  23.2 us
    ppermute x24, starting transfers between devices, reduce_ring(): lax.ppermute(running.astype(jnp.bfloat16), 'dp', ring_pairs(depth, shift))  22.4 us
  transfers between devices with their start and end apart: 99, of which 39 were waited for; matrix products, arithmetic and copies ran while one was open for 22% of the time, Pallas kernels for 12%

profile of v1, /device:TPU:15, one launch (start us, length us, event | category | flops | bytes accessed | tf_op | source)
XLA Modules:
  0.0 691.6 jit_solution(7738252651444833519)
XLA Ops:
  5.1 9.7 %copy.100 = bf16[144,15008]{0,1:T(8,128)(2,1)} copy(f32[144,15008]{1,0:T(8,128)} %param.26) | data formatting | bytes 12966912 | tf_op args[5]
  26.8 12.5 %shard_map.348 = s32[32,8,128]{2,1,0:T(8,128)S(1)} custom-call(s32[8,128]{1,0:T(8,128)S(1)} %pad.22.refs_0_), custom_call_target="tpu_custom_call" | custom-call | tf_op jit(solution)/shard_map/pallas_call | solution.py:211
  43.2 13.1 %shard_map.349 = (f32[8,32,144]{2,1,0:T(8,128)S(1)}, bf16[8,48,144]{2,1,0:T(8,128)(2,1)S(1)}) custom-call(f32[8,32,144]{2,1,0:T(8,128)S(1)} %bitcast.299, bf16[48,144]{1,0:T(8,128)(2,1)S(1)} %pad_maximum_fusion.22.refs_1_), custom_call_target="tpu_custom_call" | custom-call | tf_op jit(solution)/shard_map/pallas_call | solution.py:211
  63.3 10.2 %shard_map.350 = f32[8,8,1152]{2,1,0:T(8,128)S(1)} custom-call(f32[8,8,1152]{2,1,0:T(8,128)S(1)} %copy.105.refs_0_), custom_call_target="tpu_custom_call" | custom-call | tf_op jit(solution)/shard_map/pallas_call | solution.py:211
  119.5 7.6 %collective-permute-start = (bf16[256,1152]{1,0:T(8,128)(2,1)}, bf16[256,1152]{1,0:T(8,128)(2,1)}, u32[]{:S(2)}, u32[]{:S(2)}) collective-permute-start(bf16[256,1152]{1,0:T(8,128)(2,1)} %add_convert_fusion.7), channel_id=1, source_target_pairs={{0,1},{1,0},{2,3},{3,2},{4,5},{5,4},{6,7},{7,6},{8,9},{9,8},{10,11... | collective-permute-start | bytes 1769480 | tf_op jit(solution)/shard_map/ppermute | solution.py:328
  162.8 18.7 %shard_map.352 = (bf16[4,256,864]{2,1,0:T(8,128)(2,1)S(1)}, bf16[4,256,288]{2,1,0:T(8,128)(2,1)S(1)}, f32[4,256,4]{2,1,0:T(8,128)S(1)}) custom-call(f32[4,256,864]{2,1,0:T(8,128)} %bitcast.305, f32[4,256,72]{2,1,0:T(8,128)S(1)} %pad_maximum_fusion.10.cos_ref, f32[4,256,72]{2,1,0:T(8,128)S(1)} %pad_maximum_fusion.11.sin_ref, ...), custom_call_target="tpu_custom_call" | custom-call | tf_op jit(solution)/shard_map/pallas_call | solution.py:463
  189.7 7.1 %collective-permute-done.29.refs_2_ = bf16[3,144,384]{2,1,0:T(8,128)(2,1)S(1)} collective-permute-done((bf16[3,144,384]{2,1,0:T(8,128)(2,1)S(1)}, bf16[3,144,384]{2,1,0:T(8,128)(2,1)S(1)}, u32[]{:S(2)}, u32[]{:S(2)}) %collective-permute-start.29) | collective-permute-done | bytes 331808 | tf_op jit(solution)/shard_map/ppermute | solution.py:264
  197.5 8.9 %collective-permute-done.36.refs_10_ = bf16[3,144,384]{2,1,0:T(8,128)(2,1)S(1)} collective-permute-done((bf16[3,144,384]{2,1,0:T(8,128)(2,1)S(1)}, bf16[3,144,384]{2,1,0:T(8,128)(2,1)S(1)}, u32[]{:S(2)}, u32[]{:S(2)}) %collective-permute-start.36) | collective-permute-done | bytes 331808 | tf_op jit(solution)/shard_map/ppermute | solution.py:264
  216.4 9.4 %collective-permute-done.38.refs_12_ = bf16[3,144,384]{2,1,0:T(8,128)(2,1)S(1)} collective-permute-done((bf16[3,144,384]{2,1,0:T(8,128)(2,1)S(1)}, bf16[3,144,384]{2,1,0:T(8,128)(2,1)S(1)}, u32[]{:S(2)}, u32[]{:S(2)}) %collective-permute-start.38) | collective-permute-done | bytes 331808 | tf_op jit(solution)/shard_map/ppermute | solution.py:264
  231.8 6.2 collective-permute-done.40.refs_14_
  244.3 7.1 %collective-permute-done.34.refs_7_ = bf16[3,144,384]{2,1,0:T(8,128)(2,1)S(1)} collective-permute-done((bf16[3,144,384]{2,1,0:T(8,128)(2,1)S(1)}, bf16[3,144,384]{2,1,0:T(8,128)(2,1)S(1)}, u32[]{:S(2)}, u32[]{:S(2)}) %collective-permute-start.34) | collective-permute-done | bytes 331808 | tf_op jit(solution)/shard_map/ppermute | solution.py:284
  251.4 7.1 %collective-permute-done.41.refs_15_ = bf16[3,144,384]{2,1,0:T(8,128)(2,1)S(1)} collective-permute-done((bf16[3,144,384]{2,1,0:T(8,128)(2,1)S(1)}, bf16[3,144,384]{2,1,0:T(8,128)(2,1)S(1)}, u32[]{:S(2)}, u32[]{:S(2)}) %collective-permute-start.41) | collective-permute-done | bytes 331808 | tf_op jit(solution)/shard_map/ppermute | solution.py:284
  285.1 8.9 %collective-permute-done.46 = bf16[256,1152]{1,0:T(8,128)(2,1)} collective-permute-done((bf16[256,1152]{1,0:T(8,128)(2,1)}, bf16[256,1152]{1,0:T(8,128)(2,1)}, u32[]{:S(2)}, u32[]{:S(2)}) %collective-permute-start.46) | collective-permute-done | bytes 589856 | tf_op jit(solution)/shard_map/ppermute | solution.py:328
  344.1 12.8 %collective-permute-done.82 = bf16[4,144,768]{2,1,0:T(8,128)(2,1)S(1)} collective-permute-done((bf16[4,144,768]{2,1,0:T(8,128)(2,1)S(1)}, bf16[4,144,768]{2,1,0:T(8,128)(2,1)S(1)}, u32[]{:S(2)}, u32[]{:S(2)}) %collective-permute-start.82) | collective-permute-done | bytes 884768 | tf_op jit(solution)/shard_map/ppermute | solution.py:316
  357.4 18.5 %collective-permute-done.75 = bf16[4,144,768]{2,1,0:T(8,128)(2,1)S(1)} collective-permute-done((bf16[4,144,768]{2,1,0:T(8,128)(2,1)S(1)}, bf16[4,144,768]{2,1,0:T(8,128)(2,1)S(1)}, u32[]{:S(2)}, u32[]{:S(2)}) %collective-permute-start.75) | collective-permute-done | bytes 884768 | tf_op jit(solution)/shard_map/ppermute | solution.py:316
  376.7 18.2 %collective-permute-done.68 = bf16[4,144,768]{2,1,0:T(8,128)(2,1)S(1)} collective-permute-done((bf16[4,144,768]{2,1,0:T(8,128)(2,1)S(1)}, bf16[4,144,768]{2,1,0:T(8,128)(2,1)S(1)}, u32[]{:S(2)}, u32[]{:S(2)}) %collective-permute-start.68) | collective-permute-done | bytes 884768 | tf_op jit(solution)/shard_map/ppermute | solution.py:316
  428.4 7.7 %collective-permute-start.53 = (bf16[256,1152]{1,0:T(8,128)(2,1)S(1)}, bf16[256,1152]{1,0:T(8,128)(2,1)S(1)}, u32[]{:S(2)}, u32[]{:S(2)}) collective-permute-start(bf16[256,1152]{1,0:T(8,128)(2,1)S(1)} %get-tuple-element.73), channel_id=1, source_target_pairs={{0,1},{1,0},{2,3},{3,2},{4,5},{5,4},{6,7},{7,6},{8,9},{9,8},{10,11... | collective-permute-start | bytes 1769480 | tf_op jit(solution)/shard_map/ppermute | solution.py:328
  436.3 8.0 %collective-permute-start.55 = (bf16[256,1152]{1,0:T(8,128)(2,1)S(1)}, bf16[256,1152]{1,0:T(8,128)(2,1)S(1)}, u32[]{:S(2)}, u32[]{:S(2)}) collective-permute-start(bf16[256,1152]{1,0:T(8,128)(2,1)S(1)} %collective-permute-done.54), channel_id=1, source_target_pairs={{0,1},{1,0},{2,3},{3,2},{4,5},{5,4},{6,7},{7,6},{8,9},{9,8},{10,11... | collective-permute-start | bytes 1769480 | tf_op jit(solution)/shard_map/ppermute | solution.py:328
  452.7 13.5 %shard_map.354 = bf16[4,256,864]{2,1,0:T(8,128)(2,1)S(1)} custom-call(bf16[4,256,864]{2,1,0:T(8,128)(2,1)S(1)} %copy-done.3, f32[4,256,4]{2,1,0:T(8,128)S(1)} %get-tuple-element.28.total_ref, bf16[4,256,288]{2,1,0:T(8,128)(2,1)S(1)} %bitcast.294, f32[4,256,72]{2,1,0:T(8,128)S(1)} %pad_maximum_fusion.10.cos_ref, ...), custom_call_target="tpu_custom_call" | custom-call | tf_op jit(solution)/shard_map/pallas_call | solution.py:522
  497.6 12.3 %collective-permute-start.66 = (bf16[144,1152]{1,0:T(8,128)(2,1)S(1)}, bf16[144,1152]{1,0:T(8,128)(2,1)}, u32[]{:S(2)}, u32[]{:S(2)}) collective-permute-start(bf16[144,1152]{1,0:T(8,128)(2,1)S(1)} %fusion.50), channel_id=1, source_target_pairs={{0,1},{1,0},{2,3},{3,2},{4,5},{5,4},{6,7},{7,6},{8,9},{9,8},{10,11... | collective-permute-start | bytes 995336 | tf_op jit(solution)/shard_map/ppermute | solution.py:328
  529.1 24.3 %shard_map.356 = bf16[32,16,576]{2,1,0:T(8,128)(2,1)S(1)} custom-call(bf16[16,576]{1,0:T(8,128)(2,1)S(1)} %convert_element_type.559.refs_0_), custom_call_target="tpu_custom_call" | custom-call | tf_op jit(solution)/shard_map/pallas_call | solution.py:211
  594.6 11.8 %shard_map.355 = f32[32,16,128]{2,1,0:T(8,128)S(1)} custom-call(f32[32,16,128]{2,1,0:T(8,128)S(1)} %bitcast.298), custom_call_target="tpu_custom_call" | custom-call | tf_op jit(solution)/shard_map/pallas_call | solution.py:211
  629.0 15.0 %shard_map.358 = f32[32,24,128]{2,1,0:T(8,128)S(1)} custom-call(f32[24,128]{1,0:T(8,128)S(1)} %pad_maximum_fusion.24.refs_0_), custom_call_target="tpu_custom_call" | custom-call | tf_op jit(solution)/shard_map/pallas_call | solution.py:211
  659.9 28.1 %multiply_add_fusion = (f32[144,15008]{1,0:T(8,128)}, f32[144,15008]{1,0:T(8,128)}, f32[144,15008]{1,0:T(8,128)}, f32[144,15008]{1,0:T(8,128)}) fusion(f32[144,15008]{1,0:T(8,128)} %param.38, f32[144,15008]{1,0:T(8,128)} %param.26, f32[144,15008]{1,0:T(8,128)} %bitcast_dynamic-update-slice_fusion, f32[]{:T(128)S(6)} %min.3, f32[144,15008]{1,0:T(8,128)} %param.30, ...), kind=kLoop, calls=%fused_computation.2 | loop fusion | flops 41061888 | bytes 77801472 | tf_op jit(solution)/shard_map/add | solution.py:109
  (794 shorter events, 376.2 us)
Async XLA Ops:
  2.1 103.2 %collective-permute-start.3 = (bf16[80,864]{1,0:T(8,128)(2,1)S(1)}, bf16[80,864]{1,0:T(8,128)(2,1)S(1)}, u32[]{:S(2)}, u32[]{:S(2)}) collective-permute-start(bf16[80,864]{1,0:T(8,128)(2,1)S(1)} %slice.353.refs_0_), channel_id=1, source_target_pairs={{0,4},{4,0},{8,12},{12,8},{16,20},{20,16},{24,28},{28,24},{1,5},{5... | collective-permute-start | bytes 414728 | tf_op jit(solution)/shard_map/ppermute | solution.py:284
  2.5 96.7 %collective-permute-start.4 = (bf16[80,864]{1,0:T(8,128)(2,1)S(1)}, bf16[80,864]{1,0:T(8,128)(2,1)S(1)}, u32[]{:S(2)}, u32[]{:S(2)}) collective-permute-start(bf16[80,864]{1,0:T(8,128)(2,1)S(1)} %slice.353.refs_0_), channel_id=1, source_target_pairs={{0,8},{4,12},{8,16},{12,20},{16,24},{20,28},{24,0},{28,4},{1,9},{5... | collective-permute-start | bytes 414728 | tf_op jit(solution)/shard_map/ppermute | solution.py:264
  3.9 100.8 %collective-permute-start.10 = (bf16[64,864]{1,0:T(8,128)(2,1)S(1)}, bf16[64,864]{1,0:T(8,128)(2,1)S(1)}, u32[]{:S(2)}, u32[]{:S(2)}) collective-permute-start(bf16[64,864]{1,0:T(8,128)(2,1)S(1)} %pad_maximum_fusion.21.refs_8_), channel_id=1, source_target_pairs={{0,4},{4,0},{8,12},{12,8},{16,20},{20,16},{24,28},{28,24},{1,5},{5... | collective-permute-start | bytes 331784 | tf_op jit(solution)/shard_map/ppermute | solution.py:284
  16.1 60.3 %collective-permute-start.20 = (bf16[64,1152]{0,1:T(8,128)(2,1)S(1)}, bf16[64,1152]{0,1:T(8,128)(2,1)}, u32[]{:S(2)}, u32[]{:S(2)}) collective-permute-start(bf16[64,1152]{0,1:T(8,128)(2,1)S(1)} %slice.355), channel_id=1, source_target_pairs={{0,24},{4,28},{9,1},{13,5},{18,10},{22,14},{27,19},{31,23}} | collective-permute-start | bytes 442376 | tf_op jit(solution)/shard_map/ppermute | solution.py:370
  19.2 63.9 %collective-permute-start.17 = (bf16[80,1152]{0,1:T(8,128)(2,1)}, bf16[80,1152]{0,1:T(8,128)(2,1)}, u32[]{:S(2)}, u32[]{:S(2)}) collective-permute-start(bf16[80,1152]{0,1:T(8,128)(2,1)} %slice.354), channel_id=1, source_target_pairs={{0,8},{4,12},{9,17},{13,21},{18,26},{22,30},{27,3},{31,7}} | collective-permute-start | bytes 552968 | tf_op jit(solution)/shard_map/ppermute | solution.py:370
  99.1 30.4 %collective-permute-start.1 = (bf16[256,1152]{1,0:T(8,128)(2,1)}, bf16[256,1152]{1,0:T(8,128)(2,1)}, u32[]{:S(2)}, u32[]{:S(2)}) collective-permute-start(bf16[256,1152]{1,0:T(8,128)(2,1)} %add_convert_fusion.7), channel_id=1, source_target_pairs={{0,2},{1,3},{2,0},{3,1},{4,6},{5,7},{6,4},{7,5},{8,10},{9,11},{10,... | collective-permute-start | bytes 1769480 | tf_op jit(solution)/shard_map/ppermute | solution.py:328
  112.2 34.9 %collective-permute-start.23 = (bf16[144,1152]{1,0:T(8,128)(2,1)}, bf16[144,1152]{1,0:T(8,128)(2,1)}, u32[]{:S(2)}, u32[]{:S(2)}) collective-permute-start(bf16[144,1152]{1,0:T(8,128)(2,1)} %copy.109), channel_id=1, source_target_pairs={{0,4},{4,0},{8,12},{12,8},{16,20},{20,16},{24,28},{28,24},{1,5},{5... | collective-permute-start | bytes 995336 | tf_op jit(solution)/shard_map/ppermute | solution.py:374
  119.5 32.4 %collective-permute-start = (bf16[256,1152]{1,0:T(8,128)(2,1)}, bf16[256,1152]{1,0:T(8,128)(2,1)}, u32[]{:S(2)}, u32[]{:S(2)}) collective-permute-start(bf16[256,1152]{1,0:T(8,128)(2,1)} %add_convert_fusion.7), channel_id=1, source_target_pairs={{0,1},{1,0},{2,3},{3,2},{4,5},{5,4},{6,7},{7,6},{8,9},{9,8},{10,11... | collective-permute-start | bytes 1769480 | tf_op jit(solution)/shard_map/ppermute | solution.py:328
  184.1 23.7 %collective-permute-start.24 = (bf16[256,1152]{1,0:T(8,128)(2,1)S(1)}, bf16[256,1152]{1,0:T(8,128)(2,1)S(1)}, u32[]{:S(2)}, u32[]{:S(2)}) collective-permute-start(bf16[256,1152]{1,0:T(8,128)(2,1)S(1)} %get-tuple-element.101), channel_id=1, source_target_pairs={{0,1},{1,0},{2,3},{3,2},{4,5},{5,4},{6,7},{7,6},{8,9},{9,8},{10,11... | collective-permute-start | bytes 1769480 | tf_op jit(solution)/shard_map/ppermute | solution.py:328
  196.9 30.7 %collective-permute-start.35 = (bf16[3,144,384]{2,1,0:T(8,128)(2,1)S(1)}, bf16[3,144,384]{2,1,0:T(8,128)(2,1)S(1)}, u32[]{:S(2)}, u32[]{:S(2)}) collective-permute-start(bf16[3,144,384]{2,1,0:T(8,128)(2,1)S(1)} %get-tuple-element.122.refs_8_), channel_id=1, source_target_pairs={{0,4},{4,0},{8,12},{12,8},{16,20},{20,16},{24,28},{28,24},{1,5},{5... | collective-permute-start | bytes 995336 | tf_op jit(solution)/shard_map/ppermute | solution.py:284
  227.6 35.6 %collective-permute-start.43 = (bf16[256,1152]{1,0:T(8,128)(2,1)S(1)}, bf16[256,1152]{1,0:T(8,128)(2,1)S(1)}, u32[]{:S(2)}, u32[]{:S(2)}) collective-permute-start(bf16[256,1152]{1,0:T(8,128)(2,1)S(1)} %add_convert_fusion.5), channel_id=1, source_target_pairs={{0,2},{1,3},{2,0},{3,1},{4,6},{5,7},{6,4},{7,5},{8,10},{9,11},{10,... | collective-permute-start | bytes 1769480 | tf_op jit(solution)/shard_map/ppermute | solution.py:328
  325.9 95.0 %collective-permute-start.48 = (bf16[256,1152]{1,0:T(8,128)(2,1)S(1)}, bf16[256,1152]{1,0:T(8,128)(2,1)S(1)}, u32[]{:S(2)}, u32[]{:S(2)}) collective-permute-start(bf16[256,1152]{1,0:T(8,128)(2,1)S(1)} %slice.373), channel_id=1, source_target_pairs={{0,1},{1,0},{2,3},{3,2},{4,5},{5,4},{6,7},{7,6},{8,9},{9,8},{10,11... | collective-permute-start | bytes 1769480 | tf_op jit(solution)/shard_map/ppermute | solution.py:328
  339.6 36.3 %collective-permute-start.75 = (bf16[4,144,768]{2,1,0:T(8,128)(2,1)S(1)}, bf16[4,144,768]{2,1,0:T(8,128)(2,1)S(1)}, u32[]{:S(2)}, u32[]{:S(2)}) collective-permute-start(bf16[4,144,768]{2,1,0:T(8,128)(2,1)S(1)} %fusion.44), channel_id=1, source_target_pairs={{0,4},{4,0},{8,12},{12,8},{16,20},{20,16},{24,28},{28,24},{1,5},{5... | collective-permute-start | bytes 2654216 | tf_op jit(solution)/shard_map/ppermute | solution.py:316
  343.4 51.4 %collective-permute-start.68 = (bf16[4,144,768]{2,1,0:T(8,128)(2,1)S(1)}, bf16[4,144,768]{2,1,0:T(8,128)(2,1)S(1)}, u32[]{:S(2)}, u32[]{:S(2)}) collective-permute-start(bf16[4,144,768]{2,1,0:T(8,128)(2,1)S(1)} %fusion.43), channel_id=1, source_target_pairs={{0,4},{4,0},{8,12},{12,8},{16,20},{20,16},{24,28},{28,24},{1,5},{5... | collective-permute-start | bytes 2654216 | tf_op jit(solution)/shard_map/ppermute | solution.py:316
  344.0 77.0 %collective-permute-start.52 = (bf16[256,1152]{1,0:T(8,128)(2,1)S(1)}, bf16[256,1152]{1,0:T(8,128)(2,1)S(1)}, u32[]{:S(2)}, u32[]{:S(2)}) collective-permute-start(bf16[256,1152]{1,0:T(8,128)(2,1)S(1)} %add_convert_fusion.2), channel_id=1, source_target_pairs={{0,2},{1,3},{2,0},{3,1},{4,6},{5,7},{6,4},{7,5},{8,10},{9,11},{10,... | collective-permute-start | bytes 1769480 | tf_op jit(solution)/shard_map/ppermute | solution.py:328
  357.3 37.9 %collective-permute-start.86 = (bf16[144,384]{1,0:T(8,128)(2,1)S(1)}, bf16[144,384]{1,0:T(8,128)(2,1)S(1)}, u32[]{:S(2)}, u32[]{:S(2)}) collective-permute-start(bf16[144,384]{1,0:T(8,128)(2,1)S(1)} %fusion.86), channel_id=1, source_target_pairs={{0,24},{4,28},{8,0},{12,4},{16,8},{20,12},{24,16},{28,20},{1,25},{... | collective-permute-start | bytes 331784 | tf_op jit(solution)/shard_map/ppermute | solution.py:302
  470.6 52.5 %collective-permute-start.56 = (bf16[256,1152]{1,0:T(8,128)(2,1)}, bf16[256,1152]{1,0:T(8,128)(2,1)S(1)}, u32[]{:S(2)}, u32[]{:S(2)}) collective-permute-start(bf16[256,1152]{1,0:T(8,128)(2,1)} %get-tuple-element.99), channel_id=1, source_target_pairs={{0,1},{1,0},{2,3},{3,2},{4,5},{5,4},{6,7},{7,6},{8,9},{9,8},{10,11... | collective-permute-start | bytes 1769480 | tf_op jit(solution)/shard_map/ppermute | solution.py:328
  477.7 32.2 %collective-permute-start.89 = (bf16[4,144,864]{2,1,0:T(8,128)(2,1)S(1)}, bf16[4,144,864]{2,1,0:T(8,128)(2,1)}, u32[]{:S(2)}, u32[]{:S(2)}) collective-permute-start(bf16[4,144,864]{2,1,0:T(8,128)(2,1)S(1)} %fusion.42), channel_id=1, source_target_pairs={{0,4},{4,0},{8,12},{12,8},{16,20},{20,16},{24,28},{28,24},{1,5},{5... | collective-permute-start | bytes 2985992 | tf_op jit(solution)/shard_map/ppermute | solution.py:316
  495.8 27.3 %collective-permute-start.58 = (bf16[256,1152]{1,0:T(8,128)(2,1)S(1)}, bf16[256,1152]{1,0:T(8,128)(2,1)S(1)}, u32[]{:S(2)}, u32[]{:S(2)}) collective-permute-start(bf16[256,1152]{1,0:T(8,128)(2,1)S(1)} %add_convert_fusion.1), channel_id=1, source_target_pairs={{0,2},{1,3},{2,0},{3,1},{4,6},{5,7},{6,4},{7,5},{8,10},{9,11},{10,... | collective-permute-start | bytes 1769480 | tf_op jit(solution)/shard_map/ppermute | solution.py:328
  497.6 112.5 %collective-permute-start.66 = (bf16[144,1152]{1,0:T(8,128)(2,1)S(1)}, bf16[144,1152]{1,0:T(8,128)(2,1)}, u32[]{:S(2)}, u32[]{:S(2)}) collective-permute-start(bf16[144,1152]{1,0:T(8,128)(2,1)S(1)} %fusion.50), channel_id=1, source_target_pairs={{0,1},{1,0},{2,3},{3,2},{4,5},{5,4},{6,7},{7,6},{8,9},{9,8},{10,11... | collective-permute-start | bytes 995336 | tf_op jit(solution)/shard_map/ppermute | solution.py:328
  520.0 50.9 %collective-permute-start.91 = (bf16[144,384]{1,0:T(8,128)(2,1)}, bf16[144,384]{1,0:T(8,128)(2,1)}, u32[]{:S(2)}, u32[]{:S(2)}) collective-permute-start(bf16[144,384]{1,0:T(8,128)(2,1)} %fusion.63), channel_id=1, source_target_pairs={{0,8},{4,12},{8,16},{12,20},{16,24},{20,28},{24,0},{28,4},{1,9},{5... | collective-permute-start | bytes 331784 | tf_op jit(solution)/shard_map/ppermute | solution.py:302
  523.1 49.9 %collective-permute-start.94 = (bf16[144,480]{1,0:T(8,128)(2,1)}, bf16[144,480]{1,0:T(8,128)(2,1)}, u32[]{:S(2)}, u32[]{:S(2)}) collective-permute-start(bf16[144,480]{1,0:T(8,128)(2,1)} %fusion.60), channel_id=1, source_target_pairs={{0,24},{4,28},{8,0},{12,4},{16,8},{20,12},{24,16},{28,20},{1,25},{... | collective-permute-start | bytes 414728 | tf_op jit(solution)/shard_map/ppermute | solution.py:302
  582.9 30.3 %collective-permute-start.96 = (bf16[144,864]{1,0:T(8,128)(2,1)S(1)}, bf16[144,864]{1,0:T(8,128)(2,1)S(1)}, u32[]{:S(2)}, u32[]{:S(2)}) collective-permute-start(bf16[144,864]{1,0:T(8,128)(2,1)S(1)} %fusion.56), channel_id=1, source_target_pairs={{0,1},{1,0},{2,3},{3,2},{4,5},{5,4},{6,7},{7,6},{8,9},{9,8},{10,11... | collective-permute-start | bytes 746504 | tf_op jit(solution)/shard_map/ppermute | solution.py:328
  586.6 26.5 %collective-permute-start.98 = (bf16[144,864]{1,0:T(8,128)(2,1)S(1)}, bf16[144,864]{1,0:T(8,128)(2,1)S(1)}, u32[]{:S(2)}, u32[]{:S(2)}) collective-permute-start(bf16[144,864]{1,0:T(8,128)(2,1)S(1)} %collective-permute-done.97), channel_id=1, source_target_pairs={{0,1},{1,0},{2,3},{3,2},{4,5},{5,4},{6,7},{7,6},{8,9},{9,8},{10,11... | collective-permute-start | bytes 746504 | tf_op jit(solution)/shard_map/ppermute | solution.py:328
  (233 other events, 2158.9 us)

commit v2 on v1

--- a/solution.py
+++ b/solution.py
@@ -557,6 +557,1656 @@
 
 def valid_slots(patch_grid, length):
     return jnp.arange(length, dtype=jnp.int32)[None, :] < patch_grid[:, 0:1] * patch_grid[:, 1:2]
+
+
+def device_parts():
+    d, m = lax.axis_index("dp"), lax.axis_index("mlp")
+    return d, m, lax.div(d, NX), lax.rem(d, NX)
+
+
+class Sender:
+    def __init__(self, send_sem, recv_sem):
+        self.send_sem, self.recv_sem = send_sem, recv_sem
+
+    def __call__(self, spot, source, target, device):
+        spot = spot if isinstance(spot, tuple) else (spot,)
+        return pltpu.make_async_remote_copy(
+            src_ref=source,
+            dst_ref=target,
+            send_sem=self.send_sem.at[spot],
+            recv_sem=self.recv_sem.at[spot],
+            device_id=device,
+            device_id_type=MESH_IDS,
+        )
+
+
+def modulate_rows(values, shift_by, scale_by):
+    row_mean = jnp.mean(values, axis=-1, keepdims=True)
+    centered = values - row_mean
+    variance = jnp.mean(centered * centered, axis=-1, keepdims=True)
+    return centered * lax.rsqrt(variance + 1e-06) * (1.0 + scale_by) + shift_by
+
+
+FORWARD_IN = (
+    "facts", "trig", "small", "time_first", "first_bias", "second_bias", "time_blocks",
+    "class_table", "mod_weight", "mod_bias", "noisy", "patch_bias", "qkv_shard", "out_shard",
+    "ff_shard", "qkv_bias", "out_bias",
+)
+FORWARD_OUT = (
+    "facts_all", "trig_all", "small_all", "time_pre", "condition", "modulation", "hidden",
+    "one_rows", "qkv_weight", "out_weight", "ff", "low", "attended", "totals", "branch",
+    "hidden_mid", "two_rows",
+)
+FORWARD_SCRATCH = (
+    "time_send", "time_recv", "mod_send", "mod_recv", "mod_low", "qkv", "parts_send",
+    "parts_recv", "facts_s", "facts_r", "small_s", "small_r", "time_s", "time_r",
+    "mods_s", "mods_r", "trig_s", "trig_r", "one_s", "one_r", "two_s", "two_r", "part_s",
+    "part_r", "qz_s", "qz_r", "qx_s", "qx_r", "oz_s", "oz_r", "ox_s", "ox_r", "fz_s", "fz_r",
+    "fx_s", "fx_r", "local_sem",
+)
+
+
+def forward_kernel(sizes, *refs):
+    names = FORWARD_IN + FORWARD_OUT + FORWARD_SCRATCH
+    r = dict(zip(names, refs, strict=True))
+    bfloat, single = jnp.bfloat16, jnp.float32
+    n_data, n_model = sizes
+    everyone = n_data * n_model
+    d, m, z, x = device_parts()
+    me = d * n_model + m
+    depth = n_data // NX
+    rows = D // n_data
+    heads = HEADS // n_model
+    head_cols = heads * HDIM
+    length = r["noisy"].shape[0]
+    units = r["ff_shard"].shape[2]
+    half = units // 2
+
+    def at_dp(spot):
+        return (spot, m)
+
+    def at_mlp(bit):
+        flipped = m + 1 - 2 * lax.rem(m, 2) if bit == 1 else lax.rem(m + 2, 4)
+        return (d, flipped)
+
+    up = lax.rem(z + 1, depth) * NX + x
+    down = lax.rem(z + depth - 1, depth) * NX + x
+    side = z * NX + 1 - x
+
+    barrier = pltpu.get_barrier_semaphore()
+
+    def greet(step, carry):
+        peer = lax.rem(me + step, everyone)
+        pl.semaphore_signal(
+            barrier,
+            inc=1,
+            device_id=(lax.div(peer, n_model), lax.rem(peer, n_model)),
+            device_id_type=MESH_IDS,
+        )
+        return carry
+
+    lax.fori_loop(1, everyone, greet, 0)
+
+    load_mod = pltpu.make_async_copy(r["mod_weight"], r["mod_low"], r["local_sem"].at[0])
+    load_mod.start()
+    own_ff = pltpu.make_async_copy(
+        r["ff_shard"],
+        r["ff"].at[:, pl.ds(pl.multiple_of(d * rows, 16), rows)],
+        r["local_sem"].at[1],
+    )
+    own_ff.start()
+    pl.semaphore_wait(barrier, everyone - 1)
+
+    send_facts = Sender(r["facts_s"], r["facts_r"])
+
+    def facts_copy(step):
+        peer = lax.rem(me + step, everyone)
+        return send_facts(
+            step - 1,
+            r["facts"],
+            r["facts_all"].at[me],
+            (lax.div(peer, n_model), lax.rem(peer, n_model)),
+        )
+
+    def loop(first, last, body):
+        def step_body(step, carry):
+            body(step)
+            return carry
+
+        lax.fori_loop(first, last, step_body, 0)
+
+    loop(1, everyone, lambda step: facts_copy(step).start())
+    r["facts_all"][me] = r["facts"][...]
+
+    def qkv_rows(spot, part):
+        if part == 0:
+            return r["qkv_weight"].at[pl.ds(pl.multiple_of(spot * rows, 16), 80)]
+        return r["qkv_weight"].at[pl.ds(pl.multiple_of(spot * rows + 80, 16), rows - 80)]
+
+    def ff_block(spot, part, which):
+        return r["ff"].at[
+            which,
+            pl.ds(pl.multiple_of(spot * rows, 16), rows),
+            pl.ds(half * part, half),
+        ]
+
+    def origin(step, part):
+        return lax.rem(z + (depth - step if part == 0 else step), depth) * NX + x
+
+    qz, qx = Sender(r["qz_s"], r["qz_r"]), Sender(r["qx_s"], r["qx_r"])
+    fz, fx = Sender(r["fz_s"], r["fz_r"]), Sender(r["fx_s"], r["fx_r"])
+
+    def qkv_along(step, part):
+        block = qkv_rows(origin(step - 1, part), part)
+        return qz((part, step - 1), block, block, at_dp(up if part == 0 else down))
+
+    def qkv_aside(step, part):
+        block = qkv_rows(origin(step, part), part)
+        return qx((part, step), block, block, at_dp(side))
+
+    def ff_along(step, part, which):
+        block = ff_block(origin(step - 1, part), part, which)
+        return fz((part, step - 1, which), block, block, at_dp(up if part == 0 else down))
+
+    def ff_aside(step, part, which):
+        block = ff_block(origin(step, part), part, which)
+        return fx((part, step, which), block, block, at_dp(side))
+
+    own_rows = pl.ds(pl.multiple_of(d * rows, 16), rows)
+    r["qkv_weight"][own_rows] = r["qkv_shard"][...]
+    for part in range(2):
+        qkv_along(1, part).start()
+        qkv_aside(0, part).start()
+
+    send_small = Sender(r["small_s"], r["small_r"])
+
+    def small_copy(step):
+        return send_small(
+            step - 1,
+            r["small"],
+            r["small_all"].at[own_rows],
+            at_dp(lax.rem(d + step, n_data)),
+        )
+
+    loop(1, n_data, lambda step: small_copy(step).start())
+    r["small_all"][own_rows] = r["small"][...]
+    r["trig_all"][0] = r["trig"][...]
+
+    def spread(send, buffer):
+        return (
+            send(0, buffer.at[0], buffer.at[1], at_mlp(1)),
+            send(1, buffer.at[0], buffer.at[2], at_mlp(2)),
+            send(2, buffer.at[2], buffer.at[3], at_mlp(1)),
+        )
+
+    trig_near, trig_far, trig_on = spread(Sender(r["trig_s"], r["trig_r"]), r["trig_all"])
+    trig_near.start()
+    trig_far.start()
+
+    oz, ox = Sender(r["oz_s"], r["oz_r"]), Sender(r["ox_s"], r["ox_r"])
+    out_place = r["out_weight"].at[pl.ds(pl.multiple_of(x * rows, 16), rows)]
+    owner = z == m
+
+    def out_along(step):
+        return oz(step - 1, out_place, out_place, at_dp(lax.rem(z + step, depth) * NX + x))
+
+    out_aside = ox(0, out_place, out_place, at_dp(side))
+
+    @pl.when(owner)
+    def _():
+        r["out_weight"][pl.ds(pl.multiple_of(x * rows, 16), rows)] = r["out_shard"][...]
+        for step in range(1, depth):
+            out_along(step).start()
+        out_aside.start()
+
+    loop(1, everyone, lambda step: facts_copy(step).wait())
+    facts_all = r["facts_all"][...]
+    sinus = jnp.concatenate([facts_all[:, 0], facts_all[:, 1]], axis=1).astype(bfloat)
+    labels = facts_all[:, 2, 0:1]
+    time_pre = (
+        jnp.dot(sinus, r["time_first"][...], preferred_element_type=single) + r["first_bias"][...]
+    )
+    r["time_pre"][...] = time_pre
+    time_act = (time_pre * jax.nn.sigmoid(time_pre)).astype(bfloat)
+    send_time = Sender(r["time_s"], r["time_r"])
+
+    def time_copy(step):
+        peer = lax.rem(d + step, n_data)
+        return send_time(
+            step - 1, r["time_send"].at[peer], r["time_recv"].at[d], at_dp(peer)
+        )
+
+    for spot in range(n_data):
+        r["time_send"][spot] = jnp.dot(
+            time_act, r["time_blocks"][spot], preferred_element_type=single
+        )
+    loop(1, n_data, lambda step: time_copy(step).start())
+    r["time_recv"][d] = r["time_send"][d]
+    for part in range(2):
+        for which in range(3):
+            own = r["ff_shard"].at[which, :, pl.ds(half * part, half)]
+            fz(
+                (part, 0, which),
+                own,
+                ff_block(d, part, which),
+                at_dp(up if part == 0 else down),
+            ).start()
+            fx((part, 0, which), own, ff_block(d, part, which), at_dp(side)).start()
+    onehot = (
+        labels == lax.broadcasted_iota(jnp.int32, (everyone, CLASSES + 1), 1).astype(single)
+    ).astype(bfloat)
+    picked = jnp.dot(onehot, r["class_table"][...], preferred_element_type=single)
+    load_mod.wait()
+
+    def qkv_service(step):
+        for part in range(2):
+            qkv_along(step, part).wait_recv()
+            if step < depth - 1:
+                qkv_along(step + 1, part).start()
+            qkv_aside(step, part).start()
+
+    loop(1, n_data, lambda step: time_copy(step).wait())
+    condition = jnp.sum(r["time_recv"][...], axis=0) + r["second_bias"][...] + picked
+    r["condition"][...] = condition
+    cond_act = (condition * jax.nn.sigmoid(condition)).astype(bfloat)
+    pick = (
+        lax.broadcasted_iota(jnp.int32, (n_data, everyone), 1)
+        == lax.broadcasted_iota(jnp.int32, (n_data, everyone), 0) * n_model + m
+    ).astype(bfloat)
+    cond_rank = jnp.dot(pick, cond_act, preferred_element_type=single).astype(bfloat)
+    for kind in range(8):
+        block = jnp.dot(
+            cond_rank, r["mod_low"][:, kind * D : (kind + 1) * D], preferred_element_type=single
+        )
+        for spot in range(n_data):
+            r["mod_send"][spot, kind : kind + 1] = block[spot : spot + 1]
+    send_mods = Sender(r["mods_s"], r["mods_r"])
+
+    def mods_copy(step):
+        peer = lax.rem(d + step, n_data)
+        return send_mods(step - 1, r["mod_send"].at[peer], r["mod_recv"].at[d], at_dp(peer))
+
+    loop(1, n_data, lambda step: mods_copy(step).start())
+    r["mod_recv"][d] = r["mod_send"][d]
+    qkv_service(1)
+    loop(1, n_data, lambda step: small_copy(step).wait())
+    trig_far.wait_recv()
+    trig_on.start()
+    hidden = (
+        lax.dot_general(
+            r["noisy"][...],
+            r["small_all"][:, 0:CH],
+            (((1,), (1,)), ((), ())),
+            preferred_element_type=single,
+        )
+        + r["patch_bias"][...]
+    )
+    r["hidden"][...] = hidden
+    loop(1, n_data, lambda step: mods_copy(step).wait())
+    modulation = jnp.sum(r["mod_recv"][...], axis=0) + r["mod_bias"][...]
+    r["modulation"][...] = modulation
+
+    def kind_of(kind):
+        return r["modulation"][kind : kind + 1]
+
+    r["one_rows"][0] = modulate_rows(r["hidden"][...], kind_of(0), kind_of(1)).astype(bfloat)
+    one_near, one_far, one_on = spread(Sender(r["one_s"], r["one_r"]), r["one_rows"])
+    one_far.start()
+    one_near.start()
+    qkv_service(2)
+    qkv_service(3)
+
+    @pl.when(jnp.logical_not(owner))
+    def _():
+        oz(
+            lax.rem(z + depth - m, depth) - 1, out_place, out_place, at_dp(up)
+        ).wait_recv()
+        out_aside.start()
+
+    own_ff.wait()
+
+    def ff_service(step, which):
+        for part in range(2):
+            ff_along(step, part, which).wait_recv()
+            if step < depth - 1:
+                ff_along(step + 1, part, which).start()
+            ff_aside(step, part, which).start()
+
+    ff_service(1, 0)
+    one_far.wait_recv()
+    one_on.start()
+    for part in range(2):
+        for step in range(depth):
+            qkv_aside(step, part).wait_recv()
+    one_near.wait_recv()
+    one_on.wait_recv()
+    trig_near.wait_recv()
+    trig_on.wait_recv()
+    ff_service(1, 1)
+    ff_service(1, 2)
+
+    def image_body(step, carry):
+        image = n_model - 1 - step
+        r["qkv"][...] = (
+            jnp.dot(r["one_rows"][image], r["qkv_weight"][...], preferred_element_type=single)
+            + r["qkv_bias"][...]
+        )
+        rank = (
+            2 * lax.rem(lax.div(m, 2) + lax.div(image, 2), 2)
+            + lax.rem(lax.rem(m, 2) + lax.rem(image, 2), 2)
+        )
+        count = r["facts_all"][d * n_model + rank, 2:3, 1:2]
+        mask = lax.broadcasted_iota(jnp.int32, (1, length), 1).astype(single) < count
+        cosine, sine = r["trig_all"][image, 0], r["trig_all"][image, 1]
+        totals = []
+        for head in range(heads):
+            start = head * HDIM
+
+            def part(which):
+                return r["qkv"][:, which * head_cols + start : which * head_cols + start + HDIM]
+
+            raw_q, raw_k = part(0), part(1)
+            query = (raw_q * cosine + swapped(raw_q) * sine).astype(bfloat)
+            key = (raw_k * cosine + swapped(raw_k) * sine).astype(bfloat)
+            value = part(2).astype(bfloat)
+            for which, kept in enumerate((query, key, value)):
+                low = which * head_cols + start
+                r["low"][image, :, low : low + HDIM] = kept
+            scores = lax.dot_general(
+                query, key, (((1,), (1,)), ((), ())), preferred_element_type=single
+            ) * (1.0 / math.sqrt(HDIM))
+            scores = jnp.where(mask, scores, -1e30)
+            row_max = jnp.max(scores, axis=-1, keepdims=True)
+            exponent = jnp.exp(scores - row_max)
+            row_sum = jnp.sum(exponent, axis=-1, keepdims=True)
+            probs = exponent / row_sum
+            r["attended"][image, :, start : start + HDIM] = jnp.dot(
+                probs.astype(bfloat), value, preferred_element_type=single
+            ).astype(bfloat)
+            totals.append(row_max + jnp.log(row_sum))
+        r["totals"][image] = jnp.concatenate(totals, axis=1)
+        return carry
+
+    lax.fori_loop(0, 2, image_body, 0)
+    for which in range(3):
+        ff_service(2, which)
+    lax.fori_loop(2, n_model, image_body, 0)
+
+    @pl.when(owner)
+    def _():
+        for step in range(1, depth):
+            out_along(step).wait_send()
+
+    out_aside.wait()
+
+    def partial(image):
+        return jnp.dot(
+            r["attended"][image], r["out_weight"][...], preferred_element_type=single
+        )
+
+    send_part = Sender(r["part_s"], r["part_r"])
+    to_core = send_part(0, r["parts_send"].at[0], r["parts_recv"].at[0], at_mlp(1))
+    to_far = send_part(1, r["parts_send"].at[1], r["parts_recv"].at[1], at_mlp(2))
+    to_near = send_part(2, r["parts_send"].at[2], r["parts_recv"].at[2], at_mlp(1))
+    r["parts_send"][0] = partial(3).astype(bfloat)
+    to_core.start()
+    second = partial(2)
+    to_core.wait_recv()
+    r["parts_send"][1] = (second + r["parts_recv"][0].astype(single)).astype(bfloat)
+    to_far.start()
+    r["parts_send"][2] = partial(1).astype(bfloat)
+    to_near.start()
+    own_part = partial(0) + r["out_bias"][...]
+    for which in range(3):
+        ff_service(3, which)
+    to_near.wait_recv()
+    to_far.wait_recv()
+    branch = own_part + r["parts_recv"][2].astype(single) + r["parts_recv"][1].astype(single)
+    r["branch"][...] = branch
+    hidden_mid = r["hidden"][...] + kind_of(2) * branch
+    r["hidden_mid"][...] = hidden_mid
+    r["two_rows"][0] = modulate_rows(hidden_mid, kind_of(3), kind_of(4)).astype(bfloat)
+    two_near, two_far, two_on = spread(Sender(r["two_s"], r["two_r"]), r["two_rows"])
+    two_far.start()
+    two_near.start()
+    two_far.wait_recv()
+    two_on.start()
+
+    for part in range(2):
+        for step in range(depth):
+            for which in range(3):
+                ff_aside(step, part, which).wait()
+            qkv_aside(step, part).wait_send()
+            if step:
+                for which in range(3):
+                    ff_along(step, part, which).wait_send()
+                qkv_along(step, part).wait_send()
+    for copy in (two_near, two_on):
+        copy.wait()
+    two_far.wait_send()
+    for copy in (trig_near, trig_far, trig_on, one_near, one_far, one_on, to_core, to_far, to_near):
+        copy.wait_send()
+
+
+def forward_all(values, sizes, collective):
+    n_data, n_model = sizes
+    bfloat, single = jnp.bfloat16, jnp.float32
+    everyone = n_data * n_model
+    rows = D // n_data
+    heads = HEADS // n_model
+    head_cols = heads * HDIM
+    length = values["noisy"].shape[0]
+    units = values["ff_shard"].shape[2]
+    depth = n_data // NX
+    shapes = dict(
+        facts_all=((everyone, 8, 128), single),
+        trig_all=((n_model, 2, length, HDIM), single),
+        small_all=((D, 128), bfloat),
+        time_pre=((everyone, rows), single),
+        condition=((everyone, rows), single),
+        modulation=((8, D), single),
+        hidden=((length, D), single),
+        one_rows=((n_model, length, D), bfloat),
+        qkv_weight=((D, 3 * head_cols), bfloat),
+        out_weight=((head_cols, D), bfloat),
+        ff=((3, D, units), bfloat),
+        low=((n_model, length, 3 * head_cols), bfloat),
+        attended=((n_model, length, head_cols), bfloat),
+        totals=((n_model, length, heads), single),
+        branch=((length, D), single),
+        hidden_mid=((length, D), single),
+        two_rows=((n_model, length, D), bfloat),
+    )
+    dma = pltpu.SemaphoreType.DMA
+    scratch = dict(
+        time_send=pltpu.VMEM((n_data, everyone, rows), single),
+        time_recv=pltpu.VMEM((n_data, everyone, rows), single),
+        mod_send=pltpu.VMEM((n_data, 8, D), single),
+        mod_recv=pltpu.VMEM((n_data, 8, D), single),
+        mod_low=pltpu.VMEM((rows, 8 * D), bfloat),
+        qkv=pltpu.VMEM((length, 3 * head_cols), single),
+        parts_send=pltpu.VMEM((3, length, D), bfloat),
+        parts_recv=pltpu.VMEM((3, length, D), bfloat),
+        local_sem=dma((2,)),
+    )
+    counts = dict(
+        facts=(everyone - 1,),
+        small=(n_data - 1,),
+        time=(n_data - 1,),
+        mods=(n_data - 1,),
+        trig=(3,),
+        one=(3,),
+        two=(3,),
+        part=(3,),
+        qz=(2, depth - 1),
+        qx=(2, depth),
+        oz=(depth - 1,),
+        ox=(1,),
+        fz=(2, depth - 1, 3),
+        fx=(2, depth, 3),
+    )
+    for name, count in counts.items():
+        scratch[name + "_s"] = dma(count)
+        scratch[name + "_r"] = dma(count)
+    far = {"mod_weight", "ff_shard", "ff"}
+
+    def space(name):
+        return pl.BlockSpec(memory_space=pl.ANY if name in far else pltpu.VMEM)
+
+    outs = pl.pallas_call(
+        functools.partial(forward_kernel, sizes),
+        out_shape=[jax.ShapeDtypeStruct(*shapes[name]) for name in FORWARD_OUT],
+        in_specs=[space(name) for name in FORWARD_IN],
+        out_specs=[space(name) for name in FORWARD_OUT],
+        scratch_shapes=[scratch[name] for name in FORWARD_SCRATCH],
+        compiler_params=pltpu.CompilerParams(
+            collective_id=collective, has_side_effects=True, vmem_limit_bytes=56 * 2**20
+        ),
+    )(*[values[name] for name in FORWARD_IN])
+    return dict(zip(FORWARD_OUT, outs))
+
+
+BACK_IN = (
+    "ff", "two_rows", "hidden_mid", "hidden", "branch", "modulation", "small_all", "final_bias",
+    "clean", "noise", "consts", "valid", "noisy", "low", "totals", "trig_all", "facts_all",
+    "attended", "one_rows", "qkv_weight", "out_weight",
+)
+BACK_OUT = (
+    "grad_ff", "grad_qkv", "grad_out", "d_modulation", "hidden_sum", "branch_sum", "qkv_sum",
+    "output_sum", "loss", "grad_patch", "grad_final",
+)
+BACK_SCRATCH = (
+    "mixed", "d_end", "dm_rows", "db_rows", "hold_far", "hold_near", "parts_send", "parts_recv",
+    "normed_end", "g_ff", "x_ff", "z_ff", "g_qkv", "x_qkv", "z_qkv", "g_out", "x_out",
+    "z_out", "out_mine", "dm_s", "dm_r", "db_s", "db_r", "pa_s", "pa_r",
+    "pb_s", "pb_r", "pc_s", "pc_r", "fx_s", "fx_r", "fz_s", "fz_r", "qx_s", "qx_r", "qz_s",
+    "qz_r", "ox_s", "ox_r", "oz_s", "oz_r", "qa_s", "qa_r", "oa_s", "oa_r", "local_sem",
+)
+ROW_CHUNK = 16
+
+
+def modulate_back(values, grad, scale_by):
+    row_mean = jnp.mean(values, axis=-1, keepdims=True)
+    centered = values - row_mean
+    variance = jnp.mean(centered * centered, axis=-1, keepdims=True)
+    inverse = lax.rsqrt(variance + 1e-06)
+    normal = centered * inverse
+    inner = grad * (1.0 + scale_by)
+    back = inverse * (
+        inner
+        - jnp.mean(inner, axis=-1, keepdims=True)
+        - normal * jnp.mean(inner * normal, axis=-1, keepdims=True)
+    )
+    return back, normal
+
+
+def fold(values):
+    total = values[:8]
+    for start in range(8, values.shape[0], 8):
+        total = total + values[start : start + 8]
+    return total
+
+
+def back_kernel(sizes, total_images, *refs):
+    names = BACK_IN + BACK_OUT + BACK_SCRATCH
+    r = dict(zip(names, refs, strict=True))
+    bfloat, single = jnp.bfloat16, jnp.float32
+    n_data, n_model = sizes
+    d, m, z, x = device_parts()
+    depth = n_data // NX
+    rows = D // n_data
+    heads = HEADS // n_model
+    head_cols = heads * HDIM
+    length = r["clean"].shape[0]
+    units = r["ff"].shape[2]
+    half = units // 2
+
+    def at_dp(spot):
+        return (spot, m)
+
+    near_rank = m + 1 - 2 * lax.rem(m, 2)
+    far_rank = lax.rem(m + 2, 4)
+
+    def at_mlp(bit):
+        return (d, near_rank if bit == 1 else far_rank)
+
+    up = lax.rem(z + 1, depth) * NX + x
+    down = lax.rem(z + depth - 1, depth) * NX + x
+    side = z * NX + 1 - x
+    barrier = pltpu.get_barrier_semaphore()
+    peers = [at_dp(lax.rem(z + step, depth) * NX + x) for step in range(1, depth)]
+    peers += [at_dp(side), at_mlp(1), at_mlp(2), (d, lax.rem(near_rank + 2, 4))]
+    for peer in peers:
+        pl.semaphore_signal(barrier, inc=1, device_id=peer, device_id_type=MESH_IDS)
+    pl.semaphore_wait(barrier, len(peers))
+
+    def chunks(body, carry, amount=ROW_CHUNK, count=length):
+        def step_body(step, held):
+            return body(pl.ds(pl.multiple_of(step * amount, amount), amount), held)
+
+        return lax.fori_loop(0, count // amount, step_body, carry)
+
+    def kind_of(kind):
+        return r["modulation"][kind : kind + 1]
+
+    def dot(left, right, dims):
+        return lax.dot_general(left, right, (dims, ((), ())), preferred_element_type=single)
+
+    zeros = jnp.zeros((8, D), single)
+
+    def spread(send, buffer):
+        return (
+            send(0, buffer.at[0], buffer.at[1], at_mlp(1)),
+            send(1, buffer.at[0], buffer.at[2], at_mlp(2)),
+            send(2, buffer.at[2], buffer.at[3], at_mlp(1)),
+        )
+
+    def part_copies(tag):
+        send = Sender(r[tag + "_s"], r[tag + "_r"])
+        return tuple(
+            send(spot, r["parts_send"].at[spot], r["parts_recv"].at[spot], at_mlp(bit))
+            for spot, bit in ((0, 1), (1, 2), (2, 1))
+        )
+
+    def add_far(copies):
+        to_core, to_far, to_near = copies
+        to_core.wait_recv()
+
+        def body(at, held):
+            r["parts_send"][1, at] = (
+                r["hold_far"][at] + r["parts_recv"][0, at].astype(single)
+            ).astype(bfloat)
+            return held
+
+        chunks(body, 0)
+        to_far.start()
+
+    fx, fz = Sender(r["fx_s"], r["fx_r"]), Sender(r["fz_s"], r["fz_r"])
+    qx, qz = Sender(r["qx_s"], r["qx_r"]), Sender(r["qz_s"], r["qz_r"])
+
+    def block_rows(z_spot, x_spot):
+        return pl.ds(pl.multiple_of((z_spot * NX + x_spot) * rows, 16), rows)
+
+    def ff_aside(which, step):
+        z_spot = lax.rem(z + step, depth)
+        return fx(
+            (which, step),
+            r["g_ff"].at[which, block_rows(z_spot, 1 - x)],
+            r["x_ff"].at[which, z_spot],
+            at_dp(side),
+        )
+
+    def target_of(step, part):
+        return lax.rem(z + (depth - 1 - step if part == 0 else 1 + step), depth)
+
+    def ff_along(which, step, part):
+        lanes = pl.ds(half * part, half)
+        return fz(
+            (which, step, part),
+            r["g_ff"].at[which, block_rows(target_of(step, part), x), lanes],
+            r["z_ff"].at[which, step, part],
+            at_dp(up if part == 0 else down),
+        )
+
+    def ff_start(which):
+        for step in range(depth):
+            ff_aside(which, step).start()
+
+    def ff_beside(which):
+        for step in range(depth):
+            ff_aside(which, step).wait_recv()
+
+        def body(step, held):
+            at = block_rows(step, x)
+            r["g_ff"][which, at] = (
+                r["g_ff"][which, at].astype(single) + r["x_ff"][which, step].astype(single)
+            ).astype(bfloat)
+            return held
+
+        lax.fori_loop(0, depth, body, 0)
+        for part in range(2):
+            ff_along(which, 0, part).start()
+
+    def ff_service(which, step):
+        for part in range(2):
+            ff_along(which, step, part).wait_recv()
+            lanes = pl.ds(half * part, half)
+            at = block_rows(target_of(step + 1, part), x)
+            running = r["z_ff"][which, step, part].astype(single) + r["g_ff"][
+                which, at, lanes
+            ].astype(single)
+            if step < depth - 2:
+                r["g_ff"][which, at, lanes] = running.astype(bfloat)
+                ff_along(which, step + 1, part).start()
+            else:
+                r["grad_ff"][which, :, lanes] = running
+
+    tops = (pl.ds(0, 80), pl.ds(80, rows - 80))
+
+    def part_rows(z_spot, part):
+        start = (z_spot * NX + x) * rows + 80 * part
+        return pl.ds(pl.multiple_of(start, 16), 80 if part == 0 else rows - 80)
+
+    def qkv_aside(step):
+        z_spot = lax.rem(z + step, depth)
+        return qx(
+            step,
+            r["g_qkv"].at[block_rows(z_spot, 1 - x)],
+            r["x_qkv"].at[z_spot],
+            at_dp(side),
+        )
+
+    def qkv_along(step, part):
+        return qz(
+            (step, part),
+            r["g_qkv"].at[part_rows(target_of(step, part), part)],
+            r["z_qkv"].at[step, tops[part]],
+            at_dp(up if part == 0 else down),
+        )
+
+    def qkv_beside():
+        for step in range(depth):
+            qkv_aside(step).wait_recv()
+
+        def body(step, held):
+            at = block_rows(step, x)
+            r["g_qkv"][at] = (
+                r["g_qkv"][at].astype(single) + r["x_qkv"][step].astype(single)
+            ).astype(bfloat)
+            return held
+
+        lax.fori_loop(0, depth, body, 0)
+        for part in range(2):
+            qkv_along(0, part).start()
+
+    def qkv_service(step):
+        for part in range(2):
+            qkv_along(step, part).wait_recv()
+            at = part_rows(target_of(step + 1, part), part)
+            running = (
+                r["z_qkv"][step, tops[part]].astype(single) + r["g_qkv"][at].astype(single)
+            ).astype(bfloat)
+            if step < depth - 2:
+                r["g_qkv"][at] = running
+                qkv_along(step + 1, part).start()
+            else:
+                r["grad_qkv"][0, tops[part]] = running
+
+    dm_near, dm_far, dm_on = spread(Sender(r["dm_s"], r["dm_r"]), r["dm_rows"])
+    first_parts, second_parts, third_parts = (part_copies(tag) for tag in ("pa", "pb", "pc"))
+
+    def swiglu(ff, two_rows, gates, ups, acts, d_gates, d_ups):
+        load_ff = pltpu.make_async_copy(r["ff"], ff, r["local_sem"].at[0])
+        load_two = pltpu.make_async_copy(r["two_rows"], two_rows, r["local_sem"].at[1])
+        load_ff.start()
+        load_two.start()
+        load_two.wait()
+        load_ff.wait()
+        wide = 2 * length
+
+        def rows_of(ref, which):
+            return ref[2 * which : 2 * which + 2].reshape(wide, D)
+
+        def inner(which):
+            part = rows_of(two_rows, which)
+            spot = pl.ds(which * wide, wide)
+            gates[spot] = dot(part, ff[0], ((1,), (0,)))
+            ups[spot] = dot(part, ff[1], ((1,), (0,)))
+
+            def body(at, held):
+                at = pl.ds(pl.multiple_of(at.start + which * wide, 32), 32)
+                gate = gates[at]
+                acts[at] = (gate * jax.nn.sigmoid(gate) * ups[at]).astype(bfloat)
+                return held
+
+            chunks(body, 0, 32, wide)
+
+        def outer(image):
+            return dot(acts[image * length : (image + 1) * length], ff[2], ((1,), (1,)))
+
+        inner(1)
+        r["parts_send"][0] = outer(3).astype(bfloat)
+        first_parts[0].start()
+        r["hold_far"][...] = outer(2)
+        inner(0)
+        add_far(first_parts)
+        r["parts_send"][2] = outer(1).astype(bfloat)
+        first_parts[2].start()
+        r["hold_near"][...] = outer(0)
+        first_parts[2].wait_recv()
+        first_parts[1].wait_recv()
+
+        def ending(at, held):
+            mixed = (
+                r["hold_near"][at]
+                + r["parts_recv"][2, at].astype(single)
+                + r["parts_recv"][1, at].astype(single)
+            )
+            r["mixed"][at] = mixed
+            end = r["hidden_mid"][at] + kind_of(5) * mixed
+            r["normed_end"][at] = modulate_rows(end, kind_of(6), kind_of(7)).astype(bfloat)
+            return held
+
+        chunks(ending, 0)
+
+        eps_weight, var_weight = r["small_all"][:, 32:48], r["small_all"][:, 48:64]
+        normed_end = r["normed_end"][...]
+        eps = dot(normed_end, eps_weight, ((1,), (0,))) + r["final_bias"][0:1]
+        var = dot(normed_end, var_weight, ((1,), (0,))) + r["final_bias"][1:2]
+        clean, noise, valid = r["clean"][...], r["noise"][...], r["valid"][...]
+        root_bar, root_rest, log_beta, post_log, coefficient = (
+            r["consts"][0:1, spot : spot + 1] for spot in range(5)
+        )
+        noisy = root_bar * clean + root_rest * noise
+        fraction = (var + 1.0) * 0.5
+        model_log = fraction * log_beta + (1.0 - fraction) * post_log
+        start_est = (noisy - root_rest * eps) / root_bar
+        gap = coefficient * (clean - start_est)
+        ratio = jnp.exp(post_log - model_log)
+        gap_part = gap * gap * jnp.exp(-model_log)
+        scale_by = 0.5 / math.log(2.0)
+        terms = (eps - noise) * (eps - noise) + scale_by * (
+            -1.0 + model_log - post_log + ratio + gap_part
+        )
+        terms = jnp.where(valid > 0.0, terms, 0.0)
+        r["loss"][...] = jnp.sum(jnp.sum(terms, axis=1, keepdims=True), axis=0, keepdims=True)
+        d_eps = 2.0 * (eps - noise) + 2.0 * scale_by * gap * jnp.exp(-model_log) * (
+            coefficient * root_rest / root_bar
+        )
+        d_var = scale_by * (1.0 - ratio - gap_part) * (0.5 * (log_beta - post_log))
+        share = 1.0 / total_images
+        d_eps = jnp.where(valid > 0.0, d_eps * share, 0.0).astype(bfloat)
+        d_var = jnp.where(valid > 0.0, d_var * share, 0.0).astype(bfloat)
+        r["output_sum"][0:1] = jnp.sum(d_eps.astype(single), axis=0, keepdims=True)
+        r["output_sum"][1:2] = jnp.sum(d_var.astype(single), axis=0, keepdims=True)
+        r["grad_final"][0] = dot(d_eps, normed_end, ((0,), (0,)))
+        r["grad_final"][1] = dot(d_var, normed_end, ((0,), (0,)))
+        r["hold_far"][...] = dot(d_eps, eps_weight, ((1,), (1,))) + dot(
+            d_var, var_weight, ((1,), (1,))
+        )
+
+        def end_back(at, held):
+            shift_sum, scale_sum, gate_sum = held
+            mixed, grad = r["mixed"][at], r["hold_far"][at]
+            end = r["hidden_mid"][at] + kind_of(5) * mixed
+            back, normal = modulate_back(end, grad, kind_of(7))
+            r["d_end"][at] = back
+            r["dm_rows"][0, at] = (kind_of(5) * back).astype(bfloat)
+            return (
+                shift_sum + fold(grad),
+                scale_sum + fold(grad * normal),
+                gate_sum + fold(mixed * back),
+            )
+
+        shift_sum, scale_sum, gate_sum = chunks(end_back, (zeros, zeros, zeros))
+        dm_far.start()
+        dm_near.start()
+        for kind, value in ((6, shift_sum), (7, scale_sum), (5, gate_sum)):
+            r["d_modulation"][kind : kind + 1] = jnp.sum(value, axis=0, keepdims=True)
+
+        def inner_back(which):
+            spot = pl.ds(which * wide, wide)
+            gradient = dot(rows_of(r["dm_rows"], which), ff[2], ((1,), (0,)))
+            gate, up_val = gates[spot], ups[spot]
+            sigma = jax.nn.sigmoid(gate)
+            d_ups[spot] = (gradient * gate * sigma).astype(bfloat)
+            d_gates[spot] = (gradient * up_val * (sigma * (1.0 + gate * (1.0 - sigma)))).astype(
+                bfloat
+            )
+
+        def outer_back(image):
+            spot = pl.ds(image * length, length)
+            return dot(d_gates[spot], ff[0], ((1,), (1,))) + dot(d_ups[spot], ff[1], ((1,), (1,)))
+
+        dm_near.wait_recv()
+        inner_back(0)
+        dm_far.wait_recv()
+        dm_on.start()
+        dm_on.wait_recv()
+        inner_back(1)
+        for copy in first_parts:
+            copy.wait_send()
+        r["parts_send"][0] = outer_back(3).astype(bfloat)
+        second_parts[0].start()
+        r["hold_far"][...] = outer_back(2)
+        r["g_ff"][2] = dot(
+            r["dm_rows"][...].reshape(2 * wide, D), acts[...], ((0,), (0,))
+        ).astype(bfloat)
+        ff_start(2)
+        add_far(second_parts)
+        r["parts_send"][2] = outer_back(1).astype(bfloat)
+        second_parts[2].start()
+        r["hold_near"][...] = outer_back(0)
+        flat = two_rows[...].reshape(2 * wide, D)
+        r["g_ff"][0] = dot(flat, d_gates[...], ((0,), (0,))).astype(bfloat)
+        ff_start(0)
+        r["g_ff"][1] = dot(flat, d_ups[...], ((0,), (0,))).astype(bfloat)
+        ff_start(1)
+
+    pl.run_scoped(
+        swiglu,
+        pltpu.VMEM((3, D, units), bfloat),
+        pltpu.VMEM((n_model, length, D), bfloat),
+        pltpu.VMEM((n_model * length, units), single),
+        pltpu.VMEM((n_model * length, units), single),
+        pltpu.VMEM((n_model * length, units), bfloat),
+        pltpu.VMEM((n_model * length, units), bfloat),
+        pltpu.VMEM((n_model * length, units), bfloat),
+    )
+
+    db_near, db_far, db_on = spread(Sender(r["db_s"], r["db_r"]), r["db_rows"])
+    ox, oz = Sender(r["ox_s"], r["ox_r"]), Sender(r["oz_s"], r["oz_r"])
+    out_aside = ox(0, r["g_out"].at[1 - x], r["x_out"], at_dp(side))
+    owner = z == m
+    behind = lax.rem(z + depth - m, depth)
+    out_along = oz(
+        lax.rem(behind + depth - 1, depth),
+        r["g_out"].at[x],
+        r["z_out"].at[lax.rem(behind + depth - 1, depth)],
+        at_dp(m * NX + x),
+    )
+
+    def attend(low, attended, trig, one_rows, qkv_weight, out_weight, d_attended, d_qkv):
+        loads = []
+        for spot, (name, place) in enumerate(
+            (
+                ("out_weight", out_weight),
+                ("low", low),
+                ("trig_all", trig),
+                ("attended", attended),
+                ("one_rows", one_rows),
+                ("qkv_weight", qkv_weight),
+            )
+        ):
+            load = pltpu.make_async_copy(r[name], place, r["local_sem"].at[2 + spot])
+            load.start()
+            loads.append(load)
+        second_parts[2].wait_recv()
+        second_parts[1].wait_recv()
+
+        def mid_back(at, held):
+            shift_sum, scale_sum, gate_sum, branch_sum = held
+            grad = (
+                r["hold_near"][at]
+                + r["parts_recv"][2, at].astype(single)
+                + r["parts_recv"][1, at].astype(single)
+            )
+            back, normal = modulate_back(r["hidden_mid"][at], grad, kind_of(4))
+            total = r["d_end"][at] + back
+            r["d_end"][at] = total
+            d_branch = (kind_of(2) * total).astype(bfloat)
+            r["db_rows"][0, at] = d_branch
+            return (
+                shift_sum + fold(grad),
+                scale_sum + fold(grad * normal),
+                gate_sum + fold(r["branch"][at] * total),
+                branch_sum + fold(d_branch.astype(single)),
+            )
+
+        sums = chunks(mid_back, (zeros, zeros, zeros, zeros))
+        db_far.start()
+        db_near.start()
+        for kind, value in zip((3, 4, 2), sums):
+            r["d_modulation"][kind : kind + 1] = jnp.sum(value, axis=0, keepdims=True)
+        r["branch_sum"][...] = jnp.sum(sums[3], axis=0, keepdims=True)
+        for load in loads:
+            load.wait()
+
+        def image_body(image, carry):
+            d_attended[...] = dot(
+                r["db_rows"][image], out_weight[...], ((1,), (1,))
+            ).astype(bfloat)
+            rank = (
+                2 * lax.rem(lax.div(m, 2) + lax.div(image, 2), 2)
+                + lax.rem(lax.rem(m, 2) + lax.rem(image, 2), 2)
+            )
+            count = r["facts_all"][d * n_model + rank, 2:3, 1:2]
+            mask = lax.broadcasted_iota(jnp.int32, (1, length), 1).astype(single) < count
+            cosine, sine = trig[image, 0], trig[image, 1]
+            scale_by = 1.0 / math.sqrt(HDIM)
+            for head in range(heads):
+                start = head * HDIM
+
+                def spot(which):
+                    begin = which * head_cols + start
+                    return slice(begin, begin + HDIM)
+
+                query, key, value = (low[image, :, spot(which)] for which in range(3))
+                grad = d_attended[:, start : start + HDIM]
+                scores = dot(query, key, ((1,), (1,))) * scale_by
+                scores = jnp.where(mask, scores, -1e30)
+                probs = jnp.exp(scores - r["totals"][image, :, head : head + 1])
+                d_probs = dot(grad, value, ((1,), (1,)))
+                row = jnp.sum(probs * d_probs, axis=-1, keepdims=True)
+                d_scores = (probs * (d_probs - row)).astype(bfloat)
+                d_query = dot(d_scores, key, ((1,), (0,))) * scale_by
+                d_key = dot(d_scores, query, ((0,), (0,))) * scale_by
+                d_value = dot(probs.astype(bfloat), grad, ((0,), (0,)))
+                for which, turned in ((0, d_query), (1, d_key)):
+                    back = turned * cosine + swapped(turned * sine)
+                    d_qkv[image, :, spot(which)] = back.astype(bfloat)
+                d_qkv[image, :, spot(2)] = d_value.astype(bfloat)
+            return carry
+
+        db_near.wait_recv()
+        lax.fori_loop(0, 2, image_body, 0)
+        db_far.wait_recv()
+        db_on.start()
+        ff_beside(2)
+        db_on.wait_recv()
+        lax.fori_loop(2, n_model, image_body, 0)
+
+        def one_part(image):
+            return dot(d_qkv[image], qkv_weight[...], ((1,), (1,)))
+
+        for copy in second_parts:
+            copy.wait_send()
+        r["parts_send"][0] = one_part(3).astype(bfloat)
+        third_parts[0].start()
+        r["hold_far"][...] = one_part(2)
+        ff_beside(0)
+        ff_service(2, 0)
+        add_far(third_parts)
+        r["parts_send"][2] = one_part(1).astype(bfloat)
+        third_parts[2].start()
+        r["hold_near"][...] = one_part(0)
+        flat_grad = d_qkv[...].reshape(n_model * length, 3 * head_cols)
+        r["g_qkv"][...] = dot(
+            one_rows[...].reshape(n_model * length, D), flat_grad, ((0,), (0,))
+        ).astype(bfloat)
+        for step in range(depth):
+            qkv_aside(step).start()
+        r["g_out"][...] = (
+            dot(
+                attended[...].reshape(n_model * length, head_cols),
+                r["db_rows"][...].reshape(n_model * length, D),
+                ((0,), (0,)),
+            )
+            .astype(bfloat)
+            .reshape(NX, rows, D)
+        )
+        out_aside.start()
+        ones = jnp.ones((8, n_model * length), bfloat)
+        r["qkv_sum"][...] = dot(ones, flat_grad, ((1,), (0,)))[0:1]
+
+    pl.run_scoped(
+        attend,
+        pltpu.VMEM((n_model, length, 3 * head_cols), bfloat),
+        pltpu.VMEM((n_model, length, head_cols), bfloat),
+        pltpu.VMEM((n_model, 2, length, HDIM), single),
+        pltpu.VMEM((n_model, length, D), bfloat),
+        pltpu.VMEM((D, 3 * head_cols), bfloat),
+        pltpu.VMEM((head_cols, D), bfloat),
+        pltpu.VMEM((length, head_cols), bfloat),
+        pltpu.VMEM((n_model, length, 3 * head_cols), bfloat),
+    )
+    ff_beside(1)
+    ff_service(0, 0)
+    ff_service(2, 1)
+    third_parts[2].wait_recv()
+    third_parts[1].wait_recv()
+
+    def first_back(at, held):
+        shift_sum, scale_sum, hidden_sum = held
+        grad = (
+            r["hold_near"][at]
+            + r["parts_recv"][2, at].astype(single)
+            + r["parts_recv"][1, at].astype(single)
+        )
+        back, normal = modulate_back(r["hidden"][at], grad, kind_of(1))
+        d_hidden = (r["d_end"][at] + back).astype(bfloat)
+        r["normed_end"][at] = d_hidden
+        return (
+            shift_sum + fold(grad),
+            scale_sum + fold(grad * normal),
+            hidden_sum + fold(d_hidden.astype(single)),
+        )
+
+    sums = chunks(first_back, (zeros, zeros, zeros))
+    for kind in range(2):
+        r["d_modulation"][kind : kind + 1] = jnp.sum(sums[kind], axis=0, keepdims=True)
+    r["hidden_sum"][...] = jnp.sum(sums[2], axis=0, keepdims=True)
+    r["grad_patch"][...] = dot(r["noisy"][...], r["normed_end"][...], ((0,), (0,)))
+
+    ff_service(1, 0)
+    ff_service(0, 1)
+    ff_service(2, 2)
+    ff_service(1, 1)
+    ff_service(0, 2)
+    ff_service(1, 2)
+    qkv_beside()
+    out_aside.wait()
+    r["g_out"][x] = (r["g_out"][x].astype(single) + r["x_out"][...].astype(single)).astype(bfloat)
+
+    @pl.when(jnp.logical_not(owner))
+    def _():
+        out_along.start()
+
+    for step in range(depth - 1):
+        qkv_service(step)
+    qkv_near, qkv_far, qkv_on = spread(Sender(r["qa_s"], r["qa_r"]), r["grad_qkv"])
+    qkv_far.start()
+    qkv_near.start()
+    give = Sender(r["oa_s"], r["oa_r"])
+    partners = [(d, near_rank), (d, far_rank), (d, lax.rem(near_rank + 2, 4))]
+    gives = [
+        give(spot, r["out_mine"], r["out_mine"], partner) for spot, partner in enumerate(partners)
+    ]
+
+    @pl.when(owner)
+    def _():
+        total = r["g_out"][x].astype(single)
+        for step in range(depth - 1):
+            oz(step, r["g_out"].at[x], r["z_out"].at[step], at_dp(up)).wait_recv()
+            total = total + r["z_out"][step].astype(single)
+        r["out_mine"][...] = total.astype(bfloat)
+        for copy in gives:
+            copy.start()
+
+    for spot, partner in enumerate(partners):
+
+        @pl.when(z == partner[1])
+        def _():
+            gives[spot].wait_recv()
+
+    qkv_far.wait_recv()
+    qkv_on.start()
+    r["grad_out"][...] = r["out_mine"][...]
+
+    @pl.when(owner)
+    def _():
+        for copy in gives:
+            copy.wait_send()
+
+    @pl.when(jnp.logical_not(owner))
+    def _():
+        out_along.wait_send()
+
+    qkv_near.wait()
+    qkv_on.wait()
+    qkv_far.wait_send()
+    for copy in (dm_near, dm_far, dm_on, db_near, db_far, db_on, *third_parts):
+        copy.wait_send()
+    for step in range(depth):
+        qkv_aside(step).wait_send()
+        for which in range(3):
+            ff_aside(which, step).wait_send()
+    for step in range(depth - 1):
+        for part in range(2):
+            qkv_along(step, part).wait_send()
+            for which in range(3):
+                ff_along(which, step, part).wait_send()
+
+
+def backward_all(values, sizes, total_images, collective):
+    n_data, n_model = sizes
+    bfloat, single = jnp.bfloat16, jnp.float32
+    rows = D // n_data
+    heads = HEADS // n_model
+    head_cols = heads * HDIM
+    length = values["clean"].shape[0]
+    units = values["ff"].shape[2]
+    half = units // 2
+    depth = n_data // NX
+    shapes = dict(
+        grad_ff=((3, rows, units), single),
+        grad_qkv=((n_model, rows, 3 * head_cols), bfloat),
+        grad_out=((rows, D), bfloat),
+        d_modulation=((8, D), single),
+        hidden_sum=((1, D), single),
+        branch_sum=((1, D), single),
+        qkv_sum=((1, 3 * head_cols), single),
+        output_sum=((2, CH), single),
+        loss=((1, 1), single),
+        grad_patch=((CH, D), single),
+        grad_final=((2, CH, D), single),
+    )
+    vmem, dma = pltpu.VMEM, pltpu.SemaphoreType.DMA
+    scratch = dict(
+        mixed=vmem((length, D), single),
+        d_end=vmem((length, D), single),
+        dm_rows=vmem((n_model, length, D), bfloat),
+        db_rows=vmem((n_model, length, D), bfloat),
+        hold_far=vmem((length, D), single),
+        hold_near=vmem((length, D), single),
+        parts_send=vmem((3, length, D), bfloat),
+        parts_recv=vmem((3, length, D), bfloat),
+        normed_end=vmem((length, D), bfloat),
+        g_ff=vmem((3, D, units), bfloat),
+        x_ff=vmem((3, depth, rows, units), bfloat),
+        z_ff=vmem((3, depth - 1, 2, rows, half), bfloat),
+        g_qkv=vmem((D, 3 * head_cols), bfloat),
+        x_qkv=vmem((depth, rows, 3 * head_cols), bfloat),
+        z_qkv=vmem((depth - 1, rows, 3 * head_cols), bfloat),
+        g_out=vmem((NX, rows, D), bfloat),
+        x_out=vmem((rows, D), bfloat),
+        z_out=vmem((depth - 1, rows, D), bfloat),
+        out_mine=vmem((rows, D), bfloat),
+        local_sem=dma((8,)),
+    )
+    counts = dict(
+        dm=(3,),
+        db=(3,),
+        pa=(3,),
+        pb=(3,),
+        pc=(3,),
+        fx=(3, depth),
+        fz=(3, depth - 1, 2),
+        qx=(depth,),
+        qz=(depth - 1, 2),
+        ox=(1,),
+        oz=(depth - 1,),
+        qa=(3,),
+        oa=(3,),
+    )
+    for name, count in counts.items():
+        scratch[name + "_s"] = dma(count)
+        scratch[name + "_r"] = dma(count)
+    far = {
+        "ff", "two_rows", "low", "trig_all", "attended", "one_rows", "qkv_weight", "out_weight"
+    }
+
+    def space(name):
+        return pl.BlockSpec(memory_space=pl.ANY if name in far else pltpu.VMEM)
+
+    outs = pl.pallas_call(
+        functools.partial(back_kernel, sizes, total_images),
+        out_shape=[jax.ShapeDtypeStruct(*shapes[name]) for name in BACK_OUT],
+        in_specs=[space(name) for name in BACK_IN],
+        out_specs=[space(name) for name in BACK_OUT],
+        scratch_shapes=[scratch[name] for name in BACK_SCRATCH],
+        compiler_params=pltpu.CompilerParams(
+            collective_id=collective, has_side_effects=True, vmem_limit_bytes=60 * 2**20
+        ),
+    )(*[values[name] for name in BACK_IN])
+    return dict(zip(BACK_OUT, outs))
+
+
+def forward_plain(clean_three, noise_three, patch_grid, labels, timesteps, matrices, embeddings, swiglu_weights, biases):
+    bfloat = jnp.bfloat16
+    single = jnp.float32
+    images = labels.shape[0]
+    length = clean_three.shape[1]
+    n_model = lax.axis_size("mlp")
+    n_data = lax.axis_size("dp")
+    sizes = (n_data, n_model)
+    total_images = images * n_data * n_model
+    rows = D // n_data
+    owned_start = lax.axis_index("dp") * rows
+    data_index = lax.axis_index("dp")
+    model_index = lax.axis_index("mlp")
+    heads = HEADS // n_model
+    head_cols = heads * HDIM
+    qkv_shard = jnp.concatenate(
+        [
+            cut_columns(matrices, 9 * D + part * D + model_index * head_cols, head_cols)
+            for part in range(3)
+        ],
+        axis=1,
+    ).astype(bfloat)
+    out_shard = matrices[:, 12 * D : 13 * D].astype(bfloat)
+    swiglu_shard = swiglu_weights.astype(bfloat)
+    qkv_weight = lax.all_gather(qkv_shard, "dp", axis=0, tiled=True)
+    swiglu_use = lax.all_gather(swiglu_shard, "dp", axis=1, tiled=True)
+    out_weight = gather_out(out_shard, sizes)
+
+    time_second = matrices[:, :D].astype(bfloat)
+    mod_weight = matrices[:, D : 9 * D].astype(bfloat)
+    time_first = embeddings[CH : CH + FREQ].astype(bfloat)
+    class_table = embeddings[CH + FREQ :].astype(bfloat)
+    patch_bias = biases[:D]
+    first_bias = biases[D : 2 * D]
+    second_bias = biases[2 * D : 3 * D]
+    mod_bias = biases[3 * D : 11 * D]
+    qkv_bias = biases[11 * D : 14 * D]
+    out_bias = biases[14 * D : 15 * D]
+    final_bias = biases[15 * D :]
+
+    facts = jnp.concatenate([timesteps[:, None], labels[:, None], patch_grid], axis=1)
+    facts = jnp.pad(facts, ((0, 8 - images), (0, 124)))
+    (facts_all,) = exchange([(facts, "all")], "both", sizes, 0)
+    facts_all = facts_all[:, 0, :4]
+    steps_all, labels_all, grid_all = facts_all[:, 0], facts_all[:, 1], facts_all[:, 2:4]
+    sinus_all = sinusoid(steps_all).astype(bfloat)
+    first_bias_own = lax.dynamic_slice_in_dim(first_bias, owned_start, rows)
+    second_bias_own = lax.dynamic_slice_in_dim(second_bias, owned_start, rows)
+    time_pre = jnp.dot(sinus_all, time_first, preferred_element_type=single) + first_bias_own
+    time_act = jax.nn.silu(time_pre).astype(bfloat)
+    time_part = jnp.dot(time_act, time_second, preferred_element_type=single)
+    small_shard = jnp.concatenate(
+        [embeddings[:CH], matrices[:, 13 * D :].T], axis=0
+    ).astype(bfloat)
+    time_parts, small_all = exchange(
+        [
+            (time_part.reshape(total_images, n_data, rows).transpose(1, 0, 2), "each"),
+            (small_shard, "all"),
+        ],
+        "dp",
+        sizes,
+        1,
+    )
+    small_all = small_all.transpose(1, 0, 2).reshape(3 * CH, D)
+    patch_weight = small_all[:CH]
+    final_weight = small_all[CH:].T
+    time_emb = jnp.sum(time_parts, axis=0) + second_bias_own
+    onehot = (labels_all[:, None] == jnp.arange(CLASSES + 1, dtype=jnp.int32)[None, :]).astype(
+        bfloat
+    )
+    condition = time_emb + jnp.dot(onehot, class_table, preferred_element_type=single)
+    cond_act = jax.nn.silu(condition).astype(bfloat)
+    cond_rank = lax.dynamic_index_in_dim(
+        cond_act.reshape(n_data, n_model, rows), model_index, 1, keepdims=False
+    )
+    mod_part = jnp.dot(cond_rank, mod_weight, preferred_element_type=single)
+    (mod_parts,) = exchange(
+        [(mod_part.reshape(n_data, 8, D), "each")],
+        "dp",
+        sizes,
+        2,
+    )
+    modulation = jnp.sum(mod_parts, axis=0).reshape(1, 8 * D) + mod_bias
+    shift_one, scale_one, gate_one, shift_two, scale_two, gate_two, shift_end, scale_end = (
+        jnp.split(modulation, 8, axis=1)
+    )
+
+    group_grid = lax.dynamic_slice_in_dim(grid_all, data_index * n_model, n_model, 0)
+    group_grid = jnp.stack(
+        [
+            lax.dynamic_index_in_dim(group_grid, model_index ^ rank, 0, keepdims=False)
+            for rank in range(n_model)
+        ]
+    )
+    cosine, sine, mask = turn_tables(group_grid, length)
+    noisy_low = noisy_input(clean_three, noise_three, timesteps).astype(bfloat)
+    hidden = jnp.dot(noisy_low, patch_weight, preferred_element_type=single) + patch_bias
+    normed_one = modulate(hidden, shift_one, scale_one).astype(bfloat)
+    one_rows = jnp.concatenate(gather_rows(normed_one.reshape(length, D), n_model), axis=0)
+    qkv_bias_own = jnp.concatenate(
+        [
+            lax.dynamic_slice_in_dim(qkv_bias, part * D + model_index * head_cols, head_cols)
+            for part in range(3)
+        ]
+    )
+    qkv = jnp.dot(one_rows, qkv_weight, preferred_element_type=single) + qkv_bias_own
+    low, attended, log_total = attention(
+        qkv.reshape(n_model, length, 3 * head_cols), cosine, sine, mask, heads
+    )
+    attended_rows = attended.reshape(n_model * length, head_cols)
+    branch_part = jnp.dot(attended_rows, out_weight, preferred_element_type=single).astype(bfloat)
+    branch_part = branch_part.reshape(n_model, length, D)
+    branch = (
+        scatter_rows(
+            (branch_part[2], branch_part[3]), (branch_part[0], branch_part[1]), n_model
+        )[None]
+        + out_bias
+    )
+    hidden_mid = hidden + gate_one[:, None, :] * branch
+    normed_two = modulate(hidden_mid, shift_two, scale_two).astype(bfloat)
+    two_rows = gather_rows(normed_two.reshape(length, D), n_model)
+    return dict(
+        steps=sinus_all,
+        onehot=onehot,
+        time_pre=time_pre,
+        condition=condition,
+        modulation=modulation,
+        hidden=hidden,
+        one_rows=one_rows,
+        qkv_weight=qkv_weight,
+        out_weight=out_weight,
+        swiglu=swiglu_use,
+        low=low,
+        attended=attended,
+        totals=log_total,
+        branch=branch,
+        hidden_mid=hidden_mid,
+        two_rows=two_rows,
+        final_weight=final_weight,
+        tables=(cosine, sine, mask),
+    )
+
+
+def forward_fused(clean_three, noise_three, patch_grid, labels, timesteps, matrices, embeddings, swiglu_weights, biases):
+    bfloat = jnp.bfloat16
+    single = jnp.float32
+    length = clean_three.shape[1]
+    n_model = lax.axis_size("mlp")
+    n_data = lax.axis_size("dp")
+    everyone = n_data * n_model
+    rows = D // n_data
+    owned_start = lax.axis_index("dp") * rows
+    model_index = lax.axis_index("mlp")
+    head_cols = HEADS // n_model * HDIM
+
+    def own_bias(start, amount, offset):
+        return lax.dynamic_slice_in_dim(biases, start + offset, amount)[None]
+
+    sinus = sinusoid(timesteps).astype(bfloat).astype(single).reshape(2, 128)
+    facts = jnp.concatenate(
+        [labels, patch_grid[:, 0] * patch_grid[:, 1]]
+    ).astype(single)
+    facts = jnp.concatenate(
+        [sinus, jnp.pad(facts[None], ((0, 0), (0, 126))), jnp.zeros((5, 128), single)], axis=0
+    )
+    cosine, sine, _ = turn_tables(patch_grid, length)
+    small = jnp.concatenate(
+        [
+            embeddings[:CH].T,
+            jnp.zeros((rows, CH), single),
+            matrices[:, 13 * D :],
+            jnp.zeros((rows, 64), single),
+        ],
+        axis=1,
+    ).astype(bfloat)
+    values = dict(
+        facts=facts,
+        trig=jnp.concatenate([cosine, sine], axis=0),
+        small=small,
+        time_first=embeddings[CH : CH + FREQ].astype(bfloat),
+        first_bias=own_bias(D, rows, owned_start),
+        second_bias=own_bias(2 * D, rows, owned_start),
+        time_blocks=matrices[:, :D].astype(bfloat).reshape(rows, n_data, rows).transpose(1, 0, 2),
+        class_table=embeddings[CH + FREQ :].astype(bfloat),
+        mod_weight=matrices[:, D : 9 * D].astype(bfloat),
+        mod_bias=biases[3 * D : 11 * D].reshape(8, D),
+        noisy=noisy_input(clean_three, noise_three, timesteps).astype(bfloat)[0],
+        patch_bias=biases[None, :D],
+        qkv_shard=jnp.concatenate(
+            [
+                cut_columns(matrices, (9 + part) * D + model_index * head_cols, head_cols)
+                for part in range(3)
+            ],
+            axis=1,
+        ).astype(bfloat),
+        out_shard=matrices[:, 12 * D : 13 * D].astype(bfloat),
+        ff_shard=swiglu_weights.astype(bfloat),
+        qkv_bias=jnp.concatenate(
+            [
+                own_bias((11 + part) * D, head_cols, model_index * head_cols)
+                for part in range(3)
+            ],
+            axis=1,
+        ),
+        out_bias=biases[None, 14 * D : 15 * D],
+    )
+    out = forward_all(values, (n_data, n_model), 0)
+    raw = {name: out[name] for name in BACK_IN if name in out}
+    facts_all = out["facts_all"]
+    group = lax.dynamic_slice_in_dim(
+        facts_all[:, 2, 1], lax.axis_index("dp") * n_model, n_model
+    )
+    spots = model_index ^ jnp.arange(n_model)
+    counts = jnp.sum(
+        jnp.where(spots[:, None] == jnp.arange(n_model)[None, :], group[None, :], 0.0), axis=1
+    )
+    mask = jnp.arange(length, dtype=jnp.int32)[None, None, :] < counts[:, None, None]
+    return dict(
+        raw=dict(raw, noisy=values["noisy"]),
+        steps=facts_all[:, :2].reshape(everyone, FREQ).astype(bfloat),
+        onehot=(
+            facts_all[:, 2, 0:1] == jnp.arange(CLASSES + 1, dtype=jnp.int32)[None].astype(single)
+        ).astype(bfloat),
+        time_pre=out["time_pre"],
+        condition=out["condition"],
+        modulation=out["modulation"].reshape(1, 8 * D),
+        hidden=out["hidden"][None],
+        one_rows=out["one_rows"].reshape(n_model * length, D),
+        qkv_weight=out["qkv_weight"],
+        out_weight=out["out_weight"],
+        swiglu=out["ff"],
+        low=out["low"],
+        attended=out["attended"],
+        totals=out["totals"],
+        branch=out["branch"][None],
+        hidden_mid=out["hidden_mid"][None],
+        two_rows=tuple(out["two_rows"]),
+        final_weight=out["small_all"][:, 2 * CH : 4 * CH],
+        tables=(out["trig_all"][:, 0], out["trig_all"][:, 1], mask.astype(single)),
+    )
+
+
+def backward_plain(
+    kept, clean_three, noise_three, patch_grid, timesteps, swiglu_weights, biases, total_images
+):
+    bfloat = jnp.bfloat16
+    single = jnp.float32
+    images, length = clean_three.shape[:2]
+    n_model = lax.axis_size("mlp")
+    n_data = lax.axis_size("dp")
+    sizes = (n_data, n_model)
+    rows = D // n_data
+    model_index = lax.axis_index("mlp")
+    heads = HEADS // n_model
+    head_cols = heads * HDIM
+    hidden_units = swiglu_weights.shape[2]
+    valid_slot = valid_slots(patch_grid, length)
+    final_bias = biases[15 * D :]
+    noisy_low = noisy_input(clean_three, noise_three, timesteps).astype(bfloat)
+    modulation, hidden, hidden_mid, branch = (
+        kept[name] for name in ("modulation", "hidden", "hidden_mid", "branch")
+    )
+    shift_one, scale_one, gate_one, shift_two, scale_two, gate_two, shift_end, scale_end = (
+        jnp.split(modulation, 8, axis=1)
+    )
+    qkv_weight, out_weight, swiglu_use = kept["qkv_weight"], kept["out_weight"], kept["swiglu"]
+    final_weight, one_rows, two_rows = kept["final_weight"], kept["one_rows"], kept["two_rows"]
+    low, log_total = kept["low"], kept["totals"]
+    attended_rows = kept["attended"].reshape(n_model * length, head_cols)
+    cosine, sine, mask = kept["tables"]
+    two_halves = (
+        jnp.concatenate(two_rows[:2], axis=0),
+        jnp.concatenate(two_rows[2:], axis=0),
+    )
+    gates, ups, acts, parts = [], [], [], []
+    for part in two_halves:
+        gate_val = jnp.dot(part, swiglu_use[0], preferred_element_type=single)
+        up_val = jnp.dot(part, swiglu_use[1], preferred_element_type=single)
+        act = (jax.nn.silu(gate_val) * up_val).astype(bfloat)
+        gates.append(gate_val)
+        ups.append(up_val)
+        acts.append(act)
+        parts.append(backward_product(act, swiglu_use[2]).astype(bfloat).reshape(2, length, D))
+    mixed = scatter_rows(parts[1], parts[0], n_model)[None]
+    hidden_end = hidden_mid + gate_two[:, None, :] * mixed
+    normed_end = modulate(hidden_end, shift_end, scale_end).astype(bfloat)
+    output = jnp.dot(normed_end, final_weight, preferred_element_type=single) + final_bias
+    local_loss, loss_pull = jax.vjp(
+        lambda values_out: loss_terms(values_out, clean_three, noise_three, timesteps, valid_slot),
+        output,
+    )
+    d_output = loss_pull(jnp.asarray(1.0 / total_images, single))[0].astype(bfloat)
+    d_normed_end = backward_product(d_output, final_weight)
+    unused, pull_end = jax.vjp(modulate, hidden_end, shift_end, scale_end)
+    d_hidden_end, d_shift_end, d_scale_end = pull_end(d_normed_end)
+    d_mixed = (gate_two[:, None, :] * d_hidden_end).astype(bfloat)
+    d_gate_two = jnp.sum(mixed * d_hidden_end, axis=1)
+    dmixed_rows = gather_rows(d_mixed.reshape(length, D), n_model)
+    dmixed_halves = (
+        jnp.concatenate(dmixed_rows[:2], axis=0),
+        jnp.concatenate(dmixed_rows[2:], axis=0),
+    )
+    d_gates, d_ups, d_parts = [], [], []
+    for part, gate_val, up_val in zip(dmixed_halves, gates, ups):
+        d_inner = jnp.dot(part, swiglu_use[2], preferred_element_type=single)
+        unused, pull_glu = jax.vjp(
+            lambda gate_in, up_in: jax.nn.silu(gate_in) * up_in, gate_val, up_val
+        )
+        d_gate, d_up = pull_glu(d_inner)
+        d_gate, d_up = d_gate.astype(bfloat), d_up.astype(bfloat)
+        d_gates.append(d_gate)
+        d_ups.append(d_up)
+        d_parts.append(
+            (backward_product(d_gate, swiglu_use[0]) + backward_product(d_up, swiglu_use[1]))
+            .astype(bfloat)
+            .reshape(2, length, D)
+        )
+    d_normed_two = scatter_rows(d_parts[1], d_parts[0], n_model)[None]
+    rows_ready = jnp.concatenate(two_halves, axis=0)
+    dmixed_ready = jnp.concatenate(dmixed_halves, axis=0)
+    half = hidden_units // 2
+
+    def owned(gradient, cut):
+        return reduce_dp(gradient.reshape(n_data, rows, -1), n_data, cut)
+
+    grad_swiglu = jnp.stack(
+        [
+            owned(weight_grad(rows_ready, jnp.concatenate(d_gates, axis=0)), half),
+            owned(weight_grad(rows_ready, jnp.concatenate(d_ups, axis=0)), half),
+            owned(weight_grad(dmixed_ready, jnp.concatenate(acts, axis=0)), half),
+        ]
+    )
+    unused, pull_two = jax.vjp(modulate, hidden_mid, shift_two, scale_two)
+    d_mid_part, d_shift_two, d_scale_two = pull_two(d_normed_two)
+    d_hidden_mid = d_hidden_end + d_mid_part
+    d_branch = (gate_one[:, None, :] * d_hidden_mid).astype(bfloat)
+    d_gate_one = jnp.sum(branch * d_hidden_mid, axis=1)
+
+    dbranch_rows = jnp.concatenate(gather_rows(d_branch.reshape(length, D), n_model), axis=0)
+    d_attended = backward_product(dbranch_rows, out_weight).astype(bfloat)
+    d_qkv = attention_back(
+        low,
+        log_total,
+        d_attended.reshape(n_model, length, head_cols),
+        cosine,
+        sine,
+        mask,
+        heads,
+    ).reshape(n_model * length, 3 * head_cols)
+    grad_out = reduce_out(weight_grad(attended_rows, dbranch_rows), sizes)
+    grad_qkv_own = owned(weight_grad(one_rows, d_qkv), 384)
+    d_one_part = backward_product(d_qkv, qkv_weight).astype(bfloat).reshape(n_model, length, D)
+    d_normed_one = scatter_rows(
+        (d_one_part[2], d_one_part[3]), (d_one_part[0], d_one_part[1]), n_model
+    )[None]
+    unused, pull_one = jax.vjp(modulate, hidden, shift_one, scale_one)
+    d_hidden_part, d_shift_one, d_scale_one = pull_one(d_normed_one)
+    d_hidden = (d_hidden_mid + d_hidden_part).astype(bfloat)
+
+    return dict(
+        d_modulation=jnp.concatenate(
+            [
+                d_shift_one,
+                d_scale_one,
+                d_gate_one,
+                d_shift_two,
+                d_scale_two,
+                d_gate_two,
+                d_shift_end,
+                d_scale_end,
+            ],
+            axis=1,
+        ),
+        hidden_sum=column_sum(d_hidden),
+        branch_sum=column_sum(d_branch),
+        qkv_sum=column_sum(d_qkv),
+        output_sum=column_sum(d_output),
+        loss=local_loss.reshape(1),
+        grad_patch=weight_grad(noisy_low, d_hidden),
+        grad_final=weight_grad(normed_end, d_output).T,
+        grad_swiglu=grad_swiglu,
+        grad_out=grad_out,
+        grad_qkv=jnp.stack(gather_rows(grad_qkv_own.astype(bfloat), n_model)).astype(single),
+    )
+
+
+def backward_fused(
+    kept, clean_three, noise_three, patch_grid, timesteps, swiglu_weights, biases, total_images
+):
+    single = jnp.float32
+    length = clean_three.shape[1]
+    sizes = (lax.axis_size("dp"), lax.axis_size("mlp"))
+    beta_now, bar_now, bar_prev = plan(timesteps)
+    consts = jnp.stack(
+        [
+            jnp.sqrt(bar_now),
+            jnp.sqrt(1.0 - bar_now),
+            jnp.log(beta_now),
+            jnp.log(beta_now * (1.0 - bar_prev) / (1.0 - bar_now)),
+            beta_now * jnp.sqrt(bar_prev) / (1.0 - bar_now),
+        ],
+        axis=1,
+    )
+    values = dict(
+        kept["raw"],
+        final_bias=biases[15 * D :].reshape(2, CH),
+        clean=clean_three[0],
+        noise=noise_three[0],
+        consts=jnp.pad(consts, ((0, 7), (0, 123))),
+        valid=valid_slots(patch_grid, length).astype(single).reshape(length, 1),
+    )
+    out = backward_all(values, sizes, total_images, 1)
+    return dict(
+        d_modulation=out["d_modulation"].reshape(1, 8 * D),
+        hidden_sum=out["hidden_sum"].reshape(-1),
+        branch_sum=out["branch_sum"].reshape(-1),
+        qkv_sum=out["qkv_sum"].reshape(-1),
+        output_sum=out["output_sum"].reshape(-1),
+        loss=out["loss"].reshape(1),
+        grad_patch=out["grad_patch"],
+        grad_final=out["grad_final"].reshape(2 * CH, D),
+        grad_swiglu=out["grad_ff"],
+        grad_out=out["grad_out"].astype(single),
+        grad_qkv=out["grad_qkv"].astype(single),
+    )
 
 
 def on_device(
@@ -598,251 +2248,53 @@
     head_cols = heads * HDIM
     hidden_units = swiglu_weights.shape[2]
 
-    qkv_shard = jnp.concatenate(
-        [
-            cut_columns(matrices, 9 * D + part * D + model_index * head_cols, head_cols)
-            for part in range(3)
-        ],
-        axis=1,
-    ).astype(bfloat)
-    out_shard = matrices[:, 12 * D : 13 * D].astype(bfloat)
-    swiglu_shard = swiglu_weights.astype(bfloat)
-    if n_data == 8:
-        depth = n_data // NX
-        qkv_weight = gather_dp(
-            qkv_shard[:80],
-            qkv_shard[80:],
-            (lambda out, at: out.at[at, 0:80], lambda out, at: out.at[at, 80:144]),
-            (n_data, rows, 3 * head_cols),
-            depth,
-        ).reshape(D, 3 * head_cols)
-        half = hidden_units // 2
-        swiglu_use = gather_dp(
-            swiglu_shard[:, :, :half],
-            swiglu_shard[:, :, half:],
-            (
-                lambda out, at: out.at[:, at, :, 0:half],
-                lambda out, at: out.at[:, at, :, half : 2 * half],
-            ),
-            (3, n_data, rows, hidden_units),
-            depth,
-        ).reshape(3, D, hidden_units)
-    else:
-        qkv_weight = lax.all_gather(qkv_shard, "dp", axis=0, tiled=True)
-        swiglu_use = lax.all_gather(swiglu_shard, "dp", axis=1, tiled=True)
-    out_weight = gather_out(out_shard, sizes)
-
+    clean_three = clean_patches.reshape(images, length, CH)
+    noise_three = noise_patches.reshape(images, length, CH)
+    fused = (n_data, n_model, images) == (8, 4, 1)
+    forward = forward_fused if fused else forward_plain
+    backward = backward_fused if fused else backward_plain
+    kept = forward(
+        clean_three,
+        noise_three,
+        patch_grid,
+        labels,
+        timesteps,
+        matrices,
+        embeddings,
+        swiglu_weights,
+        biases,
+    )
+    time_pre, condition, onehot, sinus_all = (
+        kept[name] for name in ("time_pre", "condition", "onehot", "steps")
+    )
+    time_act = jax.nn.silu(time_pre).astype(bfloat)
+    cond_act = jax.nn.silu(condition).astype(bfloat)
     time_second = matrices[:, :D].astype(bfloat)
     mod_weight = matrices[:, D : 9 * D].astype(bfloat)
-    time_first = embeddings[CH : CH + FREQ].astype(bfloat)
-    class_table = embeddings[CH + FREQ :].astype(bfloat)
-    patch_bias = biases[:D]
-    first_bias = biases[D : 2 * D]
-    second_bias = biases[2 * D : 3 * D]
-    mod_bias = biases[3 * D : 11 * D]
-    qkv_bias = biases[11 * D : 14 * D]
-    out_bias = biases[14 * D : 15 * D]
-    final_bias = biases[15 * D :]
-
-    facts = jnp.concatenate([timesteps[:, None], labels[:, None], patch_grid], axis=1)
-    facts = jnp.pad(facts, ((0, 8 - images), (0, 124)))
-    (facts_all,) = exchange([(facts, "all")], "both", sizes, 0)
-    facts_all = facts_all[:, 0, :4]
-    steps_all, labels_all, grid_all = facts_all[:, 0], facts_all[:, 1], facts_all[:, 2:4]
-    sinus_all = sinusoid(steps_all).astype(bfloat)
-    first_bias_own = lax.dynamic_slice_in_dim(first_bias, owned_start, rows)
-    second_bias_own = lax.dynamic_slice_in_dim(second_bias, owned_start, rows)
-    time_pre = jnp.dot(sinus_all, time_first, preferred_element_type=single) + first_bias_own
-    time_act = jax.nn.silu(time_pre).astype(bfloat)
-    time_part = jnp.dot(time_act, time_second, preferred_element_type=single)
-    small_shard = jnp.concatenate(
-        [embeddings[:CH], matrices[:, 13 * D :].T], axis=0
-    ).astype(bfloat)
-    time_parts, small_all = exchange(
+
+    grads = backward(
+        kept,
+        clean_three,
+        noise_three,
+        patch_grid,
+        timesteps,
+        swiglu_weights,
+        biases,
+        total_images,
+    )
+    grad_swiglu, grad_out = grads["grad_swiglu"], grads["grad_out"]
+    grad_qkv_own = grads["grad_qkv"][0]
+    qkv_stack = jnp.stack(
         [
-            (time_part.reshape(total_images, n_data, rows).transpose(1, 0, 2), "each"),
-            (small_shard, "all"),
-        ],
-        "dp",
-        sizes,
-        1,
-    )
-    small_all = small_all.transpose(1, 0, 2).reshape(3 * CH, D)
-    patch_weight = small_all[:CH]
-    final_weight = small_all[CH:].T
-    time_emb = jnp.sum(time_parts, axis=0) + second_bias_own
-    onehot = (labels_all[:, None] == jnp.arange(CLASSES + 1, dtype=jnp.int32)[None, :]).astype(
-        bfloat
-    )
-    condition = time_emb + jnp.dot(onehot, class_table, preferred_element_type=single)
-    cond_act = jax.nn.silu(condition).astype(bfloat)
-    cond_rank = lax.dynamic_index_in_dim(
-        cond_act.reshape(n_data, n_model, rows), model_index, 1, keepdims=False
-    )
-    mod_part = jnp.dot(cond_rank, mod_weight, preferred_element_type=single)
-    (mod_parts,) = exchange(
-        [(mod_part.reshape(n_data, 8, D), "each")],
-        "dp",
-        sizes,
-        2,
-    )
-    modulation = jnp.sum(mod_parts, axis=0).reshape(1, 8 * D) + mod_bias
-    shift_one, scale_one, gate_one, shift_two, scale_two, gate_two, shift_end, scale_end = (
-        jnp.split(modulation, 8, axis=1)
-    )
-
-    group_grid = lax.dynamic_slice_in_dim(grid_all, data_index * n_model, n_model, 0)
-    group_grid = jnp.stack(
-        [
-            lax.dynamic_index_in_dim(group_grid, model_index ^ rank, 0, keepdims=False)
+            lax.dynamic_index_in_dim(grads["grad_qkv"], model_index ^ rank, 0, keepdims=False)
             for rank in range(n_model)
         ]
     )
-    cosine, sine, mask = turn_tables(group_grid, length)
-    valid_slot = valid_slots(patch_grid, length)
-    clean_three = clean_patches.reshape(images, length, CH)
-    noise_three = noise_patches.reshape(images, length, CH)
-    noisy_low = noisy_input(clean_three, noise_three, timesteps).astype(bfloat)
-    hidden = jnp.dot(noisy_low, patch_weight, preferred_element_type=single) + patch_bias
-    normed_one = modulate(hidden, shift_one, scale_one).astype(bfloat)
-    one_rows = jnp.concatenate(gather_rows(normed_one.reshape(length, D), n_model), axis=0)
-    qkv_bias_own = jnp.concatenate(
-        [
-            lax.dynamic_slice_in_dim(qkv_bias, part * D + model_index * head_cols, head_cols)
-            for part in range(3)
-        ]
-    )
-    qkv = jnp.dot(one_rows, qkv_weight, preferred_element_type=single) + qkv_bias_own
-    low, attended, log_total = attention(
-        qkv.reshape(n_model, length, 3 * head_cols), cosine, sine, mask, heads
-    )
-    attended_rows = attended.reshape(n_model * length, head_cols)
-    branch_part = jnp.dot(attended_rows, out_weight, preferred_element_type=single).astype(bfloat)
-    branch_part = branch_part.reshape(n_model, length, D)
-    branch = (
-        scatter_rows(
-            (branch_part[2], branch_part[3]), (branch_part[0], branch_part[1]), n_model
-        )[None]
-        + out_bias
-    )
-    hidden_mid = hidden + gate_one[:, None, :] * branch
-    normed_two = modulate(hidden_mid, shift_two, scale_two).astype(bfloat)
-
-    two_rows = gather_rows(normed_two.reshape(length, D), n_model)
-    two_halves = (
-        jnp.concatenate(two_rows[:2], axis=0),
-        jnp.concatenate(two_rows[2:], axis=0),
-    )
-    gates, ups, acts, parts = [], [], [], []
-    for part in two_halves:
-        gate_val = jnp.dot(part, swiglu_use[0], preferred_element_type=single)
-        up_val = jnp.dot(part, swiglu_use[1], preferred_element_type=single)
-        act = (jax.nn.silu(gate_val) * up_val).astype(bfloat)
-        gates.append(gate_val)
-        ups.append(up_val)
-        acts.append(act)
-        parts.append(backward_product(act, swiglu_use[2]).astype(bfloat).reshape(2, length, D))
-    mixed = scatter_rows(parts[1], parts[0], n_model)[None]
-    hidden_end = hidden_mid + gate_two[:, None, :] * mixed
-    normed_end = modulate(hidden_end, shift_end, scale_end).astype(bfloat)
-    output = jnp.dot(normed_end, final_weight, preferred_element_type=single) + final_bias
-    local_loss, loss_pull = jax.vjp(
-        lambda values_out: loss_terms(values_out, clean_three, noise_three, timesteps, valid_slot),
-        output,
-    )
-    d_output = loss_pull(jnp.asarray(1.0 / total_images, single))[0].astype(bfloat)
-    d_normed_end = backward_product(d_output, final_weight)
-    unused, pull_end = jax.vjp(modulate, hidden_end, shift_end, scale_end)
-    d_hidden_end, d_shift_end, d_scale_end = pull_end(d_normed_end)
-    d_mixed = (gate_two[:, None, :] * d_hidden_end).astype(bfloat)
-    d_gate_two = jnp.sum(mixed * d_hidden_end, axis=1)
-    dmixed_rows = gather_rows(d_mixed.reshape(length, D), n_model)
-    dmixed_halves = (
-        jnp.concatenate(dmixed_rows[:2], axis=0),
-        jnp.concatenate(dmixed_rows[2:], axis=0),
-    )
-    d_gates, d_ups, d_parts = [], [], []
-    for part, gate_val, up_val in zip(dmixed_halves, gates, ups):
-        d_inner = jnp.dot(part, swiglu_use[2], preferred_element_type=single)
-        unused, pull_glu = jax.vjp(
-            lambda gate_in, up_in: jax.nn.silu(gate_in) * up_in, gate_val, up_val
-        )
-        d_gate, d_up = pull_glu(d_inner)
-        d_gate, d_up = d_gate.astype(bfloat), d_up.astype(bfloat)
-        d_gates.append(d_gate)
-        d_ups.append(d_up)
-        d_parts.append(
-            (backward_product(d_gate, swiglu_use[0]) + backward_product(d_up, swiglu_use[1]))
-            .astype(bfloat)
-            .reshape(2, length, D)
-        )
-    d_normed_two = scatter_rows(d_parts[1], d_parts[0], n_model)[None]
-    rows_ready = jnp.concatenate(two_halves, axis=0)
-    dmixed_ready = jnp.concatenate(dmixed_halves, axis=0)
-    half = hidden_units // 2
-
-    def owned(gradient, cut):
-        return reduce_dp(gradient.reshape(n_data, rows, -1), n_data, cut)
-
-    grad_swiglu = jnp.stack(
-        [
-            owned(weight_grad(rows_ready, jnp.concatenate(d_gates, axis=0)), half),
-            owned(weight_grad(rows_ready, jnp.concatenate(d_ups, axis=0)), half),
-            owned(weight_grad(dmixed_ready, jnp.concatenate(acts, axis=0)), half),
-        ]
-    )
-    unused, pull_two = jax.vjp(modulate, hidden_mid, shift_two, scale_two)
-    d_mid_part, d_shift_two, d_scale_two = pull_two(d_normed_two)
-    d_hidden_mid = d_hidden_end + d_mid_part
-    d_branch = (gate_one[:, None, :] * d_hidden_mid).astype(bfloat)
-    d_gate_one = jnp.sum(branch * d_hidden_mid, axis=1)
-
-    dbranch_rows = jnp.concatenate(gather_rows(d_branch.reshape(length, D), n_model), axis=0)
-    d_attended = backward_product(dbranch_rows, out_weight).astype(bfloat)
-    d_qkv = attention_back(
-        low,
-        log_total,
-        d_attended.reshape(n_model, length, head_cols),
-        cosine,
-        sine,
-        mask,
-        heads,
-    ).reshape(n_model * length, 3 * head_cols)
-    grad_out = reduce_out(weight_grad(attended_rows, dbranch_rows), sizes)
-    grad_qkv_own = owned(weight_grad(one_rows, d_qkv), 384)
-    d_one_part = backward_product(d_qkv, qkv_weight).astype(bfloat).reshape(n_model, length, D)
-    d_normed_one = scatter_rows(
-        (d_one_part[2], d_one_part[3]), (d_one_part[0], d_one_part[1]), n_model
-    )[None]
-    unused, pull_one = jax.vjp(modulate, hidden, shift_one, scale_one)
-    d_hidden_part, d_shift_one, d_scale_one = pull_one(d_normed_one)
-    d_hidden = (d_hidden_mid + d_hidden_part).astype(bfloat)
-
-    qkv_blocks = gather_rows(grad_qkv_own.astype(bfloat), n_model)
-    qkv_stack = jnp.stack(qkv_blocks)
-    qkv_stack = jnp.stack(
-        [
-            lax.dynamic_index_in_dim(qkv_stack, model_index ^ rank, 0, keepdims=False)
-            for rank in range(n_model)
-        ]
-    ).astype(single)
     grad_qkv = (
         qkv_stack.reshape(n_model, rows, 3, head_cols).transpose(1, 2, 0, 3).reshape(rows, 3 * D)
     )
 
-    d_modulation = jnp.concatenate(
-        [
-            d_shift_one,
-            d_scale_one,
-            d_gate_one,
-            d_shift_two,
-            d_scale_two,
-            d_gate_two,
-            d_shift_end,
-            d_scale_end,
-        ],
-        axis=1,
-    ).astype(bfloat)
+    d_modulation = grads["d_modulation"].astype(bfloat)
     (dmod_all,) = exchange(
         [(d_modulation.reshape(16, D // 2), "all")], "both", sizes, 3
     )
@@ -870,23 +2322,21 @@
         precision=lax.Precision.HIGHEST,
         preferred_element_type=single,
     )
-    grad_final_patch = weight_grad(noisy_low, d_hidden)
-    grad_final = weight_grad(normed_end, d_output)
-
-    qkv_sums = column_sum(d_qkv).reshape(3, head_cols)
+
+    qkv_sums = grads["qkv_sum"].reshape(3, head_cols)
     qkv_bias_part = lax.dynamic_update_slice(
         jnp.zeros((3, D), single), qkv_sums, (0, model_index * head_cols)
     )
     local_sums = jnp.concatenate(
         [
-            column_sum(d_hidden),
+            grads["hidden_sum"],
             qkv_bias_part.reshape(-1),
-            column_sum(d_branch),
-            column_sum(d_output),
-            local_loss.reshape(1),
+            grads["branch_sum"],
+            grads["output_sum"],
+            grads["loss"],
             jnp.zeros((95,), single),
-            grad_final_patch.reshape(-1),
-            grad_final.T.reshape(-1),
+            grads["grad_patch"].reshape(-1),
+            grads["grad_final"].reshape(-1),
         ]
     )
     everyone = n_data * n_model

time: 701 us -> 531 us (0.76)
  Pallas kernels: 130 us -> 399 us
  waiting for transfers between devices: 165 us -> 0 us
  starting transfers between devices: 121 us -> 0 us
  matrix products: 68.6 us -> 12.9 us
  local copies, waits for them, and re-layouts: 94.4 us -> 41.4 us
  other arithmetic: 94.3 us -> 56.2 us
    pallas_call x4 -> x2, Pallas kernels: 37.7 us -> 344 us  [the longest x1 201 us: backward_all(): pl.pallas_call(functools.partial(back_kernel, sizes, total_images), out_s...]
    ppermute x99 -> x0, waiting for transfers between devices: 165 us -> none  [the longest x4 49.5 us: reduce_dp(): got = lax.ppermute(give, 'dp', swap_pairs(count)).astype(jnp.float32)]
    ppermute x99 -> x0, starting transfers between devices: 121 us -> none  [the longest x29 52.7 us: flip(): lax.ppermute(value, 'mlp', [(spot, spot ^ bit) for spot in range(count)])]
    pallas_call x7 -> x4, Pallas kernels: 92.2 us -> 54.6 us  [exchange(): pl.pallas_call(functools.partial(exchange_kernel, axes, sizes, modes), ou...]
    unnamed x334 -> x67, local copies, waits for them, and re-layouts: 41.2 us -> 7.27 us
    dot_general x14 -> x0, matrix products: 28.4 us -> none  [the longest x2 7.08 us: on_device(): d_inner = jnp.dot(part, swiglu_use[2], preferred_element_type=single)]
    dot_general x11 -> x2, matrix products: 18.9 us -> 4.58 us  [backward_product(): lax.dot_general(gradient, weight, (((gradient.ndim - 1,), (1,)), ((), ())...]
    dot_general x9 -> x2, matrix products: 17.3 us -> 5.6 us  [weight_grad(): lax.dot_general(flat_in, flat_grad, (((0,), (0,)), ((), ())), preferred_e...]
  transfers between devices with their start and end apart: 99 -> 0, of which waited for: 39 -> 0; matrix products, arithmetic and copies ran while one was open for 22% -> 0% of each run, Pallas kernels for 12% -> 0%
where the time goes in v2:
time: 531 us; the launch traced here: 527 us
  Pallas kernels  399 us (75%)
  other arithmetic  56.2 us (11%)
  local copies, waits for them, and re-layouts  41.4 us (8%)
  between operations  17.6 us (3%)
  matrix products  12.9 us (2%)
    pallas_call x1, Pallas kernels, backward_all(): pl.pallas_call(functools.partial(back_kernel, sizes, total_images), out_s...  201 us
    pallas_call x1, Pallas kernels, forward_all(): pl.pallas_call(functools.partial(forward_kernel, sizes), out_shape=[jax.S...  144 us
    pallas_call x4, Pallas kernels, exchange(): pl.pallas_call(functools.partial(exchange_kernel, axes, sizes, modes), ou...  54.6 us
    add x4, other arithmetic, adam_step(): average_decay * average + (1.0 - average_decay) * weight  35.9 us

profile of v2, /device:TPU:15, one launch (start us, length us, event | category | flops | bytes accessed | tf_op | source)
XLA Modules:
  0.0 526.9 jit_solution(2465494796912336824)
XLA Ops:
  10.2 4.0 convert.40
  14.2 2.1 copy-done
  18.8 1.9 fusion.44
  23.2 3.5 slice.146.refs_8_
  35.2 143.6 %shard_map.348 = (f32[32,8,128]{2,1,0:T(8,128)}, f32[4,2,256,72]{3,2,1,0:T(8,128)}, bf16[1152,128]{1,0:T(8,128)(2,1)}, f32[32,144]{1,0:T(8,128)}, f32[32,144]{1,...) custom-call(f32[8,128]{1,0:T(8,128)} %fusion.26.refs_0_, ...), custom_call_target="tpu_custom_call" | custom-call | tf_op jit(solution)/shard_map/pallas_call | solution.py:1056
  185.3 200.7 %shard_map.349 = (f32[3,144,768]{2,1,0:T(8,128)}, bf16[4,144,864]{2,1,0:T(8,128)(2,1)}, bf16[144,1152]{1,0:T(8,128)(2,1)}, f32[8,1152]{1,0:T(8,128)}, f32[1,1152...) custom-call(bf16[3,1152,768]{2,1,0:T(8,128)(2,1)} %get-tuple-element, ...), custom_call_target="tpu_custom_call" | custom-call | tf_op jit(solution)/shard_map/pallas_call | solution.py:1772
  386.9 21.0 %shard_map.351 = bf16[32,16,576]{2,1,0:T(8,128)(2,1)S(1)} custom-call(bf16[16,576]{1,0:T(8,128)(2,1)S(1)} %convert_element_type.147.refs_0_), custom_call_target="tpu_custom_call" | custom-call | tf_op jit(solution)/shard_map/pallas_call | solution.py:211
  408.4 3.3 fusion.33
  411.8 5.1 shard_map.352
  417.2 1.7 constant_dynamic-update-slice_fusion.3
  418.9 3.9 constant_dynamic-update-slice_fusion.2
  426.4 3.2 reshape.632
  429.6 3.7 copy.70
  433.3 2.3 reshape.633
  435.6 3.1 constant_dynamic-update-slice_fusion.1
  438.7 1.5 convert_dynamic-update-slice_fusion
  445.8 1.9 multiply_reduce_fusion.3
  451.4 1.7 concatenate.70
  453.1 13.7 %shard_map.350 = f32[32,16,128]{2,1,0:T(8,128)S(1)} custom-call(f32[32,16,128]{2,1,0:T(8,128)S(1)} %bitcast.56), custom_call_target="tpu_custom_call" | custom-call | tf_op jit(solution)/shard_map/pallas_call | solution.py:211
  466.9 14.8 %shard_map.353 = f32[32,24,128]{2,1,0:T(8,128)S(1)} custom-call(f32[24,128]{1,0:T(8,128)S(1)} %pad_maximum_fusion.2.refs_0_), custom_call_target="tpu_custom_call" | custom-call | tf_op jit(solution)/shard_map/pallas_call | solution.py:211
  487.8 28.2 %multiply_add_fusion = (f32[144,15008]{1,0:T(8,128)}, f32[144,15008]{1,0:T(8,128)}, f32[144,15008]{1,0:T(8,128)}, f32[144,15008]{1,0:T(8,128)}) fusion(f32[144,15008]{1,0:T(8,128)} %param.38, f32[144,15008]{1,0:T(8,128)} %param.26, f32[144,15008]{1,0:T(8,128)} %bitcast_dynamic-update-slice_fusion, f32[]{:T(128)S(6)} %min.3, f32[144,15008]{1,0:T(8,128)} %param.30, ...), kind=kLoop, calls=%fused_computation.2 | loop fusion | flops 41061888 | bytes 77801472 | tf_op jit(solution)/shard_map/add | solution.py:109
  516.2 1.4 concatenate.75
  517.7 3.7 multiply_add_fusion.4
  521.5 3.3 multiply_add_fusion.2
  (169 shorter events, 36.1 us)
Async XLA Ops:
  10.2 6.1 %copy-start.4 = (f32[1273,144]{0,1:T(8,128)S(1)}, f32[1273,144]{0,1:T(8,128)}, u32[]{:S(2)}) copy-start(f32[1273,144]{0,1:T(8,128)} %param.27) | copy-start | bytes 2199748
  10.2 8.0 %copy-start.10 = (f32[17312]{0:T(1024)S(1)}, f32[17312]{0:T(1024)}, u32[]{:S(2)}) copy-start(f32[17312]{0:T(1024)} %param.29) | copy-start | bytes 207748
  23.2 6.2 %copy-start.19 = (f32[256,16]{0,1:T(8,128)S(1)}, f32[256,16]{0,1:T(8,128)}, u32[]{:S(2)}) copy-start(f32[256,16]{0,1:T(8,128)} %param.21) | copy-start | bytes 49156
  23.2 6.2 %copy-start.20 = (f32[256,16]{0,1:T(8,128)S(1)}, f32[256,16]{0,1:T(8,128)}, u32[]{:S(2)}) copy-start(f32[256,16]{0,1:T(8,128)} %param.22) | copy-start | bytes 49156
  23.2 9.7 %copy-start.2 = (f32[3,144,768]{2,1,0:T(8,128)S(1)}, f32[3,144,768]{2,1,0:T(8,128)}, u32[]{:S(2)}) copy-start(f32[3,144,768]{2,1,0:T(8,128)} %param.28) | copy-start | bytes 3981316
  185.3 223.1 %copy-start.12 = (f32[32,144]{1,0:T(8,128)S(1)}, f32[32,144]{1,0:T(8,128)}, u32[]{:S(2)}) copy-start(f32[32,144]{1,0:T(8,128)} %get-tuple-element.70) | copy-start | bytes 55300
  407.8 9.3 %copy-start.25 = (f32[32,144]{1,0:T(8,128)S(1)}, f32[32,144]{1,0:T(8,128)}, u32[]{:S(2)}) copy-start(f32[32,144]{1,0:T(8,128)} %get-tuple-element.71) | copy-start | bytes 55300
  417.2 5.6 %copy-start.13 = (bf16[32,1152]{1,0:T(8,128)(2,1)}, bf16[32,1152]{1,0:T(8,128)(2,1)S(1)}, u32[]{:S(2)}) copy-start(bf16[32,1152]{1,0:T(8,128)(2,1)S(1)} %reshape.627) | copy-start | bytes 221188
  435.5 5.3 %copy-start.14 = (bf16[32,1152]{1,0:T(8,128)(2,1)S(1)}, bf16[32,1152]{1,0:T(8,128)(2,1)}, u32[]{:S(2)}) copy-start(bf16[32,1152]{1,0:T(8,128)(2,1)} %copy-done.13) | copy-start | bytes 221188
  435.5 5.4 %copy-start.26 = (f32[32,144]{1,0:T(8,128)S(1)}, f32[32,144]{1,0:T(8,128)}, u32[]{:S(2)}) copy-start(f32[32,144]{1,0:T(8,128)} %get-tuple-element.71) | copy-start | bytes 55300
  435.5 10.3 %copy-start.21 = (f32[32,144]{1,0:T(8,128)S(1)}, f32[32,144]{1,0:T(8,128)}, u32[]{:S(2)}) copy-start(f32[32,144]{1,0:T(8,128)} %get-tuple-element.129) | copy-start | bytes 55300
  435.6 12.8 %copy-start.1 = (f32[3,144,768]{2,1,0:T(8,128)S(1)}, f32[3,144,768]{2,1,0:T(8,128)}, u32[]{:S(2)}) copy-start(f32[3,144,768]{2,1,0:T(8,128)} %get-tuple-element.73) | copy-start | bytes 3981316
  438.7 12.0 %copy-start.23 = (f32[1,1152]{1,0:T(1,128)S(1)}, f32[1,1152]{1,0:T(1,128)}, u32[]{:S(2)}) copy-start(f32[1,1152]{1,0:T(1,128)} %get-tuple-element.62) | copy-start | bytes 13828
  438.7 12.1 %copy-start.24 = (f32[1,864]{1,0:T(1,128)S(1)}, f32[1,864]{1,0:T(1,128)}, u32[]{:S(2)}) copy-start(f32[1,864]{1,0:T(1,128)} %get-tuple-element.63) | copy-start | bytes 10372
  438.7 12.5 %copy-start.22 = (f32[1,1152]{1,0:T(1,128)S(1)}, f32[1,1152]{1,0:T(1,128)}, u32[]{:S(2)}) copy-start(f32[1,1152]{1,0:T(1,128)} %get-tuple-element.64) | copy-start | bytes 13828
  438.7 12.6 %copy-start.27 = (f32[2,16]{1,0:T(2,128)S(1)}, f32[2,16]{1,0:T(2,128)}, u32[]{:S(2)}) copy-start(f32[2,16]{1,0:T(2,128)} %get-tuple-element.65) | copy-start | bytes 388
  438.7 12.7 %copy-start.15 = (f32[16,1152]{1,0:T(8,128)S(1)}, f32[16,1152]{1,0:T(8,128)}, u32[]{:S(2)}) copy-start(f32[16,1152]{1,0:T(8,128)} %get-tuple-element.67) | copy-start | bytes 221188
  438.7 12.7 %copy-start.11 = (f32[2,16,1152]{2,1,0:T(8,128)S(1)}, f32[2,16,1152]{2,1,0:T(8,128)}, u32[]{:S(2)}) copy-start(f32[2,16,1152]{2,1,0:T(8,128)} %get-tuple-element.68) | copy-start | bytes 442372
  487.8 29.9 %copy-start.5 = (f32[1273,144]{0,1:T(8,128)S(1)}, f32[1273,144]{0,1:T(8,128)}, u32[]{:S(2)}) copy-start(f32[1273,144]{0,1:T(8,128)} %param.27) | copy-start | bytes 2199748
  517.7 3.8 copy-start.3
  517.7 3.8 copy-start.6
  517.7 3.8 copy-start.7
  517.7 3.8 copy-start.8
  521.5 3.3 copy-start.16
  (4 other events, 11.8 us)

commit v3 on v2

--- a/solution.py
+++ b/solution.py
@@ -1,5 +1,7 @@
 import functools
 import math
+from types import SimpleNamespace
+from typing import Any, NamedTuple
 
 import jax
 import jax.numpy as jnp
@@ -223,105 +225,13 @@
     )(*arrays)
 
 
-def place_kernel(targets, *refs):
-    pieces, out, sem = refs[:-2], refs[-2], refs[-1]
-    copies = []
-    for spot, (piece, target) in enumerate(zip(pieces, targets)):
-        copy = pltpu.make_async_copy(piece, target(out), sem.at[spot])
-        copy.start()
-        copies.append(copy)
-    for copy in copies:
-        copy.wait()
-
-
-def place(pieces, targets, shape, dtype):
-    return pl.pallas_call(
-        functools.partial(place_kernel, targets),
-        out_shape=jax.ShapeDtypeStruct(shape, dtype),
-        in_specs=[pl.BlockSpec(memory_space=pl.ANY)] * len(pieces),
-        out_specs=pl.BlockSpec(memory_space=pl.ANY),
-        scratch_shapes=[pltpu.SemaphoreType.DMA((len(pieces),))],
-        compiler_params=pltpu.CompilerParams(vmem_limit_bytes=KERNEL_VMEM),
-    )(*pieces)
-
-
 NX = 2
 
 
-def ring_pairs(depth, shift):
-    return [
-        (z * NX + x, ((z + shift) % depth) * NX + x) for z in range(depth) for x in range(NX)
-    ]
-
-
-def swap_pairs(count):
-    return [(spot, spot ^ 1) for spot in range(count)]
-
-
-def ring_pieces(half, depth, shift):
-    arrived = [half]
-    for _ in range(depth - 1):
-        arrived.append(lax.ppermute(arrived[-1], "dp", ring_pairs(depth, shift)))
-    return arrived
-
-
-def gather_dp(first, second, selects, shape, depth):
-    swaps = swap_pairs(depth * NX)
-    pieces, targets = [], []
-
-    def source(step, shift, other):
-        def spot():
-            d = lax.axis_index("dp")
-            z, x = lax.div(d, NX), lax.rem(d, NX)
-            z = lax.rem(z - step * shift + depth * NX, depth)
-            x = 1 - x if other else x
-            return z * NX + x
-
-        return spot
-
-    for half, shift, select in ((first, 1, selects[0]), (second, -1, selects[1])):
-        for step, piece in enumerate(ring_pieces(half, depth, shift)):
-            other = lax.ppermute(piece, "dp", swaps)
-            for swapped, value in ((False, piece), (True, other)):
-                pieces.append(value)
-                spot = source(step, shift, swapped)
-                targets.append(functools.partial(lambda sel, at, out: sel(out, at()), select, spot))
-    return place(pieces, targets, shape, first.dtype)
-
-
-def reduce_ring(blocks, depth, shift):
-    z = lax.div(lax.axis_index("dp"), NX)
-
-    def block(offset):
-        return lax.dynamic_index_in_dim(
-            blocks, lax.rem(z + offset + 2 * depth, depth), 0, keepdims=False
-        )
-
-    running = block(-shift)
-    for step in range(1, depth):
-        arrived = lax.ppermute(running.astype(jnp.bfloat16), "dp", ring_pairs(depth, shift))
-        running = arrived.astype(jnp.float32) + block(-shift * (step + 1))
-    return running
-
-
-def reduce_dp(value, count, cut):
-    if count != 8:
-        return lax.psum_scatter(
-            value.astype(jnp.bfloat16), "dp", scatter_dimension=0, tiled=True
-        )[0].astype(jnp.float32)
-    depth = count // NX
-    x = lax.rem(lax.axis_index("dp"), NX)
-    paired = value.reshape(depth, NX, *value.shape[1:])
-    give = lax.dynamic_index_in_dim(paired, 1 - x, 1, keepdims=False).astype(jnp.bfloat16)
-    got = lax.ppermute(give, "dp", swap_pairs(count)).astype(jnp.float32)
-    blocks = lax.dynamic_index_in_dim(paired, x, 1, keepdims=False) + got
-    return jnp.concatenate(
-        [
-            reduce_ring(blocks[:, :, :cut], depth, 1),
-            reduce_ring(blocks[:, :, cut:], depth, -1),
-        ],
-        axis=1,
-    )
+def reduce_dp(value):
+    return lax.psum_scatter(value.astype(jnp.bfloat16), "dp", scatter_dimension=0, tiled=True)[
+        0
+    ].astype(jnp.float32)
 
 
 def flip(value, bit, count):
@@ -342,75 +252,18 @@
     return near_parts[0].astype(single) + near.astype(single) + far.astype(single)
 
 
-def out_pairs(depth, ranks, step, shift):
-    pairs = []
-    for rank in range(ranks):
-        for x in range(NX):
-            start = (rank + (step - 1) * shift) % depth
-            stop = (rank + step * shift) % depth
-            pairs.append(((start * NX + x) * ranks + rank, (stop * NX + x) * ranks + rank))
-    return pairs
-
-
-def gather_out(shard, sizes):
-    n_data, n_model = sizes
-    if n_data != 8 or n_model != 4:
-        whole = lax.all_gather(shard, "dp", axis=0, tiled=True)
-        height = D // n_model
-        return lax.dynamic_slice_in_dim(whole, lax.axis_index("mlp") * height, height, 0)
-    depth = n_data // NX
-    d = lax.axis_index("dp")
-    z, x = lax.div(d, NX), lax.rem(d, NX)
-    mine = z == lax.axis_index("mlp")
-    halves = []
-    for part, shift in ((shard[:80], 1), (shard[80:], -1)):
-        total = jnp.where(mine, part, jnp.zeros_like(part))
-        moving = part
-        for step in range(1, depth):
-            moving = lax.ppermute(moving, ("dp", "mlp"), out_pairs(depth, n_model, step, shift))
-            total = total + moving
-        halves.append(total)
-    own = jnp.concatenate(halves, axis=0)
-    other = lax.ppermute(own, "dp", swap_pairs(n_data))
-    low = jnp.where(x == 0, own, other)
-    high = jnp.where(x == 0, other, own)
-    return jnp.concatenate([low, high], axis=0)
-
-
-def reduce_out(value, sizes):
-    n_data, n_model = sizes
-    single, bfloat = jnp.float32, jnp.bfloat16
-    if n_data != 8 or n_model != 4:
-        whole = jnp.zeros((D, D), single)
-        whole = lax.dynamic_update_slice_in_dim(
-            whole, value, lax.axis_index("mlp") * value.shape[0], 0
-        )
-        part = lax.psum_scatter(whole.astype(bfloat), "dp", scatter_dimension=0, tiled=True)
-        return lax.psum(part.astype(single), "mlp")
-    depth = n_data // NX
-    d = lax.axis_index("dp")
-    z, x = lax.div(d, NX), lax.rem(d, NX)
-    mine = z == lax.axis_index("mlp")
-    paired = value.reshape(NX, D // n_data, D)
-    give = lax.dynamic_index_in_dim(paired, 1 - x, 0, keepdims=False).astype(bfloat)
-    got = lax.ppermute(give, "dp", swap_pairs(n_data)).astype(single)
-    blocks = lax.dynamic_index_in_dim(paired, x, 0, keepdims=False) + got
-    halves = []
-    for part, shift in ((blocks[:80], 1), (blocks[80:], -1)):
-        running = part
-        for step in range(1, depth):
-            pairs = [
-                (source, target)
-                for source, target in out_pairs(depth, n_model, step + 1, shift)
-            ]
-            arrived = lax.ppermute(running.astype(bfloat), ("dp", "mlp"), pairs)
-            running = arrived.astype(single) + part
-        halves.append(running)
-    summed = jnp.concatenate(halves, axis=0)
-    shared = jnp.where(mine, summed, 0.0).astype(bfloat)
-    shared = shared + flip(shared, 1, n_model)
-    shared = shared + flip(shared, 2, n_model)
-    return shared.astype(single)
+def gather_out(shard):
+    whole = lax.all_gather(shard, "dp", axis=0, tiled=True)
+    height = D // lax.axis_size("mlp")
+    return lax.dynamic_slice_in_dim(whole, lax.axis_index("mlp") * height, height, 0)
+
+
+def reduce_out(value):
+    whole = lax.dynamic_update_slice_in_dim(
+        jnp.zeros((D, D), jnp.float32), value, lax.axis_index("mlp") * value.shape[0], 0
+    )
+    part = lax.psum_scatter(whole.astype(jnp.bfloat16), "dp", scatter_dimension=0, tiled=True)
+    return lax.psum(part.astype(jnp.float32), "mlp")
 
 
 def swapped(values):
@@ -587,28 +440,94 @@
     return centered * lax.rsqrt(variance + 1e-06) * (1.0 + scale_by) + shift_by
 
 
-FORWARD_IN = (
-    "facts", "trig", "small", "time_first", "first_bias", "second_bias", "time_blocks",
-    "class_table", "mod_weight", "mod_bias", "noisy", "patch_bias", "qkv_shard", "out_shard",
-    "ff_shard", "qkv_bias", "out_bias",
-)
-FORWARD_OUT = (
-    "facts_all", "trig_all", "small_all", "time_pre", "condition", "modulation", "hidden",
-    "one_rows", "qkv_weight", "out_weight", "ff", "low", "attended", "totals", "branch",
-    "hidden_mid", "two_rows",
-)
-FORWARD_SCRATCH = (
-    "time_send", "time_recv", "mod_send", "mod_recv", "mod_low", "qkv", "parts_send",
-    "parts_recv", "facts_s", "facts_r", "small_s", "small_r", "time_s", "time_r",
-    "mods_s", "mods_r", "trig_s", "trig_r", "one_s", "one_r", "two_s", "two_r", "part_s",
-    "part_r", "qz_s", "qz_r", "qx_s", "qx_r", "oz_s", "oz_r", "ox_s", "ox_r", "fz_s", "fz_r",
-    "fx_s", "fx_r", "local_sem",
-)
+def named(inputs, outputs, scratch, refs):
+    ends = len(inputs._fields), len(inputs._fields) + len(outputs._fields)
+    parts = inputs(*refs[: ends[0]]), outputs(*refs[ends[0] : ends[1]]), scratch(*refs[ends[1] :])
+    return SimpleNamespace(**{k: v for part in parts for k, v in part._asdict().items()})
+
+
+class ForwardIn(NamedTuple):
+    facts: Any
+    trig: Any
+    small: Any
+    time_first: Any
+    first_bias: Any
+    second_bias: Any
+    time_blocks: Any
+    class_table: Any
+    mod_weight: Any
+    mod_bias: Any
+    noisy: Any
+    patch_bias: Any
+    qkv_shard: Any
+    out_shard: Any
+    ff_shard: Any
+    qkv_bias: Any
+    out_bias: Any
+
+
+class ForwardOut(NamedTuple):
+    facts_all: Any
+    trig_all: Any
+    small_all: Any
+    time_pre: Any
+    condition: Any
+    modulation: Any
+    hidden: Any
+    one_rows: Any
+    qkv_weight: Any
+    out_weight: Any
+    ff: Any
+    low: Any
+    attended: Any
+    totals: Any
+    branch: Any
+    hidden_mid: Any
+    two_rows: Any
+
+
+class ForwardScratch(NamedTuple):
+    time_send: Any
+    time_recv: Any
+    mod_send: Any
+    mod_recv: Any
+    mod_low: Any
+    qkv: Any
+    parts_send: Any
+    parts_recv: Any
+    facts_s: Any
+    facts_r: Any
+    small_s: Any
+    small_r: Any
+    time_s: Any
+    time_r: Any
+    mods_s: Any
+    mods_r: Any
+    trig_s: Any
+    trig_r: Any
+    one_s: Any
+    one_r: Any
+    two_s: Any
+    two_r: Any
+    part_s: Any
+    part_r: Any
+    qz_s: Any
+    qz_r: Any
+    qx_s: Any
+    qx_r: Any
+    oz_s: Any
+    oz_r: Any
+    ox_s: Any
+    ox_r: Any
+    fz_s: Any
+    fz_r: Any
+    fx_s: Any
+    fx_r: Any
+    local_sem: Any
 
 
 def forward_kernel(sizes, *refs):
-    names = FORWARD_IN + FORWARD_OUT + FORWARD_SCRATCH
-    r = dict(zip(names, refs, strict=True))
+    r = named(ForwardIn, ForwardOut, ForwardScratch, refs)
     bfloat, single = jnp.bfloat16, jnp.float32
     n_data, n_model = sizes
     everyone = n_data * n_model
@@ -618,8 +537,8 @@
     rows = D // n_data
     heads = HEADS // n_model
     head_cols = heads * HDIM
-    length = r["noisy"].shape[0]
-    units = r["ff_shard"].shape[2]
+    length = r.noisy.shape[0]
+    units = r.ff_shard.shape[2]
     half = units // 2
 
     def at_dp(spot):
@@ -647,24 +566,24 @@
 
     lax.fori_loop(1, everyone, greet, 0)
 
-    load_mod = pltpu.make_async_copy(r["mod_weight"], r["mod_low"], r["local_sem"].at[0])
+    load_mod = pltpu.make_async_copy(r.mod_weight, r.mod_low, r.local_sem.at[0])
     load_mod.start()
     own_ff = pltpu.make_async_copy(
-        r["ff_shard"],
-        r["ff"].at[:, pl.ds(pl.multiple_of(d * rows, 16), rows)],
-        r["local_sem"].at[1],
+        r.ff_shard,
+        r.ff.at[:, pl.ds(pl.multiple_of(d * rows, 16), rows)],
+        r.local_sem.at[1],
     )
     own_ff.start()
     pl.semaphore_wait(barrier, everyone - 1)
 
-    send_facts = Sender(r["facts_s"], r["facts_r"])
+    send_facts = Sender(r.facts_s, r.facts_r)
 
     def facts_copy(step):
         peer = lax.rem(me + step, everyone)
         return send_facts(
             step - 1,
-            r["facts"],
-            r["facts_all"].at[me],
+            r.facts,
+            r.facts_all.at[me],
             (lax.div(peer, n_model), lax.rem(peer, n_model)),
         )
 
@@ -676,15 +595,15 @@
         lax.fori_loop(first, last, step_body, 0)
 
     loop(1, everyone, lambda step: facts_copy(step).start())
-    r["facts_all"][me] = r["facts"][...]
+    r.facts_all[me] = r.facts[...]
 
     def qkv_rows(spot, part):
         if part == 0:
-            return r["qkv_weight"].at[pl.ds(pl.multiple_of(spot * rows, 16), 80)]
-        return r["qkv_weight"].at[pl.ds(pl.multiple_of(spot * rows + 80, 16), rows - 80)]
+            return r.qkv_weight.at[pl.ds(pl.multiple_of(spot * rows, 16), 80)]
+        return r.qkv_weight.at[pl.ds(pl.multiple_of(spot * rows + 80, 16), rows - 80)]
 
     def ff_block(spot, part, which):
-        return r["ff"].at[
+        return r.ff.at[
             which,
             pl.ds(pl.multiple_of(spot * rows, 16), rows),
             pl.ds(half * part, half),
@@ -693,8 +612,8 @@
     def origin(step, part):
         return lax.rem(z + (depth - step if part == 0 else step), depth) * NX + x
 
-    qz, qx = Sender(r["qz_s"], r["qz_r"]), Sender(r["qx_s"], r["qx_r"])
-    fz, fx = Sender(r["fz_s"], r["fz_r"]), Sender(r["fx_s"], r["fx_r"])
+    qz, qx = Sender(r.qz_s, r.qz_r), Sender(r.qx_s, r.qx_r)
+    fz, fx = Sender(r.fz_s, r.fz_r), Sender(r.fx_s, r.fx_r)
 
     def qkv_along(step, part):
         block = qkv_rows(origin(step - 1, part), part)
@@ -713,24 +632,24 @@
         return fx((part, step, which), block, block, at_dp(side))
 
     own_rows = pl.ds(pl.multiple_of(d * rows, 16), rows)
-    r["qkv_weight"][own_rows] = r["qkv_shard"][...]
+    r.qkv_weight[own_rows] = r.qkv_shard[...]
     for part in range(2):
         qkv_along(1, part).start()
         qkv_aside(0, part).start()
 
-    send_small = Sender(r["small_s"], r["small_r"])
+    send_small = Sender(r.small_s, r.small_r)
 
     def small_copy(step):
         return send_small(
             step - 1,
-            r["small"],
-            r["small_all"].at[own_rows],
+            r.small,
+            r.small_all.at[own_rows],
             at_dp(lax.rem(d + step, n_data)),
         )
 
     loop(1, n_data, lambda step: small_copy(step).start())
-    r["small_all"][own_rows] = r["small"][...]
-    r["trig_all"][0] = r["trig"][...]
+    r.small_all[own_rows] = r.small[...]
+    r.trig_all[0] = r.trig[...]
 
     def spread(send, buffer):
         return (
@@ -739,12 +658,12 @@
             send(2, buffer.at[2], buffer.at[3], at_mlp(1)),
         )
 
-    trig_near, trig_far, trig_on = spread(Sender(r["trig_s"], r["trig_r"]), r["trig_all"])
+    trig_near, trig_far, trig_on = spread(Sender(r.trig_s, r.trig_r), r.trig_all)
     trig_near.start()
     trig_far.start()
 
-    oz, ox = Sender(r["oz_s"], r["oz_r"]), Sender(r["ox_s"], r["ox_r"])
-    out_place = r["out_weight"].at[pl.ds(pl.multiple_of(x * rows, 16), rows)]
+    oz, ox = Sender(r.oz_s, r.oz_r), Sender(r.ox_s, r.ox_r)
+    out_place = r.out_weight.at[pl.ds(pl.multiple_of(x * rows, 16), rows)]
     owner = z == m
 
     def out_along(step):
@@ -754,37 +673,37 @@
 
     @pl.when(owner)
     def _():
-        r["out_weight"][pl.ds(pl.multiple_of(x * rows, 16), rows)] = r["out_shard"][...]
+        r.out_weight[pl.ds(pl.multiple_of(x * rows, 16), rows)] = r.out_shard[...]
         for step in range(1, depth):
             out_along(step).start()
         out_aside.start()
 
     loop(1, everyone, lambda step: facts_copy(step).wait())
-    facts_all = r["facts_all"][...]
+    facts_all = r.facts_all[...]
     sinus = jnp.concatenate([facts_all[:, 0], facts_all[:, 1]], axis=1).astype(bfloat)
     labels = facts_all[:, 2, 0:1]
     time_pre = (
-        jnp.dot(sinus, r["time_first"][...], preferred_element_type=single) + r["first_bias"][...]
-    )
-    r["time_pre"][...] = time_pre
+        jnp.dot(sinus, r.time_first[...], preferred_element_type=single) + r.first_bias[...]
+    )
+    r.time_pre[...] = time_pre
     time_act = (time_pre * jax.nn.sigmoid(time_pre)).astype(bfloat)
-    send_time = Sender(r["time_s"], r["time_r"])
+    send_time = Sender(r.time_s, r.time_r)
 
     def time_copy(step):
         peer = lax.rem(d + step, n_data)
         return send_time(
-            step - 1, r["time_send"].at[peer], r["time_recv"].at[d], at_dp(peer)
+            step - 1, r.time_send.at[peer], r.time_recv.at[d], at_dp(peer)
         )
 
     for spot in range(n_data):
-        r["time_send"][spot] = jnp.dot(
-            time_act, r["time_blocks"][spot], preferred_element_type=single
+        r.time_send[spot] = jnp.dot(
+            time_act, r.time_blocks[spot], preferred_element_type=single
         )
     loop(1, n_data, lambda step: time_copy(step).start())
-    r["time_recv"][d] = r["time_send"][d]
+    r.time_recv[d] = r.time_send[d]
     for part in range(2):
         for which in range(3):
-            own = r["ff_shard"].at[which, :, pl.ds(half * part, half)]
+            own = r.ff_shard.at[which, :, pl.ds(half * part, half)]
             fz(
                 (part, 0, which),
                 own,
@@ -795,7 +714,7 @@
     onehot = (
         labels == lax.broadcasted_iota(jnp.int32, (everyone, CLASSES + 1), 1).astype(single)
     ).astype(bfloat)
-    picked = jnp.dot(onehot, r["class_table"][...], preferred_element_type=single)
+    picked = jnp.dot(onehot, r.class_table[...], preferred_element_type=single)
     load_mod.wait()
 
     def qkv_service(step):
@@ -806,8 +725,8 @@
             qkv_aside(step, part).start()
 
     loop(1, n_data, lambda step: time_copy(step).wait())
-    condition = jnp.sum(r["time_recv"][...], axis=0) + r["second_bias"][...] + picked
-    r["condition"][...] = condition
+    condition = jnp.sum(r.time_recv[...], axis=0) + r.second_bias[...] + picked
+    r.condition[...] = condition
     cond_act = (condition * jax.nn.sigmoid(condition)).astype(bfloat)
     pick = (
         lax.broadcasted_iota(jnp.int32, (n_data, everyone), 1)
@@ -816,41 +735,41 @@
     cond_rank = jnp.dot(pick, cond_act, preferred_element_type=single).astype(bfloat)
     for kind in range(8):
         block = jnp.dot(
-            cond_rank, r["mod_low"][:, kind * D : (kind + 1) * D], preferred_element_type=single
+            cond_rank, r.mod_low[:, kind * D : (kind + 1) * D], preferred_element_type=single
         )
         for spot in range(n_data):
-            r["mod_send"][spot, kind : kind + 1] = block[spot : spot + 1]
-    send_mods = Sender(r["mods_s"], r["mods_r"])
+            r.mod_send[spot, kind : kind + 1] = block[spot : spot + 1]
+    send_mods = Sender(r.mods_s, r.mods_r)
 
     def mods_copy(step):
         peer = lax.rem(d + step, n_data)
-        return send_mods(step - 1, r["mod_send"].at[peer], r["mod_recv"].at[d], at_dp(peer))
+        return send_mods(step - 1, r.mod_send.at[peer], r.mod_recv.at[d], at_dp(peer))
 
     loop(1, n_data, lambda step: mods_copy(step).start())
-    r["mod_recv"][d] = r["mod_send"][d]
+    r.mod_recv[d] = r.mod_send[d]
     qkv_service(1)
     loop(1, n_data, lambda step: small_copy(step).wait())
     trig_far.wait_recv()
     trig_on.start()
     hidden = (
         lax.dot_general(
-            r["noisy"][...],
-            r["small_all"][:, 0:CH],
+            r.noisy[...],
+            r.small_all[:, 0:CH],
             (((1,), (1,)), ((), ())),
             preferred_element_type=single,
         )
-        + r["patch_bias"][...]
-    )
-    r["hidden"][...] = hidden
+        + r.patch_bias[...]
+    )
+    r.hidden[...] = hidden
     loop(1, n_data, lambda step: mods_copy(step).wait())
-    modulation = jnp.sum(r["mod_recv"][...], axis=0) + r["mod_bias"][...]
-    r["modulation"][...] = modulation
+    modulation = jnp.sum(r.mod_recv[...], axis=0) + r.mod_bias[...]
+    r.modulation[...] = modulation
 
     def kind_of(kind):
-        return r["modulation"][kind : kind + 1]
-
-    r["one_rows"][0] = modulate_rows(r["hidden"][...], kind_of(0), kind_of(1)).astype(bfloat)
-    one_near, one_far, one_on = spread(Sender(r["one_s"], r["one_r"]), r["one_rows"])
+        return r.modulation[kind : kind + 1]
+
+    r.one_rows[0] = modulate_rows(r.hidden[...], kind_of(0), kind_of(1)).astype(bfloat)
+    one_near, one_far, one_on = spread(Sender(r.one_s, r.one_r), r.one_rows)
     one_far.start()
     one_near.start()
     qkv_service(2)
@@ -887,23 +806,23 @@
 
     def image_body(step, carry):
         image = n_model - 1 - step
-        r["qkv"][...] = (
-            jnp.dot(r["one_rows"][image], r["qkv_weight"][...], preferred_element_type=single)
-            + r["qkv_bias"][...]
+        r.qkv[...] = (
+            jnp.dot(r.one_rows[image], r.qkv_weight[...], preferred_element_type=single)
+            + r.qkv_bias[...]
         )
         rank = (
             2 * lax.rem(lax.div(m, 2) + lax.div(image, 2), 2)
             + lax.rem(lax.rem(m, 2) + lax.rem(image, 2), 2)
         )
-        count = r["facts_all"][d * n_model + rank, 2:3, 1:2]
+        count = r.facts_all[d * n_model + rank, 2:3, 1:2]
         mask = lax.broadcasted_iota(jnp.int32, (1, length), 1).astype(single) < count
-        cosine, sine = r["trig_all"][image, 0], r["trig_all"][image, 1]
+        cosine, sine = r.trig_all[image, 0], r.trig_all[image, 1]
         totals = []
         for head in range(heads):
             start = head * HDIM
 
             def part(which):
-                return r["qkv"][:, which * head_cols + start : which * head_cols + start + HDIM]
+                return r.qkv[:, which * head_cols + start : which * head_cols + start + HDIM]
 
             raw_q, raw_k = part(0), part(1)
             query = (raw_q * cosine + swapped(raw_q) * sine).astype(bfloat)
@@ -911,7 +830,7 @@
             value = part(2).astype(bfloat)
             for which, kept in enumerate((query, key, value)):
                 low = which * head_cols + start
-                r["low"][image, :, low : low + HDIM] = kept
+                r.low[image, :, low : low + HDIM] = kept
             scores = lax.dot_general(
                 query, key, (((1,), (1,)), ((), ())), preferred_element_type=single
             ) * (1.0 / math.sqrt(HDIM))
@@ -920,11 +839,11 @@
             exponent = jnp.exp(scores - row_max)
             row_sum = jnp.sum(exponent, axis=-1, keepdims=True)
             probs = exponent / row_sum
-            r["attended"][image, :, start : start + HDIM] = jnp.dot(
+            r.attended[image, :, start : start + HDIM] = jnp.dot(
                 probs.astype(bfloat), value, preferred_element_type=single
             ).astype(bfloat)
             totals.append(row_max + jnp.log(row_sum))
-        r["totals"][image] = jnp.concatenate(totals, axis=1)
+        r.totals[image] = jnp.concatenate(totals, axis=1)
         return carry
 
     lax.fori_loop(0, 2, image_body, 0)
@@ -941,32 +860,32 @@
 
     def partial(image):
         return jnp.dot(
-            r["attended"][image], r["out_weight"][...], preferred_element_type=single
-        )
-
-    send_part = Sender(r["part_s"], r["part_r"])
-    to_core = send_part(0, r["parts_send"].at[0], r["parts_recv"].at[0], at_mlp(1))
-    to_far = send_part(1, r["parts_send"].at[1], r["parts_recv"].at[1], at_mlp(2))
-    to_near = send_part(2, r["parts_send"].at[2], r["parts_recv"].at[2], at_mlp(1))
-    r["parts_send"][0] = partial(3).astype(bfloat)
+            r.attended[image], r.out_weight[...], preferred_element_type=single
+        )
+
+    send_part = Sender(r.part_s, r.part_r)
+    to_core = send_part(0, r.parts_send.at[0], r.parts_recv.at[0], at_mlp(1))
+    to_far = send_part(1, r.parts_send.at[1], r.parts_recv.at[1], at_mlp(2))
+    to_near = send_part(2, r.parts_send.at[2], r.parts_recv.at[2], at_mlp(1))
+    r.parts_send[0] = partial(3).astype(bfloat)
     to_core.start()
     second = partial(2)
     to_core.wait_recv()
-    r["parts_send"][1] = (second + r["parts_recv"][0].astype(single)).astype(bfloat)
+    r.parts_send[1] = (second + r.parts_recv[0].astype(single)).astype(bfloat)
     to_far.start()
-    r["parts_send"][2] = partial(1).astype(bfloat)
+    r.parts_send[2] = partial(1).astype(bfloat)
     to_near.start()
-    own_part = partial(0) + r["out_bias"][...]
+    own_part = partial(0) + r.out_bias[...]
     for which in range(3):
         ff_service(3, which)
     to_near.wait_recv()
     to_far.wait_recv()
-    branch = own_part + r["parts_recv"][2].astype(single) + r["parts_recv"][1].astype(single)
-    r["branch"][...] = branch
-    hidden_mid = r["hidden"][...] + kind_of(2) * branch
-    r["hidden_mid"][...] = hidden_mid
-    r["two_rows"][0] = modulate_rows(hidden_mid, kind_of(3), kind_of(4)).astype(bfloat)
-    two_near, two_far, two_on = spread(Sender(r["two_s"], r["two_r"]), r["two_rows"])
+    branch = own_part + r.parts_recv[2].astype(single) + r.parts_recv[1].astype(single)
+    r.branch[...] = branch
+    hidden_mid = r.hidden[...] + kind_of(2) * branch
+    r.hidden_mid[...] = hidden_mid
+    r.two_rows[0] = modulate_rows(hidden_mid, kind_of(3), kind_of(4)).astype(bfloat)
+    two_near, two_far, two_on = spread(Sender(r.two_s, r.two_r), r.two_rows)
     two_far.start()
     two_near.start()
     two_far.wait_recv()
@@ -995,8 +914,8 @@
     rows = D // n_data
     heads = HEADS // n_model
     head_cols = heads * HDIM
-    length = values["noisy"].shape[0]
-    units = values["ff_shard"].shape[2]
+    length = values.noisy.shape[0]
+    units = values.ff_shard.shape[2]
     depth = n_data // NX
     shapes = dict(
         facts_all=((everyone, 8, 128), single),
@@ -1055,33 +974,124 @@
 
     outs = pl.pallas_call(
         functools.partial(forward_kernel, sizes),
-        out_shape=[jax.ShapeDtypeStruct(*shapes[name]) for name in FORWARD_OUT],
-        in_specs=[space(name) for name in FORWARD_IN],
-        out_specs=[space(name) for name in FORWARD_OUT],
-        scratch_shapes=[scratch[name] for name in FORWARD_SCRATCH],
+        out_shape=[jax.ShapeDtypeStruct(*shapes[name]) for name in ForwardOut._fields],
+        in_specs=[space(name) for name in ForwardIn._fields],
+        out_specs=[space(name) for name in ForwardOut._fields],
+        scratch_shapes=[scratch[name] for name in ForwardScratch._fields],
         compiler_params=pltpu.CompilerParams(
             collective_id=collective, has_side_effects=True, vmem_limit_bytes=56 * 2**20
         ),
-    )(*[values[name] for name in FORWARD_IN])
-    return dict(zip(FORWARD_OUT, outs))
-
-
-BACK_IN = (
-    "ff", "two_rows", "hidden_mid", "hidden", "branch", "modulation", "small_all", "final_bias",
-    "clean", "noise", "consts", "valid", "noisy", "low", "totals", "trig_all", "facts_all",
-    "attended", "one_rows", "qkv_weight", "out_weight",
-)
-BACK_OUT = (
-    "grad_ff", "grad_qkv", "grad_out", "d_modulation", "hidden_sum", "branch_sum", "qkv_sum",
-    "output_sum", "loss", "grad_patch", "grad_final",
-)
-BACK_SCRATCH = (
-    "mixed", "d_end", "dm_rows", "db_rows", "hold_far", "hold_near", "parts_send", "parts_recv",
-    "normed_end", "g_ff", "x_ff", "z_ff", "g_qkv", "x_qkv", "z_qkv", "g_out", "x_out",
-    "z_out", "out_mine", "dm_s", "dm_r", "db_s", "db_r", "pa_s", "pa_r",
-    "pb_s", "pb_r", "pc_s", "pc_r", "fx_s", "fx_r", "fz_s", "fz_r", "qx_s", "qx_r", "qz_s",
-    "qz_r", "ox_s", "ox_r", "oz_s", "oz_r", "qa_s", "qa_r", "oa_s", "oa_r", "local_sem",
-)
+    )(*values)
+    return ForwardOut(*outs)
+
+
+class BackIn(NamedTuple):
+    ff: Any
+    two_rows: Any
+    hidden_mid: Any
+    hidden: Any
+    branch: Any
+    modulation: Any
+    small_all: Any
+    final_bias: Any
+    clean: Any
+    noise: Any
+    consts: Any
+    valid: Any
+    noisy: Any
+    low: Any
+    totals: Any
+    trig_all: Any
+    facts_all: Any
+    attended: Any
+    one_rows: Any
+    qkv_weight: Any
+    out_weight: Any
+    mod_weight: Any
+    time_second: Any
+    time_pre: Any
+    condition: Any
+
+
+class BackOut(NamedTuple):
+    late: Any
+    dmod: Any
+    dtime: Any
+    d_condition: Any
+    d_time_pre: Any
+    grad_ff: Any
+    grad_qkv: Any
+    grad_out: Any
+
+
+class BackScratch(NamedTuple):
+    d_modulation: Any
+    local: Any
+    sums: Any
+    sums_recv: Any
+    pay: Any
+    dmod_row: Any
+    dmod_all: Any
+    dmod_wide: Any
+    dtime_mine: Any
+    dtime_recv: Any
+    dtime_wide: Any
+    loss: Any
+    sm_s: Any
+    sm_r: Any
+    dl_s: Any
+    dl_r: Any
+    dt_s: Any
+    dt_r: Any
+    lt_s: Any
+    lt_r: Any
+    d_end: Any
+    dm_rows: Any
+    db_rows: Any
+    hold_far: Any
+    hold_near: Any
+    parts_send: Any
+    parts_recv: Any
+    normed_end: Any
+    g_ff: Any
+    x_ff: Any
+    z_ff: Any
+    g_qkv: Any
+    x_qkv: Any
+    z_qkv: Any
+    g_out: Any
+    x_out: Any
+    z_out: Any
+    out_mine: Any
+    dm_s: Any
+    dm_r: Any
+    db_s: Any
+    db_r: Any
+    pa_s: Any
+    pa_r: Any
+    pb_s: Any
+    pb_r: Any
+    pc_s: Any
+    pc_r: Any
+    fx_s: Any
+    fx_r: Any
+    fz_s: Any
+    fz_r: Any
+    qx_s: Any
+    qx_r: Any
+    qz_s: Any
+    qz_r: Any
+    ox_s: Any
+    ox_r: Any
+    oz_s: Any
+    oz_r: Any
+    qa_s: Any
+    qa_r: Any
+    oa_s: Any
+    oa_r: Any
+    local_sem: Any
+
+
 ROW_CHUNK = 16
 
 
@@ -1108,8 +1118,7 @@
 
 
 def back_kernel(sizes, total_images, *refs):
-    names = BACK_IN + BACK_OUT + BACK_SCRATCH
-    r = dict(zip(names, refs, strict=True))
+    r = named(BackIn, BackOut, BackScratch, refs)
     bfloat, single = jnp.bfloat16, jnp.float32
     n_data, n_model = sizes
     d, m, z, x = device_parts()
@@ -1117,8 +1126,8 @@
     rows = D // n_data
     heads = HEADS // n_model
     head_cols = heads * HDIM
-    length = r["clean"].shape[0]
-    units = r["ff"].shape[2]
+    length = r.clean.shape[0]
+    units = r.ff.shape[2]
     half = units // 2
 
     def at_dp(spot):
@@ -1134,11 +1143,28 @@
     down = lax.rem(z + depth - 1, depth) * NX + x
     side = z * NX + 1 - x
     barrier = pltpu.get_barrier_semaphore()
-    peers = [at_dp(lax.rem(z + step, depth) * NX + x) for step in range(1, depth)]
-    peers += [at_dp(side), at_mlp(1), at_mlp(2), (d, lax.rem(near_rank + 2, 4))]
-    for peer in peers:
-        pl.semaphore_signal(barrier, inc=1, device_id=peer, device_id_type=MESH_IDS)
-    pl.semaphore_wait(barrier, len(peers))
+    everyone = n_data * n_model
+    me = d * n_model + m
+
+    def loop(first, last, body):
+        def step_body(step, carry):
+            body(step)
+            return carry
+
+        lax.fori_loop(first, last, step_body, 0)
+
+    def anyone(step):
+        peer = lax.rem(me + step, everyone)
+        return peer, (lax.div(peer, n_model), lax.rem(peer, n_model))
+
+    loop(
+        1,
+        everyone,
+        lambda step: pl.semaphore_signal(
+            barrier, inc=1, device_id=anyone(step)[1], device_id_type=MESH_IDS
+        ),
+    )
+    pl.semaphore_wait(barrier, everyone - 1)
 
     def chunks(body, carry, amount=ROW_CHUNK, count=length):
         def step_body(step, held):
@@ -1147,7 +1173,7 @@
         return lax.fori_loop(0, count // amount, step_body, carry)
 
     def kind_of(kind):
-        return r["modulation"][kind : kind + 1]
+        return r.modulation[kind : kind + 1]
 
     def dot(left, right, dims):
         return lax.dot_general(left, right, (dims, ((), ())), preferred_element_type=single)
@@ -1161,10 +1187,10 @@
             send(2, buffer.at[2], buffer.at[3], at_mlp(1)),
         )
 
-    def part_copies(tag):
-        send = Sender(r[tag + "_s"], r[tag + "_r"])
+    def part_copies(*sems):
+        send = Sender(*sems)
         return tuple(
-            send(spot, r["parts_send"].at[spot], r["parts_recv"].at[spot], at_mlp(bit))
+            send(spot, r.parts_send.at[spot], r.parts_recv.at[spot], at_mlp(bit))
             for spot, bit in ((0, 1), (1, 2), (2, 1))
         )
 
@@ -1173,16 +1199,16 @@
         to_core.wait_recv()
 
         def body(at, held):
-            r["parts_send"][1, at] = (
-                r["hold_far"][at] + r["parts_recv"][0, at].astype(single)
+            r.parts_send[1, at] = (
+                r.hold_far[at] + r.parts_recv[0, at].astype(single)
             ).astype(bfloat)
             return held
 
         chunks(body, 0)
         to_far.start()
 
-    fx, fz = Sender(r["fx_s"], r["fx_r"]), Sender(r["fz_s"], r["fz_r"])
-    qx, qz = Sender(r["qx_s"], r["qx_r"]), Sender(r["qz_s"], r["qz_r"])
+    fx, fz = Sender(r.fx_s, r.fx_r), Sender(r.fz_s, r.fz_r)
+    qx, qz = Sender(r.qx_s, r.qx_r), Sender(r.qz_s, r.qz_r)
 
     def block_rows(z_spot, x_spot):
         return pl.ds(pl.multiple_of((z_spot * NX + x_spot) * rows, 16), rows)
@@ -1191,8 +1217,8 @@
         z_spot = lax.rem(z + step, depth)
         return fx(
             (which, step),
-            r["g_ff"].at[which, block_rows(z_spot, 1 - x)],
-            r["x_ff"].at[which, z_spot],
+            r.g_ff.at[which, block_rows(z_spot, 1 - x)],
+            r.x_ff.at[which, z_spot],
             at_dp(side),
         )
 
@@ -1203,8 +1229,8 @@
         lanes = pl.ds(half * part, half)
         return fz(
             (which, step, part),
-            r["g_ff"].at[which, block_rows(target_of(step, part), x), lanes],
-            r["z_ff"].at[which, step, part],
+            r.g_ff.at[which, block_rows(target_of(step, part), x), lanes],
+            r.z_ff.at[which, step, part],
             at_dp(up if part == 0 else down),
         )
 
@@ -1218,8 +1244,8 @@
 
         def body(step, held):
             at = block_rows(step, x)
-            r["g_ff"][which, at] = (
-                r["g_ff"][which, at].astype(single) + r["x_ff"][which, step].astype(single)
+            r.g_ff[which, at] = (
+                r.g_ff[which, at].astype(single) + r.x_ff[which, step].astype(single)
             ).astype(bfloat)
             return held
 
@@ -1232,14 +1258,14 @@
             ff_along(which, step, part).wait_recv()
             lanes = pl.ds(half * part, half)
             at = block_rows(target_of(step + 1, part), x)
-            running = r["z_ff"][which, step, part].astype(single) + r["g_ff"][
+            running = r.z_ff[which, step, part].astype(single) + r.g_ff[
                 which, at, lanes
             ].astype(single)
             if step < depth - 2:
-                r["g_ff"][which, at, lanes] = running.astype(bfloat)
+                r.g_ff[which, at, lanes] = running.astype(bfloat)
                 ff_along(which, step + 1, part).start()
             else:
-                r["grad_ff"][which, :, lanes] = running
+                r.grad_ff[which, :, lanes] = running
 
     tops = (pl.ds(0, 80), pl.ds(80, rows - 80))
 
@@ -1251,16 +1277,16 @@
         z_spot = lax.rem(z + step, depth)
         return qx(
             step,
-            r["g_qkv"].at[block_rows(z_spot, 1 - x)],
-            r["x_qkv"].at[z_spot],
+            r.g_qkv.at[block_rows(z_spot, 1 - x)],
+            r.x_qkv.at[z_spot],
             at_dp(side),
         )
 
     def qkv_along(step, part):
         return qz(
             (step, part),
-            r["g_qkv"].at[part_rows(target_of(step, part), part)],
-            r["z_qkv"].at[step, tops[part]],
+            r.g_qkv.at[part_rows(target_of(step, part), part)],
+            r.z_qkv.at[step, tops[part]],
             at_dp(up if part == 0 else down),
         )
 
@@ -1270,8 +1296,8 @@
 
         def body(step, held):
             at = block_rows(step, x)
-            r["g_qkv"][at] = (
-                r["g_qkv"][at].astype(single) + r["x_qkv"][step].astype(single)
+            r.g_qkv[at] = (
+                r.g_qkv[at].astype(single) + r.x_qkv[step].astype(single)
             ).astype(bfloat)
             return held
 
@@ -1284,20 +1310,22 @@
             qkv_along(step, part).wait_recv()
             at = part_rows(target_of(step + 1, part), part)
             running = (
-                r["z_qkv"][step, tops[part]].astype(single) + r["g_qkv"][at].astype(single)
+                r.z_qkv[step, tops[part]].astype(single) + r.g_qkv[at].astype(single)
             ).astype(bfloat)
             if step < depth - 2:
-                r["g_qkv"][at] = running
+                r.g_qkv[at] = running
                 qkv_along(step + 1, part).start()
             else:
-                r["grad_qkv"][0, tops[part]] = running
-
-    dm_near, dm_far, dm_on = spread(Sender(r["dm_s"], r["dm_r"]), r["dm_rows"])
-    first_parts, second_parts, third_parts = (part_copies(tag) for tag in ("pa", "pb", "pc"))
+                r.grad_qkv[0, tops[part]] = running
+
+    dm_near, dm_far, dm_on = spread(Sender(r.dm_s, r.dm_r), r.dm_rows)
+    first_parts = part_copies(r.pa_s, r.pa_r)
+    second_parts = part_copies(r.pb_s, r.pb_r)
+    third_parts = part_copies(r.pc_s, r.pc_r)
 
     def swiglu(ff, two_rows, gates, ups, acts, d_gates, d_ups):
-        load_ff = pltpu.make_async_copy(r["ff"], ff, r["local_sem"].at[0])
-        load_two = pltpu.make_async_copy(r["two_rows"], two_rows, r["local_sem"].at[1])
+        load_ff = pltpu.make_async_copy(r.ff, ff, r.local_sem.at[0])
+        load_two = pltpu.make_async_copy(r.two_rows, two_rows, r.local_sem.at[1])
         load_ff.start()
         load_two.start()
         load_two.wait()
@@ -1325,37 +1353,37 @@
             return dot(acts[image * length : (image + 1) * length], ff[2], ((1,), (1,)))
 
         inner(1)
-        r["parts_send"][0] = outer(3).astype(bfloat)
+        r.parts_send[0] = outer(3).astype(bfloat)
         first_parts[0].start()
-        r["hold_far"][...] = outer(2)
+        r.hold_far[...] = outer(2)
         inner(0)
         add_far(first_parts)
-        r["parts_send"][2] = outer(1).astype(bfloat)
+        r.parts_send[2] = outer(1).astype(bfloat)
         first_parts[2].start()
-        r["hold_near"][...] = outer(0)
+        r.hold_near[...] = outer(0)
         first_parts[2].wait_recv()
         first_parts[1].wait_recv()
 
         def ending(at, held):
             mixed = (
-                r["hold_near"][at]
-                + r["parts_recv"][2, at].astype(single)
-                + r["parts_recv"][1, at].astype(single)
+                r.hold_near[at]
+                + r.parts_recv[2, at].astype(single)
+                + r.parts_recv[1, at].astype(single)
             )
-            r["mixed"][at] = mixed
-            end = r["hidden_mid"][at] + kind_of(5) * mixed
-            r["normed_end"][at] = modulate_rows(end, kind_of(6), kind_of(7)).astype(bfloat)
+            r.d_end[at] = mixed
+            end = r.hidden_mid[at] + kind_of(5) * mixed
+            r.normed_end[at] = modulate_rows(end, kind_of(6), kind_of(7)).astype(bfloat)
             return held
 
         chunks(ending, 0)
 
-        eps_weight, var_weight = r["small_all"][:, 32:48], r["small_all"][:, 48:64]
-        normed_end = r["normed_end"][...]
-        eps = dot(normed_end, eps_weight, ((1,), (0,))) + r["final_bias"][0:1]
-        var = dot(normed_end, var_weight, ((1,), (0,))) + r["final_bias"][1:2]
-        clean, noise, valid = r["clean"][...], r["noise"][...], r["valid"][...]
+        eps_weight, var_weight = r.small_all[:, 32:48], r.small_all[:, 48:64]
+        normed_end = r.normed_end[...]
+        eps = dot(normed_end, eps_weight, ((1,), (0,))) + r.final_bias[0:1]
+        var = dot(normed_end, var_weight, ((1,), (0,))) + r.final_bias[1:2]
+        clean, noise, valid = r.clean[...], r.noise[...], r.valid[...]
         root_bar, root_rest, log_beta, post_log, coefficient = (
-            r["consts"][0:1, spot : spot + 1] for spot in range(5)
+            r.consts[0:1, spot : spot + 1] for spot in range(5)
         )
         noisy = root_bar * clean + root_rest * noise
         fraction = (var + 1.0) * 0.5
@@ -1369,7 +1397,7 @@
             -1.0 + model_log - post_log + ratio + gap_part
         )
         terms = jnp.where(valid > 0.0, terms, 0.0)
-        r["loss"][...] = jnp.sum(jnp.sum(terms, axis=1, keepdims=True), axis=0, keepdims=True)
+        r.loss[...] = jnp.sum(jnp.sum(terms, axis=1, keepdims=True), axis=0, keepdims=True)
         d_eps = 2.0 * (eps - noise) + 2.0 * scale_by * gap * jnp.exp(-model_log) * (
             coefficient * root_rest / root_bar
         )
@@ -1377,21 +1405,22 @@
         share = 1.0 / total_images
         d_eps = jnp.where(valid > 0.0, d_eps * share, 0.0).astype(bfloat)
         d_var = jnp.where(valid > 0.0, d_var * share, 0.0).astype(bfloat)
-        r["output_sum"][0:1] = jnp.sum(d_eps.astype(single), axis=0, keepdims=True)
-        r["output_sum"][1:2] = jnp.sum(d_var.astype(single), axis=0, keepdims=True)
-        r["grad_final"][0] = dot(d_eps, normed_end, ((0,), (0,)))
-        r["grad_final"][1] = dot(d_var, normed_end, ((0,), (0,)))
-        r["hold_far"][...] = dot(d_eps, eps_weight, ((1,), (1,))) + dot(
+        r.local[48:56] = zeros
+        r.local[54:55, 0:CH] = jnp.sum(d_eps.astype(single), axis=0, keepdims=True)
+        r.local[54:55, CH : 2 * CH] = jnp.sum(d_var.astype(single), axis=0, keepdims=True)
+        r.local[CH : 2 * CH] = dot(d_eps, normed_end, ((0,), (0,)))
+        r.local[2 * CH : 3 * CH] = dot(d_var, normed_end, ((0,), (0,)))
+        r.hold_far[...] = dot(d_eps, eps_weight, ((1,), (1,))) + dot(
             d_var, var_weight, ((1,), (1,))
         )
 
         def end_back(at, held):
             shift_sum, scale_sum, gate_sum = held
-            mixed, grad = r["mixed"][at], r["hold_far"][at]
-            end = r["hidden_mid"][at] + kind_of(5) * mixed
+            mixed, grad = r.d_end[at], r.hold_far[at]
+            end = r.hidden_mid[at] + kind_of(5) * mixed
             back, normal = modulate_back(end, grad, kind_of(7))
-            r["d_end"][at] = back
-            r["dm_rows"][0, at] = (kind_of(5) * back).astype(bfloat)
+            r.d_end[at] = back
+            r.dm_rows[0, at] = (kind_of(5) * back).astype(bfloat)
             return (
                 shift_sum + fold(grad),
                 scale_sum + fold(grad * normal),
@@ -1402,11 +1431,11 @@
         dm_far.start()
         dm_near.start()
         for kind, value in ((6, shift_sum), (7, scale_sum), (5, gate_sum)):
-            r["d_modulation"][kind : kind + 1] = jnp.sum(value, axis=0, keepdims=True)
+            r.d_modulation[kind : kind + 1] = jnp.sum(value, axis=0, keepdims=True)
 
         def inner_back(which):
             spot = pl.ds(which * wide, wide)
-            gradient = dot(rows_of(r["dm_rows"], which), ff[2], ((1,), (0,)))
+            gradient = dot(rows_of(r.dm_rows, which), ff[2], ((1,), (0,)))
             gate, up_val = gates[spot], ups[spot]
             sigma = jax.nn.sigmoid(gate)
             d_ups[spot] = (gradient * gate * sigma).astype(bfloat)
@@ -1417,6 +1446,11 @@
         def outer_back(image):
             spot = pl.ds(image * length, length)
             return dot(d_gates[spot], ff[0], ((1,), (1,))) + dot(d_ups[spot], ff[1], ((1,), (1,)))
+
+        def ff_grad(which, left, right):
+            for part in range(2):
+                lanes = slice(half * part, half * part + half)
+                r.g_ff[which, :, lanes] = dot(left, right[:, lanes], ((0,), (0,))).astype(bfloat)
 
         dm_near.wait_recv()
         inner_back(0)
@@ -1426,21 +1460,19 @@
         inner_back(1)
         for copy in first_parts:
             copy.wait_send()
-        r["parts_send"][0] = outer_back(3).astype(bfloat)
+        r.parts_send[0] = outer_back(3).astype(bfloat)
         second_parts[0].start()
-        r["hold_far"][...] = outer_back(2)
-        r["g_ff"][2] = dot(
-            r["dm_rows"][...].reshape(2 * wide, D), acts[...], ((0,), (0,))
-        ).astype(bfloat)
+        r.hold_far[...] = outer_back(2)
+        ff_grad(2, r.dm_rows[...].reshape(2 * wide, D), acts)
         ff_start(2)
         add_far(second_parts)
-        r["parts_send"][2] = outer_back(1).astype(bfloat)
+        r.parts_send[2] = outer_back(1).astype(bfloat)
         second_parts[2].start()
-        r["hold_near"][...] = outer_back(0)
+        r.hold_near[...] = outer_back(0)
         flat = two_rows[...].reshape(2 * wide, D)
-        r["g_ff"][0] = dot(flat, d_gates[...], ((0,), (0,))).astype(bfloat)
+        ff_grad(0, flat, d_gates)
         ff_start(0)
-        r["g_ff"][1] = dot(flat, d_ups[...], ((0,), (0,))).astype(bfloat)
+        ff_grad(1, flat, d_ups)
         ff_start(1)
 
     pl.run_scoped(
@@ -1454,31 +1486,31 @@
         pltpu.VMEM((n_model * length, units), bfloat),
     )
 
-    db_near, db_far, db_on = spread(Sender(r["db_s"], r["db_r"]), r["db_rows"])
-    ox, oz = Sender(r["ox_s"], r["ox_r"]), Sender(r["oz_s"], r["oz_r"])
-    out_aside = ox(0, r["g_out"].at[1 - x], r["x_out"], at_dp(side))
+    db_near, db_far, db_on = spread(Sender(r.db_s, r.db_r), r.db_rows)
+    ox, oz = Sender(r.ox_s, r.ox_r), Sender(r.oz_s, r.oz_r)
+    out_aside = ox(0, r.g_out.at[1 - x], r.x_out, at_dp(side))
     owner = z == m
     behind = lax.rem(z + depth - m, depth)
     out_along = oz(
         lax.rem(behind + depth - 1, depth),
-        r["g_out"].at[x],
-        r["z_out"].at[lax.rem(behind + depth - 1, depth)],
+        r.g_out.at[x],
+        r.z_out.at[lax.rem(behind + depth - 1, depth)],
         at_dp(m * NX + x),
     )
 
     def attend(low, attended, trig, one_rows, qkv_weight, out_weight, d_attended, d_qkv):
         loads = []
-        for spot, (name, place) in enumerate(
+        for spot, (source, target) in enumerate(
             (
-                ("out_weight", out_weight),
-                ("low", low),
-                ("trig_all", trig),
-                ("attended", attended),
-                ("one_rows", one_rows),
-                ("qkv_weight", qkv_weight),
+                (r.out_weight, out_weight),
+                (r.low, low),
+                (r.trig_all, trig),
+                (r.attended, attended),
+                (r.one_rows, one_rows),
+                (r.qkv_weight, qkv_weight),
             )
         ):
-            load = pltpu.make_async_copy(r[name], place, r["local_sem"].at[2 + spot])
+            load = pltpu.make_async_copy(source, target, r.local_sem.at[2 + spot])
             load.start()
             loads.append(load)
         second_parts[2].wait_recv()
@@ -1487,19 +1519,19 @@
         def mid_back(at, held):
             shift_sum, scale_sum, gate_sum, branch_sum = held
             grad = (
-                r["hold_near"][at]
-                + r["parts_recv"][2, at].astype(single)
-                + r["parts_recv"][1, at].astype(single)
+                r.hold_near[at]
+                + r.parts_recv[2, at].astype(single)
+                + r.parts_recv[1, at].astype(single)
             )
-            back, normal = modulate_back(r["hidden_mid"][at], grad, kind_of(4))
-            total = r["d_end"][at] + back
-            r["d_end"][at] = total
+            back, normal = modulate_back(r.hidden_mid[at], grad, kind_of(4))
+            total = r.d_end[at] + back
+            r.d_end[at] = total
             d_branch = (kind_of(2) * total).astype(bfloat)
-            r["db_rows"][0, at] = d_branch
+            r.db_rows[0, at] = d_branch
             return (
                 shift_sum + fold(grad),
                 scale_sum + fold(grad * normal),
-                gate_sum + fold(r["branch"][at] * total),
+                gate_sum + fold(r.branch[at] * total),
                 branch_sum + fold(d_branch.astype(single)),
             )
 
@@ -1507,20 +1539,20 @@
         db_far.start()
         db_near.start()
         for kind, value in zip((3, 4, 2), sums):
-            r["d_modulation"][kind : kind + 1] = jnp.sum(value, axis=0, keepdims=True)
-        r["branch_sum"][...] = jnp.sum(sums[3], axis=0, keepdims=True)
+            r.d_modulation[kind : kind + 1] = jnp.sum(value, axis=0, keepdims=True)
+        r.local[49:50] = jnp.sum(sums[3], axis=0, keepdims=True)
         for load in loads:
             load.wait()
 
         def image_body(image, carry):
             d_attended[...] = dot(
-                r["db_rows"][image], out_weight[...], ((1,), (1,))
+                r.db_rows[image], out_weight[...], ((1,), (1,))
             ).astype(bfloat)
             rank = (
                 2 * lax.rem(lax.div(m, 2) + lax.div(image, 2), 2)
                 + lax.rem(lax.rem(m, 2) + lax.rem(image, 2), 2)
             )
-            count = r["facts_all"][d * n_model + rank, 2:3, 1:2]
+            count = r.facts_all[d * n_model + rank, 2:3, 1:2]
             mask = lax.broadcasted_iota(jnp.int32, (1, length), 1).astype(single) < count
             cosine, sine = trig[image, 0], trig[image, 1]
             scale_by = 1.0 / math.sqrt(HDIM)
@@ -1535,7 +1567,7 @@
                 grad = d_attended[:, start : start + HDIM]
                 scores = dot(query, key, ((1,), (1,))) * scale_by
                 scores = jnp.where(mask, scores, -1e30)
-                probs = jnp.exp(scores - r["totals"][image, :, head : head + 1])
+                probs = jnp.exp(scores - r.totals[image, :, head : head + 1])
                 d_probs = dot(grad, value, ((1,), (1,)))
                 row = jnp.sum(probs * d_probs, axis=-1, keepdims=True)
                 d_scores = (probs * (d_probs - row)).astype(bfloat)
@@ -1561,25 +1593,25 @@
 
         for copy in second_parts:
             copy.wait_send()
-        r["parts_send"][0] = one_part(3).astype(bfloat)
+        r.parts_send[0] = one_part(3).astype(bfloat)
         third_parts[0].start()
-        r["hold_far"][...] = one_part(2)
+        r.hold_far[...] = one_part(2)
         ff_beside(0)
         ff_service(2, 0)
         add_far(third_parts)
-        r["parts_send"][2] = one_part(1).astype(bfloat)
+        r.parts_send[2] = one_part(1).astype(bfloat)
         third_parts[2].start()
-        r["hold_near"][...] = one_part(0)
+        r.hold_near[...] = one_part(0)
         flat_grad = d_qkv[...].reshape(n_model * length, 3 * head_cols)
-        r["g_qkv"][...] = dot(
+        r.g_qkv[...] = dot(
             one_rows[...].reshape(n_model * length, D), flat_grad, ((0,), (0,))
         ).astype(bfloat)
         for step in range(depth):
             qkv_aside(step).start()
-        r["g_out"][...] = (
+        r.g_out[...] = (
             dot(
                 attended[...].reshape(n_model * length, head_cols),
-                r["db_rows"][...].reshape(n_model * length, D),
+                r.db_rows[...].reshape(n_model * length, D),
                 ((0,), (0,)),
             )
             .astype(bfloat)
@@ -1587,7 +1619,9 @@
         )
         out_aside.start()
         ones = jnp.ones((8, n_model * length), bfloat)
-        r["qkv_sum"][...] = dot(ones, flat_grad, ((1,), (0,)))[0:1]
+        qkv_sum = dot(ones, flat_grad, ((1,), (0,)))[0:1]
+        for rank in range(n_model):
+            r.local[50 + rank : 51 + rank, 0 : 3 * head_cols] = jnp.where(m == rank, qkv_sum, 0.0)
 
     pl.run_scoped(
         attend,
@@ -1609,13 +1643,13 @@
     def first_back(at, held):
         shift_sum, scale_sum, hidden_sum = held
         grad = (
-            r["hold_near"][at]
-            + r["parts_recv"][2, at].astype(single)
-            + r["parts_recv"][1, at].astype(single)
-        )
-        back, normal = modulate_back(r["hidden"][at], grad, kind_of(1))
-        d_hidden = (r["d_end"][at] + back).astype(bfloat)
-        r["normed_end"][at] = d_hidden
+            r.hold_near[at]
+            + r.parts_recv[2, at].astype(single)
+            + r.parts_recv[1, at].astype(single)
+        )
+        back, normal = modulate_back(r.hidden[at], grad, kind_of(1))
+        d_hidden = (r.d_end[at] + back).astype(bfloat)
+        r.normed_end[at] = d_hidden
         return (
             shift_sum + fold(grad),
             scale_sum + fold(grad * normal),
@@ -1624,19 +1658,157 @@
 
     sums = chunks(first_back, (zeros, zeros, zeros))
     for kind in range(2):
-        r["d_modulation"][kind : kind + 1] = jnp.sum(sums[kind], axis=0, keepdims=True)
-    r["hidden_sum"][...] = jnp.sum(sums[2], axis=0, keepdims=True)
-    r["grad_patch"][...] = dot(r["noisy"][...], r["normed_end"][...], ((0,), (0,)))
-
+        r.d_modulation[kind : kind + 1] = jnp.sum(sums[kind], axis=0, keepdims=True)
+    r.local[48:49] = jnp.sum(sums[2], axis=0, keepdims=True)
+    r.local[0:CH] = dot(r.noisy[...], r.normed_end[...], ((0,), (0,)))
+
+    for kind in range(8):
+        r.dmod_wide[2 * kind : 2 * kind + 1] = r.d_modulation[kind : kind + 1, 0 : D // 2]
+        r.dmod_wide[2 * kind + 1 : 2 * kind + 2] = r.d_modulation[kind : kind + 1, D // 2 : D]
+    r.dmod_row[...] = r.dmod_wide[...].astype(bfloat)
+    r.dmod_all[me] = r.dmod_row[...]
+    send_dmod = Sender(r.dl_s, r.dl_r)
+    loop(
+        1,
+        everyone,
+        lambda step: send_dmod(
+            step - 1, r.dmod_row, r.dmod_all.at[me], anyone(step)[1]
+        ).start(),
+    )
+    tiles = D // 128
+    for top in range(7):
+        for left in range(tiles):
+            r.sums[top * tiles + left] = r.local[8 * top : 8 * top + 8, 128 * left : 128 * left + 128]
+    r.sums[7 * tiles] = jnp.zeros((8, 128), single)
+    send_sums = Sender(r.sm_s, r.sm_r)
+
+    def sums_copy(step):
+        peer, device = anyone(step)
+        return send_sums(step - 1, r.sums.at[pl.ds(2 * peer, 2)], r.sums_recv.at[me], device)
+
+    loop(1, everyone, lambda step: sums_copy(step).start())
+    r.sums_recv[me] = r.sums[pl.ds(2 * me, 2)]
     ff_service(1, 0)
     ff_service(0, 1)
     ff_service(2, 2)
+
+    time_pre, condition = r.time_pre[...], r.condition[...]
+    sigma_time, sigma_cond = jax.nn.sigmoid(time_pre), jax.nn.sigmoid(condition)
+    time_act = (time_pre * sigma_time).astype(bfloat)
+    cond_act = (condition * sigma_cond).astype(bfloat)
+
+    def gram(value, precision=None):
+        return lax.dot_general(
+            value,
+            value,
+            (((1,), (1,)), ((), ())),
+            precision=precision,
+            preferred_element_type=single,
+        )
+
+    send_dtime = Sender(r.dt_s, r.dt_r)
+
+    def dtime_copy(step):
+        return send_dtime(
+            step - 1, r.dtime_mine, r.dtime_recv.at[d], at_dp(lax.rem(d + step, n_data))
+        )
+
+    def conditioning(mod_weight):
+        load = pltpu.make_async_copy(r.mod_weight, mod_weight, r.local_sem.at[0])
+        load.start()
+        loop(
+            1,
+            everyone,
+            lambda step: send_dmod(
+                step - 1, r.dmod_row, r.dmod_all.at[me], anyone(step)[1]
+            ).wait(),
+        )
+        gathered = r.dmod_all[...].astype(single)
+        load.wait()
+        d_cond = jnp.zeros((everyone, rows), single)
+        mod_gram = jnp.zeros((everyone, everyone), single)
+        bias_squares = jnp.zeros((1, 1), single)
+        for kind in range(8):
+            r.dtime_wide[:, 0 : D // 2] = gathered[:, 2 * kind]
+            r.dtime_wide[:, D // 2 : D] = gathered[:, 2 * kind + 1]
+            part = r.dtime_wide[...]
+            column = jnp.sum(part, axis=0, keepdims=True)
+            bias_squares = bias_squares + jnp.sum(column * column, axis=1, keepdims=True)
+            part = part.astype(bfloat)
+            r.dmod[kind] = part
+            d_cond = d_cond + dot(
+                part, mod_weight[:, kind * D : (kind + 1) * D], ((1,), (1,))
+            )
+            mod_gram = mod_gram + gram(part)
+        d_condition = d_cond * (sigma_cond * (1.0 + condition * (1.0 - sigma_cond)))
+        r.d_condition[...] = d_condition
+        r.dtime_mine[...] = d_condition.astype(bfloat)
+        loop(1, n_data, lambda step: dtime_copy(step).start())
+        r.dtime_recv[d] = r.dtime_mine[...]
+        r.pay[2] = jnp.zeros((8, 128), single)
+        r.pay[2, 0:1, 0:1] = (
+            jnp.sum(jnp.sum(mod_gram * gram(cond_act), axis=1, keepdims=True), axis=0, keepdims=True)
+            / n_model
+            + bias_squares / everyone
+        )
+
+    pl.run_scoped(conditioning, pltpu.VMEM((rows, 8 * D), bfloat))
     ff_service(1, 1)
     ff_service(0, 2)
+    loop(1, n_data, lambda step: dtime_copy(step).wait())
+    for spot in range(n_data):
+        r.dtime_wide[:, spot * rows : (spot + 1) * rows] = r.dtime_recv[spot].astype(single)
+    dtime = r.dtime_wide[...]
+    column = jnp.sum(dtime, axis=0, keepdims=True)
+    dtime = dtime.astype(bfloat)
+    r.dtime[...] = dtime
+    d_time_pre = dot(dtime, r.time_second[...], ((1,), (1,))) * (
+        sigma_time * (1.0 + time_pre * (1.0 - sigma_time))
+    )
+    r.d_time_pre[...] = d_time_pre
+    first_sum = jnp.sum(d_time_pre, axis=0, keepdims=True)
+    facts = r.facts_all[...]
+    sinus = jnp.concatenate([facts[:, 0], facts[:, 1]], axis=1).astype(bfloat)
+    onehot = (
+        facts[:, 2, 0:1]
+        == lax.broadcasted_iota(jnp.int32, (everyone, CLASSES + 1), 1).astype(single)
+    ).astype(bfloat)
+    highest = lax.Precision.HIGHEST
+
+    def total_of(value):
+        return jnp.sum(jnp.sum(value, axis=1, keepdims=True), axis=0, keepdims=True)
+
+    shared_squares = (
+        total_of(gram(time_act) * gram(dtime))
+        + total_of(gram(sinus) * gram(d_time_pre, highest))
+        + total_of(gram(onehot) * gram(r.d_condition[...], highest))
+        + total_of(first_sum * first_sum)
+    ) / n_model + total_of(column * column) / everyone
+    r.pay[3] = jnp.zeros((8, 128), single)
+    r.pay[3, 0:1] = first_sum[:, 0:128]
+    r.pay[3, 1:2, 0 : rows - 128] = first_sum[:, 128:rows]
+    loop(1, everyone, lambda step: sums_copy(step).wait())
+
+    def add_sums(step, held):
+        return held + r.sums_recv[step]
+
+    chunk = lax.fori_loop(0, everyone, add_sums, jnp.zeros((2, 8, 128), single))
+    r.pay[0:2] = chunk
+    own_squares = total_of(chunk[0] * chunk[0]) + total_of(chunk[1] * chunk[1])
     ff_service(1, 2)
+
+    def ff_squares(at, held):
+        return tuple(
+            one + fold(r.grad_ff[which, at] * r.grad_ff[which, at])
+            for which, one in enumerate(held)
+        )
+
+    block = jnp.zeros((8, units), single)
+    for value in chunks(ff_squares, (block, block, block), 16, rows):
+        own_squares = own_squares + total_of(value)
     qkv_beside()
     out_aside.wait()
-    r["g_out"][x] = (r["g_out"][x].astype(single) + r["x_out"][...].astype(single)).astype(bfloat)
+    r.g_out[x] = (r.g_out[x].astype(single) + r.x_out[...].astype(single)).astype(bfloat)
 
     @pl.when(jnp.logical_not(owner))
     def _():
@@ -1644,22 +1816,22 @@
 
     for step in range(depth - 1):
         qkv_service(step)
-    qkv_near, qkv_far, qkv_on = spread(Sender(r["qa_s"], r["qa_r"]), r["grad_qkv"])
+    qkv_near, qkv_far, qkv_on = spread(Sender(r.qa_s, r.qa_r), r.grad_qkv)
     qkv_far.start()
     qkv_near.start()
-    give = Sender(r["oa_s"], r["oa_r"])
+    give = Sender(r.oa_s, r.oa_r)
     partners = [(d, near_rank), (d, far_rank), (d, lax.rem(near_rank + 2, 4))]
     gives = [
-        give(spot, r["out_mine"], r["out_mine"], partner) for spot, partner in enumerate(partners)
+        give(spot, r.out_mine, r.out_mine, partner) for spot, partner in enumerate(partners)
     ]
 
     @pl.when(owner)
     def _():
-        total = r["g_out"][x].astype(single)
+        total = r.g_out[x].astype(single)
         for step in range(depth - 1):
-            oz(step, r["g_out"].at[x], r["z_out"].at[step], at_dp(up)).wait_recv()
-            total = total + r["z_out"][step].astype(single)
-        r["out_mine"][...] = total.astype(bfloat)
+            oz(step, r.g_out.at[x], r.z_out.at[step], at_dp(up)).wait_recv()
+            total = total + r.z_out[step].astype(single)
+        r.out_mine[...] = total.astype(bfloat)
         for copy in gives:
             copy.start()
 
@@ -1671,7 +1843,23 @@
 
     qkv_far.wait_recv()
     qkv_on.start()
-    r["grad_out"][...] = r["out_mine"][...]
+    r.grad_out[...] = r.out_mine[...]
+    out_float, qkv_float = r.out_mine[...].astype(single), r.grad_qkv[0].astype(single)
+    r.pay[2, 0:1, 0:1] = (
+        r.pay[2, 0:1, 0:1]
+        + shared_squares
+        + own_squares
+        + total_of(out_float * out_float) / n_model
+        + total_of(qkv_float * qkv_float)
+    )
+    r.pay[2, 0:1, 1:2] = r.loss[...]
+    send_late = Sender(r.lt_s, r.lt_r)
+
+    def late_copy(step):
+        return send_late(step - 1, r.pay, r.late.at[me], anyone(step)[1])
+
+    loop(1, everyone, lambda step: late_copy(step).start())
+    r.late[me] = r.pay[...]
 
     @pl.when(owner)
     def _():
@@ -1685,6 +1873,7 @@
     qkv_near.wait()
     qkv_on.wait()
     qkv_far.wait_send()
+    loop(1, everyone, lambda step: late_copy(step).wait())
     for copy in (dm_near, dm_far, dm_on, db_near, db_far, db_on, *third_parts):
         copy.wait_send()
     for step in range(depth):
@@ -1701,29 +1890,26 @@
 def backward_all(values, sizes, total_images, collective):
     n_data, n_model = sizes
     bfloat, single = jnp.bfloat16, jnp.float32
+    everyone = n_data * n_model
     rows = D // n_data
     heads = HEADS // n_model
     head_cols = heads * HDIM
-    length = values["clean"].shape[0]
-    units = values["ff"].shape[2]
+    length = values.clean.shape[0]
+    units = values.ff.shape[2]
     half = units // 2
     depth = n_data // NX
     shapes = dict(
         grad_ff=((3, rows, units), single),
         grad_qkv=((n_model, rows, 3 * head_cols), bfloat),
         grad_out=((rows, D), bfloat),
-        d_modulation=((8, D), single),
-        hidden_sum=((1, D), single),
-        branch_sum=((1, D), single),
-        qkv_sum=((1, 3 * head_cols), single),
-        output_sum=((2, CH), single),
-        loss=((1, 1), single),
-        grad_patch=((CH, D), single),
-        grad_final=((2, CH, D), single),
+        late=((everyone, 4, 8, 128), single),
+        dmod=((8, everyone, D), bfloat),
+        dtime=((everyone, D), bfloat),
+        d_condition=((everyone, rows), single),
+        d_time_pre=((everyone, rows), single),
     )
     vmem, dma = pltpu.VMEM, pltpu.SemaphoreType.DMA
     scratch = dict(
-        mixed=vmem((length, D), single),
         d_end=vmem((length, D), single),
         dm_rows=vmem((n_model, length, D), bfloat),
         db_rows=vmem((n_model, length, D), bfloat),
@@ -1742,6 +1928,18 @@
         x_out=vmem((rows, D), bfloat),
         z_out=vmem((depth - 1, rows, D), bfloat),
         out_mine=vmem((rows, D), bfloat),
+        d_modulation=vmem((8, D), single),
+        local=vmem((56, D), single),
+        sums=vmem((2 * everyone, 8, 128), single),
+        sums_recv=vmem((everyone, 2, 8, 128), single),
+        pay=vmem((4, 8, 128), single),
+        dmod_row=vmem((16, D // 2), bfloat),
+        dmod_all=vmem((everyone, 16, D // 2), bfloat),
+        dmod_wide=vmem((16, D // 2), single),
+        dtime_mine=vmem((everyone, rows), bfloat),
+        dtime_recv=vmem((n_data, everyone, rows), bfloat),
+        dtime_wide=vmem((everyone, D), single),
+        loss=vmem((1, 1), single),
         local_sem=dma((8,)),
     )
     counts = dict(
@@ -1758,12 +1956,17 @@
         oz=(depth - 1,),
         qa=(3,),
         oa=(3,),
+        sm=(everyone - 1,),
+        dl=(everyone - 1,),
+        dt=(n_data - 1,),
+        lt=(everyone - 1,),
     )
     for name, count in counts.items():
         scratch[name + "_s"] = dma(count)
         scratch[name + "_r"] = dma(count)
     far = {
-        "ff", "two_rows", "low", "trig_all", "attended", "one_rows", "qkv_weight", "out_weight"
+        "ff", "two_rows", "low", "trig_all", "attended", "one_rows", "qkv_weight", "out_weight",
+        "mod_weight",
     }
 
     def space(name):
@@ -1771,15 +1974,15 @@
 
     outs = pl.pallas_call(
         functools.partial(back_kernel, sizes, total_images),
-        out_shape=[jax.ShapeDtypeStruct(*shapes[name]) for name in BACK_OUT],
-        in_specs=[space(name) for name in BACK_IN],
-        out_specs=[space(name) for name in BACK_OUT],
-        scratch_shapes=[scratch[name] for name in BACK_SCRATCH],
+        out_shape=[jax.ShapeDtypeStruct(*shapes[name]) for name in BackOut._fields],
+        in_specs=[space(name) for name in BackIn._fields],
+        out_specs=[space(name) for name in BackOut._fields],
+        scratch_shapes=[scratch[name] for name in BackScratch._fields],
         compiler_params=pltpu.CompilerParams(
             collective_id=collective, has_side_effects=True, vmem_limit_bytes=60 * 2**20
         ),
-    )(*[values[name] for name in BACK_IN])
-    return dict(zip(BACK_OUT, outs))
+    )(*values)
+    return BackOut(*outs)
 
 
 def forward_plain(clean_three, noise_three, patch_grid, labels, timesteps, matrices, embeddings, swiglu_weights, biases):
@@ -1808,7 +2011,7 @@
     swiglu_shard = swiglu_weights.astype(bfloat)
     qkv_weight = lax.all_gather(qkv_shard, "dp", axis=0, tiled=True)
     swiglu_use = lax.all_gather(swiglu_shard, "dp", axis=1, tiled=True)
-    out_weight = gather_out(out_shard, sizes)
+    out_weight = gather_out(out_shard)
 
     time_second = matrices[:, :D].astype(bfloat)
     mod_weight = matrices[:, D : 9 * D].astype(bfloat)
@@ -1903,7 +2106,7 @@
     hidden_mid = hidden + gate_one[:, None, :] * branch
     normed_two = modulate(hidden_mid, shift_two, scale_two).astype(bfloat)
     two_rows = gather_rows(normed_two.reshape(length, D), n_model)
-    return dict(
+    return SimpleNamespace(
         steps=sinus_all,
         onehot=onehot,
         time_pre=time_pre,
@@ -1957,7 +2160,7 @@
         ],
         axis=1,
     ).astype(bfloat)
-    values = dict(
+    values = ForwardIn(
         facts=facts,
         trig=jnp.concatenate([cosine, sine], axis=0),
         small=small,
@@ -1989,8 +2192,8 @@
         out_bias=biases[None, 14 * D : 15 * D],
     )
     out = forward_all(values, (n_data, n_model), 0)
-    raw = {name: out[name] for name in BACK_IN if name in out}
-    facts_all = out["facts_all"]
+    raw = {name: getattr(out, name) for name in BackIn._fields if name in ForwardOut._fields}
+    facts_all = out.facts_all
     group = lax.dynamic_slice_in_dim(
         facts_all[:, 2, 1], lax.axis_index("dp") * n_model, n_model
     )
@@ -1999,59 +2202,60 @@
         jnp.where(spots[:, None] == jnp.arange(n_model)[None, :], group[None, :], 0.0), axis=1
     )
     mask = jnp.arange(length, dtype=jnp.int32)[None, None, :] < counts[:, None, None]
-    return dict(
-        raw=dict(raw, noisy=values["noisy"]),
+    return SimpleNamespace(
+        raw=dict(
+            raw,
+            noisy=values.noisy,
+            mod_weight=values.mod_weight,
+            time_second=matrices[:, :D].astype(bfloat),
+        ),
         steps=facts_all[:, :2].reshape(everyone, FREQ).astype(bfloat),
         onehot=(
             facts_all[:, 2, 0:1] == jnp.arange(CLASSES + 1, dtype=jnp.int32)[None].astype(single)
         ).astype(bfloat),
-        time_pre=out["time_pre"],
-        condition=out["condition"],
-        modulation=out["modulation"].reshape(1, 8 * D),
-        hidden=out["hidden"][None],
-        one_rows=out["one_rows"].reshape(n_model * length, D),
-        qkv_weight=out["qkv_weight"],
-        out_weight=out["out_weight"],
-        swiglu=out["ff"],
-        low=out["low"],
-        attended=out["attended"],
-        totals=out["totals"],
-        branch=out["branch"][None],
-        hidden_mid=out["hidden_mid"][None],
-        two_rows=tuple(out["two_rows"]),
-        final_weight=out["small_all"][:, 2 * CH : 4 * CH],
-        tables=(out["trig_all"][:, 0], out["trig_all"][:, 1], mask.astype(single)),
+        time_pre=out.time_pre,
+        condition=out.condition,
+        modulation=out.modulation.reshape(1, 8 * D),
+        hidden=out.hidden[None],
+        one_rows=out.one_rows.reshape(n_model * length, D),
+        qkv_weight=out.qkv_weight,
+        out_weight=out.out_weight,
+        swiglu=out.ff,
+        low=out.low,
+        attended=out.attended,
+        totals=out.totals,
+        branch=out.branch[None],
+        hidden_mid=out.hidden_mid[None],
+        two_rows=tuple(out.two_rows),
+        final_weight=out.small_all[:, 2 * CH : 4 * CH],
+        tables=(out.trig_all[:, 0], out.trig_all[:, 1], mask.astype(single)),
     )
 
 
 def backward_plain(
-    kept, clean_three, noise_three, patch_grid, timesteps, swiglu_weights, biases, total_images
+    kept, clean_three, noise_three, patch_grid, timesteps, biases, total_images
 ):
     bfloat = jnp.bfloat16
     single = jnp.float32
     images, length = clean_three.shape[:2]
     n_model = lax.axis_size("mlp")
     n_data = lax.axis_size("dp")
-    sizes = (n_data, n_model)
     rows = D // n_data
     model_index = lax.axis_index("mlp")
     heads = HEADS // n_model
     head_cols = heads * HDIM
-    hidden_units = swiglu_weights.shape[2]
     valid_slot = valid_slots(patch_grid, length)
     final_bias = biases[15 * D :]
     noisy_low = noisy_input(clean_three, noise_three, timesteps).astype(bfloat)
-    modulation, hidden, hidden_mid, branch = (
-        kept[name] for name in ("modulation", "hidden", "hidden_mid", "branch")
-    )
+    modulation, hidden, hidden_mid, branch = kept.modulation, kept.hidden, kept.hidden_mid, kept.branch
     shift_one, scale_one, gate_one, shift_two, scale_two, gate_two, shift_end, scale_end = (
         jnp.split(modulation, 8, axis=1)
     )
-    qkv_weight, out_weight, swiglu_use = kept["qkv_weight"], kept["out_weight"], kept["swiglu"]
-    final_weight, one_rows, two_rows = kept["final_weight"], kept["one_rows"], kept["two_rows"]
-    low, log_total = kept["low"], kept["totals"]
-    attended_rows = kept["attended"].reshape(n_model * length, head_cols)
-    cosine, sine, mask = kept["tables"]
+    qkv_weight, out_weight, swiglu_use = kept.qkv_weight, kept.out_weight, kept.swiglu
+    final_weight, one_rows, two_rows = kept.final_weight, kept.one_rows, kept.two_rows
+    low, log_total = kept.low, kept.totals
+    attended_rows = kept.attended.reshape(n_model * length, head_cols)
+    cosine, sine, mask = kept.tables
     two_halves = (
         jnp.concatenate(two_rows[:2], axis=0),
         jnp.concatenate(two_rows[2:], axis=0),
@@ -2102,16 +2306,15 @@
     d_normed_two = scatter_rows(d_parts[1], d_parts[0], n_model)[None]
     rows_ready = jnp.concatenate(two_halves, axis=0)
     dmixed_ready = jnp.concatenate(dmixed_halves, axis=0)
-    half = hidden_units // 2
-
-    def owned(gradient, cut):
-        return reduce_dp(gradient.reshape(n_data, rows, -1), n_data, cut)
+
+    def owned(gradient):
+        return reduce_dp(gradient.reshape(n_data, rows, -1))
 
     grad_swiglu = jnp.stack(
         [
-            owned(weight_grad(rows_ready, jnp.concatenate(d_gates, axis=0)), half),
-            owned(weight_grad(rows_ready, jnp.concatenate(d_ups, axis=0)), half),
-            owned(weight_grad(dmixed_ready, jnp.concatenate(acts, axis=0)), half),
+            owned(weight_grad(rows_ready, jnp.concatenate(d_gates, axis=0))),
+            owned(weight_grad(rows_ready, jnp.concatenate(d_ups, axis=0))),
+            owned(weight_grad(dmixed_ready, jnp.concatenate(acts, axis=0))),
         ]
     )
     unused, pull_two = jax.vjp(modulate, hidden_mid, shift_two, scale_two)
@@ -2131,8 +2334,8 @@
         mask,
         heads,
     ).reshape(n_model * length, 3 * head_cols)
-    grad_out = reduce_out(weight_grad(attended_rows, dbranch_rows), sizes)
-    grad_qkv_own = owned(weight_grad(one_rows, d_qkv), 384)
+    grad_out = reduce_out(weight_grad(attended_rows, dbranch_rows))
+    grad_qkv_own = owned(weight_grad(one_rows, d_qkv))
     d_one_part = backward_product(d_qkv, qkv_weight).astype(bfloat).reshape(n_model, length, D)
     d_normed_one = scatter_rows(
         (d_one_part[2], d_one_part[3]), (d_one_part[0], d_one_part[1]), n_model
@@ -2141,7 +2344,7 @@
     d_hidden_part, d_shift_one, d_scale_one = pull_one(d_normed_one)
     d_hidden = (d_hidden_mid + d_hidden_part).astype(bfloat)
 
-    return dict(
+    return SimpleNamespace(
         d_modulation=jnp.concatenate(
             [
                 d_shift_one,
@@ -2168,12 +2371,16 @@
     )
 
 
-def backward_fused(
-    kept, clean_three, noise_three, patch_grid, timesteps, swiglu_weights, biases, total_images
+def finish_fused(
+    kept, clean_three, noise_three, patch_grid, timesteps, states, biases, total_images
 ):
     single = jnp.float32
     length = clean_three.shape[1]
-    sizes = (lax.axis_size("dp"), lax.axis_size("mlp"))
+    n_data, n_model = sizes = (lax.axis_size("dp"), lax.axis_size("mlp"))
+    everyone = n_data * n_model
+    rows = D // n_data
+    head_cols = HEADS // n_model * HDIM
+    owned_start = lax.axis_index("dp") * rows
     beta_now, bar_now, bar_prev = plan(timesteps)
     consts = jnp.stack(
         [
@@ -2185,8 +2392,8 @@
         ],
         axis=1,
     )
-    values = dict(
-        kept["raw"],
+    values = BackIn(
+        **kept.raw,
         final_bias=biases[15 * D :].reshape(2, CH),
         clean=clean_three[0],
         noise=noise_three[0],
@@ -2194,99 +2401,187 @@
         valid=valid_slots(patch_grid, length).astype(single).reshape(length, 1),
     )
     out = backward_all(values, sizes, total_images, 1)
-    return dict(
-        d_modulation=out["d_modulation"].reshape(1, 8 * D),
-        hidden_sum=out["hidden_sum"].reshape(-1),
-        branch_sum=out["branch_sum"].reshape(-1),
-        qkv_sum=out["qkv_sum"].reshape(-1),
-        output_sum=out["output_sum"].reshape(-1),
-        loss=out["loss"].reshape(1),
-        grad_patch=out["grad_patch"],
-        grad_final=out["grad_final"].reshape(2 * CH, D),
-        grad_swiglu=out["grad_ff"],
-        grad_out=out["grad_out"].astype(single),
-        grad_qkv=out["grad_qkv"].astype(single),
-    )
-
-
-def on_device(
-    clean_patches,
-    noise_patches,
-    patch_grid,
-    labels,
-    timesteps,
-    matrices,
-    embeddings,
-    swiglu_weights,
-    biases,
-    matrices_first,
-    embeddings_first,
-    swiglu_first,
-    biases_first,
-    matrices_second,
-    embeddings_second,
-    swiglu_second,
-    biases_second,
-    matrices_average,
-    embeddings_average,
-    swiglu_average,
-    biases_average,
+    grad_time_first = jnp.dot(
+        kept.steps.astype(single).T,
+        out.d_time_pre,
+        precision=lax.Precision.HIGHEST,
+        preferred_element_type=single,
+    )
+    grad_table = jnp.dot(
+        kept.onehot.astype(single).T,
+        out.d_condition,
+        precision=lax.Precision.HIGHEST,
+        preferred_element_type=single,
+    )
+    late = out.late
+    grad_norm = jnp.sqrt(jnp.sum(late[:, 2, 0, 0]))
+    factor = jnp.minimum(1.0, CLIP_LIMIT / grad_norm)
+    tiles = D // 128
+    sums = (
+        late[:, :2]
+        .reshape(2 * everyone, 8, 128)[: 7 * tiles]
+        .reshape(7, tiles, 8, 128)
+        .transpose(0, 2, 1, 3)
+        .reshape(56, D)
+    )
+    first_bias_grad = late.reshape(n_data, n_model, 4, 1024)[:, 0, 3, :rows].reshape(D)
+    qkv_sums = sums[50 : 50 + n_model, : 3 * head_cols].reshape(n_model, 3, head_cols)
+    grad_bias = jnp.concatenate(
+        [
+            sums[48],
+            first_bias_grad,
+            column_sum(out.dtime),
+            jnp.sum(out.dmod.astype(single), axis=1).reshape(-1),
+            qkv_sums.transpose(1, 0, 2).reshape(-1),
+            sums[49],
+            sums[54, : 2 * CH],
+        ]
+    )
+    own = cut_columns(sums[: 3 * CH], owned_start, rows)
+    mats_out = adam_matrices(
+        states,
+        jax.nn.silu(kept.time_pre).astype(jnp.bfloat16),
+        jax.nn.silu(kept.condition).astype(jnp.bfloat16),
+        out.dtime,
+        out.dmod,
+        out.grad_qkv,
+        out.grad_out,
+        jnp.pad(own[CH:].T, ((0, 0), (0, 128 - 2 * CH))),
+        factor.reshape(1, 1),
+        n_model,
+    )
+    return SimpleNamespace(
+        loss_sum=jnp.sum(late[:, 2, 0, 1]),
+        grad_norm=grad_norm,
+        factor=factor,
+        grad_bias=grad_bias,
+        grad_embed=jnp.concatenate([own[:CH], grad_time_first, grad_table], axis=0),
+        grad_swiglu=out.grad_ff,
+        mats_out=mats_out,
+    )
+
+
+def adam_matrices_kernel(
+    n_model,
+    weight_ref,
+    first_ref,
+    second_ref,
+    average_ref,
+    time_act_ref,
+    cond_act_ref,
+    dtime_ref,
+    dmod_ref,
+    qkv_ref,
+    out_ref,
+    final_ref,
+    factor_ref,
+    weight_out,
+    first_out,
+    second_out,
+    average_out,
+    grad_ref,
+):
+    single = jnp.float32
+    block = pl.program_id(0)
+    head_cols = HEADS // n_model * HDIM
+
+    def outer(left, right):
+        return lax.dot_general(left, right, (((0,), (0,)), ((), ())), preferred_element_type=single)
+
+    @pl.when(block == 0)
+    def _():
+        grad_ref[...] = outer(time_act_ref[...], dtime_ref[...])
+
+    @pl.when((block >= 1) & (block < 9))
+    def _():
+        grad_ref[...] = outer(cond_act_ref[...], dmod_ref[0])
+
+    m = lax.axis_index("mlp")
+    for part in range(3):
+
+        @pl.when(block == 9 + part)
+        def _():
+            for rank in range(n_model):
+                apart = (
+                    2 * lax.rem(lax.div(m, 2) + rank // 2, 2)
+                    + lax.rem(lax.rem(m, 2) + rank % 2, 2)
+                )
+                grad_ref[:, rank * head_cols : (rank + 1) * head_cols] = qkv_ref[
+                    apart, :, part * head_cols : (part + 1) * head_cols
+                ].astype(single)
+
+    @pl.when(block == 12)
+    def _():
+        grad_ref[...] = out_ref[...].astype(single)
+
+    @pl.when(block == 13)
+    def _():
+        grad_ref[:, 0:128] = final_ref[...]
+
+    def body(step, carry):
+        at = pl.ds(pl.multiple_of(step * 8, 8), 8)
+        done = adam_step(
+            weight_ref[at],
+            first_ref[at],
+            second_ref[at],
+            grad_ref[at],
+            average_ref[at],
+            factor_ref[...],
+            LEARN_RATE,
+        )
+        for place, value in zip((weight_out, first_out, second_out, average_out), done):
+            place[at] = value
+        return carry
+
+    lax.fori_loop(0, weight_ref.shape[0] // 8, body, 0)
+
+
+def adam_matrices(
+    states, time_act, cond_act, dtime, dmod, grad_qkv, grad_out, grad_final, factor, n_model
+):
+    rows, width = states[0].shape
+    whole = lambda array: pl.BlockSpec(array.shape, lambda i: (0,) * array.ndim)
+    strip = pl.BlockSpec((rows, D), lambda i: (0, i))
+    return pl.pallas_call(
+        functools.partial(adam_matrices_kernel, n_model),
+        grid=(pl.cdiv(width, D),),
+        out_shape=[jax.ShapeDtypeStruct((rows, width), jnp.float32)] * 4,
+        in_specs=[strip] * 4
+        + [whole(time_act), whole(cond_act), whole(dtime)]
+        + [pl.BlockSpec((1, *dmod.shape[1:]), lambda i: (jnp.clip(i - 1, 0, 7), 0, 0))]
+        + [whole(grad_qkv), whole(grad_out), whole(grad_final), whole(factor)],
+        out_specs=[strip] * 4,
+        scratch_shapes=[pltpu.VMEM((rows, D), jnp.float32)],
+        compiler_params=pltpu.CompilerParams(vmem_limit_bytes=KERNEL_VMEM),
+    )(*states, time_act, cond_act, dtime, dmod, grad_qkv, grad_out, grad_final, factor)
+
+
+def finish_plain(
+    kept, clean_three, noise_three, patch_grid, timesteps, states, biases, total_images
 ):
     bfloat = jnp.bfloat16
     single = jnp.float32
-    images = labels.shape[0]
-    length = clean_patches.shape[0] // images
-    n_model = lax.axis_size("mlp")
-    n_data = lax.axis_size("dp")
-    sizes = (n_data, n_model)
-    total_images = images * n_data * n_model
+    matrices, matrices_first, matrices_second, matrices_average = states
+    n_data, n_model = sizes = (lax.axis_size("dp"), lax.axis_size("mlp"))
     rows = D // n_data
     owned_start = lax.axis_index("dp") * rows
-    data_index = lax.axis_index("dp")
     model_index = lax.axis_index("mlp")
-    heads = HEADS // n_model
-    head_cols = heads * HDIM
-    hidden_units = swiglu_weights.shape[2]
-
-    clean_three = clean_patches.reshape(images, length, CH)
-    noise_three = noise_patches.reshape(images, length, CH)
-    fused = (n_data, n_model, images) == (8, 4, 1)
-    forward = forward_fused if fused else forward_plain
-    backward = backward_fused if fused else backward_plain
-    kept = forward(
-        clean_three,
-        noise_three,
-        patch_grid,
-        labels,
-        timesteps,
-        matrices,
-        embeddings,
-        swiglu_weights,
-        biases,
-    )
-    time_pre, condition, onehot, sinus_all = (
-        kept[name] for name in ("time_pre", "condition", "onehot", "steps")
-    )
+    head_cols = HEADS // n_model * HDIM
+    time_pre, condition = kept.time_pre, kept.condition
+    onehot, sinus_all = kept.onehot, kept.steps
     time_act = jax.nn.silu(time_pre).astype(bfloat)
     cond_act = jax.nn.silu(condition).astype(bfloat)
     time_second = matrices[:, :D].astype(bfloat)
     mod_weight = matrices[:, D : 9 * D].astype(bfloat)
 
-    grads = backward(
-        kept,
-        clean_three,
-        noise_three,
-        patch_grid,
-        timesteps,
-        swiglu_weights,
-        biases,
-        total_images,
-    )
-    grad_swiglu, grad_out = grads["grad_swiglu"], grads["grad_out"]
-    grad_qkv_own = grads["grad_qkv"][0]
+    grads = backward_plain(
+        kept, clean_three, noise_three, patch_grid, timesteps, biases, total_images
+    )
+    grad_swiglu, grad_out = grads.grad_swiglu, grads.grad_out
+    grad_qkv_own = grads.grad_qkv[0]
     qkv_stack = jnp.stack(
         [
-            lax.dynamic_index_in_dim(grads["grad_qkv"], model_index ^ rank, 0, keepdims=False)
+            lax.dynamic_index_in_dim(grads.grad_qkv, model_index ^ rank, 0, keepdims=False)
             for rank in range(n_model)
         ]
     )
@@ -2294,7 +2589,7 @@
         qkv_stack.reshape(n_model, rows, 3, head_cols).transpose(1, 2, 0, 3).reshape(rows, 3 * D)
     )
 
-    d_modulation = grads["d_modulation"].astype(bfloat)
+    d_modulation = grads.d_modulation.astype(bfloat)
     (dmod_all,) = exchange(
         [(d_modulation.reshape(16, D // 2), "all")], "both", sizes, 3
     )
@@ -2323,20 +2618,20 @@
         preferred_element_type=single,
     )
 
-    qkv_sums = grads["qkv_sum"].reshape(3, head_cols)
+    qkv_sums = grads.qkv_sum.reshape(3, head_cols)
     qkv_bias_part = lax.dynamic_update_slice(
         jnp.zeros((3, D), single), qkv_sums, (0, model_index * head_cols)
     )
     local_sums = jnp.concatenate(
         [
-            grads["hidden_sum"],
+            grads.hidden_sum,
             qkv_bias_part.reshape(-1),
-            grads["branch_sum"],
-            grads["output_sum"],
-            grads["loss"],
+            grads.branch_sum,
+            grads.output_sum,
+            grads.loss,
             jnp.zeros((95,), single),
-            grads["grad_patch"].reshape(-1),
-            grads["grad_final"].reshape(-1),
+            grads.grad_patch.reshape(-1),
+            grads.grad_final.reshape(-1),
         ]
     )
     everyone = n_data * n_model
@@ -2389,6 +2684,75 @@
     mats_out = adam_step(
         matrices, matrices_first, matrices_second, grad_mats, matrices_average, factor, LEARN_RATE
     )
+    return SimpleNamespace(
+        loss_sum=loss_sum,
+        grad_norm=grad_norm,
+        factor=factor,
+        grad_bias=grad_bias,
+        grad_embed=grad_embed,
+        grad_swiglu=grad_swiglu,
+        mats_out=mats_out,
+    )
+
+
+def on_device(
+    clean_patches,
+    noise_patches,
+    patch_grid,
+    labels,
+    timesteps,
+    matrices,
+    embeddings,
+    swiglu_weights,
+    biases,
+    matrices_first,
+    embeddings_first,
+    swiglu_first,
+    biases_first,
+    matrices_second,
+    embeddings_second,
+    swiglu_second,
+    biases_second,
+    matrices_average,
+    embeddings_average,
+    swiglu_average,
+    biases_average,
+):
+    images = labels.shape[0]
+    length = clean_patches.shape[0] // images
+    n_model = lax.axis_size("mlp")
+    n_data = lax.axis_size("dp")
+    total_images = images * n_data * n_model
+
+    clean_three = clean_patches.reshape(images, length, CH)
+    noise_three = noise_patches.reshape(images, length, CH)
+    fused = (n_data, n_model, images) == (8, 4, 1)
+    forward = forward_fused if fused else forward_plain
+    kept = forward(
+        clean_three,
+        noise_three,
+        patch_grid,
+        labels,
+        timesteps,
+        matrices,
+        embeddings,
+        swiglu_weights,
+        biases,
+    )
+    finish = finish_fused if fused else finish_plain
+    done = finish(
+        kept,
+        clean_three,
+        noise_three,
+        patch_grid,
+        timesteps,
+        (matrices, matrices_first, matrices_second, matrices_average),
+        biases,
+        total_images,
+    )
+    loss_sum, grad_norm, factor = done.loss_sum, done.grad_norm, done.factor
+    grad_embed, grad_swiglu, grad_bias = done.grad_embed, done.grad_swiglu, done.grad_bias
+    mats_out = done.mats_out
     embed_out = adam_step(
         embeddings,
         embeddings_first,

time: 531 us -> 499 us (0.940)
  other arithmetic: 56.2 us -> 26.1 us
  Pallas kernels: 399 us -> 419 us
  matrix products: 12.9 us -> 2.14 us
  between operations: 17.6 us -> 11.4 us
  local copies, waits for them, and re-layouts: 41.4 us -> 35.4 us
    pallas_call x1, Pallas kernels: 201 us -> 240 us  [backward_all(): pl.pallas_call(functools.partial(back_kernel, sizes, total_images), out_s...]
    add x4 -> x3, other arithmetic: 35.9 us -> 8.66 us  [adam_step(): average_decay * average + (1.0 - average_decay) * weight]
    pallas_call x4 -> x1, Pallas kernels: 54.6 us -> 35.5 us  [adam_matrices(): pl.pallas_call(functools.partial(adam_matrices_kernel, n_model), grid=(pl...]
    dot_general x6 -> x2, matrix products: 12.9 us -> 2.14 us  [the longest x1 1.69 us: finish_fused(): jnp.dot(kept.steps.astype(single).T, out.d_time_pre, precision=lax.Precis...]
    reshape x11 -> x6, local copies, waits for them, and re-layouts: 6.96 us -> 1.04 us  [the longest x1 0.67 us: finish_fused(): biases[15 * D:].reshape(2, CH)]
    unnamed x67 -> x53, local copies, waits for them, and re-layouts: 7.27 us -> 12.1 us
where the time goes in v3:
time: 499 us; the launch traced here: 494 us
  Pallas kernels  419 us (84%)
  local copies, waits for them, and re-layouts  35.4 us (7%)
  other arithmetic  26.1 us (5%)
  between operations  11.4 us (2%)
    pallas_call x1, Pallas kernels, backward_all(): pl.pallas_call(functools.partial(back_kernel, sizes, total_images), out_s...  240 us
    pallas_call x1, Pallas kernels, forward_all(): pl.pallas_call(functools.partial(forward_kernel, sizes), out_shape=[jax.S...  143 us
    pallas_call x1, Pallas kernels, adam_matrices(): pl.pallas_call(functools.partial(adam_matrices_kernel, n_model), grid=(pl...  35.5 us
    unnamed x53, local copies, waits for them, and re-layouts  12.1 us

profile of v3, /device:TPU:15, one launch (start us, length us, event | category | flops | bytes accessed | tf_op | source)
XLA Modules:
  0.0 493.7 jit_solution(7177335986985220080)
XLA Ops:
  3.7 1.3 fusion.24
  9.1 1.4 fusion.23
  24.4 1.5 copy.65.refs_8_
  25.8 1.5 copy.66.refs_9_
  27.3 1.3 dynamic-slice_convert_fusion.2
  34.2 3.9 convert.40
  39.6 1.8 slice.150.refs_8_.refs_21_
  43.1 143.4 %shard_map.348 = (f32[32,8,128]{2,1,0:T(8,128)}, f32[4,2,256,72]{3,2,1,0:T(8,128)}, bf16[1152,128]{1,0:T(8,128)(2,1)}, f32[32,144]{1,0:T(8,128)}, f32[32,144]{1,...) custom-call(f32[8,128]{1,0:T(8,128)} %fusion.13.refs_0_, ...), custom_call_target="tpu_custom_call" | custom-call | tf_op jit(solution)/shard_map/pallas_call | solution.py:975
  186.5 239.7 %shard_map.349 = (f32[32,4,8,128]{3,2,1,0:T(8,128)}, bf16[8,32,1152]{2,1,0:T(8,128)(2,1)}, bf16[32,1152]{1,0:T(8,128)(2,1)}, f32[32,144]{1,0:T(8,128)}, f32[32,1...) custom-call(bf16[3,1152,768]{2,1,0:T(8,128)(2,1)} %get-tuple-element.48.refs_0_, ...), custom_call_target="tpu_custom_call" | custom-call | tf_op jit(solution)/shard_map/pallas_call | solution.py:1975
  426.3 1.8 slice_reduce_fusion
  429.0 1.7 slice_reduce_fusion.1
  433.6 1.7 fusion.10
  436.0 1.3 constant_dynamic-update-slice_fusion.6
  437.3 1.3 constant_dynamic-update-slice_fusion.5
  438.6 1.3 constant_dynamic-update-slice_fusion.4
  439.9 1.4 constant_dynamic-update-slice_fusion.3
  441.3 1.3 constant_dynamic-update-slice_fusion.2
  442.7 1.3 constant_dynamic-update-slice_fusion.1
  444.0 1.3 constant_dynamic-update-slice_fusion
  446.3 1.6 multiply_add_fusion.4
  448.4 1.3 concatenate.57
  449.7 3.8 multiply_add_fusion.2
  453.6 3.2 multiply_add_fusion
  456.8 35.5 %shard_map.350 = (f32[144,15008]{1,0:T(8,128)}, f32[144,15008]{1,0:T(8,128)}, f32[144,15008]{1,0:T(8,128)}, f32[144,15008]{1,0:T(8,128)}) custom-call(f32[144,15008]{1,0:T(8,128)} %weight_ref.1, f32[144,15008]{1,0:T(8,128)} %first_ref.1, f32[144,15008]{1,0:T(8,128)} %second_ref.1, f32[144,15008]{1,0:T(8,128)} %average_ref.1, ...), custom_call_target="tpu_custom_call" | custom-call | tf_op jit(solution)/shard_map/pallas_call | solution.py:2545
  (118 shorter events, 26.6 us)
Async XLA Ops:
  0.7 28.8 %copy-start.6 = (f32[1273,144]{0,1:T(8,128)S(1)}, f32[1273,144]{0,1:T(8,128)}, u32[]{:S(2)}) copy-start(f32[1273,144]{0,1:T(8,128)} %param.27) | copy-start | bytes 2199748
  29.4 1.9 copy-start.4
  39.6 1.8 copy-start.5
  186.5 239.8 %copy-start.14 = (f32[32,144]{1,0:T(8,128)S(1)}, f32[32,144]{1,0:T(8,128)}, u32[]{:S(2)}) copy-start(f32[32,144]{1,0:T(8,128)} %get-tuple-element.64.refs_24_) | copy-start | bytes 55300
  186.5 239.8 %copy-start.13 = (f32[32,144]{1,0:T(8,128)S(1)}, f32[32,144]{1,0:T(8,128)}, u32[]{:S(2)}) copy-start(f32[32,144]{1,0:T(8,128)} %get-tuple-element.63.refs_23_) | copy-start | bytes 55300
  426.2 9.0 %copy-start.11 = (f32[32,4,8,128]{3,2,1,0:T(8,128)S(1)}, f32[32,4,8,128]{3,2,1,0:T(8,128)}, u32[]{:S(2)}) copy-start(f32[32,4,8,128]{3,2,1,0:T(8,128)} %get-tuple-element.65) | copy-start | bytes 1572868
  435.3 11.0 %copy-start.12 = (f32[17312]{0:T(1024)S(1)}, f32[17312]{0:T(1024)}, u32[]{:S(2)}) copy-start(f32[17312]{0:T(1024)} %param.29) | copy-start | bytes 207748
  435.5 10.8 %copy-start.15 = (f32[17312]{0:T(1024)S(1)}, f32[17312]{0:T(1024)}, u32[]{:S(2)}) copy-start(f32[17312]{0:T(1024)} %param.41) | copy-start | bytes 207748
  435.5 10.8 %copy-start.16 = (f32[17312]{0:T(1024)S(1)}, f32[17312]{0:T(1024)}, u32[]{:S(2)}) copy-start(f32[17312]{0:T(1024)} %param.33) | copy-start | bytes 207748
  435.5 10.7 %copy-start.17 = (f32[17312]{0:T(1024)S(1)}, f32[17312]{0:T(1024)}, u32[]{:S(2)}) copy-start(f32[17312]{0:T(1024)} %param.37) | copy-start | bytes 207748
  435.6 12.4 %copy-start.18 = (f32[32,144]{1,0:T(8,128)S(1)}, f32[32,144]{1,0:T(8,128)}, u32[]{:S(2)}) copy-start(f32[32,144]{1,0:T(8,128)} %get-tuple-element.72) | copy-start | bytes 55300
  435.6 12.4 %copy-start.19 = (f32[1001]{0:T(1024)S(1)}, f32[1001]{0:T(1024)}, u32[]{:S(2)}) copy-start(f32[1001]{0:T(1024)} %iota_convert_fusion) | copy-start | bytes 12016
  435.6 12.3 %copy-start.20 = (f32[32]{0:T(128)S(1)}, f32[32]{0:T(128)}, u32[]{:S(2)}) copy-start(f32[32]{0:T(128)} %slice_reduce_fusion) | copy-start | bytes 388
  449.7 3.9 copy-start.7
  449.7 3.8 copy-start.8
  449.7 3.8 copy-start.9
  449.7 3.8 copy-start.10
  453.5 3.3 copy-start
  453.5 3.3 copy-start.1
  453.5 3.3 copy-start.2
  453.6 3.2 copy-start.3

commit v4 on v3

--- a/solution.py
+++ b/solution.py
@@ -102,10 +102,8 @@
     clipped = gradient * factor
     first = FIRST_DECAY * first + (1.0 - FIRST_DECAY) * clipped
     second = SECOND_DECAY * second + (1.0 - SECOND_DECAY) * clipped * clipped
-    ratio = (
-        first
-        / (1.0 - FIRST_DECAY**STEP)
-        / (jnp.sqrt(second / (1.0 - SECOND_DECAY**STEP)) + ADAM_EPSILON)
+    ratio = (first * (1.0 / (1.0 - FIRST_DECAY**STEP))) / (
+        jnp.sqrt(second * (1.0 / (1.0 - SECOND_DECAY**STEP))) + ADAM_EPSILON
     )
     weight = weight - rate * (ratio + WEIGHT_DECAY * weight)
     return (weight, first, second, average_decay * average + (1.0 - average_decay) * weight)
@@ -453,14 +451,12 @@
     time_first: Any
     first_bias: Any
     second_bias: Any
-    time_blocks: Any
     class_table: Any
-    mod_weight: Any
+    matrices: Any
     mod_bias: Any
     noisy: Any
     patch_bias: Any
     qkv_shard: Any
-    out_shard: Any
     ff_shard: Any
     qkv_bias: Any
     out_bias: Any
@@ -487,6 +483,8 @@
 
 
 class ForwardScratch(NamedTuple):
+    time_low: Any
+    out_low: Any
     time_send: Any
     time_recv: Any
     mod_send: Any
@@ -505,8 +503,12 @@
     mods_r: Any
     trig_s: Any
     trig_r: Any
-    one_s: Any
-    one_r: Any
+    noisy_s: Any
+    noisy_r: Any
+    kinds_s: Any
+    kinds_r: Any
+    noisy_all: Any
+    kinds_all: Any
     two_s: Any
     two_r: Any
     part_s: Any
@@ -566,7 +568,17 @@
 
     lax.fori_loop(1, everyone, greet, 0)
 
-    load_mod = pltpu.make_async_copy(r.mod_weight, r.mod_low, r.local_sem.at[0])
+    load_out = pltpu.make_async_copy(
+        r.matrices.at[:, pl.ds(12 * D, D)], r.out_low, r.local_sem.at[2]
+    )
+    load_out.start()
+    load_time = pltpu.make_async_copy(
+        r.matrices.at[:, pl.ds(0, D)], r.time_low, r.local_sem.at[3]
+    )
+    load_time.start()
+    load_mod = pltpu.make_async_copy(
+        r.matrices.at[:, pl.ds(D, 8 * D)], r.mod_low, r.local_sem.at[0]
+    )
     load_mod.start()
     own_ff = pltpu.make_async_copy(
         r.ff_shard,
@@ -661,10 +673,25 @@
     trig_near, trig_far, trig_on = spread(Sender(r.trig_s, r.trig_r), r.trig_all)
     trig_near.start()
     trig_far.start()
+    near_rank = m + 1 - 2 * lax.rem(m, 2)
+    partners = ((d, near_rank), (d, lax.rem(m + 2, 4)), (d, lax.rem(near_rank + 2, 4)))
+    send_noisy, send_kinds = Sender(r.noisy_s, r.noisy_r), Sender(r.kinds_s, r.kinds_r)
+    noisy_copies = [
+        send_noisy(spot, r.noisy, r.noisy_all.at[spot + 1], partner)
+        for spot, partner in enumerate(partners)
+    ]
+    kinds_copies = [
+        send_kinds(spot, r.modulation, r.kinds_all.at[spot + 1], partner)
+        for spot, partner in enumerate(partners)
+    ]
+    for copy in noisy_copies:
+        copy.start()
+    r.noisy_all[0] = r.noisy[...]
 
     oz, ox = Sender(r.oz_s, r.oz_r), Sender(r.ox_s, r.ox_r)
     out_place = r.out_weight.at[pl.ds(pl.multiple_of(x * rows, 16), rows)]
     owner = z == m
+    load_out.wait()
 
     def out_along(step):
         return oz(step - 1, out_place, out_place, at_dp(lax.rem(z + step, depth) * NX + x))
@@ -673,34 +700,12 @@
 
     @pl.when(owner)
     def _():
-        r.out_weight[pl.ds(pl.multiple_of(x * rows, 16), rows)] = r.out_shard[...]
+        r.out_weight[pl.ds(pl.multiple_of(x * rows, 16), rows)] = r.out_low[...].astype(bfloat)
         for step in range(1, depth):
             out_along(step).start()
         out_aside.start()
 
-    loop(1, everyone, lambda step: facts_copy(step).wait())
-    facts_all = r.facts_all[...]
-    sinus = jnp.concatenate([facts_all[:, 0], facts_all[:, 1]], axis=1).astype(bfloat)
-    labels = facts_all[:, 2, 0:1]
-    time_pre = (
-        jnp.dot(sinus, r.time_first[...], preferred_element_type=single) + r.first_bias[...]
-    )
-    r.time_pre[...] = time_pre
-    time_act = (time_pre * jax.nn.sigmoid(time_pre)).astype(bfloat)
-    send_time = Sender(r.time_s, r.time_r)
-
-    def time_copy(step):
-        peer = lax.rem(d + step, n_data)
-        return send_time(
-            step - 1, r.time_send.at[peer], r.time_recv.at[d], at_dp(peer)
-        )
-
-    for spot in range(n_data):
-        r.time_send[spot] = jnp.dot(
-            time_act, r.time_blocks[spot], preferred_element_type=single
-        )
-    loop(1, n_data, lambda step: time_copy(step).start())
-    r.time_recv[d] = r.time_send[d]
+
     for part in range(2):
         for which in range(3):
             own = r.ff_shard.at[which, :, pl.ds(half * part, half)]
@@ -711,11 +716,30 @@
                 at_dp(up if part == 0 else down),
             ).start()
             fx((part, 0, which), own, ff_block(d, part, which), at_dp(side)).start()
-    onehot = (
-        labels == lax.broadcasted_iota(jnp.int32, (everyone, CLASSES + 1), 1).astype(single)
-    ).astype(bfloat)
-    picked = jnp.dot(onehot, r.class_table[...], preferred_element_type=single)
-    load_mod.wait()
+
+    loop(1, everyone, lambda step: facts_copy(step).wait())
+    facts_all = r.facts_all[...]
+    sinus = jnp.concatenate([facts_all[:, 0], facts_all[:, 1]], axis=1).astype(bfloat)
+    labels = facts_all[:, 2, 0:1]
+    time_pre = (
+        jnp.dot(sinus, r.time_first[...], preferred_element_type=single) + r.first_bias[...]
+    )
+    r.time_pre[...] = time_pre
+    time_act = (time_pre * jax.nn.sigmoid(time_pre)).astype(bfloat)
+    send_time = Sender(r.time_s, r.time_r)
+
+    def time_copy(step):
+        peer = lax.rem(d + step, n_data)
+        return send_time(
+            step - 1, r.time_send.at[peer], r.time_recv.at[d], at_dp(peer)
+        )
+
+    load_time.wait()
+    time_part = jnp.dot(time_act, r.time_low[...].astype(bfloat), preferred_element_type=single)
+    for spot in range(n_data):
+        r.time_send[spot] = time_part[:, spot * rows : (spot + 1) * rows]
+    loop(1, n_data, lambda step: time_copy(step).start())
+    r.time_recv[d] = r.time_send[d]
 
     def qkv_service(step):
         for part in range(2):
@@ -723,6 +747,13 @@
             if step < depth - 1:
                 qkv_along(step + 1, part).start()
             qkv_aside(step, part).start()
+
+    qkv_service(1)
+    onehot = (
+        labels == lax.broadcasted_iota(jnp.int32, (everyone, CLASSES + 1), 1).astype(single)
+    ).astype(bfloat)
+    picked = jnp.dot(onehot, r.class_table[...], preferred_element_type=single)
+    load_mod.wait()
 
     loop(1, n_data, lambda step: time_copy(step).wait())
     condition = jnp.sum(r.time_recv[...], axis=0) + r.second_bias[...] + picked
@@ -735,7 +766,9 @@
     cond_rank = jnp.dot(pick, cond_act, preferred_element_type=single).astype(bfloat)
     for kind in range(8):
         block = jnp.dot(
-            cond_rank, r.mod_low[:, kind * D : (kind + 1) * D], preferred_element_type=single
+            cond_rank,
+            r.mod_low[:, kind * D : (kind + 1) * D].astype(bfloat),
+            preferred_element_type=single,
         )
         for spot in range(n_data):
             r.mod_send[spot, kind : kind + 1] = block[spot : spot + 1]
@@ -747,7 +780,15 @@
 
     loop(1, n_data, lambda step: mods_copy(step).start())
     r.mod_recv[d] = r.mod_send[d]
-    qkv_service(1)
+    def ff_service(step, which):
+        for part in range(2):
+            ff_along(step, part, which).wait_recv()
+            if step < depth - 1:
+                ff_along(step + 1, part, which).start()
+            ff_aside(step, part, which).start()
+
+    qkv_service(2)
+    ff_service(1, 0)
     loop(1, n_data, lambda step: small_copy(step).wait())
     trig_far.wait_recv()
     trig_on.start()
@@ -768,12 +809,12 @@
     def kind_of(kind):
         return r.modulation[kind : kind + 1]
 
-    r.one_rows[0] = modulate_rows(r.hidden[...], kind_of(0), kind_of(1)).astype(bfloat)
-    one_near, one_far, one_on = spread(Sender(r.one_s, r.one_r), r.one_rows)
-    one_far.start()
-    one_near.start()
-    qkv_service(2)
+    for copy in kinds_copies:
+        copy.start()
+    r.kinds_all[0] = modulation
     qkv_service(3)
+    ff_service(1, 1)
+    ff_service(1, 2)
 
     @pl.when(jnp.logical_not(owner))
     def _():
@@ -782,30 +823,28 @@
         ).wait_recv()
         out_aside.start()
 
-    own_ff.wait()
-
-    def ff_service(step, which):
-        for part in range(2):
-            ff_along(step, part, which).wait_recv()
-            if step < depth - 1:
-                ff_along(step + 1, part, which).start()
-            ff_aside(step, part, which).start()
-
-    ff_service(1, 0)
-    one_far.wait_recv()
-    one_on.start()
     for part in range(2):
         for step in range(depth):
             qkv_aside(step, part).wait_recv()
-    one_near.wait_recv()
-    one_on.wait_recv()
+    for copy in noisy_copies + kinds_copies:
+        copy.wait_recv()
     trig_near.wait_recv()
     trig_on.wait_recv()
-    ff_service(1, 1)
-    ff_service(1, 2)
 
     def image_body(step, carry):
         image = n_model - 1 - step
+        start_rows = (
+            lax.dot_general(
+                r.noisy_all[image],
+                r.small_all[:, 0:CH],
+                (((1,), (1,)), ((), ())),
+                preferred_element_type=single,
+            )
+            + r.patch_bias[...]
+        )
+        r.one_rows[image] = modulate_rows(
+            start_rows, r.kinds_all[image, 0:1], r.kinds_all[image, 1:2]
+        ).astype(bfloat)
         r.qkv[...] = (
             jnp.dot(r.one_rows[image], r.qkv_weight[...], preferred_element_type=single)
             + r.qkv_bias[...]
@@ -847,9 +886,6 @@
         return carry
 
     lax.fori_loop(0, 2, image_body, 0)
-    for which in range(3):
-        ff_service(2, which)
-    lax.fori_loop(2, n_model, image_body, 0)
 
     @pl.when(owner)
     def _():
@@ -859,9 +895,7 @@
     out_aside.wait()
 
     def partial(image):
-        return jnp.dot(
-            r.attended[image], r.out_weight[...], preferred_element_type=single
-        )
+        return jnp.dot(r.attended[image], r.out_weight[...], preferred_element_type=single)
 
     send_part = Sender(r.part_s, r.part_r)
     to_core = send_part(0, r.parts_send.at[0], r.parts_recv.at[0], at_mlp(1))
@@ -869,15 +903,17 @@
     to_near = send_part(2, r.parts_send.at[2], r.parts_recv.at[2], at_mlp(1))
     r.parts_send[0] = partial(3).astype(bfloat)
     to_core.start()
-    second = partial(2)
+    r.branch[...] = partial(2)
     to_core.wait_recv()
-    r.parts_send[1] = (second + r.parts_recv[0].astype(single)).astype(bfloat)
+    r.parts_send[1] = (r.branch[...] + r.parts_recv[0].astype(single)).astype(bfloat)
     to_far.start()
+    for which in range(3):
+        ff_service(2, which)
+    lax.fori_loop(2, n_model, image_body, 0)
     r.parts_send[2] = partial(1).astype(bfloat)
     to_near.start()
     own_part = partial(0) + r.out_bias[...]
-    for which in range(3):
-        ff_service(3, which)
+    ff_service(3, 0)
     to_near.wait_recv()
     to_far.wait_recv()
     branch = own_part + r.parts_recv[2].astype(single) + r.parts_recv[1].astype(single)
@@ -888,9 +924,12 @@
     two_near, two_far, two_on = spread(Sender(r.two_s, r.two_r), r.two_rows)
     two_far.start()
     two_near.start()
+    ff_service(3, 1)
+    ff_service(3, 2)
     two_far.wait_recv()
     two_on.start()
 
+    own_ff.wait()
     for part in range(2):
         for step in range(depth):
             for which in range(3):
@@ -903,7 +942,9 @@
     for copy in (two_near, two_on):
         copy.wait()
     two_far.wait_send()
-    for copy in (trig_near, trig_far, trig_on, one_near, one_far, one_on, to_core, to_far, to_near):
+    for copy in (trig_near, trig_far, trig_on, to_core, to_far, to_near):
+        copy.wait_send()
+    for copy in noisy_copies + kinds_copies:
         copy.wait_send()
 
 
@@ -942,11 +983,15 @@
         time_recv=pltpu.VMEM((n_data, everyone, rows), single),
         mod_send=pltpu.VMEM((n_data, 8, D), single),
         mod_recv=pltpu.VMEM((n_data, 8, D), single),
-        mod_low=pltpu.VMEM((rows, 8 * D), bfloat),
+        mod_low=pltpu.VMEM((rows, 8 * D), single),
+        time_low=pltpu.VMEM((rows, D), single),
+        out_low=pltpu.VMEM((rows, D), single),
         qkv=pltpu.VMEM((length, 3 * head_cols), single),
+        noisy_all=pltpu.VMEM((n_model, length, CH), bfloat),
+        kinds_all=pltpu.VMEM((n_model, 8, D), single),
         parts_send=pltpu.VMEM((3, length, D), bfloat),
         parts_recv=pltpu.VMEM((3, length, D), bfloat),
-        local_sem=dma((2,)),
+        local_sem=dma((4,)),
     )
     counts = dict(
         facts=(everyone - 1,),
@@ -954,7 +999,8 @@
         time=(n_data - 1,),
         mods=(n_data - 1,),
         trig=(3,),
-        one=(3,),
+        noisy=(3,),
+        kinds=(3,),
         two=(3,),
         part=(3,),
         qz=(2, depth - 1),
@@ -967,7 +1013,7 @@
     for name, count in counts.items():
         scratch[name + "_s"] = dma(count)
         scratch[name + "_r"] = dma(count)
-    far = {"mod_weight", "ff_shard", "ff"}
+    far = {"matrices", "ff_shard", "ff"}
 
     def space(name):
         return pl.BlockSpec(memory_space=pl.ANY if name in far else pltpu.VMEM)
@@ -1007,14 +1053,15 @@
     one_rows: Any
     qkv_weight: Any
     out_weight: Any
-    mod_weight: Any
-    time_second: Any
+    matrices: Any
     time_pre: Any
     condition: Any
 
 
 class BackOut(NamedTuple):
-    late: Any
+    bias_rows: Any
+    own: Any
+    stats: Any
     dmod: Any
     dtime: Any
     d_condition: Any
@@ -1025,6 +1072,8 @@
 
 
 class BackScratch(NamedTuple):
+    time_low: Any
+    late: Any
     d_modulation: Any
     local: Any
     sums: Any
@@ -1092,7 +1141,7 @@
     local_sem: Any
 
 
-ROW_CHUNK = 16
+ROW_CHUNK = 64
 
 
 def modulate_back(values, grad, scale_by):
@@ -1235,25 +1284,26 @@
         )
 
     def ff_start(which):
-        for step in range(depth):
+        for step in (3, 1, 2, 0):
             ff_aside(which, step).start()
 
+    def ff_absorb(which, step):
+        ff_aside(which, step).wait_recv()
+        z_spot = lax.rem(z + step, depth)
+        at = block_rows(z_spot, x)
+        r.g_ff[which, at] = (
+            r.g_ff[which, at].astype(single) + r.x_ff[which, z_spot].astype(single)
+        ).astype(bfloat)
+
     def ff_beside(which):
-        for step in range(depth):
-            ff_aside(which, step).wait_recv()
-
-        def body(step, held):
-            at = block_rows(step, x)
-            r.g_ff[which, at] = (
-                r.g_ff[which, at].astype(single) + r.x_ff[which, step].astype(single)
-            ).astype(bfloat)
-            return held
-
-        lax.fori_loop(0, depth, body, 0)
+        ff_absorb(which, 3)
+        ff_absorb(which, 1)
         for part in range(2):
             ff_along(which, 0, part).start()
 
     def ff_service(which, step):
+        if step != 1:
+            ff_absorb(which, 2 - step)
         for part in range(2):
             ff_along(which, step, part).wait_recv()
             lanes = pl.ds(half * part, half)
@@ -1290,22 +1340,21 @@
             at_dp(up if part == 0 else down),
         )
 
+    def qkv_absorb(step):
+        qkv_aside(step).wait_recv()
+        z_spot = lax.rem(z + step, depth)
+        at = block_rows(z_spot, x)
+        r.g_qkv[at] = (r.g_qkv[at].astype(single) + r.x_qkv[z_spot].astype(single)).astype(bfloat)
+
     def qkv_beside():
-        for step in range(depth):
-            qkv_aside(step).wait_recv()
-
-        def body(step, held):
-            at = block_rows(step, x)
-            r.g_qkv[at] = (
-                r.g_qkv[at].astype(single) + r.x_qkv[step].astype(single)
-            ).astype(bfloat)
-            return held
-
-        lax.fori_loop(0, depth, body, 0)
+        qkv_absorb(3)
+        qkv_absorb(1)
         for part in range(2):
             qkv_along(0, part).start()
 
     def qkv_service(step):
+        if step != 1:
+            qkv_absorb(2 - step)
         for part in range(2):
             qkv_along(step, part).wait_recv()
             at = part_rows(target_of(step + 1, part), part)
@@ -1356,8 +1405,8 @@
         r.parts_send[0] = outer(3).astype(bfloat)
         first_parts[0].start()
         r.hold_far[...] = outer(2)
+        add_far(first_parts)
         inner(0)
-        add_far(first_parts)
         r.parts_send[2] = outer(1).astype(bfloat)
         first_parts[2].start()
         r.hold_near[...] = outer(0)
@@ -1463,9 +1512,9 @@
         r.parts_send[0] = outer_back(3).astype(bfloat)
         second_parts[0].start()
         r.hold_far[...] = outer_back(2)
+        add_far(second_parts)
         ff_grad(2, r.dm_rows[...].reshape(2 * wide, D), acts)
         ff_start(2)
-        add_far(second_parts)
         r.parts_send[2] = outer_back(1).astype(bfloat)
         second_parts[2].start()
         r.hold_near[...] = outer_back(0)
@@ -1596,9 +1645,9 @@
         r.parts_send[0] = one_part(3).astype(bfloat)
         third_parts[0].start()
         r.hold_far[...] = one_part(2)
+        add_far(third_parts)
         ff_beside(0)
         ff_service(2, 0)
-        add_far(third_parts)
         r.parts_send[2] = one_part(1).astype(bfloat)
         third_parts[2].start()
         r.hold_near[...] = one_part(0)
@@ -1606,7 +1655,7 @@
         r.g_qkv[...] = dot(
             one_rows[...].reshape(n_model * length, D), flat_grad, ((0,), (0,))
         ).astype(bfloat)
-        for step in range(depth):
+        for step in (3, 1, 2, 0):
             qkv_aside(step).start()
         r.g_out[...] = (
             dot(
@@ -1691,6 +1740,14 @@
     ff_service(1, 0)
     ff_service(0, 1)
     ff_service(2, 2)
+    qkv_beside()
+    out_aside.wait()
+    r.g_out[x] = (r.g_out[x].astype(single) + r.x_out[...].astype(single)).astype(bfloat)
+
+    @pl.when(jnp.logical_not(owner))
+    def _():
+        out_along.start()
+
 
     time_pre, condition = r.time_pre[...], r.condition[...]
     sigma_time, sigma_cond = jax.nn.sigmoid(time_pre), jax.nn.sigmoid(condition)
@@ -1714,8 +1771,14 @@
         )
 
     def conditioning(mod_weight):
-        load = pltpu.make_async_copy(r.mod_weight, mod_weight, r.local_sem.at[0])
+        load = pltpu.make_async_copy(
+            r.matrices.at[:, pl.ds(D, 8 * D)], mod_weight, r.local_sem.at[0]
+        )
         load.start()
+        load_time = pltpu.make_async_copy(
+            r.matrices.at[:, pl.ds(0, D)], r.time_low, r.local_sem.at[1]
+        )
+        load_time.start()
         loop(
             1,
             everyone,
@@ -1725,6 +1788,7 @@
         )
         gathered = r.dmod_all[...].astype(single)
         load.wait()
+        load_time.wait()
         d_cond = jnp.zeros((everyone, rows), single)
         mod_gram = jnp.zeros((everyone, everyone), single)
         bias_squares = jnp.zeros((1, 1), single)
@@ -1734,10 +1798,11 @@
             part = r.dtime_wide[...]
             column = jnp.sum(part, axis=0, keepdims=True)
             bias_squares = bias_squares + jnp.sum(column * column, axis=1, keepdims=True)
+            r.bias_rows[3 + kind : 4 + kind] = column
             part = part.astype(bfloat)
             r.dmod[kind] = part
             d_cond = d_cond + dot(
-                part, mod_weight[:, kind * D : (kind + 1) * D], ((1,), (1,))
+                part, mod_weight[:, kind * D : (kind + 1) * D].astype(bfloat), ((1,), (1,))
             )
             mod_gram = mod_gram + gram(part)
         d_condition = d_cond * (sigma_cond * (1.0 + condition * (1.0 - sigma_cond)))
@@ -1752,17 +1817,20 @@
             + bias_squares / everyone
         )
 
-    pl.run_scoped(conditioning, pltpu.VMEM((rows, 8 * D), bfloat))
+    pl.run_scoped(conditioning, pltpu.VMEM((rows, 8 * D), single))
+    qkv_service(0)
     ff_service(1, 1)
     ff_service(0, 2)
+    qkv_service(1)
     loop(1, n_data, lambda step: dtime_copy(step).wait())
     for spot in range(n_data):
         r.dtime_wide[:, spot * rows : (spot + 1) * rows] = r.dtime_recv[spot].astype(single)
     dtime = r.dtime_wide[...]
     column = jnp.sum(dtime, axis=0, keepdims=True)
+    r.bias_rows[2:3] = column
     dtime = dtime.astype(bfloat)
     r.dtime[...] = dtime
-    d_time_pre = dot(dtime, r.time_second[...], ((1,), (1,))) * (
+    d_time_pre = dot(dtime, r.time_low[...].astype(bfloat), ((1,), (1,))) * (
         sigma_time * (1.0 + time_pre * (1.0 - sigma_time))
     )
     r.d_time_pre[...] = d_time_pre
@@ -1787,35 +1855,8 @@
     r.pay[3] = jnp.zeros((8, 128), single)
     r.pay[3, 0:1] = first_sum[:, 0:128]
     r.pay[3, 1:2, 0 : rows - 128] = first_sum[:, 128:rows]
-    loop(1, everyone, lambda step: sums_copy(step).wait())
-
-    def add_sums(step, held):
-        return held + r.sums_recv[step]
-
-    chunk = lax.fori_loop(0, everyone, add_sums, jnp.zeros((2, 8, 128), single))
-    r.pay[0:2] = chunk
-    own_squares = total_of(chunk[0] * chunk[0]) + total_of(chunk[1] * chunk[1])
     ff_service(1, 2)
-
-    def ff_squares(at, held):
-        return tuple(
-            one + fold(r.grad_ff[which, at] * r.grad_ff[which, at])
-            for which, one in enumerate(held)
-        )
-
-    block = jnp.zeros((8, units), single)
-    for value in chunks(ff_squares, (block, block, block), 16, rows):
-        own_squares = own_squares + total_of(value)
-    qkv_beside()
-    out_aside.wait()
-    r.g_out[x] = (r.g_out[x].astype(single) + r.x_out[...].astype(single)).astype(bfloat)
-
-    @pl.when(jnp.logical_not(owner))
-    def _():
-        out_along.start()
-
-    for step in range(depth - 1):
-        qkv_service(step)
+    qkv_service(2)
     qkv_near, qkv_far, qkv_on = spread(Sender(r.qa_s, r.qa_r), r.grad_qkv)
     qkv_far.start()
     qkv_near.start()
@@ -1831,25 +1872,37 @@
         for step in range(depth - 1):
             oz(step, r.g_out.at[x], r.z_out.at[step], at_dp(up)).wait_recv()
             total = total + r.z_out[step].astype(single)
-        r.out_mine[...] = total.astype(bfloat)
+        total = total.astype(bfloat)
+        r.out_mine[...] = total
+        total = total.astype(single)
+        r.pay[2, 0:1, 2:3] = total_of(total * total)
         for copy in gives:
             copy.start()
 
-    for spot, partner in enumerate(partners):
-
-        @pl.when(z == partner[1])
-        def _():
-            gives[spot].wait_recv()
-
-    qkv_far.wait_recv()
-    qkv_on.start()
-    r.grad_out[...] = r.out_mine[...]
-    out_float, qkv_float = r.out_mine[...].astype(single), r.grad_qkv[0].astype(single)
+    loop(1, everyone, lambda step: sums_copy(step).wait())
+
+    def add_sums(step, held):
+        return held + r.sums_recv[step]
+
+    chunk = lax.fori_loop(0, everyone, add_sums, jnp.zeros((2, 8, 128), single))
+    r.pay[0:2] = chunk
+    own_squares = total_of(chunk[0] * chunk[0]) + total_of(chunk[1] * chunk[1])
+
+    def ff_squares(at, held):
+        return tuple(
+            one + fold(r.grad_ff[which, at] * r.grad_ff[which, at])
+            for which, one in enumerate(held)
+        )
+
+    block = jnp.zeros((8, units), single)
+    for value in chunks(ff_squares, (block, block, block), 16, rows):
+        own_squares = own_squares + total_of(value)
+    qkv_float = r.grad_qkv[0].astype(single)
     r.pay[2, 0:1, 0:1] = (
         r.pay[2, 0:1, 0:1]
         + shared_squares
         + own_squares
-        + total_of(out_float * out_float) / n_model
+        + r.pay[2, 0:1, 2:3]
         + total_of(qkv_float * qkv_float)
     )
     r.pay[2, 0:1, 1:2] = r.loss[...]
@@ -1860,6 +1913,16 @@
 
     loop(1, everyone, lambda step: late_copy(step).start())
     r.late[me] = r.pay[...]
+
+    for spot, partner in enumerate(partners):
+
+        @pl.when(z == partner[1])
+        def _():
+            gives[spot].wait_recv()
+
+    qkv_far.wait_recv()
+    qkv_on.start()
+    r.grad_out[...] = r.out_mine[...]
 
     @pl.when(owner)
     def _():
@@ -1874,6 +1937,38 @@
     qkv_on.wait()
     qkv_far.wait_send()
     loop(1, everyone, lambda step: late_copy(step).wait())
+    for top in range(7):
+        for left in range(tiles):
+            spot = top * tiles + left
+            r.local[8 * top : 8 * top + 8, 128 * left : 128 * left + 128] = r.late[
+                spot // 2, spot % 2
+            ]
+    r.bias_rows[0:1] = r.local[48:49]
+    r.bias_rows[14:15] = r.local[49:50]
+    r.bias_rows[15:16] = r.local[54:55]
+    for spot in range(n_data):
+        first = r.late[spot * n_model, 3]
+        r.bias_rows[1:2, spot * rows : spot * rows + 128] = first[0:1]
+        r.bias_rows[1:2, spot * rows + 128 : (spot + 1) * rows] = first[1:2, 0 : rows - 128]
+    for rank in range(n_model):
+        for part in range(3):
+            r.bias_rows[11 + part : 12 + part, rank * head_cols : (rank + 1) * head_cols] = r.local[
+                50 + rank : 51 + rank, part * head_cols : (part + 1) * head_cols
+            ]
+    for spot in range(n_data):
+
+        @pl.when(d == spot)
+        def _():
+            r.own[...] = r.local[0 : 3 * CH, spot * rows : (spot + 1) * rows]
+
+    totals = lax.fori_loop(
+        0, everyone, lambda step, held: held + r.late[step, 2, 0:1], jnp.zeros((1, 128), single)
+    )
+    norm = jnp.sqrt(totals[:, 0:1])
+    r.stats[...] = jnp.zeros((1, 128), single)
+    r.stats[0:1, 0:1] = norm
+    r.stats[0:1, 1:2] = jnp.minimum(1.0, CLIP_LIMIT / norm)
+    r.stats[0:1, 2:3] = totals[:, 1:2]
     for copy in (dm_near, dm_far, dm_on, db_near, db_far, db_on, *third_parts):
         copy.wait_send()
     for step in range(depth):
@@ -1902,7 +1997,9 @@
         grad_ff=((3, rows, units), single),
         grad_qkv=((n_model, rows, 3 * head_cols), bfloat),
         grad_out=((rows, D), bfloat),
-        late=((everyone, 4, 8, 128), single),
+        bias_rows=((16, D), single),
+        own=((3 * CH, rows), single),
+        stats=((1, 128), single),
         dmod=((8, everyone, D), bfloat),
         dtime=((everyone, D), bfloat),
         d_condition=((everyone, rows), single),
@@ -1928,6 +2025,7 @@
         x_out=vmem((rows, D), bfloat),
         z_out=vmem((depth - 1, rows, D), bfloat),
         out_mine=vmem((rows, D), bfloat),
+        late=vmem((everyone, 4, 8, 128), single),
         d_modulation=vmem((8, D), single),
         local=vmem((56, D), single),
         sums=vmem((2 * everyone, 8, 128), single),
@@ -1940,6 +2038,7 @@
         dtime_recv=vmem((n_data, everyone, rows), bfloat),
         dtime_wide=vmem((everyone, D), single),
         loss=vmem((1, 1), single),
+        time_low=vmem((rows, D), single),
         local_sem=dma((8,)),
     )
     counts = dict(
@@ -1966,7 +2065,7 @@
         scratch[name + "_r"] = dma(count)
     far = {
         "ff", "two_rows", "low", "trig_all", "attended", "one_rows", "qkv_weight", "out_weight",
-        "mod_weight",
+        "matrices",
     }
 
     def space(name):
@@ -1979,7 +2078,7 @@
         out_specs=[space(name) for name in BackOut._fields],
         scratch_shapes=[scratch[name] for name in BackScratch._fields],
         compiler_params=pltpu.CompilerParams(
-            collective_id=collective, has_side_effects=True, vmem_limit_bytes=60 * 2**20
+            collective_id=collective, has_side_effects=True, vmem_limit_bytes=62 * 2**20
         ),
     )(*values)
     return BackOut(*outs)
@@ -2167,9 +2266,8 @@
         time_first=embeddings[CH : CH + FREQ].astype(bfloat),
         first_bias=own_bias(D, rows, owned_start),
         second_bias=own_bias(2 * D, rows, owned_start),
-        time_blocks=matrices[:, :D].astype(bfloat).reshape(rows, n_data, rows).transpose(1, 0, 2),
         class_table=embeddings[CH + FREQ :].astype(bfloat),
-        mod_weight=matrices[:, D : 9 * D].astype(bfloat),
+        matrices=matrices,
         mod_bias=biases[3 * D : 11 * D].reshape(8, D),
         noisy=noisy_input(clean_three, noise_three, timesteps).astype(bfloat)[0],
         patch_bias=biases[None, :D],
@@ -2180,7 +2278,6 @@
             ],
             axis=1,
         ).astype(bfloat),
-        out_shard=matrices[:, 12 * D : 13 * D].astype(bfloat),
         ff_shard=swiglu_weights.astype(bfloat),
         qkv_bias=jnp.concatenate(
             [
@@ -2206,8 +2303,7 @@
         raw=dict(
             raw,
             noisy=values.noisy,
-            mod_weight=values.mod_weight,
-            time_second=matrices[:, :D].astype(bfloat),
+            matrices=matrices,
         ),
         steps=facts_all[:, :2].reshape(everyone, FREQ).astype(bfloat),
         onehot=(
@@ -2377,10 +2473,6 @@
     single = jnp.float32
     length = clean_three.shape[1]
     n_data, n_model = sizes = (lax.axis_size("dp"), lax.axis_size("mlp"))
-    everyone = n_data * n_model
-    rows = D // n_data
-    head_cols = HEADS // n_model * HDIM
-    owned_start = lax.axis_index("dp") * rows
     beta_now, bar_now, bar_prev = plan(timesteps)
     consts = jnp.stack(
         [
@@ -2413,31 +2505,8 @@
         precision=lax.Precision.HIGHEST,
         preferred_element_type=single,
     )
-    late = out.late
-    grad_norm = jnp.sqrt(jnp.sum(late[:, 2, 0, 0]))
-    factor = jnp.minimum(1.0, CLIP_LIMIT / grad_norm)
-    tiles = D // 128
-    sums = (
-        late[:, :2]
-        .reshape(2 * everyone, 8, 128)[: 7 * tiles]
-        .reshape(7, tiles, 8, 128)
-        .transpose(0, 2, 1, 3)
-        .reshape(56, D)
-    )
-    first_bias_grad = late.reshape(n_data, n_model, 4, 1024)[:, 0, 3, :rows].reshape(D)
-    qkv_sums = sums[50 : 50 + n_model, : 3 * head_cols].reshape(n_model, 3, head_cols)
-    grad_bias = jnp.concatenate(
-        [
-            sums[48],
-            first_bias_grad,
-            column_sum(out.dtime),
-            jnp.sum(out.dmod.astype(single), axis=1).reshape(-1),
-            qkv_sums.transpose(1, 0, 2).reshape(-1),
-            sums[49],
-            sums[54, : 2 * CH],
-        ]
-    )
-    own = cut_columns(sums[: 3 * CH], owned_start, rows)
+    grad_norm, factor, loss_sum = (out.stats[0, spot] for spot in range(3))
+    grad_bias = jnp.concatenate([out.bias_rows[:15].reshape(-1), out.bias_rows[15, : 2 * CH]])
     mats_out = adam_matrices(
         states,
         jax.nn.silu(kept.time_pre).astype(jnp.bfloat16),
@@ -2446,16 +2515,16 @@
         out.dmod,
         out.grad_qkv,
         out.grad_out,
-        jnp.pad(own[CH:].T, ((0, 0), (0, 128 - 2 * CH))),
-        factor.reshape(1, 1),
+        jnp.pad(out.own[CH:].T, ((0, 0), (0, 128 - 2 * CH))),
+        out.stats,
         n_model,
     )
     return SimpleNamespace(
-        loss_sum=jnp.sum(late[:, 2, 0, 1]),
+        loss_sum=loss_sum,
         grad_norm=grad_norm,
         factor=factor,
         grad_bias=grad_bias,
-        grad_embed=jnp.concatenate([own[:CH], grad_time_first, grad_table], axis=0),
+        grad_embed=jnp.concatenate([out.own[:CH], grad_time_first, grad_table], axis=0),
         grad_swiglu=out.grad_ff,
         mats_out=mats_out,
     )
@@ -2482,78 +2551,86 @@
     grad_ref,
 ):
     single = jnp.float32
-    block = pl.program_id(0)
     head_cols = HEADS // n_model * HDIM
+    m = lax.axis_index("mlp")
 
     def outer(left, right):
         return lax.dot_general(left, right, (((0,), (0,)), ((), ())), preferred_element_type=single)
 
-    @pl.when(block == 0)
-    def _():
-        grad_ref[...] = outer(time_act_ref[...], dtime_ref[...])
-
-    @pl.when((block >= 1) & (block < 9))
-    def _():
-        grad_ref[...] = outer(cond_act_ref[...], dmod_ref[0])
-
-    m = lax.axis_index("mlp")
-    for part in range(3):
-
-        @pl.when(block == 9 + part)
+    for side in range(2):
+        section = 2 * pl.program_id(0) + side
+        base = side * D
+        lanes = slice(base, base + D)
+
+        @pl.when((section >= 1) & (section < 9))
         def _():
-            for rank in range(n_model):
-                apart = (
-                    2 * lax.rem(lax.div(m, 2) + rank // 2, 2)
-                    + lax.rem(lax.rem(m, 2) + rank % 2, 2)
-                )
-                grad_ref[:, rank * head_cols : (rank + 1) * head_cols] = qkv_ref[
-                    apart, :, part * head_cols : (part + 1) * head_cols
-                ].astype(single)
-
-    @pl.when(block == 12)
-    def _():
-        grad_ref[...] = out_ref[...].astype(single)
-
-    @pl.when(block == 13)
-    def _():
-        grad_ref[:, 0:128] = final_ref[...]
+            grad_ref[:, lanes] = outer(cond_act_ref[...], dmod_ref[jnp.clip(section - 1, 0, 7)])
+
+        if side == 0:
+
+            @pl.when(section == 0)
+            def _():
+                grad_ref[:, lanes] = outer(time_act_ref[...], dtime_ref[...])
+
+            @pl.when(section == 12)
+            def _():
+                grad_ref[:, lanes] = out_ref[...].astype(single)
+
+        else:
+
+            @pl.when(section == 13)
+            def _():
+                grad_ref[:, base : base + 128] = final_ref[...]
+
+        for part in range(3):
+            if (9 + part) % 2 == side:
+
+                @pl.when(section == 9 + part)
+                def _():
+                    for rank in range(n_model):
+                        apart = (
+                            2 * lax.rem(lax.div(m, 2) + rank // 2, 2)
+                            + lax.rem(lax.rem(m, 2) + rank % 2, 2)
+                        )
+                        start = base + rank * head_cols
+                        grad_ref[:, start : start + head_cols] = qkv_ref[
+                            apart, :, part * head_cols : (part + 1) * head_cols
+                        ].astype(single)
 
     def body(step, carry):
-        at = pl.ds(pl.multiple_of(step * 8, 8), 8)
+        at = pl.ds(pl.multiple_of(step * 24, 24), 24)
         done = adam_step(
             weight_ref[at],
             first_ref[at],
             second_ref[at],
             grad_ref[at],
             average_ref[at],
-            factor_ref[...],
+            factor_ref[0:1, 1:2],
             LEARN_RATE,
         )
         for place, value in zip((weight_out, first_out, second_out, average_out), done):
             place[at] = value
         return carry
 
-    lax.fori_loop(0, weight_ref.shape[0] // 8, body, 0)
+    lax.fori_loop(0, weight_ref.shape[0] // 24, body, 0)
 
 
 def adam_matrices(
-    states, time_act, cond_act, dtime, dmod, grad_qkv, grad_out, grad_final, factor, n_model
+    states, time_act, cond_act, dtime, dmod, grad_qkv, grad_out, grad_final, stats, n_model
 ):
     rows, width = states[0].shape
     whole = lambda array: pl.BlockSpec(array.shape, lambda i: (0,) * array.ndim)
-    strip = pl.BlockSpec((rows, D), lambda i: (0, i))
+    strip = pl.BlockSpec((rows, 2 * D), lambda i: (0, i))
+    gradients = (time_act, cond_act, dtime, dmod, grad_qkv, grad_out, grad_final, stats)
     return pl.pallas_call(
         functools.partial(adam_matrices_kernel, n_model),
-        grid=(pl.cdiv(width, D),),
+        grid=(pl.cdiv(width, 2 * D),),
         out_shape=[jax.ShapeDtypeStruct((rows, width), jnp.float32)] * 4,
-        in_specs=[strip] * 4
-        + [whole(time_act), whole(cond_act), whole(dtime)]
-        + [pl.BlockSpec((1, *dmod.shape[1:]), lambda i: (jnp.clip(i - 1, 0, 7), 0, 0))]
-        + [whole(grad_qkv), whole(grad_out), whole(grad_final), whole(factor)],
+        in_specs=[strip] * 4 + [whole(array) for array in gradients],
         out_specs=[strip] * 4,
-        scratch_shapes=[pltpu.VMEM((rows, D), jnp.float32)],
+        scratch_shapes=[pltpu.VMEM((rows, 2 * D), jnp.float32)],
         compiler_params=pltpu.CompilerParams(vmem_limit_bytes=KERNEL_VMEM),
-    )(*states, time_act, cond_act, dtime, dmod, grad_qkv, grad_out, grad_final, factor)
+    )(*states, *gradients)
 
 
 def finish_plain(

time: 499 us -> 444 us (0.89)
  Pallas kernels: 419 us -> 388 us
  local copies, waits for them, and re-layouts: 35.4 us -> 24 us
  other arithmetic: 26.1 us -> 18.7 us
    pallas_call x1, Pallas kernels: 240 us -> 219 us  [backward_all(): pl.pallas_call(functools.partial(back_kernel, sizes, total_images), out_s...]
    unnamed x53 -> x51, local copies, waits for them, and re-layouts: 12.1 us -> 6.57 us
    pallas_call x1, Pallas kernels: 35.5 us -> 30.1 us  [adam_matrices(): pl.pallas_call(functools.partial(adam_matrices_kernel, n_model), grid=(pl...]
where the time goes in v4:
time: 444 us; the launch traced here: 441 us
  Pallas kernels  388 us (87%)
  local copies, waits for them, and re-layouts  24 us (5%)
  other arithmetic  18.7 us (4%)
  between operations  9.45 us (2%)
    pallas_call x1, Pallas kernels, backward_all(): pl.pallas_call(functools.partial(back_kernel, sizes, total_images), out_s...  219 us
    pallas_call x1, Pallas kernels, forward_all(): pl.pallas_call(functools.partial(forward_kernel, sizes), out_shape=[jax.S...  139 us
    pallas_call x1, Pallas kernels, adam_matrices(): pl.pallas_call(functools.partial(adam_matrices_kernel, n_model), grid=(pl...  30.1 us
    add x3, other arithmetic, adam_step(): average_decay * average + (1.0 - average_decay) * weight  10.3 us

profile of v4, /device:TPU:15, one launch (start us, length us, event | category | flops | bytes accessed | tf_op | source)
XLA Modules:
  0.0 440.8 jit_solution(4086911175961321099)
XLA Ops:
  0.7 1.3 fusion.24
  8.2 1.0 multiply_cosine_fusion.1
  9.2 1.0 maximum_maximum_fusion.refs_1_
  10.2 0.9 slice.121
  13.7 0.8 slice.108.refs_6_
  18.5 1.3 dynamic-slice_convert_fusion.2
  19.8 0.8 pad_maximum_fusion.refs_11_
  20.6 0.9 convert_element_type.111.refs_12_
  22.9 139.3 %shard_map.348 = (f32[32,8,128]{2,1,0:T(8,128)}, f32[4,2,256,72]{3,2,1,0:T(8,128)}, bf16[1152,128]{1,0:T(8,128)(2,1)}, f32[32,144]{1,0:T(8,128)}, f32[32,144]{1,...) custom-call(f32[8,128]{1,0:T(8,128)} %fusion.13.refs_0_, ...), custom_call_target="tpu_custom_call" | custom-call | tf_op jit(solution)/shard_map/pallas_call | solution.py:1021
  168.6 218.5 %shard_map.349 = (f32[16,1152]{1,0:T(8,128)}, f32[48,144]{1,0:T(8,128)}, f32[1,128]{1,0:T(1,128)}, bf16[8,32,1152]{2,1,0:T(8,128)(2,1)}, bf16[32,1152]{1,0:T(8,1...) custom-call(bf16[3,1152,768]{2,1,0:T(8,128)(2,1)} %get-tuple-element, ...), custom_call_target="tpu_custom_call" | custom-call | tf_op jit(solution)/shard_map/pallas_call | solution.py:2074
  387.1 1.4 fusion.23
  388.5 0.9 copy.65
  389.5 1.2 copy-done
  390.7 1.1 copy-done.1
  391.8 1.0 copy-done.2
  392.8 0.9 copy-done.3
  394.3 30.1 %shard_map.350 = (f32[144,15008]{1,0:T(8,128)}, f32[144,15008]{1,0:T(8,128)}, f32[144,15008]{1,0:T(8,128)}, f32[144,15008]{1,0:T(8,128)}) custom-call(f32[144,15008]{1,0:T(8,128)} %weight_ref.1, f32[144,15008]{1,0:T(8,128)} %first_ref.1, f32[144,15008]{1,0:T(8,128)} %second_ref.1, f32[144,15008]{1,0:T(8,128)} %average_ref.1, ...), custom_call_target="tpu_custom_call" | custom-call | tf_op jit(solution)/shard_map/pallas_call | solution.py:2625
  424.4 0.8 slice.99
  425.9 0.9 slice.122
  427.1 1.2 slice_reduce_fusion
  428.8 1.2 concatenate.57
  430.1 4.8 %multiply_add_fusion.2 = (f32[1273,144]{0,1:T(8,128)}, f32[1273,144]{0,1:T(8,128)}, f32[1273,144]{0,1:T(8,128)}, f32[1273,144]{0,1:T(8,128)}) fusion(f32[1273,144]{0,1:T(8,128)} %param.39, f32[1273,144]{0,1:T(8,128)S(1)} %copy-done.7, f32[1273,144]{0,1:T(8,128)S(1)} %concatenate.57, f32[]{:T(128)} %bitcast.23, f32[1273,144]{0,1:T(8,128)} %param.31, ...), kind=kLoop, calls=%fused_computation.7 | loop fusion | flops 3482928 | bytes 6599236 | tf_op jit(solution)/shard_map/add | solution.py:109
  435.0 4.0 multiply_add_fusion
  439.1 1.4 multiply_add_fusion.4
  (99 shorter events, 14.5 us)
Async XLA Ops:
  0.7 10.4 %copy-start.6 = (f32[1273,144]{0,1:T(8,128)S(1)}, f32[1273,144]{0,1:T(8,128)}, u32[]{:S(2)}) copy-start(f32[1273,144]{0,1:T(8,128)} %param.27) | copy-start | bytes 2199748
  9.2 3.8 copy-start.12
  11.1 6.0 %copy-start.20 = (f32[256,16]{0,1:T(8,128)S(1)}, f32[256,16]{0,1:T(8,128)}, u32[]{:S(2)}) copy-start(f32[256,16]{0,1:T(8,128)} %param.21) | copy-start | bytes 49156
  11.1 6.0 %copy-start.21 = (f32[256,16]{0,1:T(8,128)S(1)}, f32[256,16]{0,1:T(8,128)}, u32[]{:S(2)}) copy-start(f32[256,16]{0,1:T(8,128)} %param.22) | copy-start | bytes 49156
  13.7 7.0 %copy-start.5 = (f32[3,144,768]{2,1,0:T(8,128)S(1)}, f32[3,144,768]{2,1,0:T(8,128)}, u32[]{:S(2)}) copy-start(f32[3,144,768]{2,1,0:T(8,128)} %param.28) | copy-start | bytes 3981316
  168.6 219.9 %copy-start.15 = (f32[32,144]{1,0:T(8,128)S(1)}, f32[32,144]{1,0:T(8,128)}, u32[]{:S(2)}) copy-start(f32[32,144]{1,0:T(8,128)} %get-tuple-element.65.refs_22_) | copy-start | bytes 55300
  168.6 219.9 %copy-start.14 = (f32[32,144]{1,0:T(8,128)S(1)}, f32[32,144]{1,0:T(8,128)}, u32[]{:S(2)}) copy-start(f32[32,144]{1,0:T(8,128)} %get-tuple-element.66.refs_23_) | copy-start | bytes 55300
  389.5 1.2 copy-start
  390.7 1.1 copy-start.1
  391.8 1.0 copy-start.2
  392.8 0.9 copy-start.3
  393.7 0.6 copy-start.4
  394.3 32.5 %copy-start.23 = (f32[32,144]{1,0:T(8,128)S(1)}, f32[32,144]{1,0:T(8,128)}, u32[]{:S(2)}) copy-start(f32[32,144]{1,0:T(8,128)} %get-tuple-element.74) | copy-start | bytes 55300
  394.3 34.1 %copy-start.22 = (f32[32,144]{1,0:T(8,128)S(1)}, f32[32,144]{1,0:T(8,128)}, u32[]{:S(2)}) copy-start(f32[32,144]{1,0:T(8,128)} %get-tuple-element.75) | copy-start | bytes 55300
  424.4 5.7 %copy-start.7 = (f32[1273,144]{0,1:T(8,128)S(1)}, f32[1273,144]{0,1:T(8,128)}, u32[]{:S(2)}) copy-start(f32[1273,144]{0,1:T(8,128)} %param.27) | copy-start | bytes 2199748
  430.0 4.9 %copy-start.8 = (f32[3,144,768]{2,1,0:T(8,128)S(1)}, f32[3,144,768]{2,1,0:T(8,128)}, u32[]{:S(2)}) copy-start(f32[3,144,768]{2,1,0:T(8,128)} %param.40) | copy-start | bytes 3981316
  430.1 4.9 %copy-start.9 = (f32[3,144,768]{2,1,0:T(8,128)S(1)}, f32[3,144,768]{2,1,0:T(8,128)}, u32[]{:S(2)}) copy-start(f32[3,144,768]{2,1,0:T(8,128)} %param.32) | copy-start | bytes 3981316
  430.1 4.9 %copy-start.10 = (f32[3,144,768]{2,1,0:T(8,128)S(1)}, f32[3,144,768]{2,1,0:T(8,128)}, u32[]{:S(2)}) copy-start(f32[3,144,768]{2,1,0:T(8,128)} %param.36) | copy-start | bytes 3981316
  430.1 4.9 %copy-start.11 = (f32[3,144,768]{2,1,0:T(8,128)S(1)}, f32[3,144,768]{2,1,0:T(8,128)}, u32[]{:S(2)}) copy-start(f32[3,144,768]{2,1,0:T(8,128)} %get-tuple-element.76) | copy-start | bytes 3981316
  435.0 4.0 copy-start.16
  435.0 4.1 copy-start.13
  435.0 4.1 copy-start.17
  435.0 4.1 copy-start.18
  435.0 4.1 copy-start.19

commit v5 on v4

--- a/solution.py
+++ b/solution.py
@@ -5,6 +5,7 @@
 
 import jax
 import jax.numpy as jnp
+import numpy as np
 from jax import lax
 from jax.experimental import pallas as pl
 from jax.experimental.pallas import tpu as pltpu
@@ -31,8 +32,9 @@
 
 def plan(steps_in):
     step_index = jnp.arange(1000, dtype=jnp.int32)
-    beta_table = 0.0001 + (0.02 - 0.0001) * step_index.astype(jnp.float32) / 999.0
-    logbar = jnp.cumsum(jnp.log1p(-beta_table))
+    betas = 0.0001 + (0.02 - 0.0001) * np.arange(1000) / 999.0
+    beta_table = jnp.asarray(betas, jnp.float32)
+    logbar = jnp.asarray(np.cumsum(np.log1p(-betas)), jnp.float32)
 
     def lookup(values, wanted):
         return jnp.sum(
@@ -464,18 +466,18 @@
 
 class ForwardOut(NamedTuple):
     facts_all: Any
-    trig_all: Any
+    trig_all_out: Any
     small_all: Any
     time_pre: Any
     condition: Any
     modulation: Any
     hidden: Any
-    one_rows: Any
-    qkv_weight: Any
-    out_weight: Any
+    one_rows_out: Any
+    qkv_weight_out: Any
+    out_weight_out: Any
     ff: Any
-    low: Any
-    attended: Any
+    low_out: Any
+    attended_out: Any
     totals: Any
     branch: Any
     hidden_mid: Any
@@ -483,6 +485,13 @@
 
 
 class ForwardScratch(NamedTuple):
+    one_rows: Any
+    qkv_weight: Any
+    out_weight: Any
+    low: Any
+    attended: Any
+    trig_all: Any
+    leave_sem: Any
     time_low: Any
     out_low: Any
     time_send: Any
@@ -910,6 +919,21 @@
     for which in range(3):
         ff_service(2, which)
     lax.fori_loop(2, n_model, image_body, 0)
+    leaves = [
+        pltpu.make_async_copy(source, target, r.leave_sem.at[spot])
+        for spot, (source, target) in enumerate(
+            (
+                (r.one_rows, r.one_rows_out),
+                (r.qkv_weight, r.qkv_weight_out),
+                (r.out_weight, r.out_weight_out),
+                (r.low, r.low_out),
+                (r.attended, r.attended_out),
+                (r.trig_all, r.trig_all_out),
+            )
+        )
+    ]
+    for leave in leaves:
+        leave.start()
     r.parts_send[2] = partial(1).astype(bfloat)
     to_near.start()
     own_part = partial(0) + r.out_bias[...]
@@ -930,6 +954,8 @@
     two_on.start()
 
     own_ff.wait()
+    for leave in leaves:
+        leave.wait()
     for part in range(2):
         for step in range(depth):
             for which in range(3):
@@ -960,18 +986,18 @@
     depth = n_data // NX
     shapes = dict(
         facts_all=((everyone, 8, 128), single),
-        trig_all=((n_model, 2, length, HDIM), single),
+        trig_all_out=((n_model, 2, length, HDIM), single),
         small_all=((D, 128), bfloat),
         time_pre=((everyone, rows), single),
         condition=((everyone, rows), single),
         modulation=((8, D), single),
         hidden=((length, D), single),
-        one_rows=((n_model, length, D), bfloat),
-        qkv_weight=((D, 3 * head_cols), bfloat),
-        out_weight=((head_cols, D), bfloat),
+        one_rows_out=((n_model, length, D), bfloat),
+        qkv_weight_out=((D, 3 * head_cols), bfloat),
+        out_weight_out=((head_cols, D), bfloat),
         ff=((3, D, units), bfloat),
-        low=((n_model, length, 3 * head_cols), bfloat),
-        attended=((n_model, length, head_cols), bfloat),
+        low_out=((n_model, length, 3 * head_cols), bfloat),
+        attended_out=((n_model, length, head_cols), bfloat),
         totals=((n_model, length, heads), single),
         branch=((length, D), single),
         hidden_mid=((length, D), single),
@@ -992,6 +1018,7 @@
         parts_send=pltpu.VMEM((3, length, D), bfloat),
         parts_recv=pltpu.VMEM((3, length, D), bfloat),
         local_sem=dma((4,)),
+        leave_sem=dma((6,)),
     )
     counts = dict(
         facts=(everyone - 1,),
@@ -1013,10 +1040,14 @@
     for name, count in counts.items():
         scratch[name + "_s"] = dma(count)
         scratch[name + "_r"] = dma(count)
+    for name in ForwardOut._fields:
+        if name.endswith("_out"):
+            scratch[name[:-4]] = pltpu.VMEM(*shapes[name])
     far = {"matrices", "ff_shard", "ff"}
 
     def space(name):
-        return pl.BlockSpec(memory_space=pl.ANY if name in far else pltpu.VMEM)
+        outside = name in far or name.endswith("_out")
+        return pl.BlockSpec(memory_space=pl.ANY if outside else pltpu.VMEM)
 
     outs = pl.pallas_call(
         functools.partial(forward_kernel, sizes),
@@ -1061,7 +1092,9 @@
 class BackOut(NamedTuple):
     bias_rows: Any
     own: Any
-    stats: Any
+    norm: Any
+    factor: Any
+    loss_sum: Any
     dmod: Any
     dtime: Any
     d_condition: Any
@@ -1738,8 +1771,6 @@
     loop(1, everyone, lambda step: sums_copy(step).start())
     r.sums_recv[me] = r.sums[pl.ds(2 * me, 2)]
     ff_service(1, 0)
-    ff_service(0, 1)
-    ff_service(2, 2)
     qkv_beside()
     out_aside.wait()
     r.g_out[x] = (r.g_out[x].astype(single) + r.x_out[...].astype(single)).astype(bfloat)
@@ -1818,6 +1849,8 @@
         )
 
     pl.run_scoped(conditioning, pltpu.VMEM((rows, 8 * D), single))
+    ff_service(0, 1)
+    ff_service(2, 2)
     qkv_service(0)
     ff_service(1, 1)
     ff_service(0, 2)
@@ -1965,10 +1998,9 @@
         0, everyone, lambda step, held: held + r.late[step, 2, 0:1], jnp.zeros((1, 128), single)
     )
     norm = jnp.sqrt(totals[:, 0:1])
-    r.stats[...] = jnp.zeros((1, 128), single)
-    r.stats[0:1, 0:1] = norm
-    r.stats[0:1, 1:2] = jnp.minimum(1.0, CLIP_LIMIT / norm)
-    r.stats[0:1, 2:3] = totals[:, 1:2]
+    r.norm[...] = norm
+    r.factor[...] = jnp.minimum(1.0, CLIP_LIMIT / norm)
+    r.loss_sum[...] = totals[:, 1:2]
     for copy in (dm_near, dm_far, dm_on, db_near, db_far, db_on, *third_parts):
         copy.wait_send()
     for step in range(depth):
@@ -1999,7 +2031,9 @@
         grad_out=((rows, D), bfloat),
         bias_rows=((16, D), single),
         own=((3 * CH, rows), single),
-        stats=((1, 128), single),
+        norm=((1, 1), single),
+        factor=((1, 1), single),
+        loss_sum=((1, 1), single),
         dmod=((8, everyone, D), bfloat),
         dtime=((everyone, D), bfloat),
         d_condition=((everyone, rows), single),
@@ -2289,7 +2323,8 @@
         out_bias=biases[None, 14 * D : 15 * D],
     )
     out = forward_all(values, (n_data, n_model), 0)
-    raw = {name: getattr(out, name) for name in BackIn._fields if name in ForwardOut._fields}
+    found = {name.removesuffix("_out"): value for name, value in out._asdict().items()}
+    raw = {name: found[name] for name in BackIn._fields if name in found}
     facts_all = out.facts_all
     group = lax.dynamic_slice_in_dim(
         facts_all[:, 2, 1], lax.axis_index("dp") * n_model, n_model
@@ -2313,18 +2348,18 @@
         condition=out.condition,
         modulation=out.modulation.reshape(1, 8 * D),
         hidden=out.hidden[None],
-        one_rows=out.one_rows.reshape(n_model * length, D),
-        qkv_weight=out.qkv_weight,
-        out_weight=out.out_weight,
+        one_rows=out.one_rows_out.reshape(n_model * length, D),
+        qkv_weight=out.qkv_weight_out,
+        out_weight=out.out_weight_out,
         swiglu=out.ff,
-        low=out.low,
-        attended=out.attended,
+        low=out.low_out,
+        attended=out.attended_out,
         totals=out.totals,
         branch=out.branch[None],
         hidden_mid=out.hidden_mid[None],
         two_rows=tuple(out.two_rows),
         final_weight=out.small_all[:, 2 * CH : 4 * CH],
-        tables=(out.trig_all[:, 0], out.trig_all[:, 1], mask.astype(single)),
+        tables=(out.trig_all_out[:, 0], out.trig_all_out[:, 1], mask.astype(single)),
     )
 
 
@@ -2505,7 +2540,7 @@
         precision=lax.Precision.HIGHEST,
         preferred_element_type=single,
     )
-    grad_norm, factor, loss_sum = (out.stats[0, spot] for spot in range(3))
+    grad_norm, factor, loss_sum = (one.reshape(()) for one in (out.norm, out.factor, out.loss_sum))
     grad_bias = jnp.concatenate([out.bias_rows[:15].reshape(-1), out.bias_rows[15, : 2 * CH]])
     mats_out = adam_matrices(
         states,
@@ -2516,7 +2551,7 @@
         out.grad_qkv,
         out.grad_out,
         jnp.pad(out.own[CH:].T, ((0, 0), (0, 128 - 2 * CH))),
-        out.stats,
+        out.factor,
         n_model,
     )
     return SimpleNamespace(
@@ -2605,7 +2640,7 @@
             second_ref[at],
             grad_ref[at],
             average_ref[at],
-            factor_ref[0:1, 1:2],
+            factor_ref[...],
             LEARN_RATE,
         )
         for place, value in zip((weight_out, first_out, second_out, average_out), done):
@@ -2616,12 +2651,12 @@
 
 
 def adam_matrices(
-    states, time_act, cond_act, dtime, dmod, grad_qkv, grad_out, grad_final, stats, n_model
+    states, time_act, cond_act, dtime, dmod, grad_qkv, grad_out, grad_final, factor, n_model
 ):
     rows, width = states[0].shape
     whole = lambda array: pl.BlockSpec(array.shape, lambda i: (0,) * array.ndim)
     strip = pl.BlockSpec((rows, 2 * D), lambda i: (0, i))
-    gradients = (time_act, cond_act, dtime, dmod, grad_qkv, grad_out, grad_final, stats)
+    gradients = (time_act, cond_act, dtime, dmod, grad_qkv, grad_out, grad_final, factor)
     return pl.pallas_call(
         functools.partial(adam_matrices_kernel, n_model),
         grid=(pl.cdiv(width, 2 * D),),
@@ -2629,7 +2664,7 @@
         in_specs=[strip] * 4 + [whole(array) for array in gradients],
         out_specs=[strip] * 4,
         scratch_shapes=[pltpu.VMEM((rows, 2 * D), jnp.float32)],
-        compiler_params=pltpu.CompilerParams(vmem_limit_bytes=KERNEL_VMEM),
+        compiler_params=pltpu.CompilerParams(vmem_limit_bytes=62 * 2**20),
     )(*states, *gradients)
 
 

time: 444 us -> 443 us (level)
  local copies, waits for them, and re-layouts: 24 us -> 17.8 us
    unnamed x51 -> x45, local copies, waits for them, and re-layouts: 6.57 us -> 1.86 us
where the time goes in v5:
time: 443 us; the launch traced here: 438 us
  Pallas kernels  386 us (87%)
  other arithmetic  19.5 us (4%)
  local copies, waits for them, and re-layouts  17.8 us (4%)
  between operations  12.8 us (3%)
    pallas_call x1, Pallas kernels, backward_all(): pl.pallas_call(functools.partial(back_kernel, sizes, total_images), out_s...  218 us
    pallas_call x1, Pallas kernels, forward_all(): pl.pallas_call(functools.partial(forward_kernel, sizes), out_shape=[jax.S...  137 us
    pallas_call x1, Pallas kernels, adam_matrices(): pl.pallas_call(functools.partial(adam_matrices_kernel, n_model), grid=(pl...  31.4 us
    add x3, other arithmetic, adam_step(): average_decay * average + (1.0 - average_decay) * weight  10.3 us

profile of v5, /device:TPU:15, one launch (start us, length us, event | category | flops | bytes accessed | tf_op | source)
XLA Modules:
  0.0 437.8 jit_solution(15517641878785745928)
XLA Ops:
  0.7 1.3 fusion.23
  7.4 0.8 fusion.15
  8.2 1.0 multiply_cosine_fusion.1
  9.2 1.0 maximum_maximum_fusion.refs_1_
  10.2 0.9 slice.92
  13.7 0.8 slice.83.refs_6_
  16.6 0.7 copy.65.refs_9_.refs_12_
  17.9 1.3 dynamic-slice_convert_fusion.2
  19.2 0.8 pad_maximum_fusion.refs_11_
  20.1 0.9 convert_element_type.102.refs_12_
  22.3 136.8 %shard_map.375 = (f32[32,8,128]{2,1,0:T(8,128)}, f32[4,2,256,72]{3,2,1,0:T(8,128)}, bf16[1152,128]{1,0:T(8,128)(2,1)}, f32[32,144]{1,0:T(8,128)}, f32[32,144]{1,...) custom-call(f32[8,128]{1,0:T(8,128)} %fusion.13.refs_0_, ...), custom_call_target="tpu_custom_call" | custom-call | tf_op jit(solution)/shard_map/pallas_call | solution.py:1052
  159.7 0.8 copy.66.refs_8_
  160.5 0.8 copy.67.refs_9_
  165.4 218.2 %shard_map.376 = (f32[16,1152]{1,0:T(8,128)}, f32[48,144]{1,0:T(8,128)}, f32[1,1]{1,0:T(1,128)}, f32[1,1]{1,0:T(1,128)}, f32[1,1]{1,0:T(1,128)}, /*index=5*/bf16...) custom-call(bf16[3,1152,768]{2,1,0:T(8,128)(2,1)} %get-tuple-element, ...), custom_call_target="tpu_custom_call" | custom-call | tf_op jit(solution)/shard_map/pallas_call | solution.py:2108
  385.0 0.9 copy.68
  386.6 31.4 %shard_map.377 = (f32[144,15008]{1,0:T(8,128)}, f32[144,15008]{1,0:T(8,128)}, f32[144,15008]{1,0:T(8,128)}, f32[144,15008]{1,0:T(8,128)}) custom-call(f32[144,15008]{1,0:T(8,128)} %weight_ref.1, f32[144,15008]{1,0:T(8,128)} %first_ref.1, f32[144,15008]{1,0:T(8,128)} %second_ref.1, f32[144,15008]{1,0:T(8,128)} %average_ref.1, ...), custom_call_target="tpu_custom_call" | custom-call | tf_op jit(solution)/shard_map/pallas_call | solution.py:2660
  418.0 0.8 slice.75
  418.9 0.9 slice.93
  419.8 0.9 fusion.10
  420.7 1.2 slice_reduce_fusion
  422.4 1.3 concatenate.57
  423.7 4.9 %multiply_add_fusion.2 = (f32[1273,144]{0,1:T(8,128)}, f32[1273,144]{0,1:T(8,128)}, f32[1273,144]{0,1:T(8,128)}, f32[1273,144]{0,1:T(8,128)}) fusion(f32[1273,144]{0,1:T(8,128)} %param.42, f32[1273,144]{0,1:T(8,128)S(1)} %copy-done.2, f32[1273,144]{0,1:T(8,128)S(1)} %concatenate.57, f32[]{:T(128)} %bitcast.21, f32[1273,144]{0,1:T(8,128)} %param.34, ...), kind=kLoop, calls=%fused_computation.7 | loop fusion | flops 3482928 | bytes 6599236 | tf_op jit(solution)/shard_map/add | solution.py:111
  428.7 4.0 multiply_add_fusion
  432.7 1.4 multiply_add_fusion.4
  (85 shorter events, 11.3 us)
Async XLA Ops:
  0.7 10.4 %copy-start.1 = (f32[1273,144]{0,1:T(8,128)S(1)}, f32[1273,144]{0,1:T(8,128)}, u32[]{:S(2)}) copy-start(f32[1273,144]{0,1:T(8,128)} %param.30) | copy-start | bytes 2199748
  9.2 3.8 copy-start.7
  11.1 4.0 copy-start.19
  11.1 4.0 copy-start.20
  11.1 5.4 %copy-start.15 = (f32[256,16]{0,1:T(8,128)S(1)}, f32[256,16]{0,1:T(8,128)}, u32[]{:S(2)}) copy-start(f32[256,16]{0,1:T(8,128)} %param.24) | copy-start | bytes 49156
  11.1 5.4 %copy-start.16 = (f32[256,16]{0,1:T(8,128)S(1)}, f32[256,16]{0,1:T(8,128)}, u32[]{:S(2)}) copy-start(f32[256,16]{0,1:T(8,128)} %param.25) | copy-start | bytes 49156
  13.7 6.4 %copy-start = (f32[3,144,768]{2,1,0:T(8,128)S(1)}, f32[3,144,768]{2,1,0:T(8,128)}, u32[]{:S(2)}) copy-start(f32[3,144,768]{2,1,0:T(8,128)} %param.31) | copy-start | bytes 3981316
  165.4 218.3 %copy-start.10 = (f32[32,144]{1,0:T(8,128)S(1)}, f32[32,144]{1,0:T(8,128)}, u32[]{:S(2)}) copy-start(f32[32,144]{1,0:T(8,128)} %get-tuple-element.67.refs_22_) | copy-start | bytes 55300
  165.4 218.9 %copy-start.9 = (f32[32,144]{1,0:T(8,128)S(1)}, f32[32,144]{1,0:T(8,128)}, u32[]{:S(2)}) copy-start(f32[32,144]{1,0:T(8,128)} %get-tuple-element.68.refs_23_) | copy-start | bytes 55300
  386.6 33.2 %copy-start.18 = (f32[32,144]{1,0:T(8,128)S(1)}, f32[32,144]{1,0:T(8,128)}, u32[]{:S(2)}) copy-start(f32[32,144]{1,0:T(8,128)} %get-tuple-element.78) | copy-start | bytes 55300
  386.6 35.4 %copy-start.17 = (f32[32,144]{1,0:T(8,128)S(1)}, f32[32,144]{1,0:T(8,128)}, u32[]{:S(2)}) copy-start(f32[32,144]{1,0:T(8,128)} %get-tuple-element.79) | copy-start | bytes 55300
  418.0 5.7 %copy-start.2 = (f32[1273,144]{0,1:T(8,128)S(1)}, f32[1273,144]{0,1:T(8,128)}, u32[]{:S(2)}) copy-start(f32[1273,144]{0,1:T(8,128)} %param.30) | copy-start | bytes 2199748
  423.7 4.9 %copy-start.3 = (f32[3,144,768]{2,1,0:T(8,128)S(1)}, f32[3,144,768]{2,1,0:T(8,128)}, u32[]{:S(2)}) copy-start(f32[3,144,768]{2,1,0:T(8,128)} %param.43) | copy-start | bytes 3981316
  423.7 4.9 %copy-start.4 = (f32[3,144,768]{2,1,0:T(8,128)S(1)}, f32[3,144,768]{2,1,0:T(8,128)}, u32[]{:S(2)}) copy-start(f32[3,144,768]{2,1,0:T(8,128)} %param.35) | copy-start | bytes 3981316
  423.7 4.9 %copy-start.5 = (f32[3,144,768]{2,1,0:T(8,128)S(1)}, f32[3,144,768]{2,1,0:T(8,128)}, u32[]{:S(2)}) copy-start(f32[3,144,768]{2,1,0:T(8,128)} %param.39) | copy-start | bytes 3981316
  423.7 4.9 %copy-start.6 = (f32[3,144,768]{2,1,0:T(8,128)S(1)}, f32[3,144,768]{2,1,0:T(8,128)}, u32[]{:S(2)}) copy-start(f32[3,144,768]{2,1,0:T(8,128)} %get-tuple-element.80) | copy-start | bytes 3981316
  428.6 4.1 copy-start.11
  428.6 4.1 copy-start.8
  428.6 4.1 copy-start.12
  428.6 4.1 copy-start.13
  428.6 4.1 copy-start.14

commit v6 on v5

--- a/solution.py
+++ b/solution.py
@@ -1424,12 +1424,12 @@
             ups[spot] = dot(part, ff[1], ((1,), (0,)))
 
             def body(at, held):
-                at = pl.ds(pl.multiple_of(at.start + which * wide, 32), 32)
+                at = pl.ds(pl.multiple_of(at.start + which * wide, 64), 64)
                 gate = gates[at]
                 acts[at] = (gate * jax.nn.sigmoid(gate) * ups[at]).astype(bfloat)
                 return held
 
-            chunks(body, 0, 32, wide)
+            chunks(body, 0, 64, wide)
 
         def outer(image):
             return dot(acts[image * length : (image + 1) * length], ff[2], ((1,), (1,)))
@@ -1928,7 +1928,7 @@
         )
 
     block = jnp.zeros((8, units), single)
-    for value in chunks(ff_squares, (block, block, block), 16, rows):
+    for value in chunks(ff_squares, (block, block, block), 48, rows):
         own_squares = own_squares + total_of(value)
     qkv_float = r.grad_qkv[0].astype(single)
     r.pay[2, 0:1, 0:1] = (

time: 443 us -> 443 us (level)
  no operation moved by 1% of the time
where the time goes in v6:
time: 443 us; the launch traced here: 438 us
  Pallas kernels  386 us (87%)
  other arithmetic  19.5 us (4%)
  local copies, waits for them, and re-layouts  17.8 us (4%)
  between operations  12.8 us (3%)
    pallas_call x1, Pallas kernels, backward_all(): pl.pallas_call(functools.partial(back_kernel, sizes, total_images), out_s...  218 us
    pallas_call x1, Pallas kernels, forward_all(): pl.pallas_call(functools.partial(forward_kernel, sizes), out_shape=[jax.S...  137 us
    pallas_call x1, Pallas kernels, adam_matrices(): pl.pallas_call(functools.partial(adam_matrices_kernel, n_model), grid=(pl...  31.4 us
    add x3, other arithmetic, adam_step(): average_decay * average + (1.0 - average_decay) * weight  10.3 us

profile of v6, /device:TPU:15, one launch (start us, length us, event | category | flops | bytes accessed | tf_op | source)
XLA Modules:
  0.0 437.7 jit_solution(10906034627427444636)
XLA Ops:
  0.7 1.3 fusion.23
  7.4 0.8 fusion.15
  8.2 1.0 multiply_cosine_fusion.1
  9.2 1.0 maximum_maximum_fusion.refs_1_
  10.2 0.9 slice.92
  13.7 0.8 slice.83.refs_6_
  16.6 0.7 copy.65.refs_9_.refs_12_
  17.9 1.3 dynamic-slice_convert_fusion.2
  19.2 0.8 pad_maximum_fusion.refs_11_
  20.1 0.9 convert_element_type.102.refs_12_
  22.3 136.8 %shard_map.375 = (f32[32,8,128]{2,1,0:T(8,128)}, f32[4,2,256,72]{3,2,1,0:T(8,128)}, bf16[1152,128]{1,0:T(8,128)(2,1)}, f32[32,144]{1,0:T(8,128)}, f32[32,144]{1,...) custom-call(f32[8,128]{1,0:T(8,128)} %fusion.13.refs_0_, ...), custom_call_target="tpu_custom_call" | custom-call | tf_op jit(solution)/shard_map/pallas_call | solution.py:1052
  159.7 0.8 copy.66.refs_8_
  160.5 0.8 copy.67.refs_9_
  165.4 218.1 %shard_map.376 = (f32[16,1152]{1,0:T(8,128)}, f32[48,144]{1,0:T(8,128)}, f32[1,1]{1,0:T(1,128)}, f32[1,1]{1,0:T(1,128)}, f32[1,1]{1,0:T(1,128)}, /*index=5*/bf16...) custom-call(bf16[3,1152,768]{2,1,0:T(8,128)(2,1)} %get-tuple-element, ...), custom_call_target="tpu_custom_call" | custom-call | tf_op jit(solution)/shard_map/pallas_call | solution.py:2108
  384.9 0.9 copy.68
  386.5 31.4 %shard_map.377 = (f32[144,15008]{1,0:T(8,128)}, f32[144,15008]{1,0:T(8,128)}, f32[144,15008]{1,0:T(8,128)}, f32[144,15008]{1,0:T(8,128)}) custom-call(f32[144,15008]{1,0:T(8,128)} %weight_ref.1, f32[144,15008]{1,0:T(8,128)} %first_ref.1, f32[144,15008]{1,0:T(8,128)} %second_ref.1, f32[144,15008]{1,0:T(8,128)} %average_ref.1, ...), custom_call_target="tpu_custom_call" | custom-call | tf_op jit(solution)/shard_map/pallas_call | solution.py:2660
  417.9 0.8 slice.75
  418.8 0.9 slice.93
  419.7 0.9 fusion.10
  420.6 1.2 slice_reduce_fusion
  422.3 1.3 concatenate.57
  423.6 4.9 %multiply_add_fusion.2 = (f32[1273,144]{0,1:T(8,128)}, f32[1273,144]{0,1:T(8,128)}, f32[1273,144]{0,1:T(8,128)}, f32[1273,144]{0,1:T(8,128)}) fusion(f32[1273,144]{0,1:T(8,128)} %param.42, f32[1273,144]{0,1:T(8,128)S(1)} %copy-done.2, f32[1273,144]{0,1:T(8,128)S(1)} %concatenate.57, f32[]{:T(128)} %bitcast.21, f32[1273,144]{0,1:T(8,128)} %param.34, ...), kind=kLoop, calls=%fused_computation.7 | loop fusion | flops 3482928 | bytes 6599236 | tf_op jit(solution)/shard_map/add | solution.py:111
  428.6 4.0 multiply_add_fusion
  432.6 1.4 multiply_add_fusion.4
  (85 shorter events, 11.3 us)
Async XLA Ops:
  0.7 10.4 %copy-start.1 = (f32[1273,144]{0,1:T(8,128)S(1)}, f32[1273,144]{0,1:T(8,128)}, u32[]{:S(2)}) copy-start(f32[1273,144]{0,1:T(8,128)} %param.30) | copy-start | bytes 2199748
  9.2 3.8 copy-start.7
  11.1 4.0 copy-start.19
  11.1 4.0 copy-start.20
  11.1 5.4 %copy-start.15 = (f32[256,16]{0,1:T(8,128)S(1)}, f32[256,16]{0,1:T(8,128)}, u32[]{:S(2)}) copy-start(f32[256,16]{0,1:T(8,128)} %param.24) | copy-start | bytes 49156
  11.1 5.4 %copy-start.16 = (f32[256,16]{0,1:T(8,128)S(1)}, f32[256,16]{0,1:T(8,128)}, u32[]{:S(2)}) copy-start(f32[256,16]{0,1:T(8,128)} %param.25) | copy-start | bytes 49156
  13.7 6.4 %copy-start = (f32[3,144,768]{2,1,0:T(8,128)S(1)}, f32[3,144,768]{2,1,0:T(8,128)}, u32[]{:S(2)}) copy-start(f32[3,144,768]{2,1,0:T(8,128)} %param.31) | copy-start | bytes 3981316
  165.4 218.2 %copy-start.10 = (f32[32,144]{1,0:T(8,128)S(1)}, f32[32,144]{1,0:T(8,128)}, u32[]{:S(2)}) copy-start(f32[32,144]{1,0:T(8,128)} %get-tuple-element.67.refs_22_) | copy-start | bytes 55300
  165.4 218.8 %copy-start.9 = (f32[32,144]{1,0:T(8,128)S(1)}, f32[32,144]{1,0:T(8,128)}, u32[]{:S(2)}) copy-start(f32[32,144]{1,0:T(8,128)} %get-tuple-element.68.refs_23_) | copy-start | bytes 55300
  386.5 33.2 %copy-start.18 = (f32[32,144]{1,0:T(8,128)S(1)}, f32[32,144]{1,0:T(8,128)}, u32[]{:S(2)}) copy-start(f32[32,144]{1,0:T(8,128)} %get-tuple-element.78) | copy-start | bytes 55300
  386.5 35.4 %copy-start.17 = (f32[32,144]{1,0:T(8,128)S(1)}, f32[32,144]{1,0:T(8,128)}, u32[]{:S(2)}) copy-start(f32[32,144]{1,0:T(8,128)} %get-tuple-element.79) | copy-start | bytes 55300
  417.9 5.7 %copy-start.2 = (f32[1273,144]{0,1:T(8,128)S(1)}, f32[1273,144]{0,1:T(8,128)}, u32[]{:S(2)}) copy-start(f32[1273,144]{0,1:T(8,128)} %param.30) | copy-start | bytes 2199748
  423.6 4.9 %copy-start.3 = (f32[3,144,768]{2,1,0:T(8,128)S(1)}, f32[3,144,768]{2,1,0:T(8,128)}, u32[]{:S(2)}) copy-start(f32[3,144,768]{2,1,0:T(8,128)} %param.43) | copy-start | bytes 3981316
  423.6 4.9 %copy-start.4 = (f32[3,144,768]{2,1,0:T(8,128)S(1)}, f32[3,144,768]{2,1,0:T(8,128)}, u32[]{:S(2)}) copy-start(f32[3,144,768]{2,1,0:T(8,128)} %param.35) | copy-start | bytes 3981316
  423.6 4.9 %copy-start.5 = (f32[3,144,768]{2,1,0:T(8,128)S(1)}, f32[3,144,768]{2,1,0:T(8,128)}, u32[]{:S(2)}) copy-start(f32[3,144,768]{2,1,0:T(8,128)} %param.39) | copy-start | bytes 3981316
  423.6 4.9 %copy-start.6 = (f32[3,144,768]{2,1,0:T(8,128)S(1)}, f32[3,144,768]{2,1,0:T(8,128)}, u32[]{:S(2)}) copy-start(f32[3,144,768]{2,1,0:T(8,128)} %get-tuple-element.80) | copy-start | bytes 3981316
  428.5 4.1 copy-start.11
  428.5 4.1 copy-start.8
  428.5 4.1 copy-start.12
  428.5 4.1 copy-start.13
  428.5 4.1 copy-start.14
